TPU v7x, 32 devices: a whole 2x2x4 slice. The times are simulated.
32 devices in a mesh: dp: 2 (over core), ctx: 16 (over z, y, x).
Axes of the slice: x: 2, y: 2, z: 4, core: 2. Of those that a mesh axis runs over, the one named last changes fastest.
Arguments:
- tokens: bfloat16 [8192, 4096], P(('dp', 'ctx')), parts along dimension 0, may hold values from -6 to 19
- positions: int32 [8192], P('dp'), parts along dimension 0, may hold values from 0 to 4095, as said below
- lengths: int32 [64], P('dp'), parts along dimension 0, may hold values from 1 to 384, 4096 in all
- gain: bfloat16 [4096], replicated, may hold values from 0.5 to 1.5
- w_query: bfloat16 [4096, 2048], replicated, may hold values from -0.09375 to 0.09375
- w_key: bfloat16 [4096, 512], replicated, may hold values from -0.09375 to 0.09375
- value_weight: bfloat16 [4096, 512], replicated, may hold values from -0.09375 to 0.09375
Outputs:
- attended: bfloat16 [8192, 2048], P(('dp', 'ctx')), parts along dimension 0
There are 2 independent parts, one for each index of `dp`. A program takes and returns all parts, laid end to end along the dimension named above; an argument that names none is the same for every part. Nothing has to cross between parts.
Inputs may be any that keep to these rules, and one draw needn't show every extreme that they name: positions is a permutation; every aligned block of 256 rows holds exactly 16 positions of each owner j, whose positions are j * 128 to j * 128 + 127 and (2 * 16 - 1 - j) * 128 to (2 * 16 - j) * 128 - 1.
All inputs are finite; a program needn't handle non-finite values.
Results may differ from a plain program's by a relative error of at most 0.012.
The roundings to bfloat16 on the way count: a program that leaves them out, or rounds other values in their place, can miss the bound.
Values may be sent and summed in bfloat16 or wider, within the bound.
No kernel may reach another device: no remote copies, remote signals or barrier semaphores. Data moves between devices by JAX's collectives and lax.ppermute only.
A program may use at most 128 MiB of HBM per device.

v0:
```python
import jax
import jax.numpy as jnp
from jax import lax
from jax.sharding import PartitionSpec as P

HEAD_SIZE = 128


ROPE_THETA = 500000.0
EPSILON = 1e-05


def from_behind(block, axis, distance):
    devices = range(lax.axis_size(axis))
    route = [(i - distance, i) for i in devices if i - distance in devices]
    return lax.ppermute(block, axis, route)


def rope(values, where_at):
    heads = values.shape[1] // HEAD_SIZE
    half = HEAD_SIZE // 2
    shaped = values.reshape(values.shape[0], heads, HEAD_SIZE)
    freq = ROPE_THETA ** (-(jnp.arange(half, dtype=jnp.float32) * 2.0 / HEAD_SIZE))
    angle = where_at.astype(jnp.float32)[:, None, None] * freq[None, None, :]
    cosine = jnp.cos(angle)
    sine = jnp.sin(angle)
    first = shaped[..., :half]
    second = shaped[..., half:]
    turned = jnp.concatenate(
        [first * cosine - second * sine, second * cosine + first * sine], axis=-1
    )
    return turned.reshape(values.shape[0], heads * HEAD_SIZE)


def project(tokens, gain, w_query, w_key, value_weight, where_at):
    floats = tokens.astype(jnp.float32)
    score_scale = lax.rsqrt(jnp.mean(floats * floats, axis=-1, keepdims=True) + EPSILON)
    normed = (floats * score_scale * gain.astype(jnp.float32)).astype(jnp.bfloat16)
    query = rope(jnp.dot(normed, w_query, preferred_element_type=jnp.float32), where_at).astype(
        jnp.bfloat16
    )
    key = rope(jnp.dot(normed, w_key, preferred_element_type=jnp.float32), where_at).astype(
        jnp.bfloat16
    )
    value = jnp.dot(normed, value_weight, preferred_element_type=jnp.float32).astype(jnp.bfloat16)
    return (query, key, value)


def doc_of(where_at, lengths):
    ends = jnp.cumsum(lengths, dtype=jnp.int32)
    return jnp.sum((ends[None, :] <= where_at[:, None]).astype(jnp.int32), axis=1)


def attend(query, key, value, query_at, key_at, key_valid, lengths):
    rows = query.shape[0]
    keys = key.shape[0]
    kv_heads = key.shape[1] // HEAD_SIZE
    group = query.shape[1] // HEAD_SIZE // kv_heads
    query_doc = doc_of(query_at, lengths)
    key_doc = doc_of(key_at, lengths)
    allowed = (
        (key_doc[None, :] == query_doc[:, None])
        & (key_at[None, :] <= query_at[:, None])
        & key_valid[None, :]
    )
    q_heads = query.reshape(rows, kv_heads, group, HEAD_SIZE)
    k_heads = key.reshape(keys, kv_heads, HEAD_SIZE)
    v_heads = value.reshape(keys, kv_heads, HEAD_SIZE)
    scores = jnp.einsum("rhgd,khd->hgrk", q_heads, k_heads, preferred_element_type=jnp.float32) * (
        1.0 / HEAD_SIZE**0.5
    )
    scores = jnp.where(allowed[None, None], scores, jnp.float32(-1e30))
    top = jnp.max(scores, axis=-1, keepdims=True)
    weights = jnp.exp(scores - top)
    total = jnp.sum(weights, axis=-1)
    rounded = weights.astype(jnp.bfloat16)
    mixed = jnp.einsum("hgrk,khd->rhgd", rounded, v_heads, preferred_element_type=jnp.float32)
    mixed = mixed / jnp.transpose(total, (2, 0, 1))[..., None]
    return mixed.reshape(rows, kv_heads * group * HEAD_SIZE).astype(jnp.bfloat16)


def zig_positions(owner, rows, cycle_size):
    inner = jnp.arange(rows, dtype=jnp.int32)
    half_rows = rows // 2
    return jnp.where(
        inner < half_rows,
        owner * half_rows + inner,
        (2 * cycle_size - 1 - owner) * half_rows + inner - half_rows,
    )


def block_at(first, count):
    return first * count + jnp.arange(count, dtype=jnp.int32)


def inside(source, count, cycle_size):
    return jnp.broadcast_to((source >= 0) & (source < cycle_size), (count,))


def attend_pieces(query, query_at, pieces, key_at, key_valid, lengths, kv_width):
    all_kv = jnp.concatenate(pieces, axis=0)
    where_keys = jnp.concatenate(key_at, axis=0)
    valid_keys = jnp.concatenate(key_valid, axis=0)
    return attend(
        query, all_kv[:, :kv_width], all_kv[:, kv_width:], query_at, where_keys, valid_keys, lengths
    )


def shards(tokens, positions, lengths, gain, w_query, w_key, value_weight):
    cycle_size = lax.axis_size("ctx")
    device = lax.axis_index("ctx")
    rows = tokens.shape[0]
    half_rows = rows // 2
    per_peer = rows // cycle_size
    total_rows = rows * cycle_size

    def owner_of(where_at):
        block_id = where_at // half_rows
        return jnp.minimum(block_id, 2 * cycle_size - 1 - block_id)

    mine = lax.dynamic_slice_in_dim(positions, device * rows, rows, 0)
    send_order = jnp.argsort(owner_of(mine) * total_rows + mine)
    table = positions.reshape(cycle_size, rows)
    marked = jnp.where(owner_of(table) == device, table, total_rows)
    arrived = jnp.sort(marked, axis=1)[:, :per_peer].reshape(rows)
    slot_of = jnp.where(
        arrived // half_rows == device,
        arrived - device * half_rows,
        arrived - (2 * cycle_size - 1 - device) * half_rows + half_rows,
    )
    placing = jnp.argsort(slot_of)
    local_at = zig_positions(device, rows, cycle_size)
    kv_width = w_key.shape[1]
    outgoing = tokens[send_order].reshape(cycle_size, per_peer, tokens.shape[1])
    received = lax.all_to_all(outgoing, "ctx", split_axis=0, concat_axis=0, tiled=True).reshape(
        rows, tokens.shape[1]
    )[placing]
    query, key, value = project(received, gain, w_query, w_key, value_weight, local_at)
    kv_local = jnp.concatenate([key, value], axis=1)
    early_kv = kv_local[:half_rows]
    late_kv = kv_local[half_rows:]
    below_kv = []
    for offset in (1, 2, 3):
        below_kv.append(from_behind(early_kv, "ctx", offset))
    above_kv = []
    for offset in (1, 2):
        above_kv.append(from_behind(kv_local, "ctx", -offset))
    above_far = from_behind(late_kv, "ctx", -3)
    early_from = [device, device - 1, device - 2, device - 3]
    early_out = attend_pieces(
        query[:half_rows],
        local_at[:half_rows],
        [early_kv] + below_kv,
        [block_at(source, half_rows) for source in early_from],
        [inside(source, half_rows, cycle_size) for source in early_from],
        lengths,
        kv_width,
    )
    late_pieces = [kv_local, below_kv[0], below_kv[1], above_kv[0], above_kv[1], above_far]
    late_where = [
        local_at,
        block_at(device - 1, half_rows),
        block_at(device - 2, half_rows),
        zig_positions(device + 1, rows, cycle_size),
        zig_positions(device + 2, rows, cycle_size),
        block_at(2 * cycle_size - 4 - device, half_rows),
    ]
    late_valid = [
        inside(device, rows, cycle_size),
        inside(device - 1, half_rows, cycle_size),
        inside(device - 2, half_rows, cycle_size),
        inside(device + 1, rows, cycle_size),
        inside(device + 2, rows, cycle_size),
        inside(device + 3, half_rows, cycle_size),
    ]
    late_out = attend_pieces(
        query[half_rows:],
        local_at[half_rows:],
        late_pieces,
        late_where,
        late_valid,
        lengths,
        kv_width,
    )
    attended = jnp.concatenate([early_out, late_out], axis=0)
    return attended


def solution(mesh):
    in_specs = (P(("dp", "ctx"), None), P("dp"), P("dp"), P(), P(), P(), P())
    out_specs = P(("dp", "ctx"), None)
    return jax.shard_map(shards, mesh=mesh, in_specs=in_specs, out_specs=out_specs, check_vma=False)
```

profile of v0, /device:TPU:4, one launch (start us, length us, event | category | flops | bytes accessed | tf_op | source)
XLA Modules:
  0.0 155.9 jit_solution(5483815959499735756)
XLA Ops:
  7.5 3.2 %sort.39 = (s32[256]{0:T(256)}, s32[256]{0:T(256)S(1)}) sort(s32[256]{0:T(256)S(1)} %fusion.42, s32[256]{0:T(256)S(1)} %iota.53), dimensions={0}, to_apply=%region_0.1 | sort | flops 2048 | bytes 4096 | tf_op jit(solution)/shard_map/jit(argsort)/sort | solution.py:122
  10.6 3.2 %gather_fusion = bf16[256,4096]{1,0:T(8,128)(2,1)} fusion(bf16[256,4096]{1,0:T(8,128)(2,1)S(1)} %copy-done, s32[1024]{0:T(1024)S(1)} %pad_clamp_fusion.1), kind=kCustom, calls=%fused_computation | custom fusion | bytes 4195328 | tf_op jit(solution)/shard_map/gather | solution.py:134
  13.9 7.4 %all-to-all-start = ((bf16[16,16,4096]{2,1,0:T(8,128)(2,1)}), bf16[16,16,4096]{2,1,0:T(8,128)(2,1)S(1)}, u32[]{:S(2)}, u32[]{:S(2)}) async-start(bf16[16,16,4096]{2,1,0:T(8,128)(2,1)} %bitcast.62), calls=%async_computation | async-start | bytes 4194304 | tf_op jit(solution)/shard_map/all_to_all | solution.py:135
  24.8 2.5 %sort.43.cloned.1.call-done = s32[16,256]{1,0:T(8,128)} async-done(((s32[16,256]{1,0:T(8,128)}), s32[16,256]{1,0:T(8,128)}) %sort.43.cloned.1.call-update) | async-done | bytes 16400 | tf_op jit(solution)/shard_map/jit(sort)/sort | solution.py:125
  28.1 3.2 %sort.41 = (s32[256]{0:T(256)}, s32[256]{0:T(256)S(1)}) sort(s32[256]{0:T(256)S(1)} %get-tuple-element.34, s32[256]{0:T(256)S(1)} %iota.54), dimensions={0}, to_apply=%region_2.3 | sort | flops 2048 | bytes 4096 | tf_op jit(solution)/shard_map/jit(argsort)/sort | solution.py:131
  32.5 33.2 %all-to-all-done = bf16[16,16,4096]{2,1,0:T(8,128)(2,1)S(1)} async-done(((bf16[16,16,4096]{2,1,0:T(8,128)(2,1)}), bf16[16,16,4096]{2,1,0:T(8,128)(2,1)S(1)}, u32[]{:S(2)}, u32[]{:S(2)}) %all-to-all-start) | async-done | bytes 2097184 | tf_op jit(solution)/shard_map/all_to_all | solution.py:135
  65.7 3.2 %gather_fusion.1 = bf16[256,4096]{1,0:T(8,128)(2,1)} fusion(bf16[256,4096]{1,0:T(8,128)(2,1)S(1)} %bitcast.60, s32[1024]{0:T(1024)S(1)} %pad_clamp_fusion), kind=kCustom, calls=%fused_computation.1 | custom fusion | bytes 4195328 | tf_op jit(solution)/shard_map/gather | solution.py:135
  68.9 2.1 %fusion.5 = f32[256]{0:T(256)S(1)} fusion(bf16[256,4096]{1,0:T(8,128)(2,1)} %gather_fusion.1), kind=kLoop, calls=%fused_computation.10 | loop fusion | flops 3145472 | bytes 2098176 | tf_op jit(solution)/shard_map/reduce_sum | solution.py:37
  71.0 5.0 %convolution_convert_fusion = bf16[256,512]{1,0:T(8,128)(2,1)} fusion(bf16[4096,512]{1,0:T(8,128)(2,1)} %param.13, bf16[256,4096]{1,0:T(8,128)(2,1)} %gather_fusion.1, f32[4096]{0:T(1024)S(1)} %convert_element_type.57, f32[256]{0:T(256)S(1)} %add_rsqrt_fusion), kind=kOutput, calls=%fused_computation.28 | convolution fusion | flops 1078067200 | bytes 6571008 | tf_op jit(solution)/shard_map/dot_general | solution.py:45
  76.0 2.1 %fusion.48 = f32[256,512]{1,0:T(8,128)} fusion(bf16[4096,512]{1,0:T(8,128)(2,1)S(1)} %copy-done.11, bf16[256,4096]{1,0:T(8,128)(2,1)S(1)} %copy-done.2, f32[4096]{0:T(1024)S(1)} %convert_element_type.57, f32[256]{0:T(256)S(1)} %add_rsqrt_fusion), kind=kOutput, calls=%fused_computation.112 | convolution fusion | flops 1077936128 | bytes 6833152 | tf_op jit(solution)/shard_map/dot_general | solution.py:42
  81.0 6.8 %collective-permute-start.2 = (bf16[128,1024]{1,0:T(8,128)(2,1)S(1)}, bf16[128,1024]{1,0:T(8,128)(2,1)S(1)}, u32[]{:S(2)}, u32[]{:S(2)}) collective-permute-start(bf16[128,1024]{1,0:T(8,128)(2,1)S(1)} %get-tuple-element.22), channel_id=1, source_target_pairs={{0,3},{1,4},{2,5},{3,6},{4,7},{5,8},{6,9},{7,10},{8,11},{9,12},{10... | collective-permute-start | bytes 786440 | tf_op jit(solution)/shard_map/ppermute | solution.py:16
  87.8 4.2 %collective-permute-start.1 = (bf16[128,1024]{1,0:T(8,128)(2,1)S(1)}, bf16[128,1024]{1,0:T(8,128)(2,1)S(1)}, u32[]{:S(2)}, u32[]{:S(2)}) collective-permute-start(bf16[128,1024]{1,0:T(8,128)(2,1)S(1)} %get-tuple-element.22), channel_id=1, source_target_pairs={{0,2},{1,3},{2,4},{3,5},{4,6},{5,7},{6,8},{7,9},{8,10},{9,11},{10,... | collective-permute-start | bytes 786440 | tf_op jit(solution)/shard_map/ppermute | solution.py:16
  92.1 2.6 %collective-permute-start = (bf16[128,1024]{1,0:T(8,128)(2,1)S(1)}, bf16[128,1024]{1,0:T(8,128)(2,1)S(1)}, u32[]{:S(2)}, u32[]{:S(2)}) collective-permute-start(bf16[128,1024]{1,0:T(8,128)(2,1)S(1)} %get-tuple-element.22), channel_id=1, source_target_pairs={{0,1},{1,2},{2,3},{3,4},{4,5},{5,6},{6,7},{7,8},{8,9},{9,10},{10,1... | collective-permute-start | bytes 786440 | tf_op jit(solution)/shard_map/ppermute | solution.py:16
  95.8 4.1 %collective-permute-start.3 = (bf16[256,1024]{1,0:T(8,128)(2,1)}, bf16[256,1024]{1,0:T(8,128)(2,1)}, u32[]{:S(2)}, u32[]{:S(2)}) collective-permute-start(bf16[256,1024]{1,0:T(8,128)(2,1)} %get-tuple-element.23), channel_id=1, source_target_pairs={{1,0},{2,1},{3,2},{4,3},{5,4},{6,5},{7,6},{8,7},{9,8},{10,9},{11,1... | collective-permute-start | bytes 1572872 | tf_op jit(solution)/shard_map/ppermute | solution.py:16
  99.9 2.1 %collective-permute-start.4 = (bf16[256,1024]{1,0:T(8,128)(2,1)}, bf16[256,1024]{1,0:T(8,128)(2,1)}, u32[]{:S(2)}, u32[]{:S(2)}) collective-permute-start(bf16[256,1024]{1,0:T(8,128)(2,1)} %get-tuple-element.23), channel_id=1, source_target_pairs={{2,0},{3,1},{4,2},{5,3},{6,4},{7,5},{8,6},{9,7},{10,8},{11,9},{12,... | collective-permute-start | bytes 1572872 | tf_op jit(solution)/shard_map/ppermute | solution.py:16
  102.0 8.2 %convolution_bitcast_fusion = f32[32,8,16,128]{3,1,2,0:T(8,128)S(1)} fusion(bf16[4096,2048]{1,0:T(8,128)(2,1)} %param.11, bf16[256,4096]{1,0:T(8,128)(2,1)S(1)} %copy-done.2, f32[4096]{0:T(1024)S(1)} %convert_element_type.57, f32[256]{0:T(256)S(1)} %add_rsqrt_fusion), kind=kOutput, calls=%fused_computation.25 | convolution fusion | flops 4299161600 | bytes 20988928 | tf_op jit(solution)/shard_map/dot_general | solution.py:39
  120.0 1.9 %constant_dynamic-update-slice_fusion.2 = bf16[1152,1024]{1,0:T(8,128)(2,1)} fusion(bf16[1152,1024]{1,0:T(8,128)(2,1)} %constant_dynamic-update-slice_fusion.3, bf16[256,1024]{1,0:T(8,128)(2,1)} %collective-permute-done.3), kind=kLoop, calls=%fused_computation.72 | loop fusion | bytes 1048576
  121.9 10.1 %collective-permute-done.4 = bf16[256,1024]{1,0:T(8,128)(2,1)} collective-permute-done((bf16[256,1024]{1,0:T(8,128)(2,1)}, bf16[256,1024]{1,0:T(8,128)(2,1)}, u32[]{:S(2)}, u32[]{:S(2)}) %collective-permute-start.4) | collective-permute-done | bytes 524320 | tf_op jit(solution)/shard_map/ppermute | solution.py:16
  132.0 1.9 %constant_dynamic-update-slice_fusion.1 = bf16[1152,1024]{1,0:T(8,128)(2,1)} fusion(bf16[1152,1024]{1,0:T(8,128)(2,1)} %constant_dynamic-update-slice_fusion.2, bf16[256,1024]{1,0:T(8,128)(2,1)} %collective-permute-done.4), kind=kLoop, calls=%fused_computation.71 | loop fusion | bytes 1048576
  134.6 2.8 %fusion.50 = (bf16[1152,512]{1,0:T(8,128)(2,1)}, bf16[1152,512]{1,0:T(8,128)(2,1)S(1)}) fusion(bf16[1152,1024]{1,0:T(8,128)(2,1)} %constant_dynamic-update-slice_fusion), kind=kLoop, calls=%fused_computation.113 | loop fusion | bytes 4718592 | tf_op jit(solution)/shard_map/slice | solution.py:105
  137.4 2.5 %reshape.314 = bf16[1152,4,128]{2,1,0:T(4,128)(2,1)S(1)} reshape(bf16[1152,512]{1,0:T(8,128)(2,1)} %get-tuple-element.11) | data formatting | bytes 2359296 | tf_op jit(solution)/shard_map/reshape | solution.py:67
  140.0 1.4 copy.50
  141.4 1.5 fusion.53
  144.2 2.5 %fusion.27 = bf16[128,4,4,128]{0,3,2,1:T(8,128)(2,1)} fusion(bf16[1152,4,128,1]{0,2,3,1:T(8,128)(2,1)S(1)} %bitcast.69, f32[4,4,128,1152]{2,3,1,0:T(8,128)S(1)} %get-tuple-element.30, f32[4,4,128]{2,1,0:T(4,128)S(1)} %get-tuple-element.29, f32[128,4,4]{0,2,1:T(4,128)S(1)} %bitcast.75), kind=kOutput, calls=%fused_computation.31 | convolution fusion | flops 609222656 | bytes 11157504 | tf_op jit(solution)/shard_map/hgrk,khd->rhgd/dot_general | solution.py:77
  (107 shorter events, 24.2 us)
Async XLA Ops:
  6.5 4.1 %copy-start = (bf16[256,4096]{1,0:T(8,128)(2,1)S(1)}, bf16[256,4096]{1,0:T(8,128)(2,1)}, u32[]{:S(2)}) copy-start(bf16[256,4096]{1,0:T(8,128)(2,1)} %param.7) | copy-start | bytes 6291460
  13.9 7.5 %copy-start.8 = (s32[4096]{0:T(1024)S(1)}, s32[4096]{0:T(1024)}, u32[]{:S(2)}) copy-start(s32[4096]{0:T(1024)} %param.8) | copy-start | bytes 49156
  13.9 8.2 %copy-start.10 = (s32[32]{0:T(128)S(1)}, s32[32]{0:T(128)}, u32[]{:S(2)}) copy-start(s32[32]{0:T(128)} %param.9) | copy-start | bytes 388
  13.9 10.9 %copy-start.9 = (bf16[4096]{0:T(1024)(128)(2,1)S(1)}, bf16[4096]{0:T(1024)(128)(2,1)}, u32[]{:S(2)}) copy-start(bf16[4096]{0:T(1024)(128)(2,1)} %param.10) | copy-start | bytes 24580
  13.9 51.9 %all-to-all-start = ((bf16[16,16,4096]{2,1,0:T(8,128)(2,1)}), bf16[16,16,4096]{2,1,0:T(8,128)(2,1)S(1)}, u32[]{:S(2)}, u32[]{:S(2)}) async-start(bf16[16,16,4096]{2,1,0:T(8,128)(2,1)} %bitcast.62), calls=%async_computation | async-start | bytes 4194304 | tf_op jit(solution)/shard_map/all_to_all | solution.py:135
  21.3 6.0 %sort.43.cloned.1.call-start = ((), (), s32[]{:S(2)}) async-start(), calls=%async_computation.1 | async-start | bytes 49184 | tf_op jit(solution)/shard_map/jit(sort)/sort | solution.py:125
  71.0 5.0 %copy-start.2 = (bf16[256,4096]{1,0:T(8,128)(2,1)S(1)}, bf16[256,4096]{1,0:T(8,128)(2,1)}, u32[]{:S(2)}) copy-start(bf16[256,4096]{1,0:T(8,128)(2,1)} %gather_fusion.1) | copy-start | bytes 6291460
  71.0 5.0 %copy-start.11 = (bf16[4096,512]{1,0:T(8,128)(2,1)S(1)}, bf16[4096,512]{1,0:T(8,128)(2,1)}, u32[]{:S(2)}) copy-start(bf16[4096,512]{1,0:T(8,128)(2,1)} %param.12) | copy-start | bytes 12582916
  79.3 1.0 copy-start.5
  81.0 31.2 %collective-permute-start.2 = (bf16[128,1024]{1,0:T(8,128)(2,1)S(1)}, bf16[128,1024]{1,0:T(8,128)(2,1)S(1)}, u32[]{:S(2)}, u32[]{:S(2)}) collective-permute-start(bf16[128,1024]{1,0:T(8,128)(2,1)S(1)} %get-tuple-element.22), channel_id=1, source_target_pairs={{0,3},{1,4},{2,5},{3,6},{4,7},{5,8},{6,9},{7,10},{8,11},{9,12},{10... | collective-permute-start | bytes 786440 | tf_op jit(solution)/shard_map/ppermute | solution.py:16
  87.8 25.7 %collective-permute-start.1 = (bf16[128,1024]{1,0:T(8,128)(2,1)S(1)}, bf16[128,1024]{1,0:T(8,128)(2,1)S(1)}, u32[]{:S(2)}, u32[]{:S(2)}) collective-permute-start(bf16[128,1024]{1,0:T(8,128)(2,1)S(1)} %get-tuple-element.22), channel_id=1, source_target_pairs={{0,2},{1,3},{2,4},{3,5},{4,6},{5,7},{6,8},{7,9},{8,10},{9,11},{10,... | collective-permute-start | bytes 786440 | tf_op jit(solution)/shard_map/ppermute | solution.py:16
  92.1 21.5 %collective-permute-start = (bf16[128,1024]{1,0:T(8,128)(2,1)S(1)}, bf16[128,1024]{1,0:T(8,128)(2,1)S(1)}, u32[]{:S(2)}, u32[]{:S(2)}) collective-permute-start(bf16[128,1024]{1,0:T(8,128)(2,1)S(1)} %get-tuple-element.22), channel_id=1, source_target_pairs={{0,1},{1,2},{2,3},{3,4},{4,5},{5,6},{6,7},{7,8},{8,9},{9,10},{10,1... | collective-permute-start | bytes 786440 | tf_op jit(solution)/shard_map/ppermute | solution.py:16
  95.8 24.2 %collective-permute-start.3 = (bf16[256,1024]{1,0:T(8,128)(2,1)}, bf16[256,1024]{1,0:T(8,128)(2,1)}, u32[]{:S(2)}, u32[]{:S(2)}) collective-permute-start(bf16[256,1024]{1,0:T(8,128)(2,1)} %get-tuple-element.23), channel_id=1, source_target_pairs={{1,0},{2,1},{3,2},{4,3},{5,4},{6,5},{7,6},{8,7},{9,8},{10,9},{11,1... | collective-permute-start | bytes 1572872 | tf_op jit(solution)/shard_map/ppermute | solution.py:16
  99.9 32.1 %collective-permute-start.4 = (bf16[256,1024]{1,0:T(8,128)(2,1)}, bf16[256,1024]{1,0:T(8,128)(2,1)}, u32[]{:S(2)}, u32[]{:S(2)}) collective-permute-start(bf16[256,1024]{1,0:T(8,128)(2,1)} %get-tuple-element.23), channel_id=1, source_target_pairs={{2,0},{3,1},{4,2},{5,3},{6,4},{7,5},{8,6},{9,7},{10,8},{11,9},{12,... | collective-permute-start | bytes 1572872 | tf_op jit(solution)/shard_map/ppermute | solution.py:16
  112.3 21.6 %collective-permute-start.5 = (bf16[128,1024]{1,0:T(8,128)(2,1)}, bf16[128,1024]{1,0:T(8,128)(2,1)S(1)}, u32[]{:S(2)}, u32[]{:S(2)}) collective-permute-start(bf16[128,1024]{1,0:T(8,128)(2,1)} %get-tuple-element.21), channel_id=1, source_target_pairs={{3,0},{4,1},{5,2},{6,3},{7,4},{8,5},{9,6},{10,7},{11,8},{12,9},{13... | collective-permute-start | bytes 786440 | tf_op jit(solution)/shard_map/ppermute | solution.py:16
  113.6 0.7 copy-start.6
  116.3 1.2 copy-start.7
  142.9 1.3 copy-start.4
  144.2 3.8 %copy-start.3 = (bf16[128,2048]{1,0:T(8,128)(2,1)S(1)}, bf16[128,2048]{1,0:T(8,128)(2,1)}, u32[]{:S(2)}) copy-start(bf16[128,2048]{1,0:T(8,128)(2,1)} %copy.39) | copy-start | bytes 1572868
  144.2 4.8 %copy-start.1 = (bf16[256,4096]{1,0:T(8,128)(2,1)S(1)}, bf16[256,4096]{1,0:T(8,128)(2,1)}, u32[]{:S(2)}) copy-start(bf16[256,4096]{1,0:T(8,128)(2,1)} %param.7) | copy-start | bytes 6291460
Sparse Core Ops, SparseCore 0:
  24.4 2.5 sort.45.cloned.1.call-done
  (1 shorter events, 0.0 us)
where the time goes:
time: 157 us; the launch traced here: 156 us
  waiting for transfers between devices  43.3 us (28%)
  local copies, waits for them, and re-layouts  29 us (18%)
  starting transfers between devices  28.6 us (18%)
  matrix products  21.3 us (14%)
  other arithmetic  19.7 us (13%)
  between operations  14 us (9%)
    all_to_all x1, waiting for transfers between devices, shards(): lax.all_to_all(outgoing, 'ctx', split_axis=0, concat_axis=0, tiled=True)  33.2 us
    ppermute x6, starting transfers between devices, from_behind(): return lax.ppermute(block, axis, route)  21.2 us
    ppermute x6, waiting for transfers between devices, from_behind(): return lax.ppermute(block, axis, route)  10.1 us
    dot_general x1, matrix products, project(): jnp.dot(normed, w_query, preferred_element_type=jnp.float32)  8.18 us
    unnamed x36, local copies, waits for them, and re-layouts  7.53 us
    all_to_all x1, starting transfers between devices, shards(): lax.all_to_all(outgoing, 'ctx', split_axis=0, concat_axis=0, tiled=True)  7.41 us
    dot_general x1, matrix products, project(): jnp.dot(normed, value_weight, preferred_element_type=jnp.float32)  5 us
    dot_general x2, matrix products, attend(): jnp.einsum('hgrk,khd->rhgd', rounded, v_heads, preferred_element_type=jnp...  3.71 us
  transfers between devices with their start and end apart: 7, of which 2 were waited for; matrix products, arithmetic and copies ran while one was open for 19% of the time, Pallas kernels for 0%

commit v1 on v0

v1 whole, which is shorter than its diff:
```python
import functools

import jax
import jax.numpy as jnp
import numpy as np
from jax import lax
from jax.experimental import pallas as pl
from jax.experimental.pallas import tpu as pltpu
from jax.sharding import PartitionSpec as P

HEAD_SIZE = 128
REACH_BLOCKS = 3
ROPE_THETA = 500000.0
EPSILON = 1e-05

WHOLE = pl.BlockSpec(memory_space=pltpu.VMEM)
IN_PLACE = pl.BlockSpec(memory_space=pl.ANY)
SCALARS = pl.BlockSpec(memory_space=pltpu.SMEM)
MIB = 1024 * 1024


def dot(a, b):
    return jnp.dot(a, b, preferred_element_type=jnp.float32)


def project_kernel(kinds, group, tokens_hbm, gain_ref, rank_ref, cos_ref, sin_ref, *rest):
    count = len(kinds)
    weights_hbm, out_ref = rest[:count], rest[count]
    tokens, normed = rest[count + 1 : count + 3]
    weights, sems = rest[count + 3 : 2 * count + 3], rest[2 * count + 3]
    copies = [pltpu.make_async_copy(tokens_hbm, tokens, sems.at[0])]
    for i in range(count):
        copies.append(pltpu.make_async_copy(weights_hbm[i], weights[i], sems.at[i + 1]))
    for copy in copies:
        copy.start()
    rows, width = tokens.shape
    order = (lax.broadcasted_iota(jnp.int32, (rows, rows), 0) == rank_ref[...]).astype(jnp.bfloat16)
    gain = gain_ref[...].astype(jnp.float32)
    copies[0].wait()
    step = 32

    def norm(i, _):
        at = pl.ds(pl.multiple_of(i * step, step), step)
        floats = tokens[at, :].astype(jnp.float32)
        mean = jnp.sum(floats * floats, axis=1, keepdims=True) * (1.0 / width)
        normed[at, :] = (floats * lax.rsqrt(mean + EPSILON) * gain).astype(jnp.bfloat16)
        return 0

    lax.fori_loop(0, rows // step, norm, 0, unroll=True)
    groups, heads = out_ref.shape[0], out_ref.shape[1]
    cosine, sine = cos_ref[...], sin_ref[...]
    offset = 0
    for i in range(count):
        copies[i + 1].wait()
        per_head = weights[i].shape[1] // heads
        span = max(per_head, 256)
        for first in range(0, weights[i].shape[1], span):
            product = dot(normed[...], weights[i][:, first : first + span])
            parts = []
            for u in range(0, span, HEAD_SIZE):
                part = product[:, u : u + HEAD_SIZE]
                if kinds[i]:
                    part = part * cosine + pltpu.roll(part, HEAD_SIZE // 2, 1) * sine
                parts.append(part.astype(jnp.bfloat16))
            ordered = dot(order, jnp.concatenate(parts, axis=1)).astype(jnp.bfloat16)
            for u in range(0, span, per_head):
                out_ref[:, (first + u) // per_head, :, offset : offset + per_head] = ordered[
                    :, u : u + per_head
                ].reshape(groups, rows // groups, per_head)
        offset += per_head


def project(tokens, gain, rank, cosine, sine, weights, kinds, groups, heads):
    rows, width = tokens.shape
    columns = sum(w.shape[1] for w in weights)
    flops = 2 * rows * width * columns
    size = 2 * (width * columns + rows * width * 2 + rows * columns)
    return pl.pallas_call(
        functools.partial(project_kernel, kinds, groups),
        out_shape=jax.ShapeDtypeStruct((groups, heads, rows // groups, columns // heads), jnp.bfloat16),
        in_specs=[IN_PLACE] + [WHOLE] * 4 + [IN_PLACE] * len(weights),
        out_specs=WHOLE,
        scratch_shapes=[pltpu.VMEM((rows, width), jnp.bfloat16)] * 2
        + [pltpu.VMEM(w.shape, jnp.bfloat16) for w in weights]
        + [pltpu.SemaphoreType.DMA((len(weights) + 1,))],
        compiler_params=pltpu.CompilerParams(vmem_limit_bytes=size + 10 * MIB),
        cost_estimate=pl.CostEstimate(flops=flops, bytes_accessed=size, transcendentals=0),
    )(tokens, gain, rank, cosine, sine, *weights)


def place_kernel(arrived_ref, slot_ref, *outs):
    rows = arrived_ref.shape[0]
    first = 0
    for out_ref in outs:
        size = out_ref.shape[0]
        slots = lax.broadcasted_iota(jnp.int32, (size, rows), 0) + first
        chosen = (slots == slot_ref[...]).astype(jnp.bfloat16)
        out_ref[...] = dot(chosen, arrived_ref[...]).astype(jnp.bfloat16)
        first += size


def place(arrived, slot, sizes):
    width = arrived.shape[1]
    return pl.pallas_call(
        place_kernel,
        out_shape=[jax.ShapeDtypeStruct((size, width), jnp.bfloat16) for size in sizes],
        in_specs=[WHOLE, WHOLE],
        out_specs=[WHOLE] * len(sizes),
        compiler_params=pltpu.CompilerParams(vmem_limit_bytes=16 * MIB),
        cost_estimate=pl.CostEstimate(
            flops=2 * sum(sizes) * arrived.shape[0] * width,
            bytes_accessed=4 * arrived.size,
            transcendentals=0,
        ),
    )(arrived, slot)


def attend_kernel(block, scalar_ref, query_ref, slot_ref, ends_ref, *rest):
    pieces, out_ref, held = rest[:6], rest[6], rest[7]
    target, starts = scalar_ref[0], (scalar_ref[1], scalar_ref[2])
    heads = query_ref.shape[1] // HEAD_SIZE
    arrived = query_ref.shape[0]
    run = arrived // 2
    per_run = run // block
    reach = REACH_BLOCKS * block
    keys = reach + block
    slot = slot_ref[...]
    ends = ends_ref[...]
    factor = jnp.float32(np.log2(np.e) / HEAD_SIZE**0.5)
    for half in range(2):
        first = 0
        for piece in pieces[3 * half : 3 * half + 3]:
            held[half, first : first + piece.shape[0], :] = piece[...]
            first += piece.shape[0]
    for half in range(2):
        index = target if half == 0 else per_run - 1 - target
        at = pl.multiple_of(index * block, block)
        slots = lax.broadcasted_iota(jnp.int32, (block, arrived), 0) + (at + half * run)
        query = dot((slots == slot).astype(jnp.bfloat16), query_ref[...]).astype(jnp.bfloat16)
        key = held[half, pl.ds(at, keys), :HEAD_SIZE]
        value = held[half, pl.ds(at, keys), HEAD_SIZE:]
        begin = starts[half] + at
        query_at = lax.broadcasted_iota(jnp.int32, (block, 1), 0) + begin
        key_at = lax.broadcasted_iota(jnp.int32, (1, keys), 1) + (begin - reach)
        doc_start = jnp.max(jnp.where(ends <= query_at, ends, 0), axis=1, keepdims=True)
        allowed = (key_at >= doc_start) & (key_at <= query_at)
        for h in range(heads):
            columns = slice(h * HEAD_SIZE, (h + 1) * HEAD_SIZE)
            scores = lax.dot_general(
                query[:, columns], key, (((1,), (1,)), ((), ())), preferred_element_type=jnp.float32
            )
            scores = jnp.where(allowed, scores, jnp.float32(-1e30))
            top = jnp.max(scores, axis=1, keepdims=True)
            weights = jnp.exp2((scores - top) * factor)
            total = jnp.sum(weights, axis=1, keepdims=True)
            mixed = dot(weights.astype(jnp.bfloat16), value) / total
            out_ref[half * block : (half + 1) * block, columns] = mixed.astype(jnp.bfloat16)


def attend(scalars, query, slot, ends, pieces, block):
    width = query.shape[1]
    held = REACH_BLOCKS * block + query.shape[0] // 2
    heads = width // HEAD_SIZE
    reach = (REACH_BLOCKS + 1) * block
    return pl.pallas_call(
        functools.partial(attend_kernel, block),
        out_shape=jax.ShapeDtypeStruct((2 * block, width), jnp.bfloat16),
        in_specs=[SCALARS] + [WHOLE] * 9,
        out_specs=WHOLE,
        scratch_shapes=[pltpu.VMEM((2, held, 2 * HEAD_SIZE), jnp.bfloat16)],
        compiler_params=pltpu.CompilerParams(vmem_limit_bytes=16 * MIB),
        cost_estimate=pl.CostEstimate(
            flops=2 * 2 * heads * block * reach * HEAD_SIZE * 2 + 4 * block * query.size,
            bytes_accessed=2 * query.size + 8 * held * HEAD_SIZE,
            transcendentals=2 * heads * block * reach,
        ),
    )(scalars, query, slot, ends, *pieces)


def assemble_kernel(scalar_ref, *rest):
    pieces, out_ref = rest[:-1], rest[-1]
    width = pieces[0].shape[1]
    for k, piece in enumerate(pieces):
        at = pl.multiple_of((scalar_ref[0] ^ k) * width, width)
        out_ref[:, pl.ds(at, width)] = piece[...]


def assemble(scalars, pieces):
    rows, width = pieces[0].shape
    return pl.pallas_call(
        assemble_kernel,
        out_shape=jax.ShapeDtypeStruct((rows, width * len(pieces)), jnp.bfloat16),
        in_specs=[SCALARS] + [WHOLE] * len(pieces),
        out_specs=WHOLE,
        compiler_params=pltpu.CompilerParams(vmem_limit_bytes=8 * MIB),
        cost_estimate=pl.CostEstimate(
            flops=0, bytes_accessed=4 * rows * width * len(pieces), transcendentals=0
        ),
    )(scalars, *pieces)


def shards(tokens, positions, lengths, gain, w_query, w_key, value_weight):
    devices = lax.axis_size("ctx")
    device = lax.axis_index("ctx")
    rows = tokens.shape[0]
    block = rows // 2
    members = w_key.shape[1] // HEAD_SIZE
    groups = devices // members
    group = device // members
    member = device % members
    run = members * block
    group_rows = rows // groups

    def group_of(where_at):
        block_id = where_at // block
        return jnp.minimum(block_id, 2 * devices - 1 - block_id) // members

    mine = lax.dynamic_slice_in_dim(positions, device * rows, rows, 0)
    my_groups = group_of(mine)
    row = jnp.arange(rows, dtype=jnp.int32)
    earlier = (my_groups[:, None] == my_groups[None, :]) & (row[:, None] < row[None, :])
    rank = my_groups * group_rows + jnp.sum(earlier.astype(jnp.int32), axis=0)
    half = HEAD_SIZE // 2
    freq = ROPE_THETA ** (-(jnp.arange(half, dtype=jnp.float32) * 2.0 / HEAD_SIZE))
    angle = mine.astype(jnp.float32)[:, None] * freq[None, :]
    cosine, sine = jnp.cos(angle), jnp.sin(angle)
    cosine = jnp.concatenate([cosine, cosine], axis=1)
    sine = jnp.concatenate([-sine, sine], axis=1)
    gain = gain[None, :]
    rank = rank[None, :]

    def exchange(ordered):
        width = ordered.shape[3]
        flat = ordered.reshape(devices, group_rows, width)
        flat = lax.all_to_all(flat, "ctx", split_axis=0, concat_axis=0, tiled=True)
        return flat.reshape(devices * group_rows, width)

    kv = project(tokens, gain, rank, cosine, sine, (w_key, value_weight), (True, False), groups, members)
    kv = exchange(kv)
    query = project(tokens, gain, rank, cosine, sine, (w_query,), (True,), groups, members)

    table = positions.reshape(devices, rows)
    ours = group_of(table) == group
    first_run = group * run
    second_run = (2 * devices - members) * block - group * run
    slots = jnp.where(table // run == group, table - first_run, table - second_run + run)
    place_in = jnp.cumsum(ours.astype(jnp.int32), axis=1) - 1
    place_in = jnp.where(ours, place_in, -1)
    wanted = jnp.arange(group_rows, dtype=jnp.int32)[None, :, None] == place_in[:, None, :]
    slot = jnp.sum(jnp.where(wanted, slots[:, None, :], 0), axis=2).reshape(1, devices * group_rows)
    ends = jnp.cumsum(lengths, dtype=jnp.int32)[None, :]

    kv, query = lax.optimization_barrier((kv, query))
    query = exchange(query)
    reach = REACH_BLOCKS * block
    sizes = [run - reach, reach] * 2
    early_head, early_tail, late_head, late_tail = place(kv, slot, sizes)
    up = [(i, i + members) for i in range(devices - members)]
    down = [(i + members, i) for i in range(devices - members)]
    early_halo = lax.ppermute(early_tail, "ctx", up)
    late_halo = lax.ppermute(late_tail, "ctx", down)
    late_halo = jnp.where(group == groups - 1, early_tail, late_halo)
    pieces = (early_halo, early_head, early_tail, late_halo, late_head, late_tail)

    results = []
    for k in [3, 1, 2, 0][-members:]:
        target = member ^ k
        scalars = jnp.stack([target, first_run, second_run]).astype(jnp.int32)
        out = attend(scalars, query, slot, ends, pieces, block)
        if k:
            route = [(i, i // members * members + (i % members ^ k)) for i in range(devices)]
            out = lax.ppermute(out, "ctx", route)
        results.append((k, out))
    results = [out for _, out in sorted(results, key=lambda pair: pair[0])]
    return assemble(member.reshape(1).astype(jnp.int32), results)


def solution(mesh):
    in_specs = (P(("dp", "ctx"), None), P("dp"), P("dp"), P(), P(), P(), P())
    out_specs = P(("dp", "ctx"), None)
    return jax.shard_map(shards, mesh=mesh, in_specs=in_specs, out_specs=out_specs, check_vma=False)
```

time: 157 us -> 95.7 us (0.61)
  the two profiles are of different devices: /device:TPU:4 before, /device:TPU:8 now
where the time goes in v1:
time: 95.7 us; the launch traced here: 95.2 us
  Pallas kernels  32 us (33%)
  starting transfers between devices  23.7 us (25%)
  waiting for transfers between devices  23.4 us (24%)
  local copies, waits for them, and re-layouts  12.7 us (13%)
  other arithmetic  3.22 us (3%)
    ppermute x1, waiting for transfers between devices, shards(): late_halo = lax.ppermute(late_tail, 'ctx', down)  19.6 us
    pallas_call x2, Pallas kernels, project(): pl.pallas_call(functools.partial(project_kernel, kinds, groups), out_shap...  17.1 us
    all_to_all x2, starting transfers between devices, exchange(): flat = lax.all_to_all(flat, 'ctx', split_axis=0, concat_axis=0, tiled=True)  14.2 us
    pallas_call x4, Pallas kernels, attend(): pl.pallas_call(functools.partial(attend_kernel, block), out_shape=jax.Sha...  13.1 us
    unnamed x14, local copies, waits for them, and re-layouts  11.7 us
    ppermute x3, waiting for transfers between devices, shards(): out = lax.ppermute(out, 'ctx', route)  3.86 us
    ppermute x1, starting transfers between devices, shards(): early_halo = lax.ppermute(early_tail, 'ctx', up)  3.8 us
    ppermute x3, starting transfers between devices, shards(): out = lax.ppermute(out, 'ctx', route)  3.68 us
  transfers between devices with their start and end apart: 7, of which 2 were waited for; matrix products, arithmetic and copies ran while one was open for 2% of the time, Pallas kernels for 21%

profile of v1, /device:TPU:8, one launch (start us, length us, event | category | flops | bytes accessed | tf_op | source)
XLA Modules:
  0.0 95.2 jit_solution(7096800061237487972)
XLA Ops:
  0.0 0.8 dynamic-slice_convert_fusion
  0.9 0.7 broadcast_in_dim.14.gain_ref
  2.3 1.6 %copy-done.1 = bf16[256,4096]{1,0:T(8,128)(2,1)S(1)} copy-done((bf16[256,4096]{1,0:T(8,128)(2,1)S(1)}, bf16[256,4096]{1,0:T(8,128)(2,1)}, u32[]{:S(2)}) %copy-start.1) | copy-done | bytes 2097176
  3.9 2.2 %copy-done.3 = bf16[4096,512]{1,0:T(8,128)(2,1)S(1)} copy-done((bf16[4096,512]{1,0:T(8,128)(2,1)S(1)}, bf16[4096,512]{1,0:T(8,128)(2,1)}, u32[]{:S(2)}) %copy-start.3) | copy-done | bytes 4194328
  6.1 2.2 %copy-done.4 = bf16[4096,512]{1,0:T(8,128)(2,1)S(1)} copy-done((bf16[4096,512]{1,0:T(8,128)(2,1)S(1)}, bf16[4096,512]{1,0:T(8,128)(2,1)}, u32[]{:S(2)}) %copy-start.4) | copy-done | bytes 4194328
  8.3 8.0 %shard_map.73 = bf16[4,4,64,256]{3,2,1,0:T(8,128)(2,1)} custom-call(bf16[256,4096]{1,0:T(8,128)(2,1)S(1)} %copy-done.1, bf16[1,4096]{1,0:T(2,128)(2,1)S(1)} %broadcast_in_dim.14.gain_ref, s32[1,256]{1,0:T(1,128)S(1)} %bitcast.23, f32[256,128]{1,0:T(8,128)S(1)} %get-tuple-element.24.cos_ref, f32[256,128]{1,0:T(8,128)S(1)} %get-tuple-element.25.sin_ref, ...), custom_call_target="tpu_custom_call" | custom-call | flops 2147483648 | bytes 13107200 | tf_op jit(solution)/shard_map/pallas_call | solution.py:78
  16.3 7.2 %all-to-all-start = ((bf16[16,64,256]{2,1,0:T(8,128)(2,1)}), bf16[16,64,256]{2,1,0:T(8,128)(2,1)S(1)}, u32[]{:S(2)}, u32[]{:S(2)}) async-start(bf16[16,64,256]{2,1,0:T(8,128)(2,1)} %bitcast.4), calls=%async_computation | async-start | bytes 1048576 | tf_op jit(solution)/shard_map/all_to_all | solution.py:235
  23.5 5.8 %copy-done = bf16[4096,2048]{1,0:T(8,128)(2,1)S(1)} copy-done((bf16[4096,2048]{1,0:T(8,128)(2,1)S(1)}, bf16[4096,2048]{1,0:T(8,128)(2,1)}, u32[]{:S(2)}) %copy-start) | copy-done | bytes 16777240
  29.3 9.1 %shard_map.74 = bf16[4,4,64,512]{3,2,1,0:T(8,128)(2,1)} custom-call(bf16[256,4096]{1,0:T(8,128)(2,1)S(1)} %copy-done.2, bf16[1,4096]{1,0:T(2,128)(2,1)S(1)} %broadcast_in_dim.14.gain_ref, s32[1,256]{1,0:T(1,128)S(1)} %bitcast.24, f32[256,128]{1,0:T(8,128)S(1)} %get-tuple-element.24.cos_ref, f32[256,128]{1,0:T(8,128)S(1)} %get-tuple-element.25.sin_ref, ...), custom_call_target="tpu_custom_call" | custom-call | flops 4294967296 | bytes 22020096 | tf_op jit(solution)/shard_map/pallas_call | solution.py:78
  38.4 6.9 %all-to-all-start.1 = ((bf16[16,64,512]{2,1,0:T(8,128)(2,1)}), bf16[16,64,512]{2,1,0:T(8,128)(2,1)S(1)}, u32[]{:S(2)}, u32[]{:S(2)}) async-start(bf16[16,64,512]{2,1,0:T(8,128)(2,1)} %bitcast.6), calls=%async_computation.1 | async-start | bytes 2097152 | tf_op jit(solution)/shard_map/all_to_all | solution.py:235
  45.6 0.6 reduce-window.9
  47.0 0.7 shard_map.75
  47.8 2.0 %collective-permute-start.1 = (bf16[384,256]{1,0:T(8,128)(2,1)S(1)}, bf16[384,256]{1,0:T(8,128)(2,1)S(1)}, u32[]{:S(2)}, u32[]{:S(2)}) collective-permute-start(bf16[384,256]{1,0:T(8,128)(2,1)S(1)} %get-tuple-element.15.rest_5_), channel_id=1, source_target_pairs={{4,0},{5,1},{6,2},{7,3},{8,4},{9,5},{10,6},{11,7},{12,8},{13,9},{1... | collective-permute-start | bytes 589832 | tf_op jit(solution)/shard_map/ppermute | solution.py:261
  50.0 3.8 %collective-permute-start = (bf16[384,256]{1,0:T(8,128)(2,1)S(1)}, bf16[384,256]{1,0:T(8,128)(2,1)S(1)}, u32[]{:S(2)}, u32[]{:S(2)}) collective-permute-start(bf16[384,256]{1,0:T(8,128)(2,1)S(1)} %get-tuple-element.13.rest_2_), channel_id=1, source_target_pairs={{0,4},{1,5},{2,6},{3,7},{4,8},{5,9},{6,10},{7,11},{8,12},{9,13},{1... | collective-permute-start | bytes 589832 | tf_op jit(solution)/shard_map/ppermute | solution.py:260
  53.8 19.6 %collective-permute-done.1 = bf16[384,256]{1,0:T(8,128)(2,1)S(1)} collective-permute-done((bf16[384,256]{1,0:T(8,128)(2,1)S(1)}, bf16[384,256]{1,0:T(8,128)(2,1)S(1)}, u32[]{:S(2)}, u32[]{:S(2)}) %collective-permute-start.1) | collective-permute-done | bytes 196640 | tf_op jit(solution)/shard_map/ppermute | solution.py:261
  73.4 3.3 %shard_map.77 = bf16[256,512]{1,0:T(8,128)(2,1)S(1)} custom-call(s32[3]{0:T(128)S(1)} %add_add_fusion.1.scalar_ref, bf16[1024,512]{1,0:T(8,128)(2,1)S(1)} %bitcast.18, s32[1,1024]{1,0:T(1,128)S(1)} %reshape.161.slot_ref, s32[1,32]{1,0:T(1,128)S(1)} %reduce-window_2_clone.1.ends_ref, bf16[384,256]{1,0:T(8,128)(2,1)S(1)} %collective-permute-done.rest_0_, ...), custom_call_target="tpu_custom_call" | custom-call | flops 536870912 | bytes 1966080 | tf_op jit(solution)/shard_map/pallas_call | solution.py:165
  76.7 1.5 %collective-permute-start.2 = (bf16[256,512]{1,0:T(8,128)(2,1)S(1)}, bf16[256,512]{1,0:T(8,128)(2,1)S(1)}, u32[]{:S(2)}, u32[]{:S(2)}) collective-permute-start(bf16[256,512]{1,0:T(8,128)(2,1)S(1)} %shard_map.77), channel_id=1, source_target_pairs={{0,1},{1,0},{2,3},{3,2},{4,5},{5,4},{6,7},{7,6},{8,9},{9,8},{10,11... | collective-permute-start | bytes 786440 | tf_op jit(solution)/shard_map/ppermute | solution.py:272
  78.2 3.3 %shard_map.78 = bf16[256,512]{1,0:T(8,128)(2,1)S(1)} custom-call(s32[3]{0:T(128)S(1)} %add_add_fusion.2.scalar_ref, bf16[1024,512]{1,0:T(8,128)(2,1)S(1)} %bitcast.19, s32[1,1024]{1,0:T(1,128)S(1)} %reshape.161.slot_ref, s32[1,32]{1,0:T(1,128)S(1)} %reduce-window_2_clone.1.ends_ref, bf16[384,256]{1,0:T(8,128)(2,1)S(1)} %collective-permute-done.rest_0_, ...), custom_call_target="tpu_custom_call" | custom-call | flops 536870912 | bytes 1966080 | tf_op jit(solution)/shard_map/pallas_call | solution.py:165
  81.5 1.6 %collective-permute-start.3 = (bf16[256,512]{1,0:T(8,128)(2,1)S(1)}, bf16[256,512]{1,0:T(8,128)(2,1)S(1)}, u32[]{:S(2)}, u32[]{:S(2)}) collective-permute-start(bf16[256,512]{1,0:T(8,128)(2,1)S(1)} %shard_map.78), channel_id=1, source_target_pairs={{0,2},{1,3},{2,0},{3,1},{4,6},{5,7},{6,4},{7,5},{8,10},{9,11},{10,... | collective-permute-start | bytes 786440 | tf_op jit(solution)/shard_map/ppermute | solution.py:272
  83.1 3.3 %shard_map.79 = bf16[256,512]{1,0:T(8,128)(2,1)S(1)} custom-call(s32[3]{0:T(128)S(1)} %add_add_fusion.3.scalar_ref, bf16[1024,512]{1,0:T(8,128)(2,1)S(1)} %bitcast.20, s32[1,1024]{1,0:T(1,128)S(1)} %reshape.161.slot_ref, s32[1,32]{1,0:T(1,128)S(1)} %reduce-window_2_clone.1.ends_ref, bf16[384,256]{1,0:T(8,128)(2,1)S(1)} %collective-permute-done.rest_0_, ...), custom_call_target="tpu_custom_call" | custom-call | flops 536870912 | bytes 1966080 | tf_op jit(solution)/shard_map/pallas_call | solution.py:165
  86.4 0.6 collective-permute-start.4
  87.0 3.3 %shard_map.76.rest_0_ = bf16[256,512]{1,0:T(8,128)(2,1)S(1)} custom-call(s32[3]{0:T(128)S(1)} %add_add_fusion.scalar_ref, bf16[1024,512]{1,0:T(8,128)(2,1)S(1)} %bitcast.21, s32[1,1024]{1,0:T(1,128)S(1)} %reshape.161.slot_ref, s32[1,32]{1,0:T(1,128)S(1)} %reduce-window_2_clone.1.ends_ref, bf16[384,256]{1,0:T(8,128)(2,1)S(1)} %collective-permute-done.rest_0_, ...), custom_call_target="tpu_custom_call" | custom-call | flops 536870912 | bytes 1966080 | tf_op jit(solution)/shard_map/pallas_call | solution.py:165
  90.3 3.9 %collective-permute-done.3.rest_2_ = bf16[256,512]{1,0:T(8,128)(2,1)S(1)} collective-permute-done((bf16[256,512]{1,0:T(8,128)(2,1)S(1)}, bf16[256,512]{1,0:T(8,128)(2,1)S(1)}, u32[]{:S(2)}, u32[]{:S(2)}) %collective-permute-start.3) | collective-permute-done | bytes 262176 | tf_op jit(solution)/shard_map/ppermute | solution.py:272
  94.2 1.0 %shard_map.80 = bf16[256,2048]{1,0:T(8,128)(2,1)} custom-call(s32[1]{0:T(128)} %bitcast.scalar_ref, bf16[256,512]{1,0:T(8,128)(2,1)S(1)} %shard_map.76.rest_0_, bf16[256,512]{1,0:T(8,128)(2,1)S(1)} %collective-permute-done.2.rest_1_, bf16[256,512]{1,0:T(8,128)(2,1)S(1)} %collective-permute-done.3.rest_2_, bf16[256,512]{1,0:T(8,128)(2,1)S(1)} %collective-permute-done.4.rest_3_), custom_call_target="tpu_custom_call" | custom-call | bytes 2097152 | tf_op jit(solution)/shard_map/pallas_call | solution.py:190
  (34 shorter events, 2.2 us)
Async XLA Ops:
  2.3 1.6 %copy-start.1 = (bf16[256,4096]{1,0:T(8,128)(2,1)S(1)}, bf16[256,4096]{1,0:T(8,128)(2,1)}, u32[]{:S(2)}) copy-start(bf16[256,4096]{1,0:T(8,128)(2,1)} %tokens_hbm.3) | copy-start | bytes 6291460
  3.9 2.2 %copy-start.3 = (bf16[4096,512]{1,0:T(8,128)(2,1)S(1)}, bf16[4096,512]{1,0:T(8,128)(2,1)}, u32[]{:S(2)}) copy-start(bf16[4096,512]{1,0:T(8,128)(2,1)} %rest_0_.2) | copy-start | bytes 12582916
  6.1 2.2 %copy-start.4 = (bf16[4096,512]{1,0:T(8,128)(2,1)S(1)}, bf16[4096,512]{1,0:T(8,128)(2,1)}, u32[]{:S(2)}) copy-start(bf16[4096,512]{1,0:T(8,128)(2,1)} %rest_1_.1) | copy-start | bytes 12582916
  8.3 15.2 %copy-start.2 = (bf16[256,4096]{1,0:T(8,128)(2,1)S(1)}, bf16[256,4096]{1,0:T(8,128)(2,1)}, u32[]{:S(2)}) copy-start(bf16[256,4096]{1,0:T(8,128)(2,1)} %tokens_hbm.3) | copy-start | bytes 6291460
  16.3 22.1 %all-to-all-start = ((bf16[16,64,256]{2,1,0:T(8,128)(2,1)}), bf16[16,64,256]{2,1,0:T(8,128)(2,1)S(1)}, u32[]{:S(2)}, u32[]{:S(2)}) async-start(bf16[16,64,256]{2,1,0:T(8,128)(2,1)} %bitcast.4), calls=%async_computation | async-start | bytes 1048576 | tf_op jit(solution)/shard_map/all_to_all | solution.py:235
  23.5 5.8 %copy-start = (bf16[4096,2048]{1,0:T(8,128)(2,1)S(1)}, bf16[4096,2048]{1,0:T(8,128)(2,1)}, u32[]{:S(2)}) copy-start(bf16[4096,2048]{1,0:T(8,128)(2,1)} %rest_0_.3) | copy-start | bytes 50331652
  29.3 16.0 %copy-start.5 = (s32[4096]{0:T(1024)S(1)}, s32[4096]{0:T(1024)}, u32[]{:S(2)}) copy-start(s32[4096]{0:T(1024)} %param.8) | copy-start | bytes 49156
  29.3 16.1 %copy-start.6 = (s32[32]{0:T(128)S(1)}, s32[32]{0:T(128)}, u32[]{:S(2)}) copy-start(s32[32]{0:T(128)} %param.9) | copy-start | bytes 388
  38.4 35.0 %all-to-all-start.1 = ((bf16[16,64,512]{2,1,0:T(8,128)(2,1)}), bf16[16,64,512]{2,1,0:T(8,128)(2,1)S(1)}, u32[]{:S(2)}, u32[]{:S(2)}) async-start(bf16[16,64,512]{2,1,0:T(8,128)(2,1)} %bitcast.6), calls=%async_computation.1 | async-start | bytes 2097152 | tf_op jit(solution)/shard_map/all_to_all | solution.py:235
  47.8 25.6 %collective-permute-start.1 = (bf16[384,256]{1,0:T(8,128)(2,1)S(1)}, bf16[384,256]{1,0:T(8,128)(2,1)S(1)}, u32[]{:S(2)}, u32[]{:S(2)}) collective-permute-start(bf16[384,256]{1,0:T(8,128)(2,1)S(1)} %get-tuple-element.15.rest_5_), channel_id=1, source_target_pairs={{4,0},{5,1},{6,2},{7,3},{8,4},{9,5},{10,6},{11,7},{12,8},{13,9},{1... | collective-permute-start | bytes 589832 | tf_op jit(solution)/shard_map/ppermute | solution.py:261
  50.0 23.4 %collective-permute-start = (bf16[384,256]{1,0:T(8,128)(2,1)S(1)}, bf16[384,256]{1,0:T(8,128)(2,1)S(1)}, u32[]{:S(2)}, u32[]{:S(2)}) collective-permute-start(bf16[384,256]{1,0:T(8,128)(2,1)S(1)} %get-tuple-element.13.rest_2_), channel_id=1, source_target_pairs={{0,4},{1,5},{2,6},{3,7},{4,8},{5,9},{6,10},{7,11},{8,12},{9,13},{1... | collective-permute-start | bytes 589832 | tf_op jit(solution)/shard_map/ppermute | solution.py:260
  76.7 13.6 %collective-permute-start.2 = (bf16[256,512]{1,0:T(8,128)(2,1)S(1)}, bf16[256,512]{1,0:T(8,128)(2,1)S(1)}, u32[]{:S(2)}, u32[]{:S(2)}) collective-permute-start(bf16[256,512]{1,0:T(8,128)(2,1)S(1)} %shard_map.77), channel_id=1, source_target_pairs={{0,1},{1,0},{2,3},{3,2},{4,5},{5,4},{6,7},{7,6},{8,9},{9,8},{10,11... | collective-permute-start | bytes 786440 | tf_op jit(solution)/shard_map/ppermute | solution.py:272
  81.5 12.7 %collective-permute-start.3 = (bf16[256,512]{1,0:T(8,128)(2,1)S(1)}, bf16[256,512]{1,0:T(8,128)(2,1)S(1)}, u32[]{:S(2)}, u32[]{:S(2)}) collective-permute-start(bf16[256,512]{1,0:T(8,128)(2,1)S(1)} %shard_map.78), channel_id=1, source_target_pairs={{0,2},{1,3},{2,0},{3,1},{4,6},{5,7},{6,4},{7,5},{8,10},{9,11},{10,... | collective-permute-start | bytes 786440 | tf_op jit(solution)/shard_map/ppermute | solution.py:272
  86.4 7.8 %collective-permute-start.4 = (bf16[256,512]{1,0:T(8,128)(2,1)S(1)}, bf16[256,512]{1,0:T(8,128)(2,1)S(1)}, u32[]{:S(2)}, u32[]{:S(2)}) collective-permute-start(bf16[256,512]{1,0:T(8,128)(2,1)S(1)} %shard_map.79), channel_id=1, source_target_pairs={{0,3},{1,2},{2,1},{3,0},{4,7},{5,6},{6,5},{7,4},{8,11},{9,10},{10,... | collective-permute-start | bytes 786440 | tf_op jit(solution)/shard_map/ppermute | solution.py:272

commit v2 on v1

--- a/solution.py
+++ b/solution.py
@@ -23,69 +23,116 @@
     return jnp.dot(a, b, preferred_element_type=jnp.float32)
 
 
-def project_kernel(kinds, group, tokens_hbm, gain_ref, rank_ref, cos_ref, sin_ref, *rest):
+def transposed(row):
+    size = row.shape[1]
+    here = lax.broadcasted_iota(jnp.int32, (size, size), 0)
+    there = lax.broadcasted_iota(jnp.int32, (size, size), 1)
+    return jnp.sum(jnp.where(here == there, row, 0), axis=1, keepdims=True)
+
+
+def group_of(where_at, block, devices, members):
+    block_id = where_at // block
+    return jnp.minimum(block_id, 2 * devices - 1 - block_id) // members
+
+
+def project_kernel(kinds, devices, members, scalar_ref, positions_ref, freq_ref, gain_ref, tokens_hbm, *rest):
     count = len(kinds)
     weights_hbm, out_ref = rest[:count], rest[count]
-    tokens, normed = rest[count + 1 : count + 3]
-    weights, sems = rest[count + 3 : 2 * count + 3], rest[2 * count + 3]
-    copies = [pltpu.make_async_copy(tokens_hbm, tokens, sems.at[0])]
+    tokens, normed, weights, token_sems, sems = rest[count + 1 :]
+    rows, width = tokens.shape
+    chunks, _, span = weights.shape
+    parts = token_sems.shape[0]
+    part = rows // parts
+    token_copies, copies, origin = [], [], []
+    for i in range(parts):
+        at = pl.ds(i * part, part)
+        token_copies.append(pltpu.make_async_copy(tokens_hbm.at[at], tokens.at[at], token_sems.at[i]))
     for i in range(count):
-        copies.append(pltpu.make_async_copy(weights_hbm[i], weights[i], sems.at[i + 1]))
-    for copy in copies:
+        for first in range(0, weights_hbm[i].shape[1], span):
+            j = len(copies)
+            source = weights_hbm[i].at[:, pl.ds(first, span)]
+            copies.append(pltpu.make_async_copy(source, weights.at[j], sems.at[j]))
+            origin.append((i, first))
+    for copy in token_copies + copies:
         copy.start()
+
+    lanes = positions_ref.shape[1]
+    stripes = rows // lanes
+    mine = jnp.concatenate(
+        [positions_ref[pl.ds(scalar_ref[0] * stripes + i, 1), :] for i in range(stripes)], axis=1
+    )
+    owner = group_of(mine, rows // 2, devices, members)
+    here = lax.broadcasted_iota(jnp.int32, (rows, rows), 0)
+    there = lax.broadcasted_iota(jnp.int32, (rows, rows), 1)
+    earlier = jnp.where((transposed(owner) == owner) & (here < there), 1, 0)
+    rank = owner * (rows * members // devices) + jnp.sum(earlier, axis=0, keepdims=True)
+    order = here == rank
+    ordered_at = jnp.sum(jnp.where(order, mine, 0), axis=1, keepdims=True)
+    angle = ordered_at.astype(jnp.float32) * freq_ref[...]
+    lane = lax.broadcasted_iota(jnp.int32, (rows, HEAD_SIZE), 1)
+    cosine = jnp.cos(angle)
+    sine = jnp.where(lane < HEAD_SIZE // 2, -1.0, 1.0) * jnp.sin(angle)
+    order = jnp.where(order, 1.0, 0.0).astype(jnp.bfloat16)
+    gain = gain_ref[...].astype(jnp.float32).reshape(1, width)
+    step = 32
+
+    for i in range(parts):
+        token_copies[i].wait()
+
+        def norm(j, _):
+            at = pl.ds(pl.multiple_of(i * part + j * step, step), step)
+            floats = tokens[at, :].astype(jnp.float32)
+            mean = jnp.sum(floats * floats, axis=1, keepdims=True) * (1.0 / width)
+            tokens[at, :] = (floats * lax.rsqrt(mean + EPSILON) * gain).astype(jnp.bfloat16)
+            return 0
+
+        lax.fori_loop(0, part // step, norm, 0, unroll=True)
+    for first in range(0, width, 512):
+        columns = slice(first, first + 512)
+        normed[:, columns] = dot(order, tokens[:, columns]).astype(jnp.bfloat16)
+    groups, heads = out_ref.shape[0], out_ref.shape[1]
+    offsets = [0]
+    for i in range(count):
+        offsets.append(offsets[-1] + weights_hbm[i].shape[1] // heads)
+    for j in range(chunks):
+        i, first = origin[j]
+        copies[j].wait()
+        product = dot(normed[...], weights[j])
+        per_head = offsets[i + 1] - offsets[i]
+        for u in range(0, span, HEAD_SIZE):
+            values = product[:, u : u + HEAD_SIZE]
+            if kinds[i]:
+                values = values * cosine + pltpu.roll(values, HEAD_SIZE // 2, 1) * sine
+            head, inside = divmod(first + u, per_head)
+            inside += offsets[i]
+            out_ref[:, head, :, inside : inside + HEAD_SIZE] = values.astype(jnp.bfloat16).reshape(
+                groups, rows // groups, HEAD_SIZE
+            )
+
+
+def project(scalars, positions, freq, gain, tokens, weights, kinds, devices, heads):
     rows, width = tokens.shape
-    order = (lax.broadcasted_iota(jnp.int32, (rows, rows), 0) == rank_ref[...]).astype(jnp.bfloat16)
-    gain = gain_ref[...].astype(jnp.float32)
-    copies[0].wait()
-    step = 32
-
-    def norm(i, _):
-        at = pl.ds(pl.multiple_of(i * step, step), step)
-        floats = tokens[at, :].astype(jnp.float32)
-        mean = jnp.sum(floats * floats, axis=1, keepdims=True) * (1.0 / width)
-        normed[at, :] = (floats * lax.rsqrt(mean + EPSILON) * gain).astype(jnp.bfloat16)
-        return 0
-
-    lax.fori_loop(0, rows // step, norm, 0, unroll=True)
-    groups, heads = out_ref.shape[0], out_ref.shape[1]
-    cosine, sine = cos_ref[...], sin_ref[...]
-    offset = 0
-    for i in range(count):
-        copies[i + 1].wait()
-        per_head = weights[i].shape[1] // heads
-        span = max(per_head, 256)
-        for first in range(0, weights[i].shape[1], span):
-            product = dot(normed[...], weights[i][:, first : first + span])
-            parts = []
-            for u in range(0, span, HEAD_SIZE):
-                part = product[:, u : u + HEAD_SIZE]
-                if kinds[i]:
-                    part = part * cosine + pltpu.roll(part, HEAD_SIZE // 2, 1) * sine
-                parts.append(part.astype(jnp.bfloat16))
-            ordered = dot(order, jnp.concatenate(parts, axis=1)).astype(jnp.bfloat16)
-            for u in range(0, span, per_head):
-                out_ref[:, (first + u) // per_head, :, offset : offset + per_head] = ordered[
-                    :, u : u + per_head
-                ].reshape(groups, rows // groups, per_head)
-        offset += per_head
-
-
-def project(tokens, gain, rank, cosine, sine, weights, kinds, groups, heads):
-    rows, width = tokens.shape
+    groups = devices // heads
     columns = sum(w.shape[1] for w in weights)
+    span = 256
+    parts = 4
     flops = 2 * rows * width * columns
-    size = 2 * (width * columns + rows * width * 2 + rows * columns)
+    size = 2 * (width * columns + rows * width + rows * columns)
     return pl.pallas_call(
-        functools.partial(project_kernel, kinds, groups),
+        functools.partial(project_kernel, kinds, devices, heads),
         out_shape=jax.ShapeDtypeStruct((groups, heads, rows // groups, columns // heads), jnp.bfloat16),
-        in_specs=[IN_PLACE] + [WHOLE] * 4 + [IN_PLACE] * len(weights),
+        in_specs=[SCALARS] + [WHOLE] * 3 + [IN_PLACE] * (len(weights) + 1),
         out_specs=WHOLE,
-        scratch_shapes=[pltpu.VMEM((rows, width), jnp.bfloat16)] * 2
-        + [pltpu.VMEM(w.shape, jnp.bfloat16) for w in weights]
-        + [pltpu.SemaphoreType.DMA((len(weights) + 1,))],
-        compiler_params=pltpu.CompilerParams(vmem_limit_bytes=size + 10 * MIB),
+        scratch_shapes=[
+            pltpu.VMEM((rows, width), jnp.bfloat16),
+            pltpu.VMEM((rows, width), jnp.bfloat16),
+            pltpu.VMEM((columns // span, width, span), jnp.bfloat16),
+            pltpu.SemaphoreType.DMA((parts,)),
+            pltpu.SemaphoreType.DMA((columns // span,)),
+        ],
+        compiler_params=pltpu.CompilerParams(vmem_limit_bytes=56 * MIB),
         cost_estimate=pl.CostEstimate(flops=flops, bytes_accessed=size, transcendentals=0),
-    )(tokens, gain, rank, cosine, sine, *weights)
+    )(scalars, positions, freq, gain, tokens, *weights)
 
 
 def place_kernel(arrived_ref, slot_ref, *outs):
@@ -132,29 +179,32 @@
         for piece in pieces[3 * half : 3 * half + 3]:
             held[half, first : first + piece.shape[0], :] = piece[...]
             first += piece.shape[0]
+    indices = (target, per_run - 1 - target)
+    at = [pl.multiple_of(index * block, block) for index in indices]
+    iota = lax.broadcasted_iota(jnp.int32, (block, arrived), 0)
+    chosen = [(iota + (at[half] + half * run) == slot).astype(jnp.bfloat16) for half in range(2)]
+    queries = dot(jnp.concatenate(chosen, axis=0), query_ref[...]).astype(jnp.bfloat16)
     for half in range(2):
-        index = target if half == 0 else per_run - 1 - target
-        at = pl.multiple_of(index * block, block)
-        slots = lax.broadcasted_iota(jnp.int32, (block, arrived), 0) + (at + half * run)
-        query = dot((slots == slot).astype(jnp.bfloat16), query_ref[...]).astype(jnp.bfloat16)
-        key = held[half, pl.ds(at, keys), :HEAD_SIZE]
-        value = held[half, pl.ds(at, keys), HEAD_SIZE:]
-        begin = starts[half] + at
+        here = slice(half * block, (half + 1) * block)
+        key = held[half, pl.ds(at[half], keys), :HEAD_SIZE]
+        value = held[half, pl.ds(at[half], keys), HEAD_SIZE:]
+        begin = starts[half] + at[half]
         query_at = lax.broadcasted_iota(jnp.int32, (block, 1), 0) + begin
         key_at = lax.broadcasted_iota(jnp.int32, (1, keys), 1) + (begin - reach)
         doc_start = jnp.max(jnp.where(ends <= query_at, ends, 0), axis=1, keepdims=True)
         allowed = (key_at >= doc_start) & (key_at <= query_at)
+        stacked = jnp.concatenate(
+            [queries[here, h * HEAD_SIZE : (h + 1) * HEAD_SIZE] for h in range(heads)], axis=0
+        )
+        scores = lax.dot_general(stacked, key, (((1,), (1,)), ((), ())), preferred_element_type=jnp.float32)
+        scores = jnp.where(allowed[None], scores.reshape(heads, block, keys), jnp.float32(-1e30))
+        scores = scores.reshape(heads * block, keys)
+        top = jnp.max(scores, axis=1, keepdims=True)
+        weights = jnp.exp2((scores - top) * factor)
+        total = jnp.sum(weights, axis=1, keepdims=True)
+        mixed = (dot(weights.astype(jnp.bfloat16), value) / total).astype(jnp.bfloat16)
         for h in range(heads):
-            columns = slice(h * HEAD_SIZE, (h + 1) * HEAD_SIZE)
-            scores = lax.dot_general(
-                query[:, columns], key, (((1,), (1,)), ((), ())), preferred_element_type=jnp.float32
-            )
-            scores = jnp.where(allowed, scores, jnp.float32(-1e30))
-            top = jnp.max(scores, axis=1, keepdims=True)
-            weights = jnp.exp2((scores - top) * factor)
-            total = jnp.sum(weights, axis=1, keepdims=True)
-            mixed = dot(weights.astype(jnp.bfloat16), value) / total
-            out_ref[half * block : (half + 1) * block, columns] = mixed.astype(jnp.bfloat16)
+            out_ref[here, h * HEAD_SIZE : (h + 1) * HEAD_SIZE] = mixed[h * block : (h + 1) * block]
 
 
 def attend(scalars, query, slot, ends, pieces, block):
@@ -211,23 +261,9 @@
     run = members * block
     group_rows = rows // groups
 
-    def group_of(where_at):
-        block_id = where_at // block
-        return jnp.minimum(block_id, 2 * devices - 1 - block_id) // members
-
-    mine = lax.dynamic_slice_in_dim(positions, device * rows, rows, 0)
-    my_groups = group_of(mine)
-    row = jnp.arange(rows, dtype=jnp.int32)
-    earlier = (my_groups[:, None] == my_groups[None, :]) & (row[:, None] < row[None, :])
-    rank = my_groups * group_rows + jnp.sum(earlier.astype(jnp.int32), axis=0)
     half = HEAD_SIZE // 2
-    freq = ROPE_THETA ** (-(jnp.arange(half, dtype=jnp.float32) * 2.0 / HEAD_SIZE))
-    angle = mine.astype(jnp.float32)[:, None] * freq[None, :]
-    cosine, sine = jnp.cos(angle), jnp.sin(angle)
-    cosine = jnp.concatenate([cosine, cosine], axis=1)
-    sine = jnp.concatenate([-sine, sine], axis=1)
-    gain = gain[None, :]
-    rank = rank[None, :]
+    freq = ROPE_THETA ** (-(jnp.arange(HEAD_SIZE, dtype=jnp.float32) % half * 2.0 / HEAD_SIZE))
+    operands = (device.reshape(1), positions.reshape(-1, 128), freq[None, :], gain, tokens)
 
     def exchange(ordered):
         width = ordered.shape[3]
@@ -235,12 +271,12 @@
         flat = lax.all_to_all(flat, "ctx", split_axis=0, concat_axis=0, tiled=True)
         return flat.reshape(devices * group_rows, width)
 
-    kv = project(tokens, gain, rank, cosine, sine, (w_key, value_weight), (True, False), groups, members)
+    kv = project(*operands, (w_key, value_weight), (True, False), devices, members)
     kv = exchange(kv)
-    query = project(tokens, gain, rank, cosine, sine, (w_query,), (True,), groups, members)
+    query = project(*operands, (w_query,), (True,), devices, members)
 
     table = positions.reshape(devices, rows)
-    ours = group_of(table) == group
+    ours = group_of(table, block, devices, members) == group
     first_run = group * run
     second_run = (2 * devices - members) * block - group * run
     slots = jnp.where(table // run == group, table - first_run, table - second_run + run)

time: 95.7 us -> 94.1 us (0.983)
  local copies, waits for them, and re-layouts: 12.7 us -> 0.28 us
  Pallas kernels: 32 us -> 41.6 us
  waiting for transfers between devices: 23.4 us -> 25.6 us
  other arithmetic: 3.22 us -> 2.15 us
    pallas_call x2, Pallas kernels: 17.1 us -> 31.5 us  [project(): pl.pallas_call(functools.partial(project_kernel, kinds, devices, heads),...]
    unnamed x14 -> x4, local copies, waits for them, and re-layouts: 11.7 us -> 0.01 us
    pallas_call x4, Pallas kernels: 13.1 us -> 8.3 us  [attend(): pl.pallas_call(functools.partial(attend_kernel, block), out_shape=jax.Sha...]
    ppermute x3, waiting for transfers between devices: 3.86 us -> 6.26 us  [shards(): out = lax.ppermute(out, 'ctx', route)]
  transfers between devices with their start and end apart: 7 -> 7, of which waited for: 2 -> 2; matrix products, arithmetic and copies ran while one was open for 2% -> 2% of each run, Pallas kernels for 21% -> 29%
where the time goes in v2:
time: 94.1 us; the launch traced here: 93.7 us
  Pallas kernels  41.6 us (44%)
  waiting for transfers between devices  25.6 us (27%)
  starting transfers between devices  23.9 us (25%)
  other arithmetic  2.15 us (2%)
    pallas_call x2, Pallas kernels, project(): pl.pallas_call(functools.partial(project_kernel, kinds, devices, heads),...  31.5 us
    ppermute x1, waiting for transfers between devices, shards(): late_halo = lax.ppermute(late_tail, 'ctx', down)  19.3 us
    all_to_all x2, starting transfers between devices, exchange(): flat = lax.all_to_all(flat, 'ctx', split_axis=0, concat_axis=0, tiled=True)  14.2 us
    pallas_call x4, Pallas kernels, attend(): pl.pallas_call(functools.partial(attend_kernel, block), out_shape=jax.Sha...  8.3 us
    ppermute x3, waiting for transfers between devices, shards(): out = lax.ppermute(out, 'ctx', route)  6.26 us
    ppermute x1, starting transfers between devices, shards(): early_halo = lax.ppermute(early_tail, 'ctx', up)  4.03 us
    ppermute x3, starting transfers between devices, shards(): out = lax.ppermute(out, 'ctx', route)  3.68 us
    ppermute x1, starting transfers between devices, shards(): late_halo = lax.ppermute(late_tail, 'ctx', down)  2.03 us
  transfers between devices with their start and end apart: 7, of which 2 were waited for; matrix products, arithmetic and copies ran while one was open for 2% of the time, Pallas kernels for 29%

profile of v2, /device:TPU:8, one launch (start us, length us, event | category | flops | bytes accessed | tf_op | source)
XLA Modules:
  0.0 93.7 jit_solution(152133801871916021)
XLA Ops:
  0.0 0.5 fusion.15.freq_ref
  0.5 11.7 %shard_map.73 = bf16[4,4,64,256]{3,2,1,0:T(8,128)(2,1)} custom-call(s32[1]{0:T(128)} %bitcast.3.scalar_ref, s32[32,128]{1,0:T(8,128)} %bitcast.26, f32[1,128]{1,0:T(1,128)} %fusion.15.freq_ref, bf16[4096]{0:T(1024)(128)(2,1)} %gain_ref.3, bf16[256,4096]{1,0:T(8,128)(2,1)} %tokens_hbm.3, bf16[4096,512]{1,0:T(8,128)(2,1)} %rest_0_.2, bf16[4096,512]{1,0:T(8,128)(2,1)} %rest_1_.1), custom_call_target="tpu_custom_call" | custom-call | flops 2147483648 | bytes 11010048 | tf_op jit(solution)/shard_map/pallas_call | solution.py:121
  12.2 7.2 %all-to-all-start = ((bf16[16,64,256]{2,1,0:T(8,128)(2,1)}), bf16[16,64,256]{2,1,0:T(8,128)(2,1)S(1)}, u32[]{:S(2)}, u32[]{:S(2)}) async-start(bf16[16,64,256]{2,1,0:T(8,128)(2,1)} %bitcast.25), calls=%async_computation | async-start | bytes 1048576 | tf_op jit(solution)/shard_map/all_to_all | solution.py:271
  19.5 19.8 %shard_map.74 = bf16[4,4,64,512]{3,2,1,0:T(8,128)(2,1)} custom-call(s32[1]{0:T(128)} %bitcast.3.scalar_ref, s32[32,128]{1,0:T(8,128)} %bitcast.27, f32[1,128]{1,0:T(1,128)} %fusion.15.freq_ref, bf16[4096]{0:T(1024)(128)(2,1)} %gain_ref.3, bf16[256,4096]{1,0:T(8,128)(2,1)} %tokens_hbm.3, bf16[4096,2048]{1,0:T(8,128)(2,1)} %rest_0_.3), custom_call_target="tpu_custom_call" | custom-call | flops 4294967296 | bytes 19922944 | tf_op jit(solution)/shard_map/pallas_call | solution.py:121
  39.3 6.9 %all-to-all-start.1 = ((bf16[16,64,512]{2,1,0:T(8,128)(2,1)}), bf16[16,64,512]{2,1,0:T(8,128)(2,1)S(1)}, u32[]{:S(2)}, u32[]{:S(2)}) async-start(bf16[16,64,512]{2,1,0:T(8,128)(2,1)} %bitcast.24), calls=%async_computation.1 | async-start | bytes 2097152 | tf_op jit(solution)/shard_map/all_to_all | solution.py:271
  46.3 0.2 reduce-window_2_clone.1.ends_ref
  46.5 0.6 reduce-window.9
  47.1 0.2 slice_reduce_fusion
  47.3 0.1 bitcast_select_fusion
  47.4 0.4 select_reduce_fusion
  47.9 0.7 shard_map.75
  48.7 2.0 %collective-permute-start.1 = (bf16[384,256]{1,0:T(8,128)(2,1)S(1)}, bf16[384,256]{1,0:T(8,128)(2,1)S(1)}, u32[]{:S(2)}, u32[]{:S(2)}) collective-permute-start(bf16[384,256]{1,0:T(8,128)(2,1)S(1)} %get-tuple-element.15.rest_5_), channel_id=1, source_target_pairs={{4,0},{5,1},{6,2},{7,3},{8,4},{9,5},{10,6},{11,7},{12,8},{13,9},{1... | collective-permute-start | bytes 589832 | tf_op jit(solution)/shard_map/ppermute | solution.py:297
  50.7 0.1 add_add_fusion.2.scalar_ref
  50.9 4.0 %collective-permute-start = (bf16[384,256]{1,0:T(8,128)(2,1)S(1)}, bf16[384,256]{1,0:T(8,128)(2,1)S(1)}, u32[]{:S(2)}, u32[]{:S(2)}) collective-permute-start(bf16[384,256]{1,0:T(8,128)(2,1)S(1)} %get-tuple-element.13.rest_2_), channel_id=1, source_target_pairs={{0,4},{1,5},{2,6},{3,7},{4,8},{5,9},{6,10},{7,11},{8,12},{9,13},{1... | collective-permute-start | bytes 589832 | tf_op jit(solution)/shard_map/ppermute | solution.py:296
  54.9 19.3 %collective-permute-done.1 = bf16[384,256]{1,0:T(8,128)(2,1)S(1)} collective-permute-done((bf16[384,256]{1,0:T(8,128)(2,1)S(1)}, bf16[384,256]{1,0:T(8,128)(2,1)S(1)}, u32[]{:S(2)}, u32[]{:S(2)}) %collective-permute-start.1) | collective-permute-done | bytes 196640 | tf_op jit(solution)/shard_map/ppermute | solution.py:297
  74.3 2.1 %shard_map.77 = bf16[256,512]{1,0:T(8,128)(2,1)S(1)} custom-call(s32[3]{0:T(128)S(1)} %add_add_fusion.1.scalar_ref, bf16[1024,512]{1,0:T(8,128)(2,1)S(1)} %bitcast.19, s32[1,1024]{1,0:T(1,128)S(1)} %reshape.191.slot_ref, s32[1,32]{1,0:T(1,128)S(1)} %reduce-window_2_clone.1.ends_ref, bf16[384,256]{1,0:T(8,128)(2,1)S(1)} %collective-permute-done.rest_0_, ...), custom_call_target="tpu_custom_call" | custom-call | flops 536870912 | bytes 1966080 | tf_op jit(solution)/shard_map/pallas_call | solution.py:215
  76.4 1.5 %collective-permute-start.2 = (bf16[256,512]{1,0:T(8,128)(2,1)S(1)}, bf16[256,512]{1,0:T(8,128)(2,1)S(1)}, u32[]{:S(2)}, u32[]{:S(2)}) collective-permute-start(bf16[256,512]{1,0:T(8,128)(2,1)S(1)} %shard_map.77), channel_id=1, source_target_pairs={{0,1},{1,0},{2,3},{3,2},{4,5},{5,4},{6,7},{7,6},{8,9},{9,8},{10,11... | collective-permute-start | bytes 786440 | tf_op jit(solution)/shard_map/ppermute | solution.py:308
  77.9 2.1 %shard_map.78 = bf16[256,512]{1,0:T(8,128)(2,1)S(1)} custom-call(s32[3]{0:T(128)S(1)} %add_add_fusion.2.scalar_ref, bf16[1024,512]{1,0:T(8,128)(2,1)S(1)} %bitcast.20, s32[1,1024]{1,0:T(1,128)S(1)} %reshape.191.slot_ref, s32[1,32]{1,0:T(1,128)S(1)} %reduce-window_2_clone.1.ends_ref, bf16[384,256]{1,0:T(8,128)(2,1)S(1)} %collective-permute-done.rest_0_, ...), custom_call_target="tpu_custom_call" | custom-call | flops 536870912 | bytes 1966080 | tf_op jit(solution)/shard_map/pallas_call | solution.py:215
  80.0 1.6 %collective-permute-start.3 = (bf16[256,512]{1,0:T(8,128)(2,1)S(1)}, bf16[256,512]{1,0:T(8,128)(2,1)S(1)}, u32[]{:S(2)}, u32[]{:S(2)}) collective-permute-start(bf16[256,512]{1,0:T(8,128)(2,1)S(1)} %shard_map.78), channel_id=1, source_target_pairs={{0,2},{1,3},{2,0},{3,1},{4,6},{5,7},{6,4},{7,5},{8,10},{9,11},{10,... | collective-permute-start | bytes 786440 | tf_op jit(solution)/shard_map/ppermute | solution.py:308
  81.5 2.1 %shard_map.79 = bf16[256,512]{1,0:T(8,128)(2,1)S(1)} custom-call(s32[3]{0:T(128)S(1)} %add_add_fusion.3.scalar_ref, bf16[1024,512]{1,0:T(8,128)(2,1)S(1)} %bitcast.21, s32[1,1024]{1,0:T(1,128)S(1)} %reshape.191.slot_ref, s32[1,32]{1,0:T(1,128)S(1)} %reduce-window_2_clone.1.ends_ref, bf16[384,256]{1,0:T(8,128)(2,1)S(1)} %collective-permute-done.rest_0_, ...), custom_call_target="tpu_custom_call" | custom-call | flops 536870912 | bytes 1966080 | tf_op jit(solution)/shard_map/pallas_call | solution.py:215
  83.6 0.6 collective-permute-start.4
  84.3 2.1 %shard_map.76.rest_0_ = bf16[256,512]{1,0:T(8,128)(2,1)S(1)} custom-call(s32[3]{0:T(128)S(1)} %add_add_fusion.scalar_ref, bf16[1024,512]{1,0:T(8,128)(2,1)S(1)} %bitcast.22, s32[1,1024]{1,0:T(1,128)S(1)} %reshape.191.slot_ref, s32[1,32]{1,0:T(1,128)S(1)} %reduce-window_2_clone.1.ends_ref, bf16[384,256]{1,0:T(8,128)(2,1)S(1)} %collective-permute-done.rest_0_, ...), custom_call_target="tpu_custom_call" | custom-call | flops 536870912 | bytes 1966080 | tf_op jit(solution)/shard_map/pallas_call | solution.py:215
  86.4 6.3 %collective-permute-done.3.rest_2_ = bf16[256,512]{1,0:T(8,128)(2,1)S(1)} collective-permute-done((bf16[256,512]{1,0:T(8,128)(2,1)S(1)}, bf16[256,512]{1,0:T(8,128)(2,1)S(1)}, u32[]{:S(2)}, u32[]{:S(2)}) %collective-permute-start.3) | collective-permute-done | bytes 262176 | tf_op jit(solution)/shard_map/ppermute | solution.py:308
  92.6 1.0 %shard_map.80 = bf16[256,2048]{1,0:T(8,128)(2,1)} custom-call(s32[1]{0:T(128)} %bitcast.scalar_ref, bf16[256,512]{1,0:T(8,128)(2,1)S(1)} %shard_map.76.rest_0_, bf16[256,512]{1,0:T(8,128)(2,1)S(1)} %collective-permute-done.2.rest_1_, bf16[256,512]{1,0:T(8,128)(2,1)S(1)} %collective-permute-done.3.rest_2_, bf16[256,512]{1,0:T(8,128)(2,1)S(1)} %collective-permute-done.4.rest_3_), custom_call_target="tpu_custom_call" | custom-call | bytes 2097152 | tf_op jit(solution)/shard_map/pallas_call | solution.py:240
  (18 shorter events, 0.4 us)
Async XLA Ops:
  12.2 27.1 %all-to-all-start = ((bf16[16,64,256]{2,1,0:T(8,128)(2,1)}), bf16[16,64,256]{2,1,0:T(8,128)(2,1)S(1)}, u32[]{:S(2)}, u32[]{:S(2)}) async-start(bf16[16,64,256]{2,1,0:T(8,128)(2,1)} %bitcast.25), calls=%async_computation | async-start | bytes 1048576 | tf_op jit(solution)/shard_map/all_to_all | solution.py:271
  19.5 26.8 %copy-start = (s32[4096]{0:T(1024)S(1)}, s32[4096]{0:T(1024)}, u32[]{:S(2)}) copy-start(s32[4096]{0:T(1024)} %param.8) | copy-start | bytes 49156
  19.5 26.8 %copy-start.1 = (s32[32]{0:T(128)S(1)}, s32[32]{0:T(128)}, u32[]{:S(2)}) copy-start(s32[32]{0:T(128)} %param.9) | copy-start | bytes 388
  39.3 35.0 %all-to-all-start.1 = ((bf16[16,64,512]{2,1,0:T(8,128)(2,1)}), bf16[16,64,512]{2,1,0:T(8,128)(2,1)S(1)}, u32[]{:S(2)}, u32[]{:S(2)}) async-start(bf16[16,64,512]{2,1,0:T(8,128)(2,1)} %bitcast.24), calls=%async_computation.1 | async-start | bytes 2097152 | tf_op jit(solution)/shard_map/all_to_all | solution.py:271
  48.7 25.6 %collective-permute-start.1 = (bf16[384,256]{1,0:T(8,128)(2,1)S(1)}, bf16[384,256]{1,0:T(8,128)(2,1)S(1)}, u32[]{:S(2)}, u32[]{:S(2)}) collective-permute-start(bf16[384,256]{1,0:T(8,128)(2,1)S(1)} %get-tuple-element.15.rest_5_), channel_id=1, source_target_pairs={{4,0},{5,1},{6,2},{7,3},{8,4},{9,5},{10,6},{11,7},{12,8},{13,9},{1... | collective-permute-start | bytes 589832 | tf_op jit(solution)/shard_map/ppermute | solution.py:297
  50.9 23.4 %collective-permute-start = (bf16[384,256]{1,0:T(8,128)(2,1)S(1)}, bf16[384,256]{1,0:T(8,128)(2,1)S(1)}, u32[]{:S(2)}, u32[]{:S(2)}) collective-permute-start(bf16[384,256]{1,0:T(8,128)(2,1)S(1)} %get-tuple-element.13.rest_2_), channel_id=1, source_target_pairs={{0,4},{1,5},{2,6},{3,7},{4,8},{5,9},{6,10},{7,11},{8,12},{9,13},{1... | collective-permute-start | bytes 589832 | tf_op jit(solution)/shard_map/ppermute | solution.py:296
  76.4 10.0 %collective-permute-start.2 = (bf16[256,512]{1,0:T(8,128)(2,1)S(1)}, bf16[256,512]{1,0:T(8,128)(2,1)S(1)}, u32[]{:S(2)}, u32[]{:S(2)}) collective-permute-start(bf16[256,512]{1,0:T(8,128)(2,1)S(1)} %shard_map.77), channel_id=1, source_target_pairs={{0,1},{1,0},{2,3},{3,2},{4,5},{5,4},{6,7},{7,6},{8,9},{9,8},{10,11... | collective-permute-start | bytes 786440 | tf_op jit(solution)/shard_map/ppermute | solution.py:308
  80.0 12.7 %collective-permute-start.3 = (bf16[256,512]{1,0:T(8,128)(2,1)S(1)}, bf16[256,512]{1,0:T(8,128)(2,1)S(1)}, u32[]{:S(2)}, u32[]{:S(2)}) collective-permute-start(bf16[256,512]{1,0:T(8,128)(2,1)S(1)} %shard_map.78), channel_id=1, source_target_pairs={{0,2},{1,3},{2,0},{3,1},{4,6},{5,7},{6,4},{7,5},{8,10},{9,11},{10,... | collective-permute-start | bytes 786440 | tf_op jit(solution)/shard_map/ppermute | solution.py:308
  83.6 9.0 %collective-permute-start.4 = (bf16[256,512]{1,0:T(8,128)(2,1)S(1)}, bf16[256,512]{1,0:T(8,128)(2,1)S(1)}, u32[]{:S(2)}, u32[]{:S(2)}) collective-permute-start(bf16[256,512]{1,0:T(8,128)(2,1)S(1)} %shard_map.79), channel_id=1, source_target_pairs={{0,3},{1,2},{2,1},{3,0},{4,7},{5,6},{6,5},{7,4},{8,11},{9,10},{10,... | collective-permute-start | bytes 786440 | tf_op jit(solution)/shard_map/ppermute | solution.py:308

commit v3 on v2

--- a/solution.py
+++ b/solution.py
@@ -47,15 +47,15 @@
     for i in range(parts):
         at = pl.ds(i * part, part)
         token_copies.append(pltpu.make_async_copy(tokens_hbm.at[at], tokens.at[at], token_sems.at[i]))
+        token_copies[i].start()
     for i in range(count):
         for first in range(0, weights_hbm[i].shape[1], span):
             j = len(copies)
             source = weights_hbm[i].at[:, pl.ds(first, span)]
             copies.append(pltpu.make_async_copy(source, weights.at[j], sems.at[j]))
             origin.append((i, first))
-    for copy in token_copies + copies:
-        copy.start()
-
+
+    copies[0].start()
     lanes = positions_ref.shape[1]
     stripes = rows // lanes
     mine = jnp.concatenate(
@@ -87,6 +87,8 @@
             return 0
 
         lax.fori_loop(0, part // step, norm, 0, unroll=True)
+    if chunks > 1:
+        copies[1].start()
     for first in range(0, width, 512):
         columns = slice(first, first + 512)
         normed[:, columns] = dot(order, tokens[:, columns]).astype(jnp.bfloat16)
@@ -97,6 +99,8 @@
     for j in range(chunks):
         i, first = origin[j]
         copies[j].wait()
+        if j + 2 < chunks:
+            copies[j + 2].start()
         product = dot(normed[...], weights[j])
         per_head = offsets[i + 1] - offsets[i]
         for u in range(0, span, HEAD_SIZE):
@@ -114,7 +118,7 @@
     rows, width = tokens.shape
     groups = devices // heads
     columns = sum(w.shape[1] for w in weights)
-    span = 256
+    span = 512
     parts = 4
     flops = 2 * rows * width * columns
     size = 2 * (width * columns + rows * width + rows * columns)

time: 94.1 us -> 81.7 us (0.87)
  the two profiles are of different devices: /device:TPU:8 before, /device:TPU:12 now
where the time goes in v3:
time: 81.7 us; the launch traced here: 81.2 us
  waiting for transfers between devices  29.3 us (36%)
  Pallas kernels  27.5 us (34%)
  starting transfers between devices  21.8 us (27%)
  other arithmetic  2.15 us (3%)
    ppermute x1, waiting for transfers between devices, shards(): late_halo = lax.ppermute(late_tail, 'ctx', down)  19.5 us
    pallas_call x2, Pallas kernels, project(): pl.pallas_call(functools.partial(project_kernel, kinds, devices, heads),...  17.4 us
    all_to_all x2, starting transfers between devices, exchange(): flat = lax.all_to_all(flat, 'ctx', split_axis=0, concat_axis=0, tiled=True)  12.3 us
    pallas_call x4, Pallas kernels, attend(): pl.pallas_call(functools.partial(attend_kernel, block), out_shape=jax.Sha...  8.3 us
    ppermute x3, waiting for transfers between devices, shards(): out = lax.ppermute(out, 'ctx', route)  6.27 us
    ppermute x3, starting transfers between devices, shards(): out = lax.ppermute(out, 'ctx', route)  3.68 us
    all_to_all x2, waiting for transfers between devices, exchange(): flat = lax.all_to_all(flat, 'ctx', split_axis=0, concat_axis=0, tiled=True)  3.62 us
    ppermute x1, starting transfers between devices, shards(): early_halo = lax.ppermute(early_tail, 'ctx', up)  3.37 us
  transfers between devices with their start and end apart: 7, of which 3 were waited for; matrix products, arithmetic and copies ran while one was open for 2% of the time, Pallas kernels for 21%

profile of v3, /device:TPU:12, one launch (start us, length us, event | category | flops | bytes accessed | tf_op | source)
XLA Modules:
  0.0 81.2 jit_solution(7279718930030321003)
XLA Ops:
  0.0 0.5 fusion.15.freq_ref
  0.5 7.1 %shard_map.73 = bf16[4,4,64,256]{3,2,1,0:T(8,128)(2,1)} custom-call(s32[1]{0:T(128)} %bitcast.3.scalar_ref, s32[32,128]{1,0:T(8,128)} %bitcast.26, f32[1,128]{1,0:T(1,128)} %fusion.15.freq_ref, bf16[4096]{0:T(1024)(128)(2,1)} %gain_ref.3, bf16[256,4096]{1,0:T(8,128)(2,1)} %tokens_hbm.3, bf16[4096,512]{1,0:T(8,128)(2,1)} %rest_0_.2, bf16[4096,512]{1,0:T(8,128)(2,1)} %rest_1_.1), custom_call_target="tpu_custom_call" | custom-call | flops 2147483648 | bytes 11010048 | tf_op jit(solution)/shard_map/pallas_call | solution.py:125
  7.7 7.2 %all-to-all-start = ((bf16[16,64,256]{2,1,0:T(8,128)(2,1)}), bf16[16,64,256]{2,1,0:T(8,128)(2,1)S(1)}, u32[]{:S(2)}, u32[]{:S(2)}) async-start(bf16[16,64,256]{2,1,0:T(8,128)(2,1)} %bitcast.25), calls=%async_computation | async-start | bytes 1048576 | tf_op jit(solution)/shard_map/all_to_all | solution.py:275
  14.9 10.3 %shard_map.74 = bf16[4,4,64,512]{3,2,1,0:T(8,128)(2,1)} custom-call(s32[1]{0:T(128)} %bitcast.3.scalar_ref, s32[32,128]{1,0:T(8,128)} %bitcast.27, f32[1,128]{1,0:T(1,128)} %fusion.15.freq_ref, bf16[4096]{0:T(1024)(128)(2,1)} %gain_ref.3, bf16[256,4096]{1,0:T(8,128)(2,1)} %tokens_hbm.3, bf16[4096,2048]{1,0:T(8,128)(2,1)} %rest_0_.3), custom_call_target="tpu_custom_call" | custom-call | flops 4294967296 | bytes 19922944 | tf_op jit(solution)/shard_map/pallas_call | solution.py:125
  25.1 3.6 %all-to-all-done = bf16[16,64,256]{2,1,0:T(8,128)(2,1)S(1)} async-done(((bf16[16,64,256]{2,1,0:T(8,128)(2,1)}), bf16[16,64,256]{2,1,0:T(8,128)(2,1)S(1)}, u32[]{:S(2)}, u32[]{:S(2)}) %all-to-all-start) | async-done | bytes 524320 | tf_op jit(solution)/shard_map/all_to_all | solution.py:275
  28.8 5.1 %all-to-all-start.1 = ((bf16[16,64,512]{2,1,0:T(8,128)(2,1)}), bf16[16,64,512]{2,1,0:T(8,128)(2,1)S(1)}, u32[]{:S(2)}, u32[]{:S(2)}) async-start(bf16[16,64,512]{2,1,0:T(8,128)(2,1)} %bitcast.24), calls=%async_computation.1 | async-start | bytes 2097152 | tf_op jit(solution)/shard_map/all_to_all | solution.py:275
  33.9 0.2 reduce-window_2_clone.1.ends_ref
  34.2 0.6 reduce-window.9
  34.8 0.2 slice_reduce_fusion
  35.0 0.1 bitcast_select_fusion
  35.1 0.4 select_reduce_fusion
  35.6 0.7 shard_map.75
  36.3 2.5 %collective-permute-start.1 = (bf16[384,256]{1,0:T(8,128)(2,1)S(1)}, bf16[384,256]{1,0:T(8,128)(2,1)S(1)}, u32[]{:S(2)}, u32[]{:S(2)}) collective-permute-start(bf16[384,256]{1,0:T(8,128)(2,1)S(1)} %get-tuple-element.15.rest_5_), channel_id=1, source_target_pairs={{4,0},{5,1},{6,2},{7,3},{8,4},{9,5},{10,6},{11,7},{12,8},{13,9},{1... | collective-permute-start | bytes 589832 | tf_op jit(solution)/shard_map/ppermute | solution.py:301
  38.9 3.4 %collective-permute-start = (bf16[384,256]{1,0:T(8,128)(2,1)S(1)}, bf16[384,256]{1,0:T(8,128)(2,1)S(1)}, u32[]{:S(2)}, u32[]{:S(2)}) collective-permute-start(bf16[384,256]{1,0:T(8,128)(2,1)S(1)} %get-tuple-element.13.rest_2_), channel_id=1, source_target_pairs={{0,4},{1,5},{2,6},{3,7},{4,8},{5,9},{6,10},{7,11},{8,12},{9,13},{1... | collective-permute-start | bytes 589832 | tf_op jit(solution)/shard_map/ppermute | solution.py:300
  42.3 19.5 %collective-permute-done.1 = bf16[384,256]{1,0:T(8,128)(2,1)S(1)} collective-permute-done((bf16[384,256]{1,0:T(8,128)(2,1)S(1)}, bf16[384,256]{1,0:T(8,128)(2,1)S(1)}, u32[]{:S(2)}, u32[]{:S(2)}) %collective-permute-start.1) | collective-permute-done | bytes 196640 | tf_op jit(solution)/shard_map/ppermute | solution.py:301
  61.8 2.1 %shard_map.77 = bf16[256,512]{1,0:T(8,128)(2,1)S(1)} custom-call(s32[3]{0:T(128)S(1)} %add_add_fusion.1.scalar_ref, bf16[1024,512]{1,0:T(8,128)(2,1)S(1)} %bitcast.19, s32[1,1024]{1,0:T(1,128)S(1)} %reshape.191.slot_ref, s32[1,32]{1,0:T(1,128)S(1)} %reduce-window_2_clone.1.ends_ref, bf16[384,256]{1,0:T(8,128)(2,1)S(1)} %collective-permute-done.rest_0_, ...), custom_call_target="tpu_custom_call" | custom-call | flops 536870912 | bytes 1966080 | tf_op jit(solution)/shard_map/pallas_call | solution.py:219
  63.9 1.5 %collective-permute-start.2 = (bf16[256,512]{1,0:T(8,128)(2,1)S(1)}, bf16[256,512]{1,0:T(8,128)(2,1)S(1)}, u32[]{:S(2)}, u32[]{:S(2)}) collective-permute-start(bf16[256,512]{1,0:T(8,128)(2,1)S(1)} %shard_map.77), channel_id=1, source_target_pairs={{0,1},{1,0},{2,3},{3,2},{4,5},{5,4},{6,7},{7,6},{8,9},{9,8},{10,11... | collective-permute-start | bytes 786440 | tf_op jit(solution)/shard_map/ppermute | solution.py:312
  65.4 2.1 %shard_map.78 = bf16[256,512]{1,0:T(8,128)(2,1)S(1)} custom-call(s32[3]{0:T(128)S(1)} %add_add_fusion.2.scalar_ref, bf16[1024,512]{1,0:T(8,128)(2,1)S(1)} %bitcast.20, s32[1,1024]{1,0:T(1,128)S(1)} %reshape.191.slot_ref, s32[1,32]{1,0:T(1,128)S(1)} %reduce-window_2_clone.1.ends_ref, bf16[384,256]{1,0:T(8,128)(2,1)S(1)} %collective-permute-done.rest_0_, ...), custom_call_target="tpu_custom_call" | custom-call | flops 536870912 | bytes 1966080 | tf_op jit(solution)/shard_map/pallas_call | solution.py:219
  67.5 0.5 collective-permute-start.3
  68.0 2.1 %shard_map.79 = bf16[256,512]{1,0:T(8,128)(2,1)S(1)} custom-call(s32[3]{0:T(128)S(1)} %add_add_fusion.3.scalar_ref, bf16[1024,512]{1,0:T(8,128)(2,1)S(1)} %bitcast.21, s32[1,1024]{1,0:T(1,128)S(1)} %reshape.191.slot_ref, s32[1,32]{1,0:T(1,128)S(1)} %reduce-window_2_clone.1.ends_ref, bf16[384,256]{1,0:T(8,128)(2,1)S(1)} %collective-permute-done.rest_0_, ...), custom_call_target="tpu_custom_call" | custom-call | flops 536870912 | bytes 1966080 | tf_op jit(solution)/shard_map/pallas_call | solution.py:219
  70.1 1.6 %collective-permute-start.4 = (bf16[256,512]{1,0:T(8,128)(2,1)S(1)}, bf16[256,512]{1,0:T(8,128)(2,1)S(1)}, u32[]{:S(2)}, u32[]{:S(2)}) collective-permute-start(bf16[256,512]{1,0:T(8,128)(2,1)S(1)} %shard_map.79), channel_id=1, source_target_pairs={{0,3},{1,2},{2,1},{3,0},{4,7},{5,6},{6,5},{7,4},{8,11},{9,10},{10,... | collective-permute-start | bytes 786440 | tf_op jit(solution)/shard_map/ppermute | solution.py:312
  71.8 2.1 %shard_map.76.rest_0_ = bf16[256,512]{1,0:T(8,128)(2,1)S(1)} custom-call(s32[3]{0:T(128)S(1)} %add_add_fusion.scalar_ref, bf16[1024,512]{1,0:T(8,128)(2,1)S(1)} %bitcast.22, s32[1,1024]{1,0:T(1,128)S(1)} %reshape.191.slot_ref, s32[1,32]{1,0:T(1,128)S(1)} %reduce-window_2_clone.1.ends_ref, bf16[384,256]{1,0:T(8,128)(2,1)S(1)} %collective-permute-done.rest_0_, ...), custom_call_target="tpu_custom_call" | custom-call | flops 536870912 | bytes 1966080 | tf_op jit(solution)/shard_map/pallas_call | solution.py:219
  73.9 6.3 %collective-permute-done.3.rest_2_ = bf16[256,512]{1,0:T(8,128)(2,1)S(1)} collective-permute-done((bf16[256,512]{1,0:T(8,128)(2,1)S(1)}, bf16[256,512]{1,0:T(8,128)(2,1)S(1)}, u32[]{:S(2)}, u32[]{:S(2)}) %collective-permute-start.3) | collective-permute-done | bytes 262176 | tf_op jit(solution)/shard_map/ppermute | solution.py:312
  80.2 1.0 %shard_map.80 = bf16[256,2048]{1,0:T(8,128)(2,1)} custom-call(s32[1]{0:T(128)} %bitcast.scalar_ref, bf16[256,512]{1,0:T(8,128)(2,1)S(1)} %shard_map.76.rest_0_, bf16[256,512]{1,0:T(8,128)(2,1)S(1)} %collective-permute-done.2.rest_1_, bf16[256,512]{1,0:T(8,128)(2,1)S(1)} %collective-permute-done.3.rest_2_, bf16[256,512]{1,0:T(8,128)(2,1)S(1)} %collective-permute-done.4.rest_3_), custom_call_target="tpu_custom_call" | custom-call | bytes 2097152 | tf_op jit(solution)/shard_map/pallas_call | solution.py:244
  (18 shorter events, 0.5 us)
Async XLA Ops:
  7.7 21.1 %all-to-all-start = ((bf16[16,64,256]{2,1,0:T(8,128)(2,1)}), bf16[16,64,256]{2,1,0:T(8,128)(2,1)S(1)}, u32[]{:S(2)}, u32[]{:S(2)}) async-start(bf16[16,64,256]{2,1,0:T(8,128)(2,1)} %bitcast.25), calls=%async_computation | async-start | bytes 1048576 | tf_op jit(solution)/shard_map/all_to_all | solution.py:275
  14.8 19.0 %copy-start = (s32[4096]{0:T(1024)S(1)}, s32[4096]{0:T(1024)}, u32[]{:S(2)}) copy-start(s32[4096]{0:T(1024)} %param.8) | copy-start | bytes 49156
  14.8 19.1 %copy-start.1 = (s32[32]{0:T(128)S(1)}, s32[32]{0:T(128)}, u32[]{:S(2)}) copy-start(s32[32]{0:T(128)} %param.9) | copy-start | bytes 388
  28.8 33.0 %all-to-all-start.1 = ((bf16[16,64,512]{2,1,0:T(8,128)(2,1)}), bf16[16,64,512]{2,1,0:T(8,128)(2,1)S(1)}, u32[]{:S(2)}, u32[]{:S(2)}) async-start(bf16[16,64,512]{2,1,0:T(8,128)(2,1)} %bitcast.24), calls=%async_computation.1 | async-start | bytes 2097152 | tf_op jit(solution)/shard_map/all_to_all | solution.py:275
  36.3 25.5 %collective-permute-start.1 = (bf16[384,256]{1,0:T(8,128)(2,1)S(1)}, bf16[384,256]{1,0:T(8,128)(2,1)S(1)}, u32[]{:S(2)}, u32[]{:S(2)}) collective-permute-start(bf16[384,256]{1,0:T(8,128)(2,1)S(1)} %get-tuple-element.15.rest_5_), channel_id=1, source_target_pairs={{4,0},{5,1},{6,2},{7,3},{8,4},{9,5},{10,6},{11,7},{12,8},{13,9},{1... | collective-permute-start | bytes 589832 | tf_op jit(solution)/shard_map/ppermute | solution.py:301
  38.9 22.9 %collective-permute-start = (bf16[384,256]{1,0:T(8,128)(2,1)S(1)}, bf16[384,256]{1,0:T(8,128)(2,1)S(1)}, u32[]{:S(2)}, u32[]{:S(2)}) collective-permute-start(bf16[384,256]{1,0:T(8,128)(2,1)S(1)} %get-tuple-element.13.rest_2_), channel_id=1, source_target_pairs={{0,4},{1,5},{2,6},{3,7},{4,8},{5,9},{6,10},{7,11},{8,12},{9,13},{1... | collective-permute-start | bytes 589832 | tf_op jit(solution)/shard_map/ppermute | solution.py:300
  63.9 10.0 %collective-permute-start.2 = (bf16[256,512]{1,0:T(8,128)(2,1)S(1)}, bf16[256,512]{1,0:T(8,128)(2,1)S(1)}, u32[]{:S(2)}, u32[]{:S(2)}) collective-permute-start(bf16[256,512]{1,0:T(8,128)(2,1)S(1)} %shard_map.77), channel_id=1, source_target_pairs={{0,1},{1,0},{2,3},{3,2},{4,5},{5,4},{6,7},{7,6},{8,9},{9,8},{10,11... | collective-permute-start | bytes 786440 | tf_op jit(solution)/shard_map/ppermute | solution.py:312
  67.5 12.7 %collective-permute-start.3 = (bf16[256,512]{1,0:T(8,128)(2,1)S(1)}, bf16[256,512]{1,0:T(8,128)(2,1)S(1)}, u32[]{:S(2)}, u32[]{:S(2)}) collective-permute-start(bf16[256,512]{1,0:T(8,128)(2,1)S(1)} %shard_map.78), channel_id=1, source_target_pairs={{0,2},{1,3},{2,0},{3,1},{4,6},{5,7},{6,4},{7,5},{8,10},{9,11},{10,... | collective-permute-start | bytes 786440 | tf_op jit(solution)/shard_map/ppermute | solution.py:312
  70.1 10.0 %collective-permute-start.4 = (bf16[256,512]{1,0:T(8,128)(2,1)S(1)}, bf16[256,512]{1,0:T(8,128)(2,1)S(1)}, u32[]{:S(2)}, u32[]{:S(2)}) collective-permute-start(bf16[256,512]{1,0:T(8,128)(2,1)S(1)} %shard_map.79), channel_id=1, source_target_pairs={{0,3},{1,2},{2,1},{3,0},{4,7},{5,6},{6,5},{7,4},{8,11},{9,10},{10,... | collective-permute-start | bytes 786440 | tf_op jit(solution)/shard_map/ppermute | solution.py:312

commit v4 on v3

--- a/solution.py
+++ b/solution.py
@@ -35,27 +35,40 @@
     return jnp.minimum(block_id, 2 * devices - 1 - block_id) // members
 
 
-def project_kernel(kinds, devices, members, scalar_ref, positions_ref, freq_ref, gain_ref, tokens_hbm, *rest):
-    count = len(kinds)
-    weights_hbm, out_ref = rest[:count], rest[count]
-    tokens, normed, weights, token_sems, sems = rest[count + 1 :]
+def project_kernel(plan, devices, members, scalar_ref, positions_ref, freq_ref, gain_ref, tokens_hbm, *rest):
+    weights_hbm, (out_ref, tokens, normed, weights, token_sems, sems) = rest[:-6], rest[-6:]
     rows, width = tokens.shape
-    chunks, _, span = weights.shape
+    chunks = len(plan)
     parts = token_sems.shape[0]
     part = rows // parts
-    token_copies, copies, origin = [], [], []
+    token_copies, copies = [], []
     for i in range(parts):
         at = pl.ds(i * part, part)
         token_copies.append(pltpu.make_async_copy(tokens_hbm.at[at], tokens.at[at], token_sems.at[i]))
         token_copies[i].start()
-    for i in range(count):
-        for first in range(0, weights_hbm[i].shape[1], span):
-            j = len(copies)
-            source = weights_hbm[i].at[:, pl.ds(first, span)]
-            copies.append(pltpu.make_async_copy(source, weights.at[j], sems.at[j]))
-            origin.append((i, first))
-
-    copies[0].start()
+    for j, tiles in enumerate(plan):
+        joined = []
+        for i, (array, column, _, _, _) in enumerate(tiles):
+            if joined and joined[-1][:2] == [array, column - joined[-1][2]]:
+                joined[-1][2] += HEAD_SIZE
+            else:
+                joined.append([array, column, HEAD_SIZE, i * HEAD_SIZE])
+        copies.append(
+            [
+                pltpu.make_async_copy(
+                    weights_hbm[array].at[:, pl.ds(column, size)],
+                    weights.at[j, :, pl.ds(to, size)],
+                    sems.at[j, i],
+                )
+                for i, (array, column, size, to) in enumerate(joined)
+            ]
+        )
+
+    def start(j):
+        for copy in copies[j]:
+            copy.start()
+
+    start(0)
     lanes = positions_ref.shape[1]
     stripes = rows // lanes
     mine = jnp.concatenate(
@@ -88,51 +101,45 @@
 
         lax.fori_loop(0, part // step, norm, 0, unroll=True)
     if chunks > 1:
-        copies[1].start()
+        start(1)
     for first in range(0, width, 512):
         columns = slice(first, first + 512)
         normed[:, columns] = dot(order, tokens[:, columns]).astype(jnp.bfloat16)
-    groups, heads = out_ref.shape[0], out_ref.shape[1]
-    offsets = [0]
-    for i in range(count):
-        offsets.append(offsets[-1] + weights_hbm[i].shape[1] // heads)
-    for j in range(chunks):
-        i, first = origin[j]
-        copies[j].wait()
+    groups = out_ref.shape[0]
+    for j, tiles in enumerate(plan):
+        for copy in copies[j]:
+            copy.wait()
         if j + 2 < chunks:
-            copies[j + 2].start()
+            start(j + 2)
         product = dot(normed[...], weights[j])
-        per_head = offsets[i + 1] - offsets[i]
-        for u in range(0, span, HEAD_SIZE):
-            values = product[:, u : u + HEAD_SIZE]
-            if kinds[i]:
+        for i, (_, _, head, to, roped) in enumerate(tiles):
+            values = product[:, i * HEAD_SIZE : (i + 1) * HEAD_SIZE]
+            if roped:
                 values = values * cosine + pltpu.roll(values, HEAD_SIZE // 2, 1) * sine
-            head, inside = divmod(first + u, per_head)
-            inside += offsets[i]
-            out_ref[:, head, :, inside : inside + HEAD_SIZE] = values.astype(jnp.bfloat16).reshape(
-                groups, rows // groups, HEAD_SIZE
-            )
-
-
-def project(scalars, positions, freq, gain, tokens, weights, kinds, devices, heads):
+            values = values.astype(jnp.bfloat16).reshape(groups, rows // groups, HEAD_SIZE)
+            out_ref[:, head, :, to : to + HEAD_SIZE] = values
+
+
+def project(scalars, positions, freq, gain, tokens, weights, tiles, devices, heads):
     rows, width = tokens.shape
     groups = devices // heads
-    columns = sum(w.shape[1] for w in weights)
-    span = 512
+    columns = len(tiles) * HEAD_SIZE
+    per_chunk = 4
+    plan = [tiles[i : i + per_chunk] for i in range(0, len(tiles), per_chunk)]
     parts = 4
     flops = 2 * rows * width * columns
     size = 2 * (width * columns + rows * width + rows * columns)
     return pl.pallas_call(
-        functools.partial(project_kernel, kinds, devices, heads),
+        functools.partial(project_kernel, plan, devices, heads),
         out_shape=jax.ShapeDtypeStruct((groups, heads, rows // groups, columns // heads), jnp.bfloat16),
         in_specs=[SCALARS] + [WHOLE] * 3 + [IN_PLACE] * (len(weights) + 1),
         out_specs=WHOLE,
         scratch_shapes=[
             pltpu.VMEM((rows, width), jnp.bfloat16),
             pltpu.VMEM((rows, width), jnp.bfloat16),
-            pltpu.VMEM((columns // span, width, span), jnp.bfloat16),
+            pltpu.VMEM((len(plan), width, per_chunk * HEAD_SIZE), jnp.bfloat16),
             pltpu.SemaphoreType.DMA((parts,)),
-            pltpu.SemaphoreType.DMA((columns // span,)),
+            pltpu.SemaphoreType.DMA((len(plan), per_chunk)),
         ],
         compiler_params=pltpu.CompilerParams(vmem_limit_bytes=56 * MIB),
         cost_estimate=pl.CostEstimate(flops=flops, bytes_accessed=size, transcendentals=0),
@@ -146,12 +153,11 @@
         size = out_ref.shape[0]
         slots = lax.broadcasted_iota(jnp.int32, (size, rows), 0) + first
         chosen = (slots == slot_ref[...]).astype(jnp.bfloat16)
-        out_ref[...] = dot(chosen, arrived_ref[...]).astype(jnp.bfloat16)
+        out_ref[...] = dot(chosen, arrived_ref[:, : out_ref.shape[1]]).astype(jnp.bfloat16)
         first += size
 
 
-def place(arrived, slot, sizes):
-    width = arrived.shape[1]
+def place(arrived, slot, sizes, width):
     return pl.pallas_call(
         place_kernel,
         out_shape=[jax.ShapeDtypeStruct((size, width), jnp.bfloat16) for size in sizes],
@@ -166,10 +172,10 @@
     )(arrived, slot)
 
 
-def attend_kernel(block, scalar_ref, query_ref, slot_ref, ends_ref, *rest):
+def attend_kernel(block, columns, scalar_ref, query_ref, slot_ref, ends_ref, *rest):
     pieces, out_ref, held = rest[:6], rest[6], rest[7]
-    target, starts = scalar_ref[0], (scalar_ref[1], scalar_ref[2])
-    heads = query_ref.shape[1] // HEAD_SIZE
+    target, starts, last = scalar_ref[0], (scalar_ref[1], scalar_ref[2]), scalar_ref[3]
+    heads = out_ref.shape[1] // HEAD_SIZE
     arrived = query_ref.shape[0]
     run = arrived // 2
     per_run = run // block
@@ -181,13 +187,16 @@
     for half in range(2):
         first = 0
         for piece in pieces[3 * half : 3 * half + 3]:
-            held[half, first : first + piece.shape[0], :] = piece[...]
+            values = piece[...]
+            if half == 1 and first == 0:
+                values = jnp.where(last == 1, pieces[2][...], values)
+            held[half, first : first + piece.shape[0], :] = values
             first += piece.shape[0]
     indices = (target, per_run - 1 - target)
     at = [pl.multiple_of(index * block, block) for index in indices]
     iota = lax.broadcasted_iota(jnp.int32, (block, arrived), 0)
     chosen = [(iota + (at[half] + half * run) == slot).astype(jnp.bfloat16) for half in range(2)]
-    queries = dot(jnp.concatenate(chosen, axis=0), query_ref[...]).astype(jnp.bfloat16)
+    queries = dot(jnp.concatenate(chosen, axis=0), query_ref[:, columns]).astype(jnp.bfloat16)
     for half in range(2):
         here = slice(half * block, (half + 1) * block)
         key = held[half, pl.ds(at[half], keys), :HEAD_SIZE]
@@ -211,38 +220,40 @@
             out_ref[here, h * HEAD_SIZE : (h + 1) * HEAD_SIZE] = mixed[h * block : (h + 1) * block]
 
 
-def attend(scalars, query, slot, ends, pieces, block):
-    width = query.shape[1]
-    held = REACH_BLOCKS * block + query.shape[0] // 2
+def attend(scalars, query, columns, slot, ends, pieces, block):
+    width = columns.stop - columns.start
+    rows = query.shape[0]
+    held = REACH_BLOCKS * block + rows // 2
     heads = width // HEAD_SIZE
     reach = (REACH_BLOCKS + 1) * block
     return pl.pallas_call(
-        functools.partial(attend_kernel, block),
+        functools.partial(attend_kernel, block, columns),
         out_shape=jax.ShapeDtypeStruct((2 * block, width), jnp.bfloat16),
         in_specs=[SCALARS] + [WHOLE] * 9,
         out_specs=WHOLE,
         scratch_shapes=[pltpu.VMEM((2, held, 2 * HEAD_SIZE), jnp.bfloat16)],
         compiler_params=pltpu.CompilerParams(vmem_limit_bytes=16 * MIB),
         cost_estimate=pl.CostEstimate(
-            flops=2 * 2 * heads * block * reach * HEAD_SIZE * 2 + 4 * block * query.size,
+            flops=2 * 2 * heads * block * reach * HEAD_SIZE * 2 + 4 * block * rows * width,
             bytes_accessed=2 * query.size + 8 * held * HEAD_SIZE,
             transcendentals=2 * heads * block * reach,
         ),
     )(scalars, query, slot, ends, *pieces)
 
 
-def assemble_kernel(scalar_ref, *rest):
+def assemble_kernel(parts, scalar_ref, *rest):
     pieces, out_ref = rest[:-1], rest[-1]
     width = pieces[0].shape[1]
-    for k, piece in enumerate(pieces):
-        at = pl.multiple_of((scalar_ref[0] ^ k) * width, width)
+    for i, piece in enumerate(pieces):
+        k, part = divmod(i, parts)
+        at = pl.multiple_of(((scalar_ref[0] ^ k) * parts + part) * width, width)
         out_ref[:, pl.ds(at, width)] = piece[...]
 
 
-def assemble(scalars, pieces):
+def assemble(scalars, pieces, parts):
     rows, width = pieces[0].shape
     return pl.pallas_call(
-        assemble_kernel,
+        functools.partial(assemble_kernel, parts),
         out_shape=jax.ShapeDtypeStruct((rows, width * len(pieces)), jnp.bfloat16),
         in_specs=[SCALARS] + [WHOLE] * len(pieces),
         out_specs=WHOLE,
@@ -275,9 +286,22 @@
         flat = lax.all_to_all(flat, "ctx", split_axis=0, concat_axis=0, tiled=True)
         return flat.reshape(devices * group_rows, width)
 
-    kv = project(*operands, (w_key, value_weight), (True, False), devices, members)
-    kv = exchange(kv)
-    query = project(*operands, (w_query,), (True,), devices, members)
+    per_group = w_query.shape[1] // w_key.shape[1]
+    first_heads = per_group // 2
+
+    def tiles(array, heads_each, taken, to, roped):
+        return [
+            (array, (head * heads_each + i) * HEAD_SIZE, head, to + (i - taken[0]) * HEAD_SIZE, roped)
+            for head in range(members)
+            for i in taken
+        ]
+
+    first_tiles = tiles(0, 1, range(1), 0, True) + tiles(1, 1, range(1), HEAD_SIZE, False)
+    first_tiles += tiles(2, per_group, range(first_heads), 2 * HEAD_SIZE, True)
+    second_tiles = tiles(0, per_group, range(first_heads, per_group), 0, True)
+    first = project(*operands, (w_key, value_weight, w_query), first_tiles, devices, members)
+    first = exchange(first)
+    second = project(*operands, (w_query,), second_tiles, devices, members)
 
     table = positions.reshape(devices, rows)
     ours = group_of(table, block, devices, members) == group
@@ -290,29 +314,32 @@
     slot = jnp.sum(jnp.where(wanted, slots[:, None, :], 0), axis=2).reshape(1, devices * group_rows)
     ends = jnp.cumsum(lengths, dtype=jnp.int32)[None, :]
 
-    kv, query = lax.optimization_barrier((kv, query))
-    query = exchange(query)
     reach = REACH_BLOCKS * block
     sizes = [run - reach, reach] * 2
-    early_head, early_tail, late_head, late_tail = place(kv, slot, sizes)
+    placed = place(first, slot, sizes, 2 * HEAD_SIZE)
+    placed, second = lax.optimization_barrier((placed, second))
+    early_head, early_tail, late_head, late_tail = placed
     up = [(i, i + members) for i in range(devices - members)]
     down = [(i + members, i) for i in range(devices - members)]
     early_halo = lax.ppermute(early_tail, "ctx", up)
     late_halo = lax.ppermute(late_tail, "ctx", down)
-    late_halo = jnp.where(group == groups - 1, early_tail, late_halo)
     pieces = (early_halo, early_head, early_tail, late_halo, late_head, late_tail)
-
-    results = []
-    for k in [3, 1, 2, 0][-members:]:
-        target = member ^ k
-        scalars = jnp.stack([target, first_run, second_run]).astype(jnp.int32)
-        out = attend(scalars, query, slot, ends, pieces, block)
-        if k:
-            route = [(i, i // members * members + (i % members ^ k)) for i in range(devices)]
-            out = lax.ppermute(out, "ctx", route)
-        results.append((k, out))
-    results = [out for _, out in sorted(results, key=lambda pair: pair[0])]
-    return assemble(member.reshape(1).astype(jnp.int32), results)
+    second = exchange(second)
+
+    last = (group == groups - 1).astype(jnp.int32)
+    first_columns = slice(2 * HEAD_SIZE, (2 + first_heads) * HEAD_SIZE)
+    second_columns = slice(0, (per_group - first_heads) * HEAD_SIZE)
+    results = {}
+    for part, (query, columns) in enumerate([(first, first_columns), (second, second_columns)]):
+        for k in [3, 1, 2, 0][-members:]:
+            scalars = jnp.stack([member ^ k, first_run, second_run, last]).astype(jnp.int32)
+            out = attend(scalars, query, columns, slot, ends, pieces, block)
+            if k:
+                route = [(i, i // members * members + (i % members ^ k)) for i in range(devices)]
+                out = lax.ppermute(out, "ctx", route)
+            results[k, part] = out
+    results = [results[key] for key in sorted(results)]
+    return assemble(member.reshape(1).astype(jnp.int32), results, 2)
 
 
 def solution(mesh):

time: 81.7 us -> 89.7 us (1.098)
  the two profiles are of different devices: /device:TPU:12 before, /device:TPU:0 now
where the time goes in v4:
time: 89.7 us; the launch traced here: 88.4 us
  Pallas kernels  33.6 us (37%)
  starting transfers between devices  26.9 us (30%)
  waiting for transfers between devices  25.2 us (28%)
  other arithmetic  2.21 us (2%)
    pallas_call x2, Pallas kernels, project(): pl.pallas_call(functools.partial(project_kernel, plan, devices, heads), o...  17.9 us
    all_to_all x2, waiting for transfers between devices, exchange(): flat = lax.all_to_all(flat, 'ctx', split_axis=0, concat_axis=0, tiled=True)  15.4 us
    all_to_all x2, starting transfers between devices, exchange(): flat = lax.all_to_all(flat, 'ctx', split_axis=0, concat_axis=0, tiled=True)  14.2 us
    pallas_call x8, Pallas kernels, attend(): pl.pallas_call(functools.partial(attend_kernel, block, columns), out_shap...  13.9 us
    ppermute x6, starting transfers between devices, shards(): out = lax.ppermute(out, 'ctx', route)  7.37 us
    ppermute x1, waiting for transfers between devices, shards(): early_halo = lax.ppermute(early_tail, 'ctx', up)  5.59 us
    ppermute x1, starting transfers between devices, shards(): early_halo = lax.ppermute(early_tail, 'ctx', up)  3.81 us
    ppermute x1, waiting for transfers between devices, shards(): late_halo = lax.ppermute(late_tail, 'ctx', down)  2.18 us
  transfers between devices with their start and end apart: 10, of which 4 were waited for; matrix products, arithmetic and copies ran while one was open for 2% of the time, Pallas kernels for 24%

profile of v4, /device:TPU:0, one launch (start us, length us, event | category | flops | bytes accessed | tf_op | source)
XLA Modules:
  0.0 88.4 jit_solution(4380768048974655515)
XLA Ops:
  0.6 10.3 %shard_map.73 = bf16[4,4,64,512]{3,2,1,0:T(8,128)(2,1)} custom-call(s32[1]{0:T(128)} %bitcast.4.scalar_ref, s32[32,128]{1,0:T(8,128)} %bitcast.31, f32[1,128]{1,0:T(1,128)} %fusion.15.freq_ref, bf16[4096]{0:T(1024)(128)(2,1)} %gain_ref.3, bf16[256,4096]{1,0:T(8,128)(2,1)} %tokens_hbm.3, bf16[4096,512]{1,0:T(8,128)(2,1)} %rest_0_.2, ...), custom_call_target="tpu_custom_call" | custom-call | flops 4294967296 | bytes 19922944 | tf_op jit(solution)/shard_map/pallas_call | solution.py:132
  10.9 8.3 %all-to-all-start = ((bf16[16,64,512]{2,1,0:T(8,128)(2,1)}), bf16[16,64,512]{2,1,0:T(8,128)(2,1)S(1)}, u32[]{:S(2)}, u32[]{:S(2)}) async-start(bf16[16,64,512]{2,1,0:T(8,128)(2,1)} %bitcast.29), calls=%async_computation | async-start | bytes 2097152 | tf_op jit(solution)/shard_map/all_to_all | solution.py:286
  20.6 7.6 %shard_map.75 = bf16[4,4,64,256]{3,2,1,0:T(8,128)(2,1)} custom-call(s32[1]{0:T(128)} %bitcast.4.scalar_ref, s32[32,128]{1,0:T(8,128)} %bitcast.32, f32[1,128]{1,0:T(1,128)} %fusion.15.freq_ref, bf16[4096]{0:T(1024)(128)(2,1)} %gain_ref.3, bf16[256,4096]{1,0:T(8,128)(2,1)} %tokens_hbm.3, bf16[4096,2048]{1,0:T(8,128)(2,1)} %rest_0_.3), custom_call_target="tpu_custom_call" | custom-call | flops 2147483648 | bytes 11010048 | tf_op jit(solution)/shard_map/pallas_call | solution.py:132
  28.2 15.4 %all-to-all-done = bf16[16,64,512]{2,1,0:T(8,128)(2,1)S(1)} async-done(((bf16[16,64,512]{2,1,0:T(8,128)(2,1)}), bf16[16,64,512]{2,1,0:T(8,128)(2,1)S(1)}, u32[]{:S(2)}, u32[]{:S(2)}) %all-to-all-start) | async-done | bytes 1048608 | tf_op jit(solution)/shard_map/all_to_all | solution.py:286
  43.7 0.7 shard_map.74
  44.4 5.8 %all-to-all-start.1 = ((bf16[16,64,256]{2,1,0:T(8,128)(2,1)}), bf16[16,64,256]{2,1,0:T(8,128)(2,1)S(1)}, u32[]{:S(2)}, u32[]{:S(2)}) async-start(bf16[16,64,256]{2,1,0:T(8,128)(2,1)} %bitcast.30), calls=%async_computation.1 | async-start | bytes 1048576 | tf_op jit(solution)/shard_map/all_to_all | solution.py:286
  50.5 3.8 %collective-permute-start = (bf16[384,256]{1,0:T(8,128)(2,1)S(1)}, bf16[384,256]{1,0:T(8,128)(2,1)S(1)}, u32[]{:S(2)}, u32[]{:S(2)}) collective-permute-start(bf16[384,256]{1,0:T(8,128)(2,1)S(1)} %get-tuple-element.18.rest_2_), channel_id=1, source_target_pairs={{0,4},{1,5},{2,6},{3,7},{4,8},{5,9},{6,10},{7,11},{8,12},{9,13},{1... | collective-permute-start | bytes 589832 | tf_op jit(solution)/shard_map/ppermute | solution.py:324
  54.3 1.5 %collective-permute-start.1 = (bf16[384,256]{1,0:T(8,128)(2,1)S(1)}, bf16[384,256]{1,0:T(8,128)(2,1)S(1)}, u32[]{:S(2)}, u32[]{:S(2)}) collective-permute-start(bf16[384,256]{1,0:T(8,128)(2,1)S(1)} %get-tuple-element.20.rest_5_), channel_id=1, source_target_pairs={{4,0},{5,1},{6,2},{7,3},{8,4},{9,5},{10,6},{11,7},{12,8},{13,9},{1... | collective-permute-start | bytes 589832 | tf_op jit(solution)/shard_map/ppermute | solution.py:325
  56.0 5.6 %collective-permute-done.rest_0_ = bf16[384,256]{1,0:T(8,128)(2,1)S(1)} collective-permute-done((bf16[384,256]{1,0:T(8,128)(2,1)S(1)}, bf16[384,256]{1,0:T(8,128)(2,1)S(1)}, u32[]{:S(2)}, u32[]{:S(2)}) %collective-permute-start) | collective-permute-done | bytes 196640 | tf_op jit(solution)/shard_map/ppermute | solution.py:324
  61.5 2.2 %collective-permute-done.1.rest_3_ = bf16[384,256]{1,0:T(8,128)(2,1)S(1)} collective-permute-done((bf16[384,256]{1,0:T(8,128)(2,1)S(1)}, bf16[384,256]{1,0:T(8,128)(2,1)S(1)}, u32[]{:S(2)}, u32[]{:S(2)}) %collective-permute-start.1) | collective-permute-done | bytes 196640 | tf_op jit(solution)/shard_map/ppermute | solution.py:325
  63.7 1.7 %shard_map.78 = bf16[256,256]{1,0:T(8,128)(2,1)S(1)} custom-call(s32[4]{0:T(128)S(1)} %add_add_fusion.1.scalar_ref, bf16[1024,512]{1,0:T(8,128)(2,1)S(1)} %bitcast.21, s32[1,1024]{1,0:T(1,128)S(1)} %reshape.189.slot_ref, s32[1,32]{1,0:T(1,128)S(1)} %reduce-window_2_clone.1.ends_ref, bf16[384,256]{1,0:T(8,128)(2,1)S(1)} %collective-permute-done.rest_0_, ...), custom_call_target="tpu_custom_call" | custom-call | flops 268435456 | bytes 1966080 | tf_op jit(solution)/shard_map/pallas_call | solution.py:229
  65.5 1.5 %collective-permute-start.2 = (bf16[256,256]{1,0:T(8,128)(2,1)S(1)}, bf16[256,256]{1,0:T(8,128)(2,1)S(1)}, u32[]{:S(2)}, u32[]{:S(2)}) collective-permute-start(bf16[256,256]{1,0:T(8,128)(2,1)S(1)} %shard_map.78), channel_id=1, source_target_pairs={{0,1},{1,0},{2,3},{3,2},{4,5},{5,4},{6,7},{7,6},{8,9},{9,8},{10,11... | collective-permute-start | bytes 393224 | tf_op jit(solution)/shard_map/ppermute | solution.py:339
  67.1 1.7 %shard_map.80 = bf16[256,256]{1,0:T(8,128)(2,1)S(1)} custom-call(s32[4]{0:T(128)S(1)} %add_add_fusion.2.scalar_ref, bf16[1024,512]{1,0:T(8,128)(2,1)S(1)} %bitcast.22, s32[1,1024]{1,0:T(1,128)S(1)} %reshape.189.slot_ref, s32[1,32]{1,0:T(1,128)S(1)} %reduce-window_2_clone.1.ends_ref, bf16[384,256]{1,0:T(8,128)(2,1)S(1)} %collective-permute-done.rest_0_, ...), custom_call_target="tpu_custom_call" | custom-call | flops 268435456 | bytes 1966080 | tf_op jit(solution)/shard_map/pallas_call | solution.py:229
  68.8 1.9 %collective-permute-start.4 = (bf16[256,256]{1,0:T(8,128)(2,1)S(1)}, bf16[256,256]{1,0:T(8,128)(2,1)S(1)}, u32[]{:S(2)}, u32[]{:S(2)}) collective-permute-start(bf16[256,256]{1,0:T(8,128)(2,1)S(1)} %shard_map.80), channel_id=1, source_target_pairs={{0,2},{1,3},{2,0},{3,1},{4,6},{5,7},{6,4},{7,5},{8,10},{9,11},{10,... | collective-permute-start | bytes 393224 | tf_op jit(solution)/shard_map/ppermute | solution.py:339
  70.7 1.7 %shard_map.82 = bf16[256,256]{1,0:T(8,128)(2,1)S(1)} custom-call(s32[4]{0:T(128)S(1)} %add_add_fusion.3.scalar_ref, bf16[1024,512]{1,0:T(8,128)(2,1)S(1)} %bitcast.23, s32[1,1024]{1,0:T(1,128)S(1)} %reshape.189.slot_ref, s32[1,32]{1,0:T(1,128)S(1)} %reduce-window_2_clone.1.ends_ref, bf16[384,256]{1,0:T(8,128)(2,1)S(1)} %collective-permute-done.rest_0_, ...), custom_call_target="tpu_custom_call" | custom-call | flops 268435456 | bytes 1966080 | tf_op jit(solution)/shard_map/pallas_call | solution.py:229
  72.7 1.7 %shard_map.79 = bf16[256,256]{1,0:T(8,128)(2,1)S(1)} custom-call(s32[4]{0:T(128)S(1)} %add_add_fusion.1.scalar_ref, bf16[1024,256]{1,0:T(8,128)(2,1)S(1)} %bitcast.25, s32[1,1024]{1,0:T(1,128)S(1)} %reshape.189.slot_ref, s32[1,32]{1,0:T(1,128)S(1)} %reduce-window_2_clone.1.ends_ref, bf16[384,256]{1,0:T(8,128)(2,1)S(1)} %collective-permute-done.rest_0_, ...), custom_call_target="tpu_custom_call" | custom-call | flops 268435456 | bytes 1441792 | tf_op jit(solution)/shard_map/pallas_call | solution.py:229
  74.5 1.5 %collective-permute-start.3 = (bf16[256,256]{1,0:T(8,128)(2,1)S(1)}, bf16[256,256]{1,0:T(8,128)(2,1)S(1)}, u32[]{:S(2)}, u32[]{:S(2)}) collective-permute-start(bf16[256,256]{1,0:T(8,128)(2,1)S(1)} %shard_map.79), channel_id=1, source_target_pairs={{0,1},{1,0},{2,3},{3,2},{4,5},{5,4},{6,7},{7,6},{8,9},{9,8},{10,11... | collective-permute-start | bytes 393224 | tf_op jit(solution)/shard_map/ppermute | solution.py:339
  76.0 1.7 %shard_map.81 = bf16[256,256]{1,0:T(8,128)(2,1)S(1)} custom-call(s32[4]{0:T(128)S(1)} %add_add_fusion.2.scalar_ref, bf16[1024,256]{1,0:T(8,128)(2,1)S(1)} %bitcast.26, s32[1,1024]{1,0:T(1,128)S(1)} %reshape.189.slot_ref, s32[1,32]{1,0:T(1,128)S(1)} %reduce-window_2_clone.1.ends_ref, bf16[384,256]{1,0:T(8,128)(2,1)S(1)} %collective-permute-done.rest_0_, ...), custom_call_target="tpu_custom_call" | custom-call | flops 268435456 | bytes 1441792 | tf_op jit(solution)/shard_map/pallas_call | solution.py:229
  77.7 1.9 %collective-permute-start.5 = (bf16[256,256]{1,0:T(8,128)(2,1)S(1)}, bf16[256,256]{1,0:T(8,128)(2,1)S(1)}, u32[]{:S(2)}, u32[]{:S(2)}) collective-permute-start(bf16[256,256]{1,0:T(8,128)(2,1)S(1)} %shard_map.81), channel_id=1, source_target_pairs={{0,2},{1,3},{2,0},{3,1},{4,6},{5,7},{6,4},{7,5},{8,10},{9,11},{10,... | collective-permute-start | bytes 393224 | tf_op jit(solution)/shard_map/ppermute | solution.py:339
  79.6 1.7 %shard_map.83 = bf16[256,256]{1,0:T(8,128)(2,1)S(1)} custom-call(s32[4]{0:T(128)S(1)} %add_add_fusion.3.scalar_ref, bf16[1024,256]{1,0:T(8,128)(2,1)S(1)} %bitcast.27, s32[1,1024]{1,0:T(1,128)S(1)} %reshape.189.slot_ref, s32[1,32]{1,0:T(1,128)S(1)} %reduce-window_2_clone.1.ends_ref, bf16[384,256]{1,0:T(8,128)(2,1)S(1)} %collective-permute-done.rest_0_, ...), custom_call_target="tpu_custom_call" | custom-call | flops 268435456 | bytes 1441792 | tf_op jit(solution)/shard_map/pallas_call | solution.py:229
  81.7 1.7 %shard_map.76.rest_0_ = bf16[256,256]{1,0:T(8,128)(2,1)S(1)} custom-call(s32[4]{0:T(128)S(1)} %add_add_fusion.scalar_ref, bf16[1024,512]{1,0:T(8,128)(2,1)S(1)} %bitcast.24, s32[1,1024]{1,0:T(1,128)S(1)} %reshape.189.slot_ref, s32[1,32]{1,0:T(1,128)S(1)} %reduce-window_2_clone.1.ends_ref, bf16[384,256]{1,0:T(8,128)(2,1)S(1)} %collective-permute-done.rest_0_, ...), custom_call_target="tpu_custom_call" | custom-call | flops 268435456 | bytes 1966080 | tf_op jit(solution)/shard_map/pallas_call | solution.py:229
  83.5 1.7 %shard_map.77.rest_1_ = bf16[256,256]{1,0:T(8,128)(2,1)S(1)} custom-call(s32[4]{0:T(128)S(1)} %add_add_fusion.scalar_ref, bf16[1024,256]{1,0:T(8,128)(2,1)S(1)} %bitcast.28, s32[1,1024]{1,0:T(1,128)S(1)} %reshape.189.slot_ref, s32[1,32]{1,0:T(1,128)S(1)} %reduce-window_2_clone.1.ends_ref, bf16[384,256]{1,0:T(8,128)(2,1)S(1)} %collective-permute-done.rest_0_, ...), custom_call_target="tpu_custom_call" | custom-call | flops 268435456 | bytes 1441792 | tf_op jit(solution)/shard_map/pallas_call | solution.py:229
  85.3 2.0 %collective-permute-done.7.rest_7_ = bf16[256,256]{1,0:T(8,128)(2,1)S(1)} collective-permute-done((bf16[256,256]{1,0:T(8,128)(2,1)S(1)}, bf16[256,256]{1,0:T(8,128)(2,1)S(1)}, u32[]{:S(2)}, u32[]{:S(2)}) %collective-permute-start.7) | collective-permute-done | bytes 131104 | tf_op jit(solution)/shard_map/ppermute | solution.py:339
  87.3 1.1 %shard_map.84 = bf16[256,2048]{1,0:T(8,128)(2,1)} custom-call(s32[1]{0:T(128)} %bitcast.scalar_ref, bf16[256,256]{1,0:T(8,128)(2,1)S(1)} %shard_map.76.rest_0_, bf16[256,256]{1,0:T(8,128)(2,1)S(1)} %shard_map.77.rest_1_, bf16[256,256]{1,0:T(8,128)(2,1)S(1)} %collective-permute-done.2.rest_2_, bf16[256,256]{1,0:T(8,128)(2,1)S(1)} %collective-permute-done.3.rest_3_, ...), custom_call_target="tpu_custom_call" | custom-call | bytes 2097152 | tf_op jit(solution)/shard_map/pallas_call | solution.py:255
  (27 shorter events, 3.1 us)
Async XLA Ops:
  0.6 18.6 %copy-start = (s32[4096]{0:T(1024)S(1)}, s32[4096]{0:T(1024)}, u32[]{:S(2)}) copy-start(s32[4096]{0:T(1024)} %param.8) | copy-start | bytes 49156
  10.9 32.8 %all-to-all-start = ((bf16[16,64,512]{2,1,0:T(8,128)(2,1)}), bf16[16,64,512]{2,1,0:T(8,128)(2,1)S(1)}, u32[]{:S(2)}, u32[]{:S(2)}) async-start(bf16[16,64,512]{2,1,0:T(8,128)(2,1)} %bitcast.29), calls=%async_computation | async-start | bytes 2097152 | tf_op jit(solution)/shard_map/all_to_all | solution.py:286
  20.6 29.6 %copy-start.1 = (s32[32]{0:T(128)S(1)}, s32[32]{0:T(128)}, u32[]{:S(2)}) copy-start(s32[32]{0:T(128)} %param.9) | copy-start | bytes 388
  44.4 28.3 %all-to-all-start.1 = ((bf16[16,64,256]{2,1,0:T(8,128)(2,1)}), bf16[16,64,256]{2,1,0:T(8,128)(2,1)S(1)}, u32[]{:S(2)}, u32[]{:S(2)}) async-start(bf16[16,64,256]{2,1,0:T(8,128)(2,1)} %bitcast.30), calls=%async_computation.1 | async-start | bytes 1048576 | tf_op jit(solution)/shard_map/all_to_all | solution.py:286
  50.5 11.1 %collective-permute-start = (bf16[384,256]{1,0:T(8,128)(2,1)S(1)}, bf16[384,256]{1,0:T(8,128)(2,1)S(1)}, u32[]{:S(2)}, u32[]{:S(2)}) collective-permute-start(bf16[384,256]{1,0:T(8,128)(2,1)S(1)} %get-tuple-element.18.rest_2_), channel_id=1, source_target_pairs={{0,4},{1,5},{2,6},{3,7},{4,8},{5,9},{6,10},{7,11},{8,12},{9,13},{1... | collective-permute-start | bytes 589832 | tf_op jit(solution)/shard_map/ppermute | solution.py:324
  54.3 9.4 %collective-permute-start.1 = (bf16[384,256]{1,0:T(8,128)(2,1)S(1)}, bf16[384,256]{1,0:T(8,128)(2,1)S(1)}, u32[]{:S(2)}, u32[]{:S(2)}) collective-permute-start(bf16[384,256]{1,0:T(8,128)(2,1)S(1)} %get-tuple-element.20.rest_5_), channel_id=1, source_target_pairs={{4,0},{5,1},{6,2},{7,3},{8,4},{9,5},{10,6},{11,7},{12,8},{13,9},{1... | collective-permute-start | bytes 589832 | tf_op jit(solution)/shard_map/ppermute | solution.py:325
  65.5 15.9 %collective-permute-start.2 = (bf16[256,256]{1,0:T(8,128)(2,1)S(1)}, bf16[256,256]{1,0:T(8,128)(2,1)S(1)}, u32[]{:S(2)}, u32[]{:S(2)}) collective-permute-start(bf16[256,256]{1,0:T(8,128)(2,1)S(1)} %shard_map.78), channel_id=1, source_target_pairs={{0,1},{1,0},{2,3},{3,2},{4,5},{5,4},{6,7},{7,6},{8,9},{9,8},{10,11... | collective-permute-start | bytes 393224 | tf_op jit(solution)/shard_map/ppermute | solution.py:339
  68.8 16.4 %collective-permute-start.4 = (bf16[256,256]{1,0:T(8,128)(2,1)S(1)}, bf16[256,256]{1,0:T(8,128)(2,1)S(1)}, u32[]{:S(2)}, u32[]{:S(2)}) collective-permute-start(bf16[256,256]{1,0:T(8,128)(2,1)S(1)} %shard_map.80), channel_id=1, source_target_pairs={{0,2},{1,3},{2,0},{3,1},{4,6},{5,7},{6,4},{7,5},{8,10},{9,11},{10,... | collective-permute-start | bytes 393224 | tf_op jit(solution)/shard_map/ppermute | solution.py:339
  72.4 12.8 %collective-permute-start.6 = (bf16[256,256]{1,0:T(8,128)(2,1)S(1)}, bf16[256,256]{1,0:T(8,128)(2,1)S(1)}, u32[]{:S(2)}, u32[]{:S(2)}) collective-permute-start(bf16[256,256]{1,0:T(8,128)(2,1)S(1)} %shard_map.82), channel_id=1, source_target_pairs={{0,3},{1,2},{2,1},{3,0},{4,7},{5,6},{6,5},{7,4},{8,11},{9,10},{10,... | collective-permute-start | bytes 393224 | tf_op jit(solution)/shard_map/ppermute | solution.py:339
  74.5 10.8 %collective-permute-start.3 = (bf16[256,256]{1,0:T(8,128)(2,1)S(1)}, bf16[256,256]{1,0:T(8,128)(2,1)S(1)}, u32[]{:S(2)}, u32[]{:S(2)}) collective-permute-start(bf16[256,256]{1,0:T(8,128)(2,1)S(1)} %shard_map.79), channel_id=1, source_target_pairs={{0,1},{1,0},{2,3},{3,2},{4,5},{5,4},{6,7},{7,6},{8,9},{9,8},{10,11... | collective-permute-start | bytes 393224 | tf_op jit(solution)/shard_map/ppermute | solution.py:339
  77.7 7.5 %collective-permute-start.5 = (bf16[256,256]{1,0:T(8,128)(2,1)S(1)}, bf16[256,256]{1,0:T(8,128)(2,1)S(1)}, u32[]{:S(2)}, u32[]{:S(2)}) collective-permute-start(bf16[256,256]{1,0:T(8,128)(2,1)S(1)} %shard_map.81), channel_id=1, source_target_pairs={{0,2},{1,3},{2,0},{3,1},{4,6},{5,7},{6,4},{7,5},{8,10},{9,11},{10,... | collective-permute-start | bytes 393224 | tf_op jit(solution)/shard_map/ppermute | solution.py:339
  81.4 5.9 %collective-permute-start.7 = (bf16[256,256]{1,0:T(8,128)(2,1)S(1)}, bf16[256,256]{1,0:T(8,128)(2,1)S(1)}, u32[]{:S(2)}, u32[]{:S(2)}) collective-permute-start(bf16[256,256]{1,0:T(8,128)(2,1)S(1)} %shard_map.83), channel_id=1, source_target_pairs={{0,3},{1,2},{2,1},{3,0},{4,7},{5,6},{6,5},{7,4},{8,11},{9,10},{10,... | collective-permute-start | bytes 393224 | tf_op jit(solution)/shard_map/ppermute | solution.py:339

commit v5 on v3

--- a/solution.py
+++ b/solution.py
@@ -139,118 +139,138 @@
     )(scalars, positions, freq, gain, tokens, *weights)
 
 
-def place_kernel(arrived_ref, slot_ref, *outs):
+def place_kernel(block, scalar_ref, arrived_ref, slot_ref, ends_ref, *outs):
+    outs, order_ref, mask_ref = outs[:-2], outs[-2], outs[-1]
     rows = arrived_ref.shape[0]
+    slot = slot_ref[...]
+    ends = ends_ref[...]
     first = 0
     for out_ref in outs:
         size = out_ref.shape[0]
         slots = lax.broadcasted_iota(jnp.int32, (size, rows), 0) + first
-        chosen = (slots == slot_ref[...]).astype(jnp.bfloat16)
+        chosen = (slots == slot).astype(jnp.bfloat16)
+        order_ref[first : first + size, :] = chosen
         out_ref[...] = dot(chosen, arrived_ref[...]).astype(jnp.bfloat16)
         first += size
-
-
-def place(arrived, slot, sizes):
-    width = arrived.shape[1]
+    _, per_run, _, keys = mask_ref.shape
+    for half in range(2):
+        for index in range(per_run):
+            begin = scalar_ref[half] + index * block
+            query_at = lax.broadcasted_iota(jnp.int32, (block, 1), 0) + begin
+            key_at = lax.broadcasted_iota(jnp.int32, (1, keys), 1) + (begin + block - keys)
+            doc_start = jnp.max(jnp.where(ends <= query_at, ends, 0), axis=1, keepdims=True)
+            allowed = (key_at >= doc_start) & (key_at <= query_at)
+            mask_ref[half, index] = jnp.where(allowed, jnp.float32(0), jnp.float32(-1e30))
+
+
+def place(scalars, arrived, slot, ends, sizes, block):
+    rows, width = arrived.shape
+    per_run = rows // 2 // block
+    mask = (2, per_run, block, (REACH_BLOCKS + 1) * block)
     return pl.pallas_call(
-        place_kernel,
-        out_shape=[jax.ShapeDtypeStruct((size, width), jnp.bfloat16) for size in sizes],
-        in_specs=[WHOLE, WHOLE],
-        out_specs=[WHOLE] * len(sizes),
+        functools.partial(place_kernel, block),
+        out_shape=[jax.ShapeDtypeStruct((size, width), jnp.bfloat16) for size in sizes]
+        + [jax.ShapeDtypeStruct((rows, rows), jnp.bfloat16), jax.ShapeDtypeStruct(mask, jnp.float32)],
+        in_specs=[SCALARS] + [WHOLE] * 3,
+        out_specs=[WHOLE] * (len(sizes) + 2),
         compiler_params=pltpu.CompilerParams(vmem_limit_bytes=16 * MIB),
         cost_estimate=pl.CostEstimate(
-            flops=2 * sum(sizes) * arrived.shape[0] * width,
+            flops=2 * rows * rows * width,
             bytes_accessed=4 * arrived.size,
             transcendentals=0,
         ),
-    )(arrived, slot)
-
-
-def attend_kernel(block, scalar_ref, query_ref, slot_ref, ends_ref, *rest):
+    )(scalars, arrived, slot, ends)
+
+
+def attend_kernel(scalar_ref, query_ref, order_ref, mask_ref, *rest):
     pieces, out_ref, held = rest[:6], rest[6], rest[7]
-    target, starts = scalar_ref[0], (scalar_ref[1], scalar_ref[2])
+    target, last = scalar_ref[0], scalar_ref[1]
     heads = query_ref.shape[1] // HEAD_SIZE
-    arrived = query_ref.shape[0]
-    run = arrived // 2
-    per_run = run // block
-    reach = REACH_BLOCKS * block
-    keys = reach + block
-    slot = slot_ref[...]
-    ends = ends_ref[...]
+    _, per_run, block, keys = mask_ref.shape
+    run = per_run * block
     factor = jnp.float32(np.log2(np.e) / HEAD_SIZE**0.5)
     for half in range(2):
         first = 0
         for piece in pieces[3 * half : 3 * half + 3]:
-            held[half, first : first + piece.shape[0], :] = piece[...]
+            values = piece[...]
+            if half == 1 and first == 0:
+                values = jnp.where(last == 1, pieces[2][...], values)
+            held[half, first : first + piece.shape[0], :] = values
             first += piece.shape[0]
     indices = (target, per_run - 1 - target)
     at = [pl.multiple_of(index * block, block) for index in indices]
-    iota = lax.broadcasted_iota(jnp.int32, (block, arrived), 0)
-    chosen = [(iota + (at[half] + half * run) == slot).astype(jnp.bfloat16) for half in range(2)]
+    chosen = [order_ref[pl.ds(pl.multiple_of(at[half] + half * run, block), block), :] for half in range(2)]
     queries = dot(jnp.concatenate(chosen, axis=0), query_ref[...]).astype(jnp.bfloat16)
-    for half in range(2):
-        here = slice(half * block, (half + 1) * block)
+    here = [slice(half * block, (half + 1) * block) for half in range(2)]
+    scores, weights, totals = [], [], []
+    for half in range(2):
+        stacked = jnp.concatenate(
+            [queries[here[half], h * HEAD_SIZE : (h + 1) * HEAD_SIZE] for h in range(heads)], axis=0
+        )
         key = held[half, pl.ds(at[half], keys), :HEAD_SIZE]
+        scores.append(
+            lax.dot_general(stacked, key, (((1,), (1,)), ((), ())), preferred_element_type=jnp.float32)
+        )
+    for half in range(2):
+        masked = scores[half].reshape(heads, block, keys) + mask_ref[half, indices[half]][None]
+        masked = masked.reshape(heads * block, keys)
+        top = jnp.max(masked, axis=1, keepdims=True)
+        exact = jnp.exp2((masked - top) * factor)
+        totals.append(jnp.sum(exact, axis=1, keepdims=True))
+        weights.append(exact.astype(jnp.bfloat16))
+    for half in range(2):
         value = held[half, pl.ds(at[half], keys), HEAD_SIZE:]
-        begin = starts[half] + at[half]
-        query_at = lax.broadcasted_iota(jnp.int32, (block, 1), 0) + begin
-        key_at = lax.broadcasted_iota(jnp.int32, (1, keys), 1) + (begin - reach)
-        doc_start = jnp.max(jnp.where(ends <= query_at, ends, 0), axis=1, keepdims=True)
-        allowed = (key_at >= doc_start) & (key_at <= query_at)
-        stacked = jnp.concatenate(
-            [queries[here, h * HEAD_SIZE : (h + 1) * HEAD_SIZE] for h in range(heads)], axis=0
-        )
-        scores = lax.dot_general(stacked, key, (((1,), (1,)), ((), ())), preferred_element_type=jnp.float32)
-        scores = jnp.where(allowed[None], scores.reshape(heads, block, keys), jnp.float32(-1e30))
-        scores = scores.reshape(heads * block, keys)
-        top = jnp.max(scores, axis=1, keepdims=True)
-        weights = jnp.exp2((scores - top) * factor)
-        total = jnp.sum(weights, axis=1, keepdims=True)
-        mixed = (dot(weights.astype(jnp.bfloat16), value) / total).astype(jnp.bfloat16)
+        mixed = (dot(weights[half], value) / totals[half]).astype(jnp.bfloat16)
         for h in range(heads):
-            out_ref[here, h * HEAD_SIZE : (h + 1) * HEAD_SIZE] = mixed[h * block : (h + 1) * block]
-
-
-def attend(scalars, query, slot, ends, pieces, block):
-    width = query.shape[1]
-    held = REACH_BLOCKS * block + query.shape[0] // 2
+            out_ref[here[half], h * HEAD_SIZE : (h + 1) * HEAD_SIZE] = mixed[h * block : (h + 1) * block]
+
+
+def attend(scalars, query, order, mask, pieces):
+    rows, width = query.shape
+    _, per_run, block, keys = mask.shape
+    held = (per_run - 1) * block + keys
     heads = width // HEAD_SIZE
-    reach = (REACH_BLOCKS + 1) * block
     return pl.pallas_call(
-        functools.partial(attend_kernel, block),
+        attend_kernel,
         out_shape=jax.ShapeDtypeStruct((2 * block, width), jnp.bfloat16),
         in_specs=[SCALARS] + [WHOLE] * 9,
         out_specs=WHOLE,
         scratch_shapes=[pltpu.VMEM((2, held, 2 * HEAD_SIZE), jnp.bfloat16)],
         compiler_params=pltpu.CompilerParams(vmem_limit_bytes=16 * MIB),
         cost_estimate=pl.CostEstimate(
-            flops=2 * 2 * heads * block * reach * HEAD_SIZE * 2 + 4 * block * query.size,
+            flops=2 * 2 * heads * block * keys * HEAD_SIZE * 2 + 4 * block * rows * width,
             bytes_accessed=2 * query.size + 8 * held * HEAD_SIZE,
-            transcendentals=2 * heads * block * reach,
+            transcendentals=2 * heads * block * keys,
         ),
-    )(scalars, query, slot, ends, *pieces)
-
-
-def assemble_kernel(scalar_ref, *rest):
-    pieces, out_ref = rest[:-1], rest[-1]
+    )(scalars, query, order, mask, *pieces)
+
+
+def assemble_kernel(member_ref, *rest):
+    count = len(rest) - 2
+    pieces, out_hbm, sems = rest[:count], rest[count], rest[count + 1]
     width = pieces[0].shape[1]
-    for k, piece in enumerate(pieces):
-        at = pl.multiple_of((scalar_ref[0] ^ k) * width, width)
-        out_ref[:, pl.ds(at, width)] = piece[...]
-
-
-def assemble(scalars, pieces):
+    copies = []
+    for i, piece in enumerate(pieces):
+        at = pl.multiple_of(member_ref[i] * width, width)
+        copies.append(pltpu.make_async_copy(piece, out_hbm.at[:, pl.ds(at, width)], sems.at[i]))
+        copies[i].start()
+    for copy in copies:
+        copy.wait()
+
+
+def assemble(sources, pieces):
     rows, width = pieces[0].shape
     return pl.pallas_call(
         assemble_kernel,
         out_shape=jax.ShapeDtypeStruct((rows, width * len(pieces)), jnp.bfloat16),
         in_specs=[SCALARS] + [WHOLE] * len(pieces),
-        out_specs=WHOLE,
+        out_specs=IN_PLACE,
+        scratch_shapes=[pltpu.SemaphoreType.DMA((len(pieces),))],
         compiler_params=pltpu.CompilerParams(vmem_limit_bytes=8 * MIB),
         cost_estimate=pl.CostEstimate(
             flops=0, bytes_accessed=4 * rows * width * len(pieces), transcendentals=0
         ),
-    )(scalars, *pieces)
+    )(sources, *pieces)
 
 
 def shards(tokens, positions, lengths, gain, w_query, w_key, value_weight):
@@ -266,8 +286,8 @@
     group_rows = rows // groups
 
     half = HEAD_SIZE // 2
-    freq = ROPE_THETA ** (-(jnp.arange(HEAD_SIZE, dtype=jnp.float32) % half * 2.0 / HEAD_SIZE))
-    operands = (device.reshape(1), positions.reshape(-1, 128), freq[None, :], gain, tokens)
+    freq = np.float32(ROPE_THETA ** (-(np.arange(HEAD_SIZE) % half * 2.0 / HEAD_SIZE)))
+    operands = (device.reshape(1), positions.reshape(-1, 128), jnp.asarray(freq[None, :]), gain, tokens)
 
     def exchange(ordered):
         width = ordered.shape[3]
@@ -294,25 +314,35 @@
     query = exchange(query)
     reach = REACH_BLOCKS * block
     sizes = [run - reach, reach] * 2
-    early_head, early_tail, late_head, late_tail = place(kv, slot, sizes)
+    scalars = jnp.stack([first_run, second_run]).astype(jnp.int32)
+    early_head, early_tail, late_head, late_tail, order, mask = place(scalars, kv, slot, ends, sizes, block)
     up = [(i, i + members) for i in range(devices - members)]
     down = [(i + members, i) for i in range(devices - members)]
     early_halo = lax.ppermute(early_tail, "ctx", up)
     late_halo = lax.ppermute(late_tail, "ctx", down)
-    late_halo = jnp.where(group == groups - 1, early_tail, late_halo)
     pieces = (early_halo, early_head, early_tail, late_halo, late_head, late_tail)
 
-    results = []
-    for k in [3, 1, 2, 0][-members:]:
-        target = member ^ k
-        scalars = jnp.stack([target, first_run, second_run]).astype(jnp.int32)
-        out = attend(scalars, query, slot, ends, pieces, block)
-        if k:
-            route = [(i, i // members * members + (i % members ^ k)) for i in range(devices)]
-            out = lax.ppermute(out, "ctx", route)
-        results.append((k, out))
-    results = [out for _, out in sorted(results, key=lambda pair: pair[0])]
-    return assemble(member.reshape(1).astype(jnp.int32), results)
+    last = group == groups - 1
+    lanes = lax.axis_size("dp")
+    lane = lax.axis_index("dp")
+    farthest = members - 1
+    between = list(range(1, farthest))
+    turns = [[farthest] + (between if i % 2 == 0 else between[::-1]) + [0] for i in range(lanes)]
+    sources, results = [], []
+    for turn in range(members):
+        distance = jnp.asarray([order_of[turn] for order_of in turns], jnp.int32)[lane]
+        scalars = jnp.stack([member ^ distance, last]).astype(jnp.int32)
+        out = attend(scalars, query, order, mask, pieces)
+        if turn < members - 1:
+            route = [
+                (i * devices + j, i * devices + (j // members * members + (j % members ^ turns[i][turn])))
+                for i in range(lanes)
+                for j in range(devices)
+            ]
+            out = lax.ppermute(out, ("dp", "ctx"), route)
+        sources.append(member ^ distance)
+        results.append(out)
+    return assemble(jnp.stack(sources).astype(jnp.int32), results)
 
 
 def solution(mesh):

time: 81.7 us -> 85.3 us (1.044)
  the two profiles are of different devices: /device:TPU:12 before, /device:TPU:8 now
where the time goes in v5:
time: 85.3 us; the launch traced here: 84.6 us
  Pallas kernels  28 us (33%)
  starting transfers between devices  21.3 us (25%)
  waiting for transfers between devices  20 us (23%)
  local copies, waits for them, and re-layouts  11.7 us (14%)
  other arithmetic  1.75 us (2%)
  between operations  1.72 us (2%)
    pallas_call x2, Pallas kernels, project(): pl.pallas_call(functools.partial(project_kernel, kinds, devices, heads),...  17.4 us
    all_to_all x2, starting transfers between devices, exchange(): flat = lax.all_to_all(flat, 'ctx', split_axis=0, concat_axis=0, tiled=True)  11.8 us
    unnamed x32, local copies, waits for them, and re-layouts  10.1 us
    ppermute x1, waiting for transfers between devices, shards(): early_halo = lax.ppermute(early_tail, 'ctx', up)  10 us
    pallas_call x4, Pallas kernels, attend(): pl.pallas_call(attend_kernel, out_shape=jax.ShapeDtypeStruct((2 * block,...  7.42 us
    ppermute x3, waiting for transfers between devices, shards(): out = lax.ppermute(out, ('dp', 'ctx'), route)  4.54 us
    all_to_all x2, waiting for transfers between devices, exchange(): flat = lax.all_to_all(flat, 'ctx', split_axis=0, concat_axis=0, tiled=True)  4.17 us
    ppermute x3, starting transfers between devices, shards(): out = lax.ppermute(out, ('dp', 'ctx'), route)  3.68 us
  transfers between devices with their start and end apart: 7, of which 4 were waited for; matrix products, arithmetic and copies ran while one was open for 4% of the time, Pallas kernels for 21%

profile of v5, /device:TPU:8, one launch (start us, length us, event | category | flops | bytes accessed | tf_op | source)
XLA Modules:
  0.0 84.6 jit_solution(8844978130676743728)
XLA Ops:
  0.0 7.1 %shard_map.118 = bf16[4,4,64,256]{3,2,1,0:T(8,128)(2,1)} custom-call(s32[1]{0:T(128)} %bitcast.7.scalar_ref, s32[32,128]{1,0:T(8,128)} %bitcast.29, f32[1,128]{1,0:T(1,128)} %constant.94.clone.freq_ref, bf16[4096]{0:T(1024)(128)(2,1)} %gain_ref.3, bf16[256,4096]{1,0:T(8,128)(2,1)} %tokens_hbm.3, bf16[4096,512]{1,0:T(8,128)(2,1)} %rest_0_.2, ...), custom_call_target="tpu_custom_call" | custom-call | flops 2147483648 | bytes 11010048 | tf_op jit(solution)/shard_map/pallas_call | solution.py:125
  7.2 7.2 %all-to-all-start = ((bf16[16,64,256]{2,1,0:T(8,128)(2,1)}), bf16[16,64,256]{2,1,0:T(8,128)(2,1)S(1)}, u32[]{:S(2)}, u32[]{:S(2)}) async-start(bf16[16,64,256]{2,1,0:T(8,128)(2,1)} %bitcast.28), calls=%async_computation | async-start | bytes 1048576 | tf_op jit(solution)/shard_map/all_to_all | solution.py:295
  14.4 10.3 %shard_map.119 = bf16[4,4,64,512]{3,2,1,0:T(8,128)(2,1)} custom-call(s32[1]{0:T(128)} %bitcast.7.scalar_ref, s32[32,128]{1,0:T(8,128)} %bitcast.30, f32[1,128]{1,0:T(1,128)} %constant.94.clone.freq_ref, bf16[4096]{0:T(1024)(128)(2,1)} %gain_ref.3, bf16[256,4096]{1,0:T(8,128)(2,1)} %tokens_hbm.3, bf16[4096,2048]{1,0:T(8,128)(2,1)} %rest_0_.3), custom_call_target="tpu_custom_call" | custom-call | flops 4294967296 | bytes 19922944 | tf_op jit(solution)/shard_map/pallas_call | solution.py:125
  24.7 4.2 %all-to-all-done = bf16[16,64,256]{2,1,0:T(8,128)(2,1)S(1)} async-done(((bf16[16,64,256]{2,1,0:T(8,128)(2,1)}), bf16[16,64,256]{2,1,0:T(8,128)(2,1)S(1)}, u32[]{:S(2)}, u32[]{:S(2)}) %all-to-all-start) | async-done | bytes 524320 | tf_op jit(solution)/shard_map/all_to_all | solution.py:295
  28.9 4.6 %all-to-all-start.1 = ((bf16[16,64,512]{2,1,0:T(8,128)(2,1)}), bf16[16,64,512]{2,1,0:T(8,128)(2,1)S(1)}, u32[]{:S(2)}, u32[]{:S(2)}) async-start(bf16[16,64,512]{2,1,0:T(8,128)(2,1)} %bitcast.27), calls=%async_computation.1 | async-start | bytes 2097152 | tf_op jit(solution)/shard_map/all_to_all | solution.py:295
  37.9 1.0 %copy-done.11 = bf16[16,64,256]{2,1,0:T(8,128)(2,1)S(1)} copy-done((bf16[16,64,256]{2,1,0:T(8,128)(2,1)S(1)}, bf16[16,64,256]{2,1,0:T(8,128)(2,1)}, u32[]{:S(2)}) %copy-start.11) | copy-done | bytes 524312
  39.0 1.7 %shard_map.120 = (bf16[128,256]{1,0:T(8,128)(2,1)S(1)}, bf16[384,256]{1,0:T(8,128)(2,1)S(1)}, bf16[128,256]{1,0:T(8,128)(2,1)S(1)}, bf16[384,256]{1,0:T(8,128)(2...) custom-call(s32[2]{0:T(128)S(1)} %pad_add_fusion.2.scalar_ref, bf16[1024,256]{1,0:T(8,128)(2,1)S(1)} %bitcast.26, ...), custom_call_target="tpu_custom_call" | custom-call | flops 536870912 | bytes 1048576 | tf_op jit(solution)/shard_map/pallas_call | solution.py:170
  40.6 1.3 %copy-done = f32[2,4,128,512]{3,2,1,0:T(8,128)} copy-done((f32[2,4,128,512]{3,2,1,0:T(8,128)}, f32[2,4,128,512]{3,2,1,0:T(8,128)S(1)}, u32[]{:S(2)}) %copy-start) | copy-done | bytes 2097176
  43.2 3.4 %collective-permute-start = (bf16[384,256]{1,0:T(8,128)(2,1)S(1)}, bf16[384,256]{1,0:T(8,128)(2,1)S(1)}, u32[]{:S(2)}, u32[]{:S(2)}) collective-permute-start(bf16[384,256]{1,0:T(8,128)(2,1)S(1)} %get-tuple-element.17.rest_2_), channel_id=1, source_target_pairs={{0,4},{1,5},{2,6},{3,7},{4,8},{5,9},{6,10},{7,11},{8,12},{9,13},{1... | collective-permute-start | bytes 589832 | tf_op jit(solution)/shard_map/ppermute | solution.py:321
  46.6 2.5 %collective-permute-start.1 = (bf16[384,256]{1,0:T(8,128)(2,1)S(1)}, bf16[384,256]{1,0:T(8,128)(2,1)S(1)}, u32[]{:S(2)}, u32[]{:S(2)}) collective-permute-start(bf16[384,256]{1,0:T(8,128)(2,1)S(1)} %get-tuple-element.19.rest_5_), channel_id=1, source_target_pairs={{4,0},{5,1},{6,2},{7,3},{8,4},{9,5},{10,6},{11,7},{12,8},{13,9},{1... | collective-permute-start | bytes 589832 | tf_op jit(solution)/shard_map/ppermute | solution.py:322
  49.2 10.0 %collective-permute-done.rest_0_ = bf16[384,256]{1,0:T(8,128)(2,1)S(1)} collective-permute-done((bf16[384,256]{1,0:T(8,128)(2,1)S(1)}, bf16[384,256]{1,0:T(8,128)(2,1)S(1)}, u32[]{:S(2)}, u32[]{:S(2)}) %collective-permute-start) | collective-permute-done | bytes 196640 | tf_op jit(solution)/shard_map/ppermute | solution.py:321
  59.9 1.3 %collective-permute-done.1.rest_3_ = bf16[384,256]{1,0:T(8,128)(2,1)S(1)} collective-permute-done((bf16[384,256]{1,0:T(8,128)(2,1)S(1)}, bf16[384,256]{1,0:T(8,128)(2,1)S(1)}, u32[]{:S(2)}, u32[]{:S(2)}) %collective-permute-start.1) | collective-permute-done | bytes 196640 | tf_op jit(solution)/shard_map/ppermute | solution.py:322
  61.9 1.6 %copy-done.1 = f32[2,4,128,512]{3,2,1,0:T(8,128)S(1)} copy-done((f32[2,4,128,512]{3,2,1,0:T(8,128)S(1)}, f32[2,4,128,512]{3,2,1,0:T(8,128)}, u32[]{:S(2)}) %copy-start.1) | copy-done | bytes 2097176
  63.5 0.9 %copy-done.3 = bf16[384,256]{1,0:T(8,128)(2,1)S(1)} copy-done((bf16[384,256]{1,0:T(8,128)(2,1)S(1)}, bf16[384,256]{1,0:T(8,128)(2,1)}, u32[]{:S(2)}) %copy-start.3) | copy-done | bytes 196632
  64.4 0.9 %copy-done.5 = bf16[384,256]{1,0:T(8,128)(2,1)S(1)} copy-done((bf16[384,256]{1,0:T(8,128)(2,1)S(1)}, bf16[384,256]{1,0:T(8,128)(2,1)}, u32[]{:S(2)}) %copy-start.5) | copy-done | bytes 196632
  65.4 0.8 copy-done.7
  66.2 0.8 copy-done.9
  67.0 1.9 %shard_map.121 = bf16[256,512]{1,0:T(8,128)(2,1)S(1)} custom-call(s32[2]{0:T(128)S(1)} %pad_add_fusion.1.scalar_ref, bf16[1024,512]{1,0:T(8,128)(2,1)S(1)} %bitcast.22, bf16[1024,1024]{1,0:T(8,128)(2,1)S(1)} %get-tuple-element.15.order_ref, f32[2,4,128,512]{3,2,1,0:T(8,128)S(1)} %copy-done.1, bf16[384,256]{1,0:T(8,128)(2,1)S(1)} %copy-done.3, ...), custom_call_target="tpu_custom_call" | custom-call | flops 536870912 | bytes 1966080 | tf_op jit(solution)/shard_map/pallas_call | solution.py:233
  68.9 2.5 %collective-permute-start.2 = (bf16[256,512]{1,0:T(8,128)(2,1)S(1)}, bf16[256,512]{1,0:T(8,128)(2,1)S(1)}, u32[]{:S(2)}, u32[]{:S(2)}) collective-permute-start(bf16[256,512]{1,0:T(8,128)(2,1)S(1)} %shard_map.121), channel_id=1, source_target_pairs={{0,3},{1,2},{2,1},{3,0},{4,7},{5,6},{6,5},{7,4},{8,11},{9,10},{10,... | collective-permute-start | bytes 786440 | tf_op jit(solution)/shard_map/ppermute | solution.py:342
  71.4 1.9 %shard_map.122 = bf16[256,512]{1,0:T(8,128)(2,1)S(1)} custom-call(s32[2]{0:T(128)S(1)} %pad_add_fusion.3.scalar_ref, bf16[1024,512]{1,0:T(8,128)(2,1)S(1)} %bitcast.23, bf16[1024,1024]{1,0:T(8,128)(2,1)S(1)} %get-tuple-element.15.order_ref, f32[2,4,128,512]{3,2,1,0:T(8,128)S(1)} %copy-done.1, bf16[384,256]{1,0:T(8,128)(2,1)S(1)} %copy-done.3, ...), custom_call_target="tpu_custom_call" | custom-call | flops 536870912 | bytes 1966080 | tf_op jit(solution)/shard_map/pallas_call | solution.py:233
  73.9 1.9 %shard_map.123 = bf16[256,512]{1,0:T(8,128)(2,1)S(1)} custom-call(s32[2]{0:T(128)S(1)} %pad_add_fusion.4.scalar_ref, bf16[1024,512]{1,0:T(8,128)(2,1)S(1)} %bitcast.24, bf16[1024,1024]{1,0:T(8,128)(2,1)S(1)} %get-tuple-element.15.order_ref, f32[2,4,128,512]{3,2,1,0:T(8,128)S(1)} %copy-done.1, bf16[384,256]{1,0:T(8,128)(2,1)S(1)} %copy-done.3, ...), custom_call_target="tpu_custom_call" | custom-call | flops 536870912 | bytes 1966080 | tf_op jit(solution)/shard_map/pallas_call | solution.py:233
  76.5 1.9 %shard_map.124.rest_3_ = bf16[256,512]{1,0:T(8,128)(2,1)S(1)} custom-call(s32[2]{0:T(128)S(1)} %pad_add_fusion.5.scalar_ref, bf16[1024,512]{1,0:T(8,128)(2,1)S(1)} %bitcast.25, bf16[1024,1024]{1,0:T(8,128)(2,1)S(1)} %get-tuple-element.15.order_ref, f32[2,4,128,512]{3,2,1,0:T(8,128)S(1)} %copy-done.1, bf16[384,256]{1,0:T(8,128)(2,1)S(1)} %copy-done.3, ...), custom_call_target="tpu_custom_call" | custom-call | flops 536870912 | bytes 1966080 | tf_op jit(solution)/shard_map/pallas_call | solution.py:233
  78.3 4.5 %collective-permute-done.3.rest_1_ = bf16[256,512]{1,0:T(8,128)(2,1)S(1)} collective-permute-done((bf16[256,512]{1,0:T(8,128)(2,1)S(1)}, bf16[256,512]{1,0:T(8,128)(2,1)S(1)}, u32[]{:S(2)}, u32[]{:S(2)}) %collective-permute-start.3) | collective-permute-done | bytes 262176 | tf_op jit(solution)/shard_map/ppermute | solution.py:342
  82.9 1.5 %shard_map.125 = bf16[256,2048]{1,0:T(8,128)(2,1)} custom-call(s32[4]{0:T(128)S(1)} %pad_add_fusion.member_ref, bf16[256,512]{1,0:T(8,128)(2,1)S(1)} %collective-permute-done.2.rest_0_, bf16[256,512]{1,0:T(8,128)(2,1)S(1)} %collective-permute-done.3.rest_1_, bf16[256,512]{1,0:T(8,128)(2,1)S(1)} %collective-permute-done.4.rest_2_, ...), custom_call_target="tpu_custom_call" | custom-call | bytes 2097152 | tf_op jit(solution)/shard_map/pallas_call | solution.py:263
  (48 shorter events, 7.1 us)
Async XLA Ops:
  7.2 21.7 %all-to-all-start = ((bf16[16,64,256]{2,1,0:T(8,128)(2,1)}), bf16[16,64,256]{2,1,0:T(8,128)(2,1)S(1)}, u32[]{:S(2)}, u32[]{:S(2)}) async-start(bf16[16,64,256]{2,1,0:T(8,128)(2,1)} %bitcast.28), calls=%async_computation | async-start | bytes 1048576 | tf_op jit(solution)/shard_map/all_to_all | solution.py:295
  14.4 19.0 %copy-start.12 = (s32[4096]{0:T(1024)S(1)}, s32[4096]{0:T(1024)}, u32[]{:S(2)}) copy-start(s32[4096]{0:T(1024)} %param.13) | copy-start | bytes 49156
  14.4 19.1 %copy-start.15 = (s32[2]{0:T(128)S(1)}, s32[2]{0:T(128)}, u32[]{:S(2)}) copy-start(s32[2]{0:T(128)} %constant.97.clone) | copy-start | bytes 28
  14.4 20.4 %copy-start.14 = (s32[2]{0:T(128)S(1)}, s32[2]{0:T(128)}, u32[]{:S(2)}) copy-start(s32[2]{0:T(128)} %constant.96.clone) | copy-start | bytes 28
  14.4 21.7 %copy-start.13 = (s32[32]{0:T(128)S(1)}, s32[32]{0:T(128)}, u32[]{:S(2)}) copy-start(s32[32]{0:T(128)} %param.14) | copy-start | bytes 388
  28.9 9.0 %copy-start.10 = (bf16[16,64,256]{2,1,0:T(8,128)(2,1)}, bf16[16,64,256]{2,1,0:T(8,128)(2,1)S(1)}, u32[]{:S(2)}) copy-start(bf16[16,64,256]{2,1,0:T(8,128)(2,1)S(1)} %all-to-all-done) | copy-start | bytes 1572868
  28.9 33.0 %all-to-all-start.1 = ((bf16[16,64,512]{2,1,0:T(8,128)(2,1)}), bf16[16,64,512]{2,1,0:T(8,128)(2,1)S(1)}, u32[]{:S(2)}, u32[]{:S(2)}) async-start(bf16[16,64,512]{2,1,0:T(8,128)(2,1)} %bitcast.27), calls=%async_computation.1 | async-start | bytes 2097152 | tf_op jit(solution)/shard_map/all_to_all | solution.py:295
  37.9 1.0 %copy-start.11 = (bf16[16,64,256]{2,1,0:T(8,128)(2,1)S(1)}, bf16[16,64,256]{2,1,0:T(8,128)(2,1)}, u32[]{:S(2)}) copy-start(bf16[16,64,256]{2,1,0:T(8,128)(2,1)} %copy-done.10) | copy-start | bytes 1572868
  40.6 1.3 %copy-start = (f32[2,4,128,512]{3,2,1,0:T(8,128)}, f32[2,4,128,512]{3,2,1,0:T(8,128)S(1)}, u32[]{:S(2)}) copy-start(f32[2,4,128,512]{3,2,1,0:T(8,128)S(1)} %get-tuple-element.16.mask_ref) | copy-start | bytes 6291460
  42.0 0.6 copy-start.6
  42.6 0.6 copy-start.8
  43.2 16.0 %collective-permute-start = (bf16[384,256]{1,0:T(8,128)(2,1)S(1)}, bf16[384,256]{1,0:T(8,128)(2,1)S(1)}, u32[]{:S(2)}, u32[]{:S(2)}) collective-permute-start(bf16[384,256]{1,0:T(8,128)(2,1)S(1)} %get-tuple-element.17.rest_2_), channel_id=1, source_target_pairs={{0,4},{1,5},{2,6},{3,7},{4,8},{5,9},{6,10},{7,11},{8,12},{9,13},{1... | collective-permute-start | bytes 589832 | tf_op jit(solution)/shard_map/ppermute | solution.py:321
  46.6 14.7 %collective-permute-start.1 = (bf16[384,256]{1,0:T(8,128)(2,1)S(1)}, bf16[384,256]{1,0:T(8,128)(2,1)S(1)}, u32[]{:S(2)}, u32[]{:S(2)}) collective-permute-start(bf16[384,256]{1,0:T(8,128)(2,1)S(1)} %get-tuple-element.19.rest_5_), channel_id=1, source_target_pairs={{4,0},{5,1},{6,2},{7,3},{8,4},{9,5},{10,6},{11,7},{12,8},{13,9},{1... | collective-permute-start | bytes 589832 | tf_op jit(solution)/shard_map/ppermute | solution.py:322
  59.2 0.7 copy-start.2
  61.2 0.7 copy-start.4
  61.9 1.6 %copy-start.1 = (f32[2,4,128,512]{3,2,1,0:T(8,128)S(1)}, f32[2,4,128,512]{3,2,1,0:T(8,128)}, u32[]{:S(2)}) copy-start(f32[2,4,128,512]{3,2,1,0:T(8,128)} %copy-done) | copy-start | bytes 6291460
  63.5 0.9 %copy-start.3 = (bf16[384,256]{1,0:T(8,128)(2,1)S(1)}, bf16[384,256]{1,0:T(8,128)(2,1)}, u32[]{:S(2)}) copy-start(bf16[384,256]{1,0:T(8,128)(2,1)} %copy-done.2) | copy-start | bytes 589828
  64.4 0.9 %copy-start.5 = (bf16[384,256]{1,0:T(8,128)(2,1)S(1)}, bf16[384,256]{1,0:T(8,128)(2,1)}, u32[]{:S(2)}) copy-start(bf16[384,256]{1,0:T(8,128)(2,1)} %copy-done.4) | copy-start | bytes 589828
  65.4 0.8 copy-start.7
  66.2 0.8 copy-start.9
  68.9 9.4 %collective-permute-start.2 = (bf16[256,512]{1,0:T(8,128)(2,1)S(1)}, bf16[256,512]{1,0:T(8,128)(2,1)S(1)}, u32[]{:S(2)}, u32[]{:S(2)}) collective-permute-start(bf16[256,512]{1,0:T(8,128)(2,1)S(1)} %shard_map.121), channel_id=1, source_target_pairs={{0,3},{1,2},{2,1},{3,0},{4,7},{5,6},{6,5},{7,4},{8,11},{9,10},{10,... | collective-permute-start | bytes 786440 | tf_op jit(solution)/shard_map/ppermute | solution.py:342
  73.3 9.6 %collective-permute-start.3 = (bf16[256,512]{1,0:T(8,128)(2,1)S(1)}, bf16[256,512]{1,0:T(8,128)(2,1)S(1)}, u32[]{:S(2)}, u32[]{:S(2)}) collective-permute-start(bf16[256,512]{1,0:T(8,128)(2,1)S(1)} %shard_map.122), channel_id=1, source_target_pairs={{0,1},{1,0},{2,3},{3,2},{4,5},{5,4},{6,7},{7,6},{8,9},{9,8},{10,11... | collective-permute-start | bytes 786440 | tf_op jit(solution)/shard_map/ppermute | solution.py:342
  75.8 7.1 %collective-permute-start.4 = (bf16[256,512]{1,0:T(8,128)(2,1)S(1)}, bf16[256,512]{1,0:T(8,128)(2,1)S(1)}, u32[]{:S(2)}, u32[]{:S(2)}) collective-permute-start(bf16[256,512]{1,0:T(8,128)(2,1)S(1)} %shard_map.123), channel_id=1, source_target_pairs={{0,2},{1,3},{2,0},{3,1},{4,6},{5,7},{6,4},{7,5},{8,10},{9,11},{10,... | collective-permute-start | bytes 786440 | tf_op jit(solution)/shard_map/ppermute | solution.py:342

commit v6 on v3

--- a/solution.py
+++ b/solution.py
@@ -168,7 +168,7 @@
 
 def attend_kernel(block, scalar_ref, query_ref, slot_ref, ends_ref, *rest):
     pieces, out_ref, held = rest[:6], rest[6], rest[7]
-    target, starts = scalar_ref[0], (scalar_ref[1], scalar_ref[2])
+    target, starts, last = scalar_ref[0], (scalar_ref[1], scalar_ref[2]), scalar_ref[3]
     heads = query_ref.shape[1] // HEAD_SIZE
     arrived = query_ref.shape[0]
     run = arrived // 2
@@ -181,34 +181,43 @@
     for half in range(2):
         first = 0
         for piece in pieces[3 * half : 3 * half + 3]:
-            held[half, first : first + piece.shape[0], :] = piece[...]
+            values = piece[...]
+            if half == 1 and first == 0:
+                values = jnp.where(last == 1, pieces[2][...], values)
+            held[half, first : first + piece.shape[0], :] = values
             first += piece.shape[0]
     indices = (target, per_run - 1 - target)
     at = [pl.multiple_of(index * block, block) for index in indices]
     iota = lax.broadcasted_iota(jnp.int32, (block, arrived), 0)
     chosen = [(iota + (at[half] + half * run) == slot).astype(jnp.bfloat16) for half in range(2)]
     queries = dot(jnp.concatenate(chosen, axis=0), query_ref[...]).astype(jnp.bfloat16)
+    here = [slice(half * block, (half + 1) * block) for half in range(2)]
+    scores, weights, totals = [], [], []
     for half in range(2):
-        here = slice(half * block, (half + 1) * block)
+        stacked = jnp.concatenate(
+            [queries[here[half], h * HEAD_SIZE : (h + 1) * HEAD_SIZE] for h in range(heads)], axis=0
+        )
         key = held[half, pl.ds(at[half], keys), :HEAD_SIZE]
-        value = held[half, pl.ds(at[half], keys), HEAD_SIZE:]
+        scores.append(
+            lax.dot_general(stacked, key, (((1,), (1,)), ((), ())), preferred_element_type=jnp.float32)
+        )
+    for half in range(2):
         begin = starts[half] + at[half]
         query_at = lax.broadcasted_iota(jnp.int32, (block, 1), 0) + begin
         key_at = lax.broadcasted_iota(jnp.int32, (1, keys), 1) + (begin - reach)
         doc_start = jnp.max(jnp.where(ends <= query_at, ends, 0), axis=1, keepdims=True)
         allowed = (key_at >= doc_start) & (key_at <= query_at)
-        stacked = jnp.concatenate(
-            [queries[here, h * HEAD_SIZE : (h + 1) * HEAD_SIZE] for h in range(heads)], axis=0
-        )
-        scores = lax.dot_general(stacked, key, (((1,), (1,)), ((), ())), preferred_element_type=jnp.float32)
-        scores = jnp.where(allowed[None], scores.reshape(heads, block, keys), jnp.float32(-1e30))
-        scores = scores.reshape(heads * block, keys)
-        top = jnp.max(scores, axis=1, keepdims=True)
-        weights = jnp.exp2((scores - top) * factor)
-        total = jnp.sum(weights, axis=1, keepdims=True)
-        mixed = (dot(weights.astype(jnp.bfloat16), value) / total).astype(jnp.bfloat16)
+        masked = jnp.where(allowed[None], scores[half].reshape(heads, block, keys), jnp.float32(-1e30))
+        masked = masked.reshape(heads * block, keys)
+        top = jnp.max(masked, axis=1, keepdims=True)
+        exact = jnp.exp2((masked - top) * factor)
+        totals.append(jnp.sum(exact, axis=1, keepdims=True))
+        weights.append(exact.astype(jnp.bfloat16))
+    for half in range(2):
+        value = held[half, pl.ds(at[half], keys), HEAD_SIZE:]
+        mixed = (dot(weights[half], value) / totals[half]).astype(jnp.bfloat16)
         for h in range(heads):
-            out_ref[here, h * HEAD_SIZE : (h + 1) * HEAD_SIZE] = mixed[h * block : (h + 1) * block]
+            out_ref[here[half], h * HEAD_SIZE : (h + 1) * HEAD_SIZE] = mixed[h * block : (h + 1) * block]
 
 
 def attend(scalars, query, slot, ends, pieces, block):
@@ -231,15 +240,15 @@
     )(scalars, query, slot, ends, *pieces)
 
 
-def assemble_kernel(scalar_ref, *rest):
+def assemble_kernel(source_ref, *rest):
     pieces, out_ref = rest[:-1], rest[-1]
     width = pieces[0].shape[1]
-    for k, piece in enumerate(pieces):
-        at = pl.multiple_of((scalar_ref[0] ^ k) * width, width)
+    for i, piece in enumerate(pieces):
+        at = pl.multiple_of(source_ref[i] * width, width)
         out_ref[:, pl.ds(at, width)] = piece[...]
 
 
-def assemble(scalars, pieces):
+def assemble(sources, pieces):
     rows, width = pieces[0].shape
     return pl.pallas_call(
         assemble_kernel,
@@ -250,7 +259,7 @@
         cost_estimate=pl.CostEstimate(
             flops=0, bytes_accessed=4 * rows * width * len(pieces), transcendentals=0
         ),
-    )(scalars, *pieces)
+    )(sources, *pieces)
 
 
 def shards(tokens, positions, lengths, gain, w_query, w_key, value_weight):
@@ -266,8 +275,8 @@
     group_rows = rows // groups
 
     half = HEAD_SIZE // 2
-    freq = ROPE_THETA ** (-(jnp.arange(HEAD_SIZE, dtype=jnp.float32) % half * 2.0 / HEAD_SIZE))
-    operands = (device.reshape(1), positions.reshape(-1, 128), freq[None, :], gain, tokens)
+    freq = np.float32(ROPE_THETA ** (-(np.arange(HEAD_SIZE) % half * 2.0 / HEAD_SIZE)))
+    operands = (device.reshape(1), positions.reshape(-1, 128), jnp.asarray(freq[None, :]), gain, tokens)
 
     def exchange(ordered):
         width = ordered.shape[3]
@@ -299,20 +308,29 @@
     down = [(i + members, i) for i in range(devices - members)]
     early_halo = lax.ppermute(early_tail, "ctx", up)
     late_halo = lax.ppermute(late_tail, "ctx", down)
-    late_halo = jnp.where(group == groups - 1, early_tail, late_halo)
     pieces = (early_halo, early_head, early_tail, late_halo, late_head, late_tail)
 
-    results = []
-    for k in [3, 1, 2, 0][-members:]:
-        target = member ^ k
-        scalars = jnp.stack([target, first_run, second_run]).astype(jnp.int32)
+    last = (group == groups - 1).astype(jnp.int32)
+    lanes = lax.axis_size("dp")
+    odd = lax.axis_index("dp") % 2 == 1
+    farthest = members - 1
+    between = list(range(1, farthest))
+    turns = ([farthest] + between + [0], [farthest] + between[::-1] + [0])
+    sources, results = [], []
+    for turn in range(members):
+        other = member ^ jnp.where(odd, turns[1][turn], turns[0][turn])
+        scalars = jnp.stack([other, first_run, second_run, last]).astype(jnp.int32)
         out = attend(scalars, query, slot, ends, pieces, block)
-        if k:
-            route = [(i, i // members * members + (i % members ^ k)) for i in range(devices)]
-            out = lax.ppermute(out, "ctx", route)
-        results.append((k, out))
-    results = [out for _, out in sorted(results, key=lambda pair: pair[0])]
-    return assemble(member.reshape(1).astype(jnp.int32), results)
+        if turn < farthest:
+            route = [
+                (i * devices + j, i * devices + j // members * members + (j % members ^ turns[i % 2][turn]))
+                for i in range(lanes)
+                for j in range(devices)
+            ]
+            out = lax.ppermute(out, ("dp", "ctx"), route)
+        sources.append(other)
+        results.append(out)
+    return assemble(jnp.stack(sources).astype(jnp.int32), results)
 
 
 def solution(mesh):

time: 81.7 us -> 79.3 us (0.971)
  the two profiles are of different devices: /device:TPU:12 before, /device:TPU:9 now
where the time goes in v6:
time: 79.3 us; the launch traced here: 78.8 us
  waiting for transfers between devices  29.5 us (37%)
  Pallas kernels  27.4 us (35%)
  starting transfers between devices  19.8 us (25%)
  other arithmetic  1.61 us (2%)
    ppermute x1, waiting for transfers between devices, shards(): early_halo = lax.ppermute(early_tail, 'ctx', up)  18 us
    pallas_call x2, Pallas kernels, project(): pl.pallas_call(functools.partial(project_kernel, kinds, devices, heads),...  17.4 us
    all_to_all x2, starting transfers between devices, exchange(): flat = lax.all_to_all(flat, 'ctx', split_axis=0, concat_axis=0, tiled=True)  11.7 us
    pallas_call x4, Pallas kernels, attend(): pl.pallas_call(functools.partial(attend_kernel, block), out_shape=jax.Sha...  7.72 us
    ppermute x3, waiting for transfers between devices, shards(): out = lax.ppermute(out, ('dp', 'ctx'), route)  6.08 us
    ppermute x1, starting transfers between devices, shards(): early_halo = lax.ppermute(early_tail, 'ctx', up)  3.09 us
    all_to_all x2, waiting for transfers between devices, exchange(): flat = lax.all_to_all(flat, 'ctx', split_axis=0, concat_axis=0, tiled=True)  2.97 us
    ppermute x3, starting transfers between devices, shards(): out = lax.ppermute(out, ('dp', 'ctx'), route)  2.85 us
  transfers between devices with their start and end apart: 7, of which 5 were waited for; matrix products, arithmetic and copies ran while one was open for 2% of the time, Pallas kernels for 21%

profile of v6, /device:TPU:9, one launch (start us, length us, event | category | flops | bytes accessed | tf_op | source)
XLA Modules:
  0.0 78.8 jit_solution(14249902321798873602)
XLA Ops:
  0.0 7.1 %shard_map.82 = bf16[4,4,64,256]{3,2,1,0:T(8,128)(2,1)} custom-call(s32[1]{0:T(128)} %bitcast.7.scalar_ref, s32[32,128]{1,0:T(8,128)} %bitcast.27, f32[1,128]{1,0:T(1,128)} %constant.94.clone.freq_ref, bf16[4096]{0:T(1024)(128)(2,1)} %gain_ref.3, bf16[256,4096]{1,0:T(8,128)(2,1)} %tokens_hbm.3, bf16[4096,512]{1,0:T(8,128)(2,1)} %rest_0_.2, ...), custom_call_target="tpu_custom_call" | custom-call | flops 2147483648 | bytes 11010048 | tf_op jit(solution)/shard_map/pallas_call | solution.py:125
  7.1 6.7 %all-to-all-start = ((bf16[16,64,256]{2,1,0:T(8,128)(2,1)}), bf16[16,64,256]{2,1,0:T(8,128)(2,1)S(1)}, u32[]{:S(2)}, u32[]{:S(2)}) async-start(bf16[16,64,256]{2,1,0:T(8,128)(2,1)} %bitcast.26), calls=%async_computation | async-start | bytes 1048576 | tf_op jit(solution)/shard_map/all_to_all | solution.py:284
  13.8 10.3 %shard_map.83 = bf16[4,4,64,512]{3,2,1,0:T(8,128)(2,1)} custom-call(s32[1]{0:T(128)} %bitcast.7.scalar_ref, s32[32,128]{1,0:T(8,128)} %bitcast.28, f32[1,128]{1,0:T(1,128)} %constant.94.clone.freq_ref, bf16[4096]{0:T(1024)(128)(2,1)} %gain_ref.3, bf16[256,4096]{1,0:T(8,128)(2,1)} %tokens_hbm.3, bf16[4096,2048]{1,0:T(8,128)(2,1)} %rest_0_.3), custom_call_target="tpu_custom_call" | custom-call | flops 4294967296 | bytes 19922944 | tf_op jit(solution)/shard_map/pallas_call | solution.py:125
  24.1 3.0 %all-to-all-done = bf16[16,64,256]{2,1,0:T(8,128)(2,1)S(1)} async-done(((bf16[16,64,256]{2,1,0:T(8,128)(2,1)}), bf16[16,64,256]{2,1,0:T(8,128)(2,1)S(1)}, u32[]{:S(2)}, u32[]{:S(2)}) %all-to-all-start) | async-done | bytes 524320 | tf_op jit(solution)/shard_map/all_to_all | solution.py:284
  27.1 5.0 %all-to-all-start.1 = ((bf16[16,64,512]{2,1,0:T(8,128)(2,1)}), bf16[16,64,512]{2,1,0:T(8,128)(2,1)S(1)}, u32[]{:S(2)}, u32[]{:S(2)}) async-start(bf16[16,64,512]{2,1,0:T(8,128)(2,1)} %bitcast.25), calls=%async_computation.1 | async-start | bytes 2097152 | tf_op jit(solution)/shard_map/all_to_all | solution.py:284
  32.2 0.2 reduce-window_2_clone.1.ends_ref
  32.4 0.6 reduce-window.9
  33.0 0.2 slice_reduce_fusion
  33.3 0.4 select_reduce_fusion
  33.8 0.7 shard_map.84
  34.5 3.1 %collective-permute-start = (bf16[384,256]{1,0:T(8,128)(2,1)S(1)}, bf16[384,256]{1,0:T(8,128)(2,1)S(1)}, u32[]{:S(2)}, u32[]{:S(2)}) collective-permute-start(bf16[384,256]{1,0:T(8,128)(2,1)S(1)} %get-tuple-element.13.rest_2_), channel_id=1, source_target_pairs={{0,4},{1,5},{2,6},{3,7},{4,8},{5,9},{6,10},{7,11},{8,12},{9,13},{1... | collective-permute-start | bytes 589832 | tf_op jit(solution)/shard_map/ppermute | solution.py:309
  37.6 2.2 %collective-permute-start.1 = (bf16[384,256]{1,0:T(8,128)(2,1)S(1)}, bf16[384,256]{1,0:T(8,128)(2,1)S(1)}, u32[]{:S(2)}, u32[]{:S(2)}) collective-permute-start(bf16[384,256]{1,0:T(8,128)(2,1)S(1)} %get-tuple-element.15.rest_5_), channel_id=1, source_target_pairs={{4,0},{5,1},{6,2},{7,3},{8,4},{9,5},{10,6},{11,7},{12,8},{13,9},{1... | collective-permute-start | bytes 589832 | tf_op jit(solution)/shard_map/ppermute | solution.py:310
  40.0 18.0 %collective-permute-done.rest_0_ = bf16[384,256]{1,0:T(8,128)(2,1)S(1)} collective-permute-done((bf16[384,256]{1,0:T(8,128)(2,1)S(1)}, bf16[384,256]{1,0:T(8,128)(2,1)S(1)}, u32[]{:S(2)}, u32[]{:S(2)}) %collective-permute-start) | collective-permute-done | bytes 196640 | tf_op jit(solution)/shard_map/ppermute | solution.py:309
  58.0 2.4 %collective-permute-done.1.rest_3_ = bf16[384,256]{1,0:T(8,128)(2,1)S(1)} collective-permute-done((bf16[384,256]{1,0:T(8,128)(2,1)S(1)}, bf16[384,256]{1,0:T(8,128)(2,1)S(1)}, u32[]{:S(2)}, u32[]{:S(2)}) %collective-permute-start.1) | collective-permute-done | bytes 196640 | tf_op jit(solution)/shard_map/ppermute | solution.py:310
  60.4 1.9 %shard_map.85 = bf16[256,512]{1,0:T(8,128)(2,1)S(1)} custom-call(s32[4]{0:T(128)S(1)} %add_add_fusion.scalar_ref, bf16[1024,512]{1,0:T(8,128)(2,1)S(1)} %bitcast.20, s32[1,1024]{1,0:T(1,128)S(1)} %reshape.156.slot_ref, s32[1,32]{1,0:T(1,128)S(1)} %reduce-window_2_clone.1.ends_ref, bf16[384,256]{1,0:T(8,128)(2,1)S(1)} %collective-permute-done.rest_0_, ...), custom_call_target="tpu_custom_call" | custom-call | flops 536870912 | bytes 1966080 | tf_op jit(solution)/shard_map/pallas_call | solution.py:228
  62.4 2.2 %collective-permute-start.2 = (bf16[256,512]{1,0:T(8,128)(2,1)S(1)}, bf16[256,512]{1,0:T(8,128)(2,1)S(1)}, u32[]{:S(2)}, u32[]{:S(2)}) collective-permute-start(bf16[256,512]{1,0:T(8,128)(2,1)S(1)} %shard_map.85), channel_id=1, source_target_pairs={{0,3},{1,2},{2,1},{3,0},{4,7},{5,6},{6,5},{7,4},{8,11},{9,10},{10,... | collective-permute-start | bytes 786440 | tf_op jit(solution)/shard_map/ppermute | solution.py:330
  64.6 1.9 %shard_map.86 = bf16[256,512]{1,0:T(8,128)(2,1)S(1)} custom-call(s32[4]{0:T(128)S(1)} %add_add_fusion.1.scalar_ref, bf16[1024,512]{1,0:T(8,128)(2,1)S(1)} %bitcast.21, s32[1,1024]{1,0:T(1,128)S(1)} %reshape.156.slot_ref, s32[1,32]{1,0:T(1,128)S(1)} %reduce-window_2_clone.1.ends_ref, bf16[384,256]{1,0:T(8,128)(2,1)S(1)} %collective-permute-done.rest_0_, ...), custom_call_target="tpu_custom_call" | custom-call | flops 536870912 | bytes 1966080 | tf_op jit(solution)/shard_map/pallas_call | solution.py:228
  66.5 0.3 collective-permute-start.3
  66.8 1.9 %shard_map.87 = bf16[256,512]{1,0:T(8,128)(2,1)S(1)} custom-call(s32[4]{0:T(128)S(1)} %add_add_fusion.2.scalar_ref, bf16[1024,512]{1,0:T(8,128)(2,1)S(1)} %bitcast.22, s32[1,1024]{1,0:T(1,128)S(1)} %reshape.156.slot_ref, s32[1,32]{1,0:T(1,128)S(1)} %reduce-window_2_clone.1.ends_ref, bf16[384,256]{1,0:T(8,128)(2,1)S(1)} %collective-permute-done.rest_0_, ...), custom_call_target="tpu_custom_call" | custom-call | flops 536870912 | bytes 1966080 | tf_op jit(solution)/shard_map/pallas_call | solution.py:228
  68.7 0.3 collective-permute-start.4
  69.2 1.9 %shard_map.88.rest_3_ = bf16[256,512]{1,0:T(8,128)(2,1)S(1)} custom-call(s32[4]{0:T(128)S(1)} %get-tuple-element.20.scalar_ref, bf16[1024,512]{1,0:T(8,128)(2,1)S(1)} %bitcast.23, s32[1,1024]{1,0:T(1,128)S(1)} %reshape.156.slot_ref, s32[1,32]{1,0:T(1,128)S(1)} %reduce-window_2_clone.1.ends_ref, bf16[384,256]{1,0:T(8,128)(2,1)S(1)} %collective-permute-done.rest_0_, ...), custom_call_target="tpu_custom_call" | custom-call | flops 536870912 | bytes 1966080 | tf_op jit(solution)/shard_map/pallas_call | solution.py:228
  71.1 3.8 %collective-permute-done.3.rest_1_ = bf16[256,512]{1,0:T(8,128)(2,1)S(1)} collective-permute-done((bf16[256,512]{1,0:T(8,128)(2,1)S(1)}, bf16[256,512]{1,0:T(8,128)(2,1)S(1)}, u32[]{:S(2)}, u32[]{:S(2)}) %collective-permute-start.3) | collective-permute-done | bytes 262176 | tf_op jit(solution)/shard_map/ppermute | solution.py:330
  74.9 2.3 %collective-permute-done.4.rest_2_ = bf16[256,512]{1,0:T(8,128)(2,1)S(1)} collective-permute-done((bf16[256,512]{1,0:T(8,128)(2,1)S(1)}, bf16[256,512]{1,0:T(8,128)(2,1)S(1)}, u32[]{:S(2)}, u32[]{:S(2)}) %collective-permute-start.4) | collective-permute-done | bytes 262176 | tf_op jit(solution)/shard_map/ppermute | solution.py:330
  77.2 1.6 %shard_map.89 = bf16[256,2048]{1,0:T(8,128)(2,1)} custom-call(s32[4]{0:T(128)S(1)} %get-tuple-element.19.source_ref, bf16[256,512]{1,0:T(8,128)(2,1)S(1)} %collective-permute-done.2.rest_0_, bf16[256,512]{1,0:T(8,128)(2,1)S(1)} %collective-permute-done.3.rest_1_, bf16[256,512]{1,0:T(8,128)(2,1)S(1)} %collective-permute-done.4.rest_2_, ...), custom_call_target="tpu_custom_call" | custom-call | bytes 2097152 | tf_op jit(solution)/shard_map/pallas_call | solution.py:253
  (16 shorter events, 0.6 us)
Async XLA Ops:
  7.1 19.9 %all-to-all-start = ((bf16[16,64,256]{2,1,0:T(8,128)(2,1)}), bf16[16,64,256]{2,1,0:T(8,128)(2,1)S(1)}, u32[]{:S(2)}, u32[]{:S(2)}) async-start(bf16[16,64,256]{2,1,0:T(8,128)(2,1)} %bitcast.26), calls=%async_computation | async-start | bytes 1048576 | tf_op jit(solution)/shard_map/all_to_all | solution.py:284
  13.8 18.3 %copy-start = (s32[4096]{0:T(1024)S(1)}, s32[4096]{0:T(1024)}, u32[]{:S(2)}) copy-start(s32[4096]{0:T(1024)} %param.9) | copy-start | bytes 49156
  13.8 18.3 %copy-start.1 = (s32[32]{0:T(128)S(1)}, s32[32]{0:T(128)}, u32[]{:S(2)}) copy-start(s32[32]{0:T(128)} %param.10) | copy-start | bytes 388
  27.1 33.3 %all-to-all-start.1 = ((bf16[16,64,512]{2,1,0:T(8,128)(2,1)}), bf16[16,64,512]{2,1,0:T(8,128)(2,1)S(1)}, u32[]{:S(2)}, u32[]{:S(2)}) async-start(bf16[16,64,512]{2,1,0:T(8,128)(2,1)} %bitcast.25), calls=%async_computation.1 | async-start | bytes 2097152 | tf_op jit(solution)/shard_map/all_to_all | solution.py:284
  34.5 23.5 %collective-permute-start = (bf16[384,256]{1,0:T(8,128)(2,1)S(1)}, bf16[384,256]{1,0:T(8,128)(2,1)S(1)}, u32[]{:S(2)}, u32[]{:S(2)}) collective-permute-start(bf16[384,256]{1,0:T(8,128)(2,1)S(1)} %get-tuple-element.13.rest_2_), channel_id=1, source_target_pairs={{0,4},{1,5},{2,6},{3,7},{4,8},{5,9},{6,10},{7,11},{8,12},{9,13},{1... | collective-permute-start | bytes 589832 | tf_op jit(solution)/shard_map/ppermute | solution.py:309
  37.6 22.8 %collective-permute-start.1 = (bf16[384,256]{1,0:T(8,128)(2,1)S(1)}, bf16[384,256]{1,0:T(8,128)(2,1)S(1)}, u32[]{:S(2)}, u32[]{:S(2)}) collective-permute-start(bf16[384,256]{1,0:T(8,128)(2,1)S(1)} %get-tuple-element.15.rest_5_), channel_id=1, source_target_pairs={{4,0},{5,1},{6,2},{7,3},{8,4},{9,5},{10,6},{11,7},{12,8},{13,9},{1... | collective-permute-start | bytes 589832 | tf_op jit(solution)/shard_map/ppermute | solution.py:310
  62.4 8.7 %collective-permute-start.2 = (bf16[256,512]{1,0:T(8,128)(2,1)S(1)}, bf16[256,512]{1,0:T(8,128)(2,1)S(1)}, u32[]{:S(2)}, u32[]{:S(2)}) collective-permute-start(bf16[256,512]{1,0:T(8,128)(2,1)S(1)} %shard_map.85), channel_id=1, source_target_pairs={{0,3},{1,2},{2,1},{3,0},{4,7},{5,6},{6,5},{7,4},{8,11},{9,10},{10,... | collective-permute-start | bytes 786440 | tf_op jit(solution)/shard_map/ppermute | solution.py:330
  66.5 8.4 %collective-permute-start.3 = (bf16[256,512]{1,0:T(8,128)(2,1)S(1)}, bf16[256,512]{1,0:T(8,128)(2,1)S(1)}, u32[]{:S(2)}, u32[]{:S(2)}) collective-permute-start(bf16[256,512]{1,0:T(8,128)(2,1)S(1)} %shard_map.86), channel_id=1, source_target_pairs={{0,1},{1,0},{2,3},{3,2},{4,5},{5,4},{6,7},{7,6},{8,9},{9,8},{10,11... | collective-permute-start | bytes 786440 | tf_op jit(solution)/shard_map/ppermute | solution.py:330
  68.7 8.5 %collective-permute-start.4 = (bf16[256,512]{1,0:T(8,128)(2,1)S(1)}, bf16[256,512]{1,0:T(8,128)(2,1)S(1)}, u32[]{:S(2)}, u32[]{:S(2)}) collective-permute-start(bf16[256,512]{1,0:T(8,128)(2,1)S(1)} %shard_map.87), channel_id=1, source_target_pairs={{0,2},{1,3},{2,0},{3,1},{4,6},{5,7},{6,4},{7,5},{8,10},{9,11},{10,... | collective-permute-start | bytes 786440 | tf_op jit(solution)/shard_map/ppermute | solution.py:330

commit v7 on v6

--- a/solution.py
+++ b/solution.py
@@ -15,7 +15,6 @@
 
 WHOLE = pl.BlockSpec(memory_space=pltpu.VMEM)
 IN_PLACE = pl.BlockSpec(memory_space=pl.ANY)
-SCALARS = pl.BlockSpec(memory_space=pltpu.SMEM)
 MIB = 1024 * 1024
 
 
@@ -35,15 +34,24 @@
     return jnp.minimum(block_id, 2 * devices - 1 - block_id) // members
 
 
-def project_kernel(kinds, devices, members, scalar_ref, positions_ref, freq_ref, gain_ref, tokens_hbm, *rest):
+def project_kernel(kinds, devices, members, positions_hbm, freq_hbm, gain_hbm, tokens_hbm, *rest):
     count = len(kinds)
-    weights_hbm, out_ref = rest[:count], rest[count]
-    tokens, normed, weights, token_sems, sems = rest[count + 1 :]
+    weights_hbm, out_hbm = rest[:count], rest[count]
+    positions_ref, freq_ref, gain_ref, tokens, normed, weights, out_ref = rest[count + 1 : count + 8]
+    small_sems, token_sems, sems, out_sems = rest[count + 8 :]
     rows, width = tokens.shape
     chunks, _, span = weights.shape
     parts = token_sems.shape[0]
     part = rows // parts
     token_copies, copies, origin = [], [], []
+    small_copies = [
+        pltpu.make_async_copy(source, target, small_sems.at[i])
+        for i, (source, target) in enumerate(
+            [(positions_hbm, positions_ref), (freq_hbm, freq_ref), (gain_hbm, gain_ref)]
+        )
+    ]
+    for copy in small_copies:
+        copy.start()
     for i in range(parts):
         at = pl.ds(i * part, part)
         token_copies.append(pltpu.make_async_copy(tokens_hbm.at[at], tokens.at[at], token_sems.at[i]))
@@ -54,12 +62,13 @@
             source = weights_hbm[i].at[:, pl.ds(first, span)]
             copies.append(pltpu.make_async_copy(source, weights.at[j], sems.at[j]))
             origin.append((i, first))
-
     copies[0].start()
+    for copy in small_copies:
+        copy.wait()
     lanes = positions_ref.shape[1]
     stripes = rows // lanes
     mine = jnp.concatenate(
-        [positions_ref[pl.ds(scalar_ref[0] * stripes + i, 1), :] for i in range(stripes)], axis=1
+        [positions_ref[pl.ds(lax.axis_index("ctx") * stripes + i, 1), :] for i in range(stripes)], axis=1
     )
     owner = group_of(mine, rows // 2, devices, members)
     here = lax.broadcasted_iota(jnp.int32, (rows, rows), 0)
@@ -92,10 +101,11 @@
     for first in range(0, width, 512):
         columns = slice(first, first + 512)
         normed[:, columns] = dot(order, tokens[:, columns]).astype(jnp.bfloat16)
-    groups, heads = out_ref.shape[0], out_ref.shape[1]
+    groups, heads = out_ref.shape[:2]
     offsets = [0]
     for i in range(count):
         offsets.append(offsets[-1] + weights_hbm[i].shape[1] // heads)
+    written = []
     for j in range(chunks):
         i, first = origin[j]
         copies[j].wait()
@@ -112,9 +122,15 @@
             out_ref[:, head, :, inside : inside + HEAD_SIZE] = values.astype(jnp.bfloat16).reshape(
                 groups, rows // groups, HEAD_SIZE
             )
-
-
-def project(scalars, positions, freq, gain, tokens, weights, kinds, devices, heads):
+        done = (pl.ds(0, groups), pl.ds(first // per_head, max(span // per_head, 1)))
+        done += (pl.ds(0, rows // groups), pl.ds(offsets[i] + first % per_head, min(span, per_head)))
+        written.append(pltpu.make_async_copy(out_ref.at[done], out_hbm.at[done], out_sems.at[j]))
+        written[j].start()
+    for copy in written:
+        copy.wait()
+
+
+def project(positions, freq, gain, tokens, weights, kinds, devices, heads):
     rows, width = tokens.shape
     groups = devices // heads
     columns = sum(w.shape[1] for w in weights)
@@ -125,18 +141,24 @@
     return pl.pallas_call(
         functools.partial(project_kernel, kinds, devices, heads),
         out_shape=jax.ShapeDtypeStruct((groups, heads, rows // groups, columns // heads), jnp.bfloat16),
-        in_specs=[SCALARS] + [WHOLE] * 3 + [IN_PLACE] * (len(weights) + 1),
-        out_specs=WHOLE,
+        in_specs=[IN_PLACE] * (len(weights) + 4),
+        out_specs=IN_PLACE,
         scratch_shapes=[
+            pltpu.VMEM(positions.shape, jnp.int32),
+            pltpu.VMEM(freq.shape, jnp.float32),
+            pltpu.VMEM(gain.shape, jnp.bfloat16),
             pltpu.VMEM((rows, width), jnp.bfloat16),
             pltpu.VMEM((rows, width), jnp.bfloat16),
             pltpu.VMEM((columns // span, width, span), jnp.bfloat16),
+            pltpu.VMEM((groups, heads, rows // groups, columns // heads), jnp.bfloat16),
+            pltpu.SemaphoreType.DMA((3,)),
             pltpu.SemaphoreType.DMA((parts,)),
+            pltpu.SemaphoreType.DMA((columns // span,)),
             pltpu.SemaphoreType.DMA((columns // span,)),
         ],
         compiler_params=pltpu.CompilerParams(vmem_limit_bytes=56 * MIB),
         cost_estimate=pl.CostEstimate(flops=flops, bytes_accessed=size, transcendentals=0),
-    )(scalars, positions, freq, gain, tokens, *weights)
+    )(positions, freq, gain, tokens, *weights)
 
 
 def place_kernel(arrived_ref, slot_ref, *outs):
@@ -166,9 +188,25 @@
     )(arrived, slot)
 
 
-def attend_kernel(block, scalar_ref, query_ref, slot_ref, ends_ref, *rest):
+def taken_at(turn, members):
+    distances = distances_at(turn, members)
+    odd = lax.axis_index("dp") % 2
+    distance = odd * distances[1] + (1 - odd) * distances[0]
+    return (lax.axis_index("ctx") % members) ^ distance
+
+
+def distances_at(turn, members):
+    if turn in (0, members - 1):
+        return (members - 1 - turn,) * 2
+    return (turn, members - 1 - turn)
+
+
+def attend_kernel(block, turn, members, devices, query_ref, slot_ref, ends_ref, *rest):
     pieces, out_ref, held = rest[:6], rest[6], rest[7]
-    target, starts, last = scalar_ref[0], (scalar_ref[1], scalar_ref[2]), scalar_ref[3]
+    target = taken_at(turn, members)
+    group = lax.axis_index("ctx") // members
+    starts = (group * members * block, (2 * devices - members - group * members) * block)
+    last = group == devices // members - 1
     heads = query_ref.shape[1] // HEAD_SIZE
     arrived = query_ref.shape[0]
     run = arrived // 2
@@ -183,7 +221,7 @@
         for piece in pieces[3 * half : 3 * half + 3]:
             values = piece[...]
             if half == 1 and first == 0:
-                values = jnp.where(last == 1, pieces[2][...], values)
+                values = jnp.where(last, pieces[2][...], values)
             held[half, first : first + piece.shape[0], :] = values
             first += piece.shape[0]
     indices = (target, per_run - 1 - target)
@@ -220,15 +258,15 @@
             out_ref[here[half], h * HEAD_SIZE : (h + 1) * HEAD_SIZE] = mixed[h * block : (h + 1) * block]
 
 
-def attend(scalars, query, slot, ends, pieces, block):
+def attend(turn, members, devices, query, slot, ends, pieces, block):
     width = query.shape[1]
     held = REACH_BLOCKS * block + query.shape[0] // 2
     heads = width // HEAD_SIZE
     reach = (REACH_BLOCKS + 1) * block
     return pl.pallas_call(
-        functools.partial(attend_kernel, block),
+        functools.partial(attend_kernel, block, turn, members, devices),
         out_shape=jax.ShapeDtypeStruct((2 * block, width), jnp.bfloat16),
-        in_specs=[SCALARS] + [WHOLE] * 9,
+        in_specs=[WHOLE] * 9,
         out_specs=WHOLE,
         scratch_shapes=[pltpu.VMEM((2, held, 2 * HEAD_SIZE), jnp.bfloat16)],
         compiler_params=pltpu.CompilerParams(vmem_limit_bytes=16 * MIB),
@@ -237,29 +275,29 @@
             bytes_accessed=2 * query.size + 8 * held * HEAD_SIZE,
             transcendentals=2 * heads * block * reach,
         ),
-    )(scalars, query, slot, ends, *pieces)
-
-
-def assemble_kernel(source_ref, *rest):
-    pieces, out_ref = rest[:-1], rest[-1]
+    )(query, slot, ends, *pieces)
+
+
+def assemble_kernel(*refs):
+    pieces, out_ref = refs[:-1], refs[-1]
     width = pieces[0].shape[1]
-    for i, piece in enumerate(pieces):
-        at = pl.multiple_of(source_ref[i] * width, width)
+    for turn, piece in enumerate(pieces):
+        at = pl.multiple_of(taken_at(turn, len(pieces)) * width, width)
         out_ref[:, pl.ds(at, width)] = piece[...]
 
 
-def assemble(sources, pieces):
+def assemble(pieces):
     rows, width = pieces[0].shape
     return pl.pallas_call(
         assemble_kernel,
         out_shape=jax.ShapeDtypeStruct((rows, width * len(pieces)), jnp.bfloat16),
-        in_specs=[SCALARS] + [WHOLE] * len(pieces),
+        in_specs=[WHOLE] * len(pieces),
         out_specs=WHOLE,
         compiler_params=pltpu.CompilerParams(vmem_limit_bytes=8 * MIB),
         cost_estimate=pl.CostEstimate(
             flops=0, bytes_accessed=4 * rows * width * len(pieces), transcendentals=0
         ),
-    )(sources, *pieces)
+    )(*pieces)
 
 
 def shards(tokens, positions, lengths, gain, w_query, w_key, value_weight):
@@ -270,13 +308,12 @@
     members = w_key.shape[1] // HEAD_SIZE
     groups = devices // members
     group = device // members
-    member = device % members
     run = members * block
     group_rows = rows // groups
 
     half = HEAD_SIZE // 2
     freq = np.float32(ROPE_THETA ** (-(np.arange(HEAD_SIZE) % half * 2.0 / HEAD_SIZE)))
-    operands = (device.reshape(1), positions.reshape(-1, 128), jnp.asarray(freq[None, :]), gain, tokens)
+    operands = (positions.reshape(-1, 128), jnp.asarray(freq[None, :]), gain, tokens)
 
     def exchange(ordered):
         width = ordered.shape[3]
@@ -310,27 +347,19 @@
     late_halo = lax.ppermute(late_tail, "ctx", down)
     pieces = (early_halo, early_head, early_tail, late_halo, late_head, late_tail)
 
-    last = (group == groups - 1).astype(jnp.int32)
-    lanes = lax.axis_size("dp")
-    odd = lax.axis_index("dp") % 2 == 1
-    farthest = members - 1
-    between = list(range(1, farthest))
-    turns = ([farthest] + between + [0], [farthest] + between[::-1] + [0])
-    sources, results = [], []
+    results = []
     for turn in range(members):
-        other = member ^ jnp.where(odd, turns[1][turn], turns[0][turn])
-        scalars = jnp.stack([other, first_run, second_run, last]).astype(jnp.int32)
-        out = attend(scalars, query, slot, ends, pieces, block)
-        if turn < farthest:
+        out = attend(turn, members, devices, query, slot, ends, pieces, block)
+        if turn < members - 1:
+            distances = distances_at(turn, members)
             route = [
-                (i * devices + j, i * devices + j // members * members + (j % members ^ turns[i % 2][turn]))
-                for i in range(lanes)
+                (i * devices + j, i * devices + j // members * members + (j % members ^ distances[i % 2]))
+                for i in range(lax.axis_size("dp"))
                 for j in range(devices)
             ]
             out = lax.ppermute(out, ("dp", "ctx"), route)
-        sources.append(other)
         results.append(out)
-    return assemble(jnp.stack(sources).astype(jnp.int32), results)
+    return assemble(results)
 
 
 def solution(mesh):

time: 79.3 us -> 78.1 us (0.985)
  the two profiles are of different devices: /device:TPU:9 before, /device:TPU:8 now
where the time goes in v7:
time: 78.1 us; the launch traced here: 77.7 us
  waiting for transfers between devices  29.9 us (38%)
  Pallas kernels  24.8 us (32%)
  starting transfers between devices  21.3 us (27%)
  other arithmetic  1.3 us (2%)
    ppermute x1, waiting for transfers between devices, shards(): early_halo = lax.ppermute(early_tail, 'ctx', up)  17.6 us
    pallas_call x2, Pallas kernels, project(): pl.pallas_call(functools.partial(project_kernel, kinds, devices, heads),...  17.4 us
    all_to_all x2, starting transfers between devices, exchange(): flat = lax.all_to_all(flat, 'ctx', split_axis=0, concat_axis=0, tiled=True)  11.8 us
    ppermute x3, waiting for transfers between devices, shards(): out = lax.ppermute(out, ('dp', 'ctx'), route)  6.07 us
    pallas_call x4, Pallas kernels, attend(): pl.pallas_call(functools.partial(attend_kernel, block, turn, members, dev...  5.59 us
    all_to_all x2, waiting for transfers between devices, exchange(): flat = lax.all_to_all(flat, 'ctx', split_axis=0, concat_axis=0, tiled=True)  4.26 us
    ppermute x3, starting transfers between devices, shards(): out = lax.ppermute(out, ('dp', 'ctx'), route)  3.68 us
    ppermute x1, starting transfers between devices, shards(): early_halo = lax.ppermute(early_tail, 'ctx', up)  3.37 us
  transfers between devices with their start and end apart: 7, of which 5 were waited for; matrix products, arithmetic and copies ran while one was open for 2% of the time, Pallas kernels for 19%

profile of v7, /device:TPU:8, one launch (start us, length us, event | category | flops | bytes accessed | tf_op | source)
XLA Modules:
  0.0 77.7 jit_solution(16887368675028125874)
XLA Ops:
  0.0 7.2 %shard_map.82 = bf16[4,4,64,256]{3,2,1,0:T(8,128)(2,1)} custom-call(s32[32,128]{1,0:T(8,128)} %bitcast.19, f32[1,128]{1,0:T(1,128)} %constant.69.clone.freq_hbm, bf16[4096]{0:T(1024)(128)(2,1)} %gain_hbm.3, bf16[256,4096]{1,0:T(8,128)(2,1)} %tokens_hbm.3, bf16[4096,512]{1,0:T(8,128)(2,1)} %rest_0_.2, bf16[4096,512]{1,0:T(8,128)(2,1)} %rest_1_.1), custom_call_target="tpu_custom_call" | custom-call | flops 2147483648 | bytes 11010048 | tf_op jit(solution)/shard_map/pallas_call | solution.py:141
  7.2 7.2 %all-to-all-start = ((bf16[16,64,256]{2,1,0:T(8,128)(2,1)}), bf16[16,64,256]{2,1,0:T(8,128)(2,1)S(1)}, u32[]{:S(2)}, u32[]{:S(2)}) async-start(bf16[16,64,256]{2,1,0:T(8,128)(2,1)} %bitcast.18), calls=%async_computation | async-start | bytes 1048576 | tf_op jit(solution)/shard_map/all_to_all | solution.py:321
  14.5 10.2 %shard_map.83 = bf16[4,4,64,512]{3,2,1,0:T(8,128)(2,1)} custom-call(s32[32,128]{1,0:T(8,128)} %bitcast.20, f32[1,128]{1,0:T(1,128)} %constant.69.clone.freq_hbm, bf16[4096]{0:T(1024)(128)(2,1)} %gain_hbm.3, bf16[256,4096]{1,0:T(8,128)(2,1)} %tokens_hbm.3, bf16[4096,2048]{1,0:T(8,128)(2,1)} %rest_0_.3), custom_call_target="tpu_custom_call" | custom-call | flops 4294967296 | bytes 19922944 | tf_op jit(solution)/shard_map/pallas_call | solution.py:141
  24.7 4.3 %all-to-all-done = bf16[16,64,256]{2,1,0:T(8,128)(2,1)S(1)} async-done(((bf16[16,64,256]{2,1,0:T(8,128)(2,1)}), bf16[16,64,256]{2,1,0:T(8,128)(2,1)S(1)}, u32[]{:S(2)}, u32[]{:S(2)}) %all-to-all-start) | async-done | bytes 524320 | tf_op jit(solution)/shard_map/all_to_all | solution.py:321
  28.9 4.6 %all-to-all-start.1 = ((bf16[16,64,512]{2,1,0:T(8,128)(2,1)}), bf16[16,64,512]{2,1,0:T(8,128)(2,1)S(1)}, u32[]{:S(2)}, u32[]{:S(2)}) async-start(bf16[16,64,512]{2,1,0:T(8,128)(2,1)} %bitcast.17), calls=%async_computation.1 | async-start | bytes 2097152 | tf_op jit(solution)/shard_map/all_to_all | solution.py:321
  33.6 0.6 reduce-window.9
  34.1 0.2 slice_reduce_fusion
  34.5 0.4 select_reduce_fusion
  34.9 0.7 shard_map.84
  35.6 3.4 %collective-permute-start = (bf16[384,256]{1,0:T(8,128)(2,1)S(1)}, bf16[384,256]{1,0:T(8,128)(2,1)S(1)}, u32[]{:S(2)}, u32[]{:S(2)}) collective-permute-start(bf16[384,256]{1,0:T(8,128)(2,1)S(1)} %get-tuple-element.13.rest_2_), channel_id=1, source_target_pairs={{0,4},{1,5},{2,6},{3,7},{4,8},{5,9},{6,10},{7,11},{8,12},{9,13},{1... | collective-permute-start | bytes 589832 | tf_op jit(solution)/shard_map/ppermute | solution.py:346
  39.0 2.5 %collective-permute-start.1 = (bf16[384,256]{1,0:T(8,128)(2,1)S(1)}, bf16[384,256]{1,0:T(8,128)(2,1)S(1)}, u32[]{:S(2)}, u32[]{:S(2)}) collective-permute-start(bf16[384,256]{1,0:T(8,128)(2,1)S(1)} %get-tuple-element.15.rest_5_), channel_id=1, source_target_pairs={{4,0},{5,1},{6,2},{7,3},{8,4},{9,5},{10,6},{11,7},{12,8},{13,9},{1... | collective-permute-start | bytes 589832 | tf_op jit(solution)/shard_map/ppermute | solution.py:347
  41.5 0.2 reduce-window_2_clone.1.ends_ref
  41.7 17.6 %collective-permute-done.rest_0_ = bf16[384,256]{1,0:T(8,128)(2,1)S(1)} collective-permute-done((bf16[384,256]{1,0:T(8,128)(2,1)S(1)}, bf16[384,256]{1,0:T(8,128)(2,1)S(1)}, u32[]{:S(2)}, u32[]{:S(2)}) %collective-permute-start) | collective-permute-done | bytes 196640 | tf_op jit(solution)/shard_map/ppermute | solution.py:346
  59.3 2.0 %collective-permute-done.1.rest_3_ = bf16[384,256]{1,0:T(8,128)(2,1)S(1)} collective-permute-done((bf16[384,256]{1,0:T(8,128)(2,1)S(1)}, bf16[384,256]{1,0:T(8,128)(2,1)S(1)}, u32[]{:S(2)}, u32[]{:S(2)}) %collective-permute-start.1) | collective-permute-done | bytes 196640 | tf_op jit(solution)/shard_map/ppermute | solution.py:347
  61.3 1.4 %shard_map.85 = bf16[256,512]{1,0:T(8,128)(2,1)S(1)} custom-call(bf16[1024,512]{1,0:T(8,128)(2,1)S(1)} %bitcast.12, s32[1,1024]{1,0:T(1,128)S(1)} %reshape.152.slot_ref, s32[1,32]{1,0:T(1,128)S(1)} %reduce-window_2_clone.1.ends_ref, bf16[384,256]{1,0:T(8,128)(2,1)S(1)} %collective-permute-done.rest_0_, bf16[128,256]{1,0:T(8,128)(2,1)S(1)} %get-tuple-element.14.rest_1_, ...), custom_call_target="tpu_custom_call" | custom-call | flops 536870912 | bytes 1966080 | tf_op jit(solution)/shard_map/pallas_call | solution.py:266
  62.7 2.5 %collective-permute-start.2 = (bf16[256,512]{1,0:T(8,128)(2,1)S(1)}, bf16[256,512]{1,0:T(8,128)(2,1)S(1)}, u32[]{:S(2)}, u32[]{:S(2)}) collective-permute-start(bf16[256,512]{1,0:T(8,128)(2,1)S(1)} %shard_map.85), channel_id=1, source_target_pairs={{0,3},{1,2},{2,1},{3,0},{4,7},{5,6},{6,5},{7,4},{8,11},{9,10},{10,... | collective-permute-start | bytes 786440 | tf_op jit(solution)/shard_map/ppermute | solution.py:360
  65.2 1.4 %shard_map.86 = bf16[256,512]{1,0:T(8,128)(2,1)S(1)} custom-call(bf16[1024,512]{1,0:T(8,128)(2,1)S(1)} %bitcast.13, s32[1,1024]{1,0:T(1,128)S(1)} %reshape.152.slot_ref, s32[1,32]{1,0:T(1,128)S(1)} %reduce-window_2_clone.1.ends_ref, bf16[384,256]{1,0:T(8,128)(2,1)S(1)} %collective-permute-done.rest_0_, bf16[128,256]{1,0:T(8,128)(2,1)S(1)} %get-tuple-element.14.rest_1_, ...), custom_call_target="tpu_custom_call" | custom-call | flops 536870912 | bytes 1966080 | tf_op jit(solution)/shard_map/pallas_call | solution.py:266
  66.6 0.6 collective-permute-start.3
  67.2 1.4 %shard_map.87 = bf16[256,512]{1,0:T(8,128)(2,1)S(1)} custom-call(bf16[1024,512]{1,0:T(8,128)(2,1)S(1)} %bitcast.14, s32[1,1024]{1,0:T(1,128)S(1)} %reshape.152.slot_ref, s32[1,32]{1,0:T(1,128)S(1)} %reduce-window_2_clone.1.ends_ref, bf16[384,256]{1,0:T(8,128)(2,1)S(1)} %collective-permute-done.rest_0_, bf16[128,256]{1,0:T(8,128)(2,1)S(1)} %get-tuple-element.14.rest_1_, ...), custom_call_target="tpu_custom_call" | custom-call | flops 536870912 | bytes 1966080 | tf_op jit(solution)/shard_map/pallas_call | solution.py:266
  68.6 0.5 collective-permute-start.4
  69.2 1.4 %shard_map.88.refs_3_ = bf16[256,512]{1,0:T(8,128)(2,1)S(1)} custom-call(bf16[1024,512]{1,0:T(8,128)(2,1)S(1)} %bitcast.15, s32[1,1024]{1,0:T(1,128)S(1)} %reshape.152.slot_ref, s32[1,32]{1,0:T(1,128)S(1)} %reduce-window_2_clone.1.ends_ref, bf16[384,256]{1,0:T(8,128)(2,1)S(1)} %collective-permute-done.rest_0_, ...), custom_call_target="tpu_custom_call" | custom-call | flops 536870912 | bytes 1966080 | tf_op jit(solution)/shard_map/pallas_call | solution.py:266
  70.6 1.4 %collective-permute-done.2.refs_0_ = bf16[256,512]{1,0:T(8,128)(2,1)S(1)} collective-permute-done((bf16[256,512]{1,0:T(8,128)(2,1)S(1)}, bf16[256,512]{1,0:T(8,128)(2,1)S(1)}, u32[]{:S(2)}, u32[]{:S(2)}) %collective-permute-start.2) | collective-permute-done | bytes 262176 | tf_op jit(solution)/shard_map/ppermute | solution.py:360
  72.0 4.6 %collective-permute-done.3.refs_1_ = bf16[256,512]{1,0:T(8,128)(2,1)S(1)} collective-permute-done((bf16[256,512]{1,0:T(8,128)(2,1)S(1)}, bf16[256,512]{1,0:T(8,128)(2,1)S(1)}, u32[]{:S(2)}, u32[]{:S(2)}) %collective-permute-start.3) | collective-permute-done | bytes 262176 | tf_op jit(solution)/shard_map/ppermute | solution.py:360
  76.7 1.1 %shard_map.89 = bf16[256,2048]{1,0:T(8,128)(2,1)} custom-call(bf16[256,512]{1,0:T(8,128)(2,1)S(1)} %collective-permute-done.2.refs_0_, bf16[256,512]{1,0:T(8,128)(2,1)S(1)} %collective-permute-done.3.refs_1_, bf16[256,512]{1,0:T(8,128)(2,1)S(1)} %collective-permute-done.4.refs_2_, bf16[256,512]{1,0:T(8,128)(2,1)S(1)} %shard_map.88.refs_3_), custom_call_target="tpu_custom_call" | custom-call | bytes 2097152 | tf_op jit(solution)/shard_map/pallas_call | solution.py:291
  (12 shorter events, 0.3 us)
Async XLA Ops:
  7.2 21.7 %all-to-all-start = ((bf16[16,64,256]{2,1,0:T(8,128)(2,1)}), bf16[16,64,256]{2,1,0:T(8,128)(2,1)S(1)}, u32[]{:S(2)}, u32[]{:S(2)}) async-start(bf16[16,64,256]{2,1,0:T(8,128)(2,1)} %bitcast.18), calls=%async_computation | async-start | bytes 1048576 | tf_op jit(solution)/shard_map/all_to_all | solution.py:321
  14.4 19.0 %copy-start = (s32[4096]{0:T(1024)S(1)}, s32[4096]{0:T(1024)}, u32[]{:S(2)}) copy-start(s32[4096]{0:T(1024)} %param.9) | copy-start | bytes 49156
  24.6 16.8 %copy-start.1 = (s32[32]{0:T(128)S(1)}, s32[32]{0:T(128)}, u32[]{:S(2)}) copy-start(s32[32]{0:T(128)} %param.10) | copy-start | bytes 388
  28.9 32.4 %all-to-all-start.1 = ((bf16[16,64,512]{2,1,0:T(8,128)(2,1)}), bf16[16,64,512]{2,1,0:T(8,128)(2,1)S(1)}, u32[]{:S(2)}, u32[]{:S(2)}) async-start(bf16[16,64,512]{2,1,0:T(8,128)(2,1)} %bitcast.17), calls=%async_computation.1 | async-start | bytes 2097152 | tf_op jit(solution)/shard_map/all_to_all | solution.py:321
  35.6 23.7 %collective-permute-start = (bf16[384,256]{1,0:T(8,128)(2,1)S(1)}, bf16[384,256]{1,0:T(8,128)(2,1)S(1)}, u32[]{:S(2)}, u32[]{:S(2)}) collective-permute-start(bf16[384,256]{1,0:T(8,128)(2,1)S(1)} %get-tuple-element.13.rest_2_), channel_id=1, source_target_pairs={{0,4},{1,5},{2,6},{3,7},{4,8},{5,9},{6,10},{7,11},{8,12},{9,13},{1... | collective-permute-start | bytes 589832 | tf_op jit(solution)/shard_map/ppermute | solution.py:346
  39.0 22.3 %collective-permute-start.1 = (bf16[384,256]{1,0:T(8,128)(2,1)S(1)}, bf16[384,256]{1,0:T(8,128)(2,1)S(1)}, u32[]{:S(2)}, u32[]{:S(2)}) collective-permute-start(bf16[384,256]{1,0:T(8,128)(2,1)S(1)} %get-tuple-element.15.rest_5_), channel_id=1, source_target_pairs={{4,0},{5,1},{6,2},{7,3},{8,4},{9,5},{10,6},{11,7},{12,8},{13,9},{1... | collective-permute-start | bytes 589832 | tf_op jit(solution)/shard_map/ppermute | solution.py:347
  62.7 9.3 %collective-permute-start.2 = (bf16[256,512]{1,0:T(8,128)(2,1)S(1)}, bf16[256,512]{1,0:T(8,128)(2,1)S(1)}, u32[]{:S(2)}, u32[]{:S(2)}) collective-permute-start(bf16[256,512]{1,0:T(8,128)(2,1)S(1)} %shard_map.85), channel_id=1, source_target_pairs={{0,3},{1,2},{2,1},{3,0},{4,7},{5,6},{6,5},{7,4},{8,11},{9,10},{10,... | collective-permute-start | bytes 786440 | tf_op jit(solution)/shard_map/ppermute | solution.py:360
  66.6 10.0 %collective-permute-start.3 = (bf16[256,512]{1,0:T(8,128)(2,1)S(1)}, bf16[256,512]{1,0:T(8,128)(2,1)S(1)}, u32[]{:S(2)}, u32[]{:S(2)}) collective-permute-start(bf16[256,512]{1,0:T(8,128)(2,1)S(1)} %shard_map.86), channel_id=1, source_target_pairs={{0,1},{1,0},{2,3},{3,2},{4,5},{5,4},{6,7},{7,6},{8,9},{9,8},{10,11... | collective-permute-start | bytes 786440 | tf_op jit(solution)/shard_map/ppermute | solution.py:360
  68.6 8.0 %collective-permute-start.4 = (bf16[256,512]{1,0:T(8,128)(2,1)S(1)}, bf16[256,512]{1,0:T(8,128)(2,1)S(1)}, u32[]{:S(2)}, u32[]{:S(2)}) collective-permute-start(bf16[256,512]{1,0:T(8,128)(2,1)S(1)} %shard_map.87), channel_id=1, source_target_pairs={{0,2},{1,3},{2,0},{3,1},{4,6},{5,7},{6,4},{7,5},{8,10},{9,11},{10,... | collective-permute-start | bytes 786440 | tf_op jit(solution)/shard_map/ppermute | solution.py:360

commit v8 on v7

--- a/solution.py
+++ b/solution.py
@@ -34,9 +34,10 @@
     return jnp.minimum(block_id, 2 * devices - 1 - block_id) // members
 
 
-def project_kernel(kinds, devices, members, positions_hbm, freq_hbm, gain_hbm, tokens_hbm, *rest):
+def project_kernel(kinds, devices, members, apart, positions_hbm, freq_hbm, gain_hbm, tokens_hbm, *rest):
     count = len(kinds)
-    weights_hbm, out_hbm = rest[:count], rest[count]
+    weights_hbm, rest = rest[:count], rest[count:]
+    outs_hbm, rest = rest[: 1 + apart], (None,) * (count + 1) + rest[1 + apart :]
     positions_ref, freq_ref, gain_ref, tokens, normed, weights, out_ref = rest[count + 1 : count + 8]
     small_sems, token_sems, sems, out_sems = rest[count + 8 :]
     rows, width = tokens.shape
@@ -122,15 +123,27 @@
             out_ref[:, head, :, inside : inside + HEAD_SIZE] = values.astype(jnp.bfloat16).reshape(
                 groups, rows // groups, HEAD_SIZE
             )
+        if apart:
+            continue
         done = (pl.ds(0, groups), pl.ds(first // per_head, max(span // per_head, 1)))
         done += (pl.ds(0, rows // groups), pl.ds(offsets[i] + first % per_head, min(span, per_head)))
-        written.append(pltpu.make_async_copy(out_ref.at[done], out_hbm.at[done], out_sems.at[j]))
+        written.append(pltpu.make_async_copy(out_ref.at[done], outs_hbm[0].at[done], out_sems.at[j]))
         written[j].start()
+    if apart:
+        me = lax.axis_index("ctx")
+        here = pl.ds(me // apart * (groups // 2), groups // 2)
+        written.append(pltpu.make_async_copy(out_ref.at[here], outs_hbm[0], out_sems.at[0]))
+        for i in range(apart):
+            to = me ^ (apart + i)
+            source = out_ref.at[to // members, to % members]
+            written.append(pltpu.make_async_copy(source, outs_hbm[1 + i], out_sems.at[1 + i]))
+        for copy in written:
+            copy.start()
     for copy in written:
         copy.wait()
 
 
-def project(positions, freq, gain, tokens, weights, kinds, devices, heads):
+def project(positions, freq, gain, tokens, weights, kinds, devices, heads, apart=0):
     rows, width = tokens.shape
     groups = devices // heads
     columns = sum(w.shape[1] for w in weights)
@@ -138,11 +151,13 @@
     parts = 4
     flops = 2 * rows * width * columns
     size = 2 * (width * columns + rows * width + rows * columns)
+    out_shape = (groups // 2 if apart else groups, heads, rows // groups, columns // heads)
+    out_shapes = [out_shape] + [out_shape[2:]] * apart
     return pl.pallas_call(
-        functools.partial(project_kernel, kinds, devices, heads),
-        out_shape=jax.ShapeDtypeStruct((groups, heads, rows // groups, columns // heads), jnp.bfloat16),
+        functools.partial(project_kernel, kinds, devices, heads, apart),
+        out_shape=[jax.ShapeDtypeStruct(shape, jnp.bfloat16) for shape in out_shapes],
         in_specs=[IN_PLACE] * (len(weights) + 4),
-        out_specs=IN_PLACE,
+        out_specs=[IN_PLACE] * (1 + apart),
         scratch_shapes=[
             pltpu.VMEM(positions.shape, jnp.int32),
             pltpu.VMEM(freq.shape, jnp.float32),
@@ -154,7 +169,7 @@
             pltpu.SemaphoreType.DMA((3,)),
             pltpu.SemaphoreType.DMA((parts,)),
             pltpu.SemaphoreType.DMA((columns // span,)),
-            pltpu.SemaphoreType.DMA((columns // span,)),
+            pltpu.SemaphoreType.DMA((max(1 + apart, columns // span),)),
         ],
         compiler_params=pltpu.CompilerParams(vmem_limit_bytes=56 * MIB),
         cost_estimate=pl.CostEstimate(flops=flops, bytes_accessed=size, transcendentals=0),
@@ -201,8 +216,13 @@
     return (turn, members - 1 - turn)
 
 
-def attend_kernel(block, turn, members, devices, query_ref, slot_ref, ends_ref, *rest):
-    pieces, out_ref, held = rest[:6], rest[6], rest[7]
+def attend_kernel(block, turn, members, devices, slot_ref, ends_ref, *rest):
+    queries_refs, rest = rest[:-9], rest[-9:]
+    pieces, out_ref, held, query_ref = rest[:6], rest[6], rest[7], rest[8]
+    first = 0
+    for ref in queries_refs:
+        query_ref[first : first + ref.shape[0], :] = ref[...]
+        first += ref.shape[0]
     target = taken_at(turn, members)
     group = lax.axis_index("ctx") // members
     starts = (group * members * block, (2 * devices - members - group * members) * block)
@@ -258,24 +278,27 @@
             out_ref[here[half], h * HEAD_SIZE : (h + 1) * HEAD_SIZE] = mixed[h * block : (h + 1) * block]
 
 
-def attend(turn, members, devices, query, slot, ends, pieces, block):
-    width = query.shape[1]
-    held = REACH_BLOCKS * block + query.shape[0] // 2
+def attend(turn, members, devices, queries, slot, ends, pieces, block):
+    rows, width = slot.shape[1], queries[0].shape[1]
+    held = REACH_BLOCKS * block + rows // 2
     heads = width // HEAD_SIZE
     reach = (REACH_BLOCKS + 1) * block
     return pl.pallas_call(
         functools.partial(attend_kernel, block, turn, members, devices),
         out_shape=jax.ShapeDtypeStruct((2 * block, width), jnp.bfloat16),
-        in_specs=[WHOLE] * 9,
+        in_specs=[WHOLE] * (8 + len(queries)),
         out_specs=WHOLE,
-        scratch_shapes=[pltpu.VMEM((2, held, 2 * HEAD_SIZE), jnp.bfloat16)],
+        scratch_shapes=[
+            pltpu.VMEM((2, held, 2 * HEAD_SIZE), jnp.bfloat16),
+            pltpu.VMEM((rows, width), jnp.bfloat16),
+        ],
         compiler_params=pltpu.CompilerParams(vmem_limit_bytes=16 * MIB),
         cost_estimate=pl.CostEstimate(
-            flops=2 * 2 * heads * block * reach * HEAD_SIZE * 2 + 4 * block * query.size,
-            bytes_accessed=2 * query.size + 8 * held * HEAD_SIZE,
+            flops=2 * 2 * heads * block * reach * HEAD_SIZE * 2 + 4 * block * rows * width,
+            bytes_accessed=2 * rows * width + 8 * held * HEAD_SIZE,
             transcendentals=2 * heads * block * reach,
         ),
-    )(query, slot, ends, *pieces)
+    )(slot, ends, *queries, *pieces)
 
 
 def assemble_kernel(*refs):
@@ -315,15 +338,22 @@
     freq = np.float32(ROPE_THETA ** (-(np.arange(HEAD_SIZE) % half * 2.0 / HEAD_SIZE)))
     operands = (positions.reshape(-1, 128), jnp.asarray(freq[None, :]), gain, tokens)
 
-    def exchange(ordered):
+    half_devices = devices // 2
+    halves = [list(range(i, i + half_devices)) for i in (0, half_devices)]
+
+    def exchange(ordered, among):
         width = ordered.shape[3]
-        flat = ordered.reshape(devices, group_rows, width)
-        flat = lax.all_to_all(flat, "ctx", split_axis=0, concat_axis=0, tiled=True)
-        return flat.reshape(devices * group_rows, width)
-
-    kv = project(*operands, (w_key, value_weight), (True, False), devices, members)
-    kv = exchange(kv)
-    query = project(*operands, (w_query,), (True,), devices, members)
+        flat = ordered.reshape(-1, group_rows, width)
+        flat = lax.all_to_all(flat, "ctx", split_axis=0, concat_axis=0, tiled=True, axis_index_groups=among)
+        return flat.reshape(-1, width)
+
+    (kv,) = project(*operands, (w_key, value_weight), (True, False), devices, members)
+    kv = exchange(kv, None)
+    near, *far = project(*operands, (w_query,), (True,), devices, members, half_devices)
+    queries = []
+    for i, piece in enumerate(far):
+        distance = half_devices + i
+        queries.append(lax.ppermute(piece, "ctx", [(j, j ^ distance) for j in range(devices)]))
 
     table = positions.reshape(devices, rows)
     ours = group_of(table, block, devices, members) == group
@@ -333,11 +363,15 @@
     place_in = jnp.cumsum(ours.astype(jnp.int32), axis=1) - 1
     place_in = jnp.where(ours, place_in, -1)
     wanted = jnp.arange(group_rows, dtype=jnp.int32)[None, :, None] == place_in[:, None, :]
-    slot = jnp.sum(jnp.where(wanted, slots[:, None, :], 0), axis=2).reshape(1, devices * group_rows)
+    slot = jnp.sum(jnp.where(wanted, slots[:, None, :], 0), axis=2)
+    index = jnp.arange(half_devices, dtype=jnp.int32)
+    sources = [device // half_devices * half_devices + index, device ^ (half_devices + index)]
+    query_slot = slot[jnp.concatenate(sources)].reshape(1, devices * group_rows)
+    slot = slot.reshape(1, devices * group_rows)
     ends = jnp.cumsum(lengths, dtype=jnp.int32)[None, :]
 
-    kv, query = lax.optimization_barrier((kv, query))
-    query = exchange(query)
+    kv, near = lax.optimization_barrier((kv, near))
+    queries.insert(0, exchange(near, halves))
     reach = REACH_BLOCKS * block
     sizes = [run - reach, reach] * 2
     early_head, early_tail, late_head, late_tail = place(kv, slot, sizes)
@@ -349,7 +383,7 @@
 
     results = []
     for turn in range(members):
-        out = attend(turn, members, devices, query, slot, ends, pieces, block)
+        out = attend(turn, members, devices, queries, query_slot, ends, pieces, block)
         if turn < members - 1:
             distances = distances_at(turn, members)
             route = [

time: 78.1 us -> 77.1 us (0.987)
  the two profiles are of different devices: /device:TPU:8 before, /device:TPU:0 now
where the time goes in v8:
time: 77.1 us; the launch traced here: 76.8 us
  starting transfers between devices  40.6 us (53%)
  Pallas kernels  25 us (32%)
  waiting for transfers between devices  8.71 us (11%)
  other arithmetic  1.39 us (2%)
  local copies, waits for them, and re-layouts  0.92 us (1%)
    ppermute x8, starting transfers between devices, shards(): lax.ppermute(piece, 'ctx', [(j, j ^ distance) for j in range(devices)])  19.7 us
    pallas_call x2, Pallas kernels, project(): pl.pallas_call(functools.partial(project_kernel, kinds, devices, heads, a...  17.7 us
    all_to_all x2, starting transfers between devices, exchange(): lax.all_to_all(flat, 'ctx', split_axis=0, concat_axis=0, tiled=True, axis...  12 us
    pallas_call x4, Pallas kernels, attend(): pl.pallas_call(functools.partial(attend_kernel, block, turn, members, dev...  5.58 us
    ppermute x8, waiting for transfers between devices, shards(): lax.ppermute(piece, 'ctx', [(j, j ^ distance) for j in range(devices)])  4.9 us
    ppermute x1, starting transfers between devices, shards(): early_halo = lax.ppermute(early_tail, 'ctx', up)  3.87 us
    ppermute x3, waiting for transfers between devices, shards(): out = lax.ppermute(out, ('dp', 'ctx'), route)  3.8 us
    ppermute x3, starting transfers between devices, shards(): out = lax.ppermute(out, ('dp', 'ctx'), route)  3.68 us
  transfers between devices with their start and end apart: 15, of which 5 were waited for; matrix products, arithmetic and copies ran while one was open for 3% of the time, Pallas kernels for 20%

profile of v8, /device:TPU:0, one launch (start us, length us, event | category | flops | bytes accessed | tf_op | source)
XLA Modules:
  0.0 76.8 jit_solution(13223990247373969513)
XLA Ops:
  0.0 7.2 %shard_map.82 = bf16[4,4,64,256]{3,2,1,0:T(8,128)(2,1)} custom-call(s32[32,128]{1,0:T(8,128)} %bitcast.25, f32[1,128]{1,0:T(1,128)} %constant.83.clone.freq_hbm, bf16[4096]{0:T(1024)(128)(2,1)} %gain_hbm.3, bf16[256,4096]{1,0:T(8,128)(2,1)} %tokens_hbm.3, bf16[4096,512]{1,0:T(8,128)(2,1)} %rest_0_.2, bf16[4096,512]{1,0:T(8,128)(2,1)} %rest_1_.1), custom_call_target="tpu_custom_call" | custom-call | flops 2147483648 | bytes 11010048 | tf_op jit(solution)/shard_map/pallas_call | solution.py:156
  7.2 8.3 %all-to-all-start = ((bf16[16,64,256]{2,1,0:T(8,128)(2,1)}), bf16[16,64,256]{2,1,0:T(8,128)(2,1)S(1)}, u32[]{:S(2)}, u32[]{:S(2)}) async-start(bf16[16,64,256]{2,1,0:T(8,128)(2,1)} %bitcast.23), calls=%async_computation | async-start | bytes 1048576 | tf_op jit(solution)/shard_map/all_to_all | solution.py:347
  15.6 10.4 %shard_map.83 = (bf16[2,4,64,512]{3,2,1,0:T(8,128)(2,1)}, bf16[64,512]{1,0:T(8,128)(2,1)}, bf16[64,512]{1,0:T(8,128)(2,1)}, bf16[64,512]{1,0:T(8,128)(2,1)}, bf1...) custom-call(s32[32,128]{1,0:T(8,128)} %bitcast.26, ...), custom_call_target="tpu_custom_call" | custom-call | flops 4294967296 | bytes 19922944 | tf_op jit(solution)/shard_map/pallas_call | solution.py:156
  26.0 2.9 %collective-permute-start = (bf16[64,512]{1,0:T(8,128)(2,1)}, bf16[64,512]{1,0:T(8,128)(2,1)S(1)}, u32[]{:S(2)}, u32[]{:S(2)}) collective-permute-start(bf16[64,512]{1,0:T(8,128)(2,1)} %get-tuple-element.22), channel_id=1, source_target_pairs={{0,8},{1,9},{2,10},{3,11},{4,12},{5,13},{6,14},{7,15},{8,0},{9,1},... | collective-permute-start | bytes 196616 | tf_op jit(solution)/shard_map/ppermute | solution.py:356
  28.9 1.5 %collective-permute-start.1 = (bf16[64,512]{1,0:T(8,128)(2,1)}, bf16[64,512]{1,0:T(8,128)(2,1)S(1)}, u32[]{:S(2)}, u32[]{:S(2)}) collective-permute-start(bf16[64,512]{1,0:T(8,128)(2,1)} %get-tuple-element.23), channel_id=1, source_target_pairs={{0,9},{1,8},{2,11},{3,10},{4,13},{5,12},{6,15},{7,14},{8,1},{9,0},... | collective-permute-start | bytes 196616 | tf_op jit(solution)/shard_map/ppermute | solution.py:356
  30.4 3.3 %collective-permute-start.2 = (bf16[64,512]{1,0:T(8,128)(2,1)}, bf16[64,512]{1,0:T(8,128)(2,1)S(1)}, u32[]{:S(2)}, u32[]{:S(2)}) collective-permute-start(bf16[64,512]{1,0:T(8,128)(2,1)} %get-tuple-element.24), channel_id=1, source_target_pairs={{0,10},{1,11},{2,8},{3,9},{4,14},{5,15},{6,12},{7,13},{8,2},{9,3},... | collective-permute-start | bytes 196616 | tf_op jit(solution)/shard_map/ppermute | solution.py:356
  33.7 3.7 %collective-permute-start.4 = (bf16[64,512]{1,0:T(8,128)(2,1)}, bf16[64,512]{1,0:T(8,128)(2,1)S(1)}, u32[]{:S(2)}, u32[]{:S(2)}) collective-permute-start(bf16[64,512]{1,0:T(8,128)(2,1)} %get-tuple-element.26), channel_id=1, source_target_pairs={{0,12},{1,13},{2,14},{3,15},{4,8},{5,9},{6,10},{7,11},{8,4},{9,5},... | collective-permute-start | bytes 196616 | tf_op jit(solution)/shard_map/ppermute | solution.py:356
  37.5 3.7 %all-to-all-start.1 = ((bf16[8,64,512]{2,1,0:T(8,128)(2,1)}), bf16[8,64,512]{2,1,0:T(8,128)(2,1)S(1)}, u32[]{:S(2)}, u32[]{:S(2)}) async-start(bf16[8,64,512]{2,1,0:T(8,128)(2,1)} %bitcast.24), calls=%async_computation.1 | async-start | bytes 1048576 | tf_op jit(solution)/shard_map/all_to_all | solution.py:347
  43.5 3.9 %collective-permute-start.8 = (bf16[384,256]{1,0:T(8,128)(2,1)S(1)}, bf16[384,256]{1,0:T(8,128)(2,1)S(1)}, u32[]{:S(2)}, u32[]{:S(2)}) collective-permute-start(bf16[384,256]{1,0:T(8,128)(2,1)S(1)} %get-tuple-element.31.rest_11_), channel_id=1, source_target_pairs={{0,4},{1,5},{2,6},{3,7},{4,8},{5,9},{6,10},{7,11},{8,12},{9,13},{1... | collective-permute-start | bytes 589832 | tf_op jit(solution)/shard_map/ppermute | solution.py:380
  47.4 1.3 %collective-permute-start.9 = (bf16[384,256]{1,0:T(8,128)(2,1)S(1)}, bf16[384,256]{1,0:T(8,128)(2,1)S(1)}, u32[]{:S(2)}, u32[]{:S(2)}) collective-permute-start(bf16[384,256]{1,0:T(8,128)(2,1)S(1)} %get-tuple-element.33.rest_14_), channel_id=1, source_target_pairs={{4,0},{5,1},{6,2},{7,3},{8,4},{9,5},{10,6},{11,7},{12,8},{13,9},{1... | collective-permute-start | bytes 589832 | tf_op jit(solution)/shard_map/ppermute | solution.py:381
  48.8 3.6 %collective-permute-start.5 = (bf16[64,512]{1,0:T(8,128)(2,1)}, bf16[64,512]{1,0:T(8,128)(2,1)S(1)}, u32[]{:S(2)}, u32[]{:S(2)}) collective-permute-start(bf16[64,512]{1,0:T(8,128)(2,1)} %get-tuple-element.27), channel_id=1, source_target_pairs={{0,13},{1,12},{2,15},{3,14},{4,9},{5,8},{6,11},{7,10},{8,5},{9,4},... | collective-permute-start | bytes 196616 | tf_op jit(solution)/shard_map/ppermute | solution.py:356
  52.4 2.1 %collective-permute-start.6 = (bf16[64,512]{1,0:T(8,128)(2,1)}, bf16[64,512]{1,0:T(8,128)(2,1)S(1)}, u32[]{:S(2)}, u32[]{:S(2)}) collective-permute-start(bf16[64,512]{1,0:T(8,128)(2,1)} %get-tuple-element.28), channel_id=1, source_target_pairs={{0,14},{1,15},{2,12},{3,13},{4,10},{5,11},{6,8},{7,9},{8,6},{9,7},... | collective-permute-start | bytes 196616 | tf_op jit(solution)/shard_map/ppermute | solution.py:356
  54.5 2.6 %collective-permute-start.7 = (bf16[64,512]{1,0:T(8,128)(2,1)}, bf16[64,512]{1,0:T(8,128)(2,1)S(1)}, u32[]{:S(2)}, u32[]{:S(2)}) collective-permute-start(bf16[64,512]{1,0:T(8,128)(2,1)} %get-tuple-element.29), channel_id=1, source_target_pairs={{0,15},{1,14},{2,13},{3,12},{4,11},{5,10},{6,9},{7,8},{8,7},{9,6},... | collective-permute-start | bytes 196616 | tf_op jit(solution)/shard_map/ppermute | solution.py:356
  58.1 1.5 %collective-permute-done.6.rest_7_ = bf16[64,512]{1,0:T(8,128)(2,1)S(1)} collective-permute-done((bf16[64,512]{1,0:T(8,128)(2,1)}, bf16[64,512]{1,0:T(8,128)(2,1)S(1)}, u32[]{:S(2)}, u32[]{:S(2)}) %collective-permute-start.6) | collective-permute-done | bytes 65568 | tf_op jit(solution)/shard_map/ppermute | solution.py:356
  59.6 3.0 %collective-permute-done.7.rest_8_ = bf16[64,512]{1,0:T(8,128)(2,1)S(1)} collective-permute-done((bf16[64,512]{1,0:T(8,128)(2,1)}, bf16[64,512]{1,0:T(8,128)(2,1)S(1)}, u32[]{:S(2)}, u32[]{:S(2)}) %collective-permute-start.7) | collective-permute-done | bytes 65568 | tf_op jit(solution)/shard_map/ppermute | solution.py:356
  62.6 1.4 %shard_map.85 = bf16[256,512]{1,0:T(8,128)(2,1)S(1)} custom-call(s32[1,1024]{1,0:T(1,128)S(1)} %reshape.203.slot_ref, s32[1,32]{1,0:T(1,128)S(1)} %reduce-window_2_clone.1.ends_ref, bf16[512,512]{1,0:T(8,128)(2,1)S(1)} %bitcast.18, bf16[64,512]{1,0:T(8,128)(2,1)S(1)} %collective-permute-done.rest_1_, bf16[64,512]{1,0:T(8,128)(2,1)S(1)} %collective-permute-done.1.rest_2_, ...), custom_call_target="tpu_custom_call" | custom-call | flops 536870912 | bytes 1966080 | tf_op jit(solution)/shard_map/pallas_call | solution.py:286
  64.6 1.4 %shard_map.86 = bf16[256,512]{1,0:T(8,128)(2,1)S(1)} custom-call(s32[1,1024]{1,0:T(1,128)S(1)} %reshape.203.slot_ref, s32[1,32]{1,0:T(1,128)S(1)} %reduce-window_2_clone.1.ends_ref, bf16[512,512]{1,0:T(8,128)(2,1)S(1)} %bitcast.19, bf16[64,512]{1,0:T(8,128)(2,1)S(1)} %collective-permute-done.rest_1_, bf16[64,512]{1,0:T(8,128)(2,1)S(1)} %collective-permute-done.1.rest_2_, ...), custom_call_target="tpu_custom_call" | custom-call | flops 536870912 | bytes 1966080 | tf_op jit(solution)/shard_map/pallas_call | solution.py:286
  66.0 1.6 %collective-permute-start.11 = (bf16[256,512]{1,0:T(8,128)(2,1)S(1)}, bf16[256,512]{1,0:T(8,128)(2,1)S(1)}, u32[]{:S(2)}, u32[]{:S(2)}) collective-permute-start(bf16[256,512]{1,0:T(8,128)(2,1)S(1)} %shard_map.86), channel_id=1, source_target_pairs={{0,1},{1,0},{2,3},{3,2},{4,5},{5,4},{6,7},{7,6},{8,9},{9,8},{10,11... | collective-permute-start | bytes 786440 | tf_op jit(solution)/shard_map/ppermute | solution.py:394
  67.6 1.4 %shard_map.87 = bf16[256,512]{1,0:T(8,128)(2,1)S(1)} custom-call(s32[1,1024]{1,0:T(1,128)S(1)} %reshape.203.slot_ref, s32[1,32]{1,0:T(1,128)S(1)} %reduce-window_2_clone.1.ends_ref, bf16[512,512]{1,0:T(8,128)(2,1)S(1)} %bitcast.20, bf16[64,512]{1,0:T(8,128)(2,1)S(1)} %collective-permute-done.rest_1_, bf16[64,512]{1,0:T(8,128)(2,1)S(1)} %collective-permute-done.1.rest_2_, ...), custom_call_target="tpu_custom_call" | custom-call | flops 536870912 | bytes 1966080 | tf_op jit(solution)/shard_map/pallas_call | solution.py:286
  69.0 1.5 %collective-permute-start.12 = (bf16[256,512]{1,0:T(8,128)(2,1)S(1)}, bf16[256,512]{1,0:T(8,128)(2,1)S(1)}, u32[]{:S(2)}, u32[]{:S(2)}) collective-permute-start(bf16[256,512]{1,0:T(8,128)(2,1)S(1)} %shard_map.87), channel_id=1, source_target_pairs={{0,2},{1,3},{2,0},{3,1},{4,6},{5,7},{6,4},{7,5},{8,10},{9,11},{10,... | collective-permute-start | bytes 786440 | tf_op jit(solution)/shard_map/ppermute | solution.py:394
  70.5 1.4 %shard_map.88.refs_3_ = bf16[256,512]{1,0:T(8,128)(2,1)S(1)} custom-call(s32[1,1024]{1,0:T(1,128)S(1)} %reshape.203.slot_ref, s32[1,32]{1,0:T(1,128)S(1)} %reduce-window_2_clone.1.ends_ref, bf16[512,512]{1,0:T(8,128)(2,1)S(1)} %bitcast.21, bf16[64,512]{1,0:T(8,128)(2,1)S(1)} %collective-permute-done.rest_1_, ...), custom_call_target="tpu_custom_call" | custom-call | flops 536870912 | bytes 1966080 | tf_op jit(solution)/shard_map/pallas_call | solution.py:286
  71.9 1.0 %collective-permute-done.10.refs_0_ = bf16[256,512]{1,0:T(8,128)(2,1)S(1)} collective-permute-done((bf16[256,512]{1,0:T(8,128)(2,1)S(1)}, bf16[256,512]{1,0:T(8,128)(2,1)S(1)}, u32[]{:S(2)}, u32[]{:S(2)}) %collective-permute-start.10) | collective-permute-done | bytes 262176 | tf_op jit(solution)/shard_map/ppermute | solution.py:394
  72.9 2.8 %collective-permute-done.11.refs_1_ = bf16[256,512]{1,0:T(8,128)(2,1)S(1)} collective-permute-done((bf16[256,512]{1,0:T(8,128)(2,1)S(1)}, bf16[256,512]{1,0:T(8,128)(2,1)S(1)}, u32[]{:S(2)}, u32[]{:S(2)}) %collective-permute-start.11) | collective-permute-done | bytes 262176 | tf_op jit(solution)/shard_map/ppermute | solution.py:394
  75.7 1.1 %shard_map.89 = bf16[256,2048]{1,0:T(8,128)(2,1)} custom-call(bf16[256,512]{1,0:T(8,128)(2,1)S(1)} %collective-permute-done.10.refs_0_, bf16[256,512]{1,0:T(8,128)(2,1)S(1)} %collective-permute-done.11.refs_1_, bf16[256,512]{1,0:T(8,128)(2,1)S(1)} %collective-permute-done.12.refs_2_, bf16[256,512]{1,0:T(8,128)(2,1)S(1)} %shard_map.88.refs_3_), custom_call_target="tpu_custom_call" | custom-call | bytes 2097152 | tf_op jit(solution)/shard_map/pallas_call | solution.py:314
  (33 shorter events, 4.0 us)
Async XLA Ops:
  7.2 30.3 %all-to-all-start = ((bf16[16,64,256]{2,1,0:T(8,128)(2,1)}), bf16[16,64,256]{2,1,0:T(8,128)(2,1)S(1)}, u32[]{:S(2)}, u32[]{:S(2)}) async-start(bf16[16,64,256]{2,1,0:T(8,128)(2,1)} %bitcast.23), calls=%async_computation | async-start | bytes 1048576 | tf_op jit(solution)/shard_map/all_to_all | solution.py:347
  15.5 25.6 %copy-start = (s32[4096]{0:T(1024)S(1)}, s32[4096]{0:T(1024)}, u32[]{:S(2)}) copy-start(s32[4096]{0:T(1024)} %param.9) | copy-start | bytes 49156
  15.6 26.9 %copy-start.1 = (s32[32]{0:T(128)S(1)}, s32[32]{0:T(128)}, u32[]{:S(2)}) copy-start(s32[32]{0:T(128)} %param.10) | copy-start | bytes 388
  26.0 17.5 %collective-permute-start = (bf16[64,512]{1,0:T(8,128)(2,1)}, bf16[64,512]{1,0:T(8,128)(2,1)S(1)}, u32[]{:S(2)}, u32[]{:S(2)}) collective-permute-start(bf16[64,512]{1,0:T(8,128)(2,1)} %get-tuple-element.22), channel_id=1, source_target_pairs={{0,8},{1,9},{2,10},{3,11},{4,12},{5,13},{6,14},{7,15},{8,0},{9,1},... | collective-permute-start | bytes 196616 | tf_op jit(solution)/shard_map/ppermute | solution.py:356
  28.9 18.5 %collective-permute-start.1 = (bf16[64,512]{1,0:T(8,128)(2,1)}, bf16[64,512]{1,0:T(8,128)(2,1)S(1)}, u32[]{:S(2)}, u32[]{:S(2)}) collective-permute-start(bf16[64,512]{1,0:T(8,128)(2,1)} %get-tuple-element.23), channel_id=1, source_target_pairs={{0,9},{1,8},{2,11},{3,10},{4,13},{5,12},{6,15},{7,14},{8,1},{9,0},... | collective-permute-start | bytes 196616 | tf_op jit(solution)/shard_map/ppermute | solution.py:356
  30.4 18.4 %collective-permute-start.2 = (bf16[64,512]{1,0:T(8,128)(2,1)}, bf16[64,512]{1,0:T(8,128)(2,1)S(1)}, u32[]{:S(2)}, u32[]{:S(2)}) collective-permute-start(bf16[64,512]{1,0:T(8,128)(2,1)} %get-tuple-element.24), channel_id=1, source_target_pairs={{0,10},{1,11},{2,8},{3,9},{4,14},{5,15},{6,12},{7,13},{8,2},{9,3},... | collective-permute-start | bytes 196616 | tf_op jit(solution)/shard_map/ppermute | solution.py:356
  33.6 18.7 %collective-permute-start.3 = (bf16[64,512]{1,0:T(8,128)(2,1)}, bf16[64,512]{1,0:T(8,128)(2,1)S(1)}, u32[]{:S(2)}, u32[]{:S(2)}) collective-permute-start(bf16[64,512]{1,0:T(8,128)(2,1)} %get-tuple-element.25), channel_id=1, source_target_pairs={{0,11},{1,10},{2,9},{3,8},{4,15},{5,14},{6,13},{7,12},{8,3},{9,2},... | collective-permute-start | bytes 196616 | tf_op jit(solution)/shard_map/ppermute | solution.py:356
  33.7 20.7 %collective-permute-start.4 = (bf16[64,512]{1,0:T(8,128)(2,1)}, bf16[64,512]{1,0:T(8,128)(2,1)S(1)}, u32[]{:S(2)}, u32[]{:S(2)}) collective-permute-start(bf16[64,512]{1,0:T(8,128)(2,1)} %get-tuple-element.26), channel_id=1, source_target_pairs={{0,12},{1,13},{2,14},{3,15},{4,8},{5,9},{6,10},{7,11},{8,4},{9,5},... | collective-permute-start | bytes 196616 | tf_op jit(solution)/shard_map/ppermute | solution.py:356
  37.5 25.2 %all-to-all-start.1 = ((bf16[8,64,512]{2,1,0:T(8,128)(2,1)}), bf16[8,64,512]{2,1,0:T(8,128)(2,1)S(1)}, u32[]{:S(2)}, u32[]{:S(2)}) async-start(bf16[8,64,512]{2,1,0:T(8,128)(2,1)} %bitcast.24), calls=%async_computation.1 | async-start | bytes 1048576 | tf_op jit(solution)/shard_map/all_to_all | solution.py:347
  43.5 19.1 %collective-permute-start.8 = (bf16[384,256]{1,0:T(8,128)(2,1)S(1)}, bf16[384,256]{1,0:T(8,128)(2,1)S(1)}, u32[]{:S(2)}, u32[]{:S(2)}) collective-permute-start(bf16[384,256]{1,0:T(8,128)(2,1)S(1)} %get-tuple-element.31.rest_11_), channel_id=1, source_target_pairs={{0,4},{1,5},{2,6},{3,7},{4,8},{5,9},{6,10},{7,11},{8,12},{9,13},{1... | collective-permute-start | bytes 589832 | tf_op jit(solution)/shard_map/ppermute | solution.py:380
  47.4 15.2 %collective-permute-start.9 = (bf16[384,256]{1,0:T(8,128)(2,1)S(1)}, bf16[384,256]{1,0:T(8,128)(2,1)S(1)}, u32[]{:S(2)}, u32[]{:S(2)}) collective-permute-start(bf16[384,256]{1,0:T(8,128)(2,1)S(1)} %get-tuple-element.33.rest_14_), channel_id=1, source_target_pairs={{4,0},{5,1},{6,2},{7,3},{8,4},{9,5},{10,6},{11,7},{12,8},{13,9},{1... | collective-permute-start | bytes 589832 | tf_op jit(solution)/shard_map/ppermute | solution.py:381
  48.8 9.3 %collective-permute-start.5 = (bf16[64,512]{1,0:T(8,128)(2,1)}, bf16[64,512]{1,0:T(8,128)(2,1)S(1)}, u32[]{:S(2)}, u32[]{:S(2)}) collective-permute-start(bf16[64,512]{1,0:T(8,128)(2,1)} %get-tuple-element.27), channel_id=1, source_target_pairs={{0,13},{1,12},{2,15},{3,14},{4,9},{5,8},{6,11},{7,10},{8,5},{9,4},... | collective-permute-start | bytes 196616 | tf_op jit(solution)/shard_map/ppermute | solution.py:356
  52.4 7.3 %collective-permute-start.6 = (bf16[64,512]{1,0:T(8,128)(2,1)}, bf16[64,512]{1,0:T(8,128)(2,1)S(1)}, u32[]{:S(2)}, u32[]{:S(2)}) collective-permute-start(bf16[64,512]{1,0:T(8,128)(2,1)} %get-tuple-element.28), channel_id=1, source_target_pairs={{0,14},{1,15},{2,12},{3,13},{4,10},{5,11},{6,8},{7,9},{8,6},{9,7},... | collective-permute-start | bytes 196616 | tf_op jit(solution)/shard_map/ppermute | solution.py:356
  54.5 8.2 %collective-permute-start.7 = (bf16[64,512]{1,0:T(8,128)(2,1)}, bf16[64,512]{1,0:T(8,128)(2,1)S(1)}, u32[]{:S(2)}, u32[]{:S(2)}) collective-permute-start(bf16[64,512]{1,0:T(8,128)(2,1)} %get-tuple-element.29), channel_id=1, source_target_pairs={{0,15},{1,14},{2,13},{3,12},{4,11},{5,10},{6,9},{7,8},{8,7},{9,6},... | collective-permute-start | bytes 196616 | tf_op jit(solution)/shard_map/ppermute | solution.py:356
  64.0 8.9 %collective-permute-start.10 = (bf16[256,512]{1,0:T(8,128)(2,1)S(1)}, bf16[256,512]{1,0:T(8,128)(2,1)S(1)}, u32[]{:S(2)}, u32[]{:S(2)}) collective-permute-start(bf16[256,512]{1,0:T(8,128)(2,1)S(1)} %shard_map.85), channel_id=1, source_target_pairs={{0,3},{1,2},{2,1},{3,0},{4,7},{5,6},{6,5},{7,4},{8,11},{9,10},{10,... | collective-permute-start | bytes 786440 | tf_op jit(solution)/shard_map/ppermute | solution.py:394
  66.0 9.8 %collective-permute-start.11 = (bf16[256,512]{1,0:T(8,128)(2,1)S(1)}, bf16[256,512]{1,0:T(8,128)(2,1)S(1)}, u32[]{:S(2)}, u32[]{:S(2)}) collective-permute-start(bf16[256,512]{1,0:T(8,128)(2,1)S(1)} %shard_map.86), channel_id=1, source_target_pairs={{0,1},{1,0},{2,3},{3,2},{4,5},{5,4},{6,7},{7,6},{8,9},{9,8},{10,11... | collective-permute-start | bytes 786440 | tf_op jit(solution)/shard_map/ppermute | solution.py:394
  69.0 6.7 %collective-permute-start.12 = (bf16[256,512]{1,0:T(8,128)(2,1)S(1)}, bf16[256,512]{1,0:T(8,128)(2,1)S(1)}, u32[]{:S(2)}, u32[]{:S(2)}) collective-permute-start(bf16[256,512]{1,0:T(8,128)(2,1)S(1)} %shard_map.87), channel_id=1, source_target_pairs={{0,2},{1,3},{2,0},{3,1},{4,6},{5,7},{6,4},{7,5},{8,10},{9,11},{10,... | collective-permute-start | bytes 786440 | tf_op jit(solution)/shard_map/ppermute | solution.py:394

commit v9 on v8

--- a/solution.py
+++ b/solution.py
@@ -37,7 +37,8 @@
 def project_kernel(kinds, devices, members, apart, positions_hbm, freq_hbm, gain_hbm, tokens_hbm, *rest):
     count = len(kinds)
     weights_hbm, rest = rest[:count], rest[count:]
-    outs_hbm, rest = rest[: 1 + apart], (None,) * (count + 1) + rest[1 + apart :]
+    outputs = 1 + len(apart)
+    outs_hbm, rest = rest[:outputs], (None,) * (count + 1) + rest[outputs:]
     positions_ref, freq_ref, gain_ref, tokens, normed, weights, out_ref = rest[count + 1 : count + 8]
     small_sems, token_sems, sems, out_sems = rest[count + 8 :]
     rows, width = tokens.shape
@@ -131,19 +132,23 @@
         written[j].start()
     if apart:
         me = lax.axis_index("ctx")
-        here = pl.ds(me // apart * (groups // 2), groups // 2)
-        written.append(pltpu.make_async_copy(out_ref.at[here], outs_hbm[0], out_sems.at[0]))
-        for i in range(apart):
-            to = me ^ (apart + i)
+        quarter = groups // 4
+        same = me // members // quarter % 2
+        for upper in range(2):
+            source = out_ref.at[pl.ds((2 * upper + same) * quarter, quarter)]
+            target = outs_hbm[0].at[pl.ds(upper * quarter, quarter)]
+            written.append(pltpu.make_async_copy(source, target, out_sems.at[upper]))
+        for i, distance in enumerate(apart):
+            to = me ^ distance
             source = out_ref.at[to // members, to % members]
-            written.append(pltpu.make_async_copy(source, outs_hbm[1 + i], out_sems.at[1 + i]))
+            written.append(pltpu.make_async_copy(source, outs_hbm[1 + i], out_sems.at[2 + i]))
         for copy in written:
             copy.start()
     for copy in written:
         copy.wait()
 
 
-def project(positions, freq, gain, tokens, weights, kinds, devices, heads, apart=0):
+def project(positions, freq, gain, tokens, weights, kinds, devices, heads, apart=()):
     rows, width = tokens.shape
     groups = devices // heads
     columns = sum(w.shape[1] for w in weights)
@@ -152,12 +157,12 @@
     flops = 2 * rows * width * columns
     size = 2 * (width * columns + rows * width + rows * columns)
     out_shape = (groups // 2 if apart else groups, heads, rows // groups, columns // heads)
-    out_shapes = [out_shape] + [out_shape[2:]] * apart
+    out_shapes = [out_shape] + [out_shape[2:]] * len(apart)
     return pl.pallas_call(
         functools.partial(project_kernel, kinds, devices, heads, apart),
         out_shape=[jax.ShapeDtypeStruct(shape, jnp.bfloat16) for shape in out_shapes],
         in_specs=[IN_PLACE] * (len(weights) + 4),
-        out_specs=[IN_PLACE] * (1 + apart),
+        out_specs=[IN_PLACE] * (1 + len(apart)),
         scratch_shapes=[
             pltpu.VMEM(positions.shape, jnp.int32),
             pltpu.VMEM(freq.shape, jnp.float32),
@@ -169,7 +174,7 @@
             pltpu.SemaphoreType.DMA((3,)),
             pltpu.SemaphoreType.DMA((parts,)),
             pltpu.SemaphoreType.DMA((columns // span,)),
-            pltpu.SemaphoreType.DMA((max(1 + apart, columns // span),)),
+            pltpu.SemaphoreType.DMA((max(2 + len(apart), columns // span),)),
         ],
         compiler_params=pltpu.CompilerParams(vmem_limit_bytes=56 * MIB),
         cost_estimate=pl.CostEstimate(flops=flops, bytes_accessed=size, transcendentals=0),
@@ -338,8 +343,9 @@
     freq = np.float32(ROPE_THETA ** (-(np.arange(HEAD_SIZE) % half * 2.0 / HEAD_SIZE)))
     operands = (positions.reshape(-1, 128), jnp.asarray(freq[None, :]), gain, tokens)
 
-    half_devices = devices // 2
-    halves = [list(range(i, i + half_devices)) for i in (0, half_devices)]
+    bit = devices // 4
+    alike = [[j for j in range(devices) if j // bit % 2 == value] for value in range(2)]
+    apart = list(range(3 * bit, 4 * bit)) + list(range(bit, 2 * bit))
 
     def exchange(ordered, among):
         width = ordered.shape[3]
@@ -349,10 +355,9 @@
 
     (kv,) = project(*operands, (w_key, value_weight), (True, False), devices, members)
     kv = exchange(kv, None)
-    near, *far = project(*operands, (w_query,), (True,), devices, members, half_devices)
+    near, *far = project(*operands, (w_query,), (True,), devices, members, apart)
     queries = []
-    for i, piece in enumerate(far):
-        distance = half_devices + i
+    for distance, piece in zip(apart, far):
         queries.append(lax.ppermute(piece, "ctx", [(j, j ^ distance) for j in range(devices)]))
 
     table = positions.reshape(devices, rows)
@@ -364,14 +369,14 @@
     place_in = jnp.where(ours, place_in, -1)
     wanted = jnp.arange(group_rows, dtype=jnp.int32)[None, :, None] == place_in[:, None, :]
     slot = jnp.sum(jnp.where(wanted, slots[:, None, :], 0), axis=2)
-    index = jnp.arange(half_devices, dtype=jnp.int32)
-    sources = [device // half_devices * half_devices + index, device ^ (half_devices + index)]
+    index = jnp.arange(2 * bit, dtype=jnp.int32)
+    sources = [index // bit * 2 * bit + device // bit % 2 * bit + index % bit, device ^ jnp.asarray(np.int32(apart))]
     query_slot = slot[jnp.concatenate(sources)].reshape(1, devices * group_rows)
     slot = slot.reshape(1, devices * group_rows)
     ends = jnp.cumsum(lengths, dtype=jnp.int32)[None, :]
 
     kv, near = lax.optimization_barrier((kv, near))
-    queries.insert(0, exchange(near, halves))
+    queries.insert(0, exchange(near, alike))
     reach = REACH_BLOCKS * block
     sizes = [run - reach, reach] * 2
     early_head, early_tail, late_head, late_tail = place(kv, slot, sizes)

time: 77.1 us -> 83.7 us (1.086)
  waiting for transfers between devices: 8.71 us -> 15.7 us
    ppermute x8, waiting for transfers between devices: 4.9 us -> 8.81 us  [shards(): lax.ppermute(piece, 'ctx', [(j, j ^ distance) for j in range(devices)])]
    all_to_all x2, starting transfers between devices: 12 us -> 15.7 us  [exchange(): lax.all_to_all(flat, 'ctx', split_axis=0, concat_axis=0, tiled=True, axis...]
    ppermute x3, waiting for transfers between devices: 3.8 us -> 6.92 us  [shards(): out = lax.ppermute(out, ('dp', 'ctx'), route)]
    ppermute x8, starting transfers between devices: 19.7 us -> 17.5 us  [shards(): lax.ppermute(piece, 'ctx', [(j, j ^ distance) for j in range(devices)])]
    ppermute x1, starting transfers between devices: 3.87 us -> 1.91 us  [shards(): early_halo = lax.ppermute(early_tail, 'ctx', up)]
  transfers between devices with their start and end apart: 15 -> 15, of which waited for: 5 -> 6; matrix products, arithmetic and copies ran while one was open for 3% -> 3% of each run, Pallas kernels for 20% -> 18%
where the time goes in v9:
time: 83.7 us; the launch traced here: 83.3 us
  starting transfers between devices  40 us (48%)
  Pallas kernels  25 us (30%)
  waiting for transfers between devices  15.7 us (19%)
  other arithmetic  1.38 us (2%)
  local copies, waits for them, and re-layouts  0.93 us (1%)
    pallas_call x2, Pallas kernels, project(): pl.pallas_call(functools.partial(project_kernel, kinds, devices, heads, a...  17.7 us
    ppermute x8, starting transfers between devices, shards(): lax.ppermute(piece, 'ctx', [(j, j ^ distance) for j in range(devices)])  17.5 us
    all_to_all x2, starting transfers between devices, exchange(): lax.all_to_all(flat, 'ctx', split_axis=0, concat_axis=0, tiled=True, axis...  15.7 us
    ppermute x8, waiting for transfers between devices, shards(): lax.ppermute(piece, 'ctx', [(j, j ^ distance) for j in range(devices)])  8.81 us
    ppermute x3, waiting for transfers between devices, shards(): out = lax.ppermute(out, ('dp', 'ctx'), route)  6.92 us
    pallas_call x4, Pallas kernels, attend(): pl.pallas_call(functools.partial(attend_kernel, block, turn, members, dev...  5.58 us
    ppermute x3, starting transfers between devices, shards(): out = lax.ppermute(out, ('dp', 'ctx'), route)  3.69 us
    ppermute x1, starting transfers between devices, shards(): early_halo = lax.ppermute(early_tail, 'ctx', up)  1.91 us
  transfers between devices with their start and end apart: 15, of which 6 were waited for; matrix products, arithmetic and copies ran while one was open for 3% of the time, Pallas kernels for 18%

profile of v9, /device:TPU:0, one launch (start us, length us, event | category | flops | bytes accessed | tf_op | source)
XLA Modules:
  0.0 83.3 jit_solution(12512908517869760557)
XLA Ops:
  0.0 7.2 %shard_map.91 = bf16[4,4,64,256]{3,2,1,0:T(8,128)(2,1)} custom-call(s32[32,128]{1,0:T(8,128)} %bitcast.25, f32[1,128]{1,0:T(1,128)} %constant.114.clone.freq_hbm, bf16[4096]{0:T(1024)(128)(2,1)} %gain_hbm.3, bf16[256,4096]{1,0:T(8,128)(2,1)} %tokens_hbm.3, bf16[4096,512]{1,0:T(8,128)(2,1)} %rest_0_.2, bf16[4096,512]{1,0:T(8,128)(2,1)} %rest_1_.1), custom_call_target="tpu_custom_call" | custom-call | flops 2147483648 | bytes 11010048 | tf_op jit(solution)/shard_map/pallas_call | solution.py:161
  7.2 8.3 %all-to-all-start = ((bf16[16,64,256]{2,1,0:T(8,128)(2,1)}), bf16[16,64,256]{2,1,0:T(8,128)(2,1)S(1)}, u32[]{:S(2)}, u32[]{:S(2)}) async-start(bf16[16,64,256]{2,1,0:T(8,128)(2,1)} %bitcast.23), calls=%async_computation | async-start | bytes 1048576 | tf_op jit(solution)/shard_map/all_to_all | solution.py:353
  15.6 10.4 %shard_map.92 = (bf16[2,4,64,512]{3,2,1,0:T(8,128)(2,1)}, bf16[64,512]{1,0:T(8,128)(2,1)}, bf16[64,512]{1,0:T(8,128)(2,1)}, bf16[64,512]{1,0:T(8,128)(2,1)}, bf1...) custom-call(s32[32,128]{1,0:T(8,128)} %bitcast.26, ...), custom_call_target="tpu_custom_call" | custom-call | flops 4294967296 | bytes 19922944 | tf_op jit(solution)/shard_map/pallas_call | solution.py:161
  26.1 3.8 %collective-permute-start = (bf16[64,512]{1,0:T(8,128)(2,1)}, bf16[64,512]{1,0:T(8,128)(2,1)S(1)}, u32[]{:S(2)}, u32[]{:S(2)}) collective-permute-start(bf16[64,512]{1,0:T(8,128)(2,1)} %get-tuple-element.22), channel_id=1, source_target_pairs={{0,12},{1,13},{2,14},{3,15},{4,8},{5,9},{6,10},{7,11},{8,4},{9,5},... | collective-permute-start | bytes 196616 | tf_op jit(solution)/shard_map/ppermute | solution.py:361
  29.9 1.5 %collective-permute-start.1 = (bf16[64,512]{1,0:T(8,128)(2,1)}, bf16[64,512]{1,0:T(8,128)(2,1)S(1)}, u32[]{:S(2)}, u32[]{:S(2)}) collective-permute-start(bf16[64,512]{1,0:T(8,128)(2,1)} %get-tuple-element.23), channel_id=1, source_target_pairs={{0,13},{1,12},{2,15},{3,14},{4,9},{5,8},{6,11},{7,10},{8,5},{9,4},... | collective-permute-start | bytes 196616 | tf_op jit(solution)/shard_map/ppermute | solution.py:361
  31.3 4.2 %collective-permute-start.2 = (bf16[64,512]{1,0:T(8,128)(2,1)}, bf16[64,512]{1,0:T(8,128)(2,1)S(1)}, u32[]{:S(2)}, u32[]{:S(2)}) collective-permute-start(bf16[64,512]{1,0:T(8,128)(2,1)} %get-tuple-element.24), channel_id=1, source_target_pairs={{0,14},{1,15},{2,12},{3,13},{4,10},{5,11},{6,8},{7,9},{8,6},{9,7},... | collective-permute-start | bytes 196616 | tf_op jit(solution)/shard_map/ppermute | solution.py:361
  36.2 7.4 %all-to-all-start.1 = ((bf16[8,64,512]{2,1,0:T(8,128)(2,1)}), bf16[8,64,512]{2,1,0:T(8,128)(2,1)S(1)}, u32[]{:S(2)}, u32[]{:S(2)}) async-start(bf16[8,64,512]{2,1,0:T(8,128)(2,1)} %bitcast.24), calls=%async_computation.1 | async-start | bytes 1048576 | tf_op jit(solution)/shard_map/all_to_all | solution.py:353
  45.3 1.9 %collective-permute-start.8 = (bf16[384,256]{1,0:T(8,128)(2,1)S(1)}, bf16[384,256]{1,0:T(8,128)(2,1)S(1)}, u32[]{:S(2)}, u32[]{:S(2)}) collective-permute-start(bf16[384,256]{1,0:T(8,128)(2,1)S(1)} %get-tuple-element.31.rest_11_), channel_id=1, source_target_pairs={{0,4},{1,5},{2,6},{3,7},{4,8},{5,9},{6,10},{7,11},{8,12},{9,13},{1... | collective-permute-start | bytes 589832 | tf_op jit(solution)/shard_map/ppermute | solution.py:385
  47.3 1.3 %collective-permute-start.9 = (bf16[384,256]{1,0:T(8,128)(2,1)S(1)}, bf16[384,256]{1,0:T(8,128)(2,1)S(1)}, u32[]{:S(2)}, u32[]{:S(2)}) collective-permute-start(bf16[384,256]{1,0:T(8,128)(2,1)S(1)} %get-tuple-element.33.rest_14_), channel_id=1, source_target_pairs={{4,0},{5,1},{6,2},{7,3},{8,4},{9,5},{10,6},{11,7},{12,8},{13,9},{1... | collective-permute-start | bytes 589832 | tf_op jit(solution)/shard_map/ppermute | solution.py:386
  48.6 5.0 %collective-permute-start.5 = (bf16[64,512]{1,0:T(8,128)(2,1)}, bf16[64,512]{1,0:T(8,128)(2,1)S(1)}, u32[]{:S(2)}, u32[]{:S(2)}) collective-permute-start(bf16[64,512]{1,0:T(8,128)(2,1)} %get-tuple-element.27), channel_id=1, source_target_pairs={{0,5},{1,4},{2,7},{3,6},{4,1},{5,0},{6,3},{7,2},{8,13},{9,12},{10,... | collective-permute-start | bytes 196616 | tf_op jit(solution)/shard_map/ppermute | solution.py:361
  53.8 2.8 %collective-permute-start.7 = (bf16[64,512]{1,0:T(8,128)(2,1)}, bf16[64,512]{1,0:T(8,128)(2,1)S(1)}, u32[]{:S(2)}, u32[]{:S(2)}) collective-permute-start(bf16[64,512]{1,0:T(8,128)(2,1)} %get-tuple-element.29), channel_id=1, source_target_pairs={{0,7},{1,6},{2,5},{3,4},{4,3},{5,2},{6,1},{7,0},{8,15},{9,14},{10,... | collective-permute-start | bytes 196616 | tf_op jit(solution)/shard_map/ppermute | solution.py:361
  57.2 5.2 %collective-permute-done.5.rest_6_ = bf16[64,512]{1,0:T(8,128)(2,1)S(1)} collective-permute-done((bf16[64,512]{1,0:T(8,128)(2,1)}, bf16[64,512]{1,0:T(8,128)(2,1)S(1)}, u32[]{:S(2)}, u32[]{:S(2)}) %collective-permute-start.5) | collective-permute-done | bytes 65568 | tf_op jit(solution)/shard_map/ppermute | solution.py:361
  62.4 1.4 %collective-permute-done.6.rest_7_ = bf16[64,512]{1,0:T(8,128)(2,1)S(1)} collective-permute-done((bf16[64,512]{1,0:T(8,128)(2,1)}, bf16[64,512]{1,0:T(8,128)(2,1)S(1)}, u32[]{:S(2)}, u32[]{:S(2)}) %collective-permute-start.6) | collective-permute-done | bytes 65568 | tf_op jit(solution)/shard_map/ppermute | solution.py:361
  63.8 2.2 %collective-permute-done.7.rest_8_ = bf16[64,512]{1,0:T(8,128)(2,1)S(1)} collective-permute-done((bf16[64,512]{1,0:T(8,128)(2,1)}, bf16[64,512]{1,0:T(8,128)(2,1)S(1)}, u32[]{:S(2)}, u32[]{:S(2)}) %collective-permute-start.7) | collective-permute-done | bytes 65568 | tf_op jit(solution)/shard_map/ppermute | solution.py:361
  66.0 1.4 %shard_map.94 = bf16[256,512]{1,0:T(8,128)(2,1)S(1)} custom-call(s32[1,1024]{1,0:T(1,128)S(1)} %reshape.218.slot_ref, s32[1,32]{1,0:T(1,128)S(1)} %reduce-window_2_clone.1.ends_ref, bf16[512,512]{1,0:T(8,128)(2,1)S(1)} %bitcast.18, bf16[64,512]{1,0:T(8,128)(2,1)S(1)} %collective-permute-done.rest_1_, bf16[64,512]{1,0:T(8,128)(2,1)S(1)} %collective-permute-done.1.rest_2_, ...), custom_call_target="tpu_custom_call" | custom-call | flops 536870912 | bytes 1966080 | tf_op jit(solution)/shard_map/pallas_call | solution.py:291
  68.1 1.4 %shard_map.95 = bf16[256,512]{1,0:T(8,128)(2,1)S(1)} custom-call(s32[1,1024]{1,0:T(1,128)S(1)} %reshape.218.slot_ref, s32[1,32]{1,0:T(1,128)S(1)} %reduce-window_2_clone.1.ends_ref, bf16[512,512]{1,0:T(8,128)(2,1)S(1)} %bitcast.19, bf16[64,512]{1,0:T(8,128)(2,1)S(1)} %collective-permute-done.rest_1_, bf16[64,512]{1,0:T(8,128)(2,1)S(1)} %collective-permute-done.1.rest_2_, ...), custom_call_target="tpu_custom_call" | custom-call | flops 536870912 | bytes 1966080 | tf_op jit(solution)/shard_map/pallas_call | solution.py:291
  69.5 1.5 %collective-permute-start.11 = (bf16[256,512]{1,0:T(8,128)(2,1)S(1)}, bf16[256,512]{1,0:T(8,128)(2,1)S(1)}, u32[]{:S(2)}, u32[]{:S(2)}) collective-permute-start(bf16[256,512]{1,0:T(8,128)(2,1)S(1)} %shard_map.95), channel_id=1, source_target_pairs={{0,1},{1,0},{2,3},{3,2},{4,5},{5,4},{6,7},{7,6},{8,9},{9,8},{10,11... | collective-permute-start | bytes 786440 | tf_op jit(solution)/shard_map/ppermute | solution.py:399
  71.0 1.4 %shard_map.96 = bf16[256,512]{1,0:T(8,128)(2,1)S(1)} custom-call(s32[1,1024]{1,0:T(1,128)S(1)} %reshape.218.slot_ref, s32[1,32]{1,0:T(1,128)S(1)} %reduce-window_2_clone.1.ends_ref, bf16[512,512]{1,0:T(8,128)(2,1)S(1)} %bitcast.20, bf16[64,512]{1,0:T(8,128)(2,1)S(1)} %collective-permute-done.rest_1_, bf16[64,512]{1,0:T(8,128)(2,1)S(1)} %collective-permute-done.1.rest_2_, ...), custom_call_target="tpu_custom_call" | custom-call | flops 536870912 | bytes 1966080 | tf_op jit(solution)/shard_map/pallas_call | solution.py:291
  72.4 1.5 %collective-permute-start.12 = (bf16[256,512]{1,0:T(8,128)(2,1)S(1)}, bf16[256,512]{1,0:T(8,128)(2,1)S(1)}, u32[]{:S(2)}, u32[]{:S(2)}) collective-permute-start(bf16[256,512]{1,0:T(8,128)(2,1)S(1)} %shard_map.96), channel_id=1, source_target_pairs={{0,2},{1,3},{2,0},{3,1},{4,6},{5,7},{6,4},{7,5},{8,10},{9,11},{10,... | collective-permute-start | bytes 786440 | tf_op jit(solution)/shard_map/ppermute | solution.py:399
  73.9 1.4 %shard_map.97.refs_3_ = bf16[256,512]{1,0:T(8,128)(2,1)S(1)} custom-call(s32[1,1024]{1,0:T(1,128)S(1)} %reshape.218.slot_ref, s32[1,32]{1,0:T(1,128)S(1)} %reduce-window_2_clone.1.ends_ref, bf16[512,512]{1,0:T(8,128)(2,1)S(1)} %bitcast.21, bf16[64,512]{1,0:T(8,128)(2,1)S(1)} %collective-permute-done.rest_1_, ...), custom_call_target="tpu_custom_call" | custom-call | flops 536870912 | bytes 1966080 | tf_op jit(solution)/shard_map/pallas_call | solution.py:291
  75.3 2.3 %collective-permute-done.10.refs_0_ = bf16[256,512]{1,0:T(8,128)(2,1)S(1)} collective-permute-done((bf16[256,512]{1,0:T(8,128)(2,1)S(1)}, bf16[256,512]{1,0:T(8,128)(2,1)S(1)}, u32[]{:S(2)}, u32[]{:S(2)}) %collective-permute-start.10) | collective-permute-done | bytes 262176 | tf_op jit(solution)/shard_map/ppermute | solution.py:399
  77.6 3.8 %collective-permute-done.11.refs_1_ = bf16[256,512]{1,0:T(8,128)(2,1)S(1)} collective-permute-done((bf16[256,512]{1,0:T(8,128)(2,1)S(1)}, bf16[256,512]{1,0:T(8,128)(2,1)S(1)}, u32[]{:S(2)}, u32[]{:S(2)}) %collective-permute-start.11) | collective-permute-done | bytes 262176 | tf_op jit(solution)/shard_map/ppermute | solution.py:399
  81.4 0.9 %collective-permute-done.12.refs_2_ = bf16[256,512]{1,0:T(8,128)(2,1)S(1)} collective-permute-done((bf16[256,512]{1,0:T(8,128)(2,1)S(1)}, bf16[256,512]{1,0:T(8,128)(2,1)S(1)}, u32[]{:S(2)}, u32[]{:S(2)}) %collective-permute-start.12) | collective-permute-done | bytes 262176 | tf_op jit(solution)/shard_map/ppermute | solution.py:399
  82.3 1.1 %shard_map.98 = bf16[256,2048]{1,0:T(8,128)(2,1)} custom-call(bf16[256,512]{1,0:T(8,128)(2,1)S(1)} %collective-permute-done.10.refs_0_, bf16[256,512]{1,0:T(8,128)(2,1)S(1)} %collective-permute-done.11.refs_1_, bf16[256,512]{1,0:T(8,128)(2,1)S(1)} %collective-permute-done.12.refs_2_, bf16[256,512]{1,0:T(8,128)(2,1)S(1)} %shard_map.97.refs_3_), custom_call_target="tpu_custom_call" | custom-call | bytes 2097152 | tf_op jit(solution)/shard_map/pallas_call | solution.py:319
  (35 shorter events, 3.8 us)
Async XLA Ops:
  7.2 29.0 %all-to-all-start = ((bf16[16,64,256]{2,1,0:T(8,128)(2,1)}), bf16[16,64,256]{2,1,0:T(8,128)(2,1)S(1)}, u32[]{:S(2)}, u32[]{:S(2)}) async-start(bf16[16,64,256]{2,1,0:T(8,128)(2,1)} %bitcast.23), calls=%async_computation | async-start | bytes 1048576 | tf_op jit(solution)/shard_map/all_to_all | solution.py:353
  15.6 20.0 %copy-start = (s32[4096]{0:T(1024)S(1)}, s32[4096]{0:T(1024)}, u32[]{:S(2)}) copy-start(s32[4096]{0:T(1024)} %param.10) | copy-start | bytes 49156
  15.6 28.3 %copy-start.1 = (s32[8]{0:T(128)S(1)}, s32[8]{0:T(128)}, u32[]{:S(2)}) copy-start(s32[8]{0:T(128)} %constant.115.clone) | copy-start | bytes 100
  15.6 28.7 %copy-start.2 = (s32[32]{0:T(128)S(1)}, s32[32]{0:T(128)}, u32[]{:S(2)}) copy-start(s32[32]{0:T(128)} %param.11) | copy-start | bytes 388
  26.1 19.3 %collective-permute-start = (bf16[64,512]{1,0:T(8,128)(2,1)}, bf16[64,512]{1,0:T(8,128)(2,1)S(1)}, u32[]{:S(2)}, u32[]{:S(2)}) collective-permute-start(bf16[64,512]{1,0:T(8,128)(2,1)} %get-tuple-element.22), channel_id=1, source_target_pairs={{0,12},{1,13},{2,14},{3,15},{4,8},{5,9},{6,10},{7,11},{8,4},{9,5},... | collective-permute-start | bytes 196616 | tf_op jit(solution)/shard_map/ppermute | solution.py:361
  29.9 17.4 %collective-permute-start.1 = (bf16[64,512]{1,0:T(8,128)(2,1)}, bf16[64,512]{1,0:T(8,128)(2,1)S(1)}, u32[]{:S(2)}, u32[]{:S(2)}) collective-permute-start(bf16[64,512]{1,0:T(8,128)(2,1)} %get-tuple-element.23), channel_id=1, source_target_pairs={{0,13},{1,12},{2,15},{3,14},{4,9},{5,8},{6,11},{7,10},{8,5},{9,4},... | collective-permute-start | bytes 196616 | tf_op jit(solution)/shard_map/ppermute | solution.py:361
  31.3 17.3 %collective-permute-start.2 = (bf16[64,512]{1,0:T(8,128)(2,1)}, bf16[64,512]{1,0:T(8,128)(2,1)S(1)}, u32[]{:S(2)}, u32[]{:S(2)}) collective-permute-start(bf16[64,512]{1,0:T(8,128)(2,1)} %get-tuple-element.24), channel_id=1, source_target_pairs={{0,14},{1,15},{2,12},{3,13},{4,10},{5,11},{6,8},{7,9},{8,6},{9,7},... | collective-permute-start | bytes 196616 | tf_op jit(solution)/shard_map/ppermute | solution.py:361
  35.5 18.2 %collective-permute-start.3 = (bf16[64,512]{1,0:T(8,128)(2,1)}, bf16[64,512]{1,0:T(8,128)(2,1)S(1)}, u32[]{:S(2)}, u32[]{:S(2)}) collective-permute-start(bf16[64,512]{1,0:T(8,128)(2,1)} %get-tuple-element.25), channel_id=1, source_target_pairs={{0,15},{1,14},{2,13},{3,12},{4,11},{5,10},{6,9},{7,8},{8,7},{9,6},... | collective-permute-start | bytes 196616 | tf_op jit(solution)/shard_map/ppermute | solution.py:361
  35.6 18.2 %collective-permute-start.4 = (bf16[64,512]{1,0:T(8,128)(2,1)}, bf16[64,512]{1,0:T(8,128)(2,1)S(1)}, u32[]{:S(2)}, u32[]{:S(2)}) collective-permute-start(bf16[64,512]{1,0:T(8,128)(2,1)} %get-tuple-element.26), channel_id=1, source_target_pairs={{0,4},{1,5},{2,6},{3,7},{4,0},{5,1},{6,2},{7,3},{8,12},{9,13},{10,... | collective-permute-start | bytes 196616 | tf_op jit(solution)/shard_map/ppermute | solution.py:361
  36.2 29.8 %all-to-all-start.1 = ((bf16[8,64,512]{2,1,0:T(8,128)(2,1)}), bf16[8,64,512]{2,1,0:T(8,128)(2,1)S(1)}, u32[]{:S(2)}, u32[]{:S(2)}) async-start(bf16[8,64,512]{2,1,0:T(8,128)(2,1)} %bitcast.24), calls=%async_computation.1 | async-start | bytes 1048576 | tf_op jit(solution)/shard_map/all_to_all | solution.py:353
  45.3 20.7 %collective-permute-start.8 = (bf16[384,256]{1,0:T(8,128)(2,1)S(1)}, bf16[384,256]{1,0:T(8,128)(2,1)S(1)}, u32[]{:S(2)}, u32[]{:S(2)}) collective-permute-start(bf16[384,256]{1,0:T(8,128)(2,1)S(1)} %get-tuple-element.31.rest_11_), channel_id=1, source_target_pairs={{0,4},{1,5},{2,6},{3,7},{4,8},{5,9},{6,10},{7,11},{8,12},{9,13},{1... | collective-permute-start | bytes 589832 | tf_op jit(solution)/shard_map/ppermute | solution.py:385
  47.3 18.8 %collective-permute-start.9 = (bf16[384,256]{1,0:T(8,128)(2,1)S(1)}, bf16[384,256]{1,0:T(8,128)(2,1)S(1)}, u32[]{:S(2)}, u32[]{:S(2)}) collective-permute-start(bf16[384,256]{1,0:T(8,128)(2,1)S(1)} %get-tuple-element.33.rest_14_), channel_id=1, source_target_pairs={{4,0},{5,1},{6,2},{7,3},{8,4},{9,5},{10,6},{11,7},{12,8},{13,9},{1... | collective-permute-start | bytes 589832 | tf_op jit(solution)/shard_map/ppermute | solution.py:386
  48.6 13.8 %collective-permute-start.5 = (bf16[64,512]{1,0:T(8,128)(2,1)}, bf16[64,512]{1,0:T(8,128)(2,1)S(1)}, u32[]{:S(2)}, u32[]{:S(2)}) collective-permute-start(bf16[64,512]{1,0:T(8,128)(2,1)} %get-tuple-element.27), channel_id=1, source_target_pairs={{0,5},{1,4},{2,7},{3,6},{4,1},{5,0},{6,3},{7,2},{8,13},{9,12},{10,... | collective-permute-start | bytes 196616 | tf_op jit(solution)/shard_map/ppermute | solution.py:361
  53.7 10.2 %collective-permute-start.6 = (bf16[64,512]{1,0:T(8,128)(2,1)}, bf16[64,512]{1,0:T(8,128)(2,1)S(1)}, u32[]{:S(2)}, u32[]{:S(2)}) collective-permute-start(bf16[64,512]{1,0:T(8,128)(2,1)} %get-tuple-element.28), channel_id=1, source_target_pairs={{0,6},{1,7},{2,4},{3,5},{4,2},{5,3},{6,0},{7,1},{8,14},{9,15},{10,... | collective-permute-start | bytes 196616 | tf_op jit(solution)/shard_map/ppermute | solution.py:361
  53.8 12.3 %collective-permute-start.7 = (bf16[64,512]{1,0:T(8,128)(2,1)}, bf16[64,512]{1,0:T(8,128)(2,1)S(1)}, u32[]{:S(2)}, u32[]{:S(2)}) collective-permute-start(bf16[64,512]{1,0:T(8,128)(2,1)} %get-tuple-element.29), channel_id=1, source_target_pairs={{0,7},{1,6},{2,5},{3,4},{4,3},{5,2},{6,1},{7,0},{8,15},{9,14},{10,... | collective-permute-start | bytes 196616 | tf_op jit(solution)/shard_map/ppermute | solution.py:361
  67.5 10.2 %collective-permute-start.10 = (bf16[256,512]{1,0:T(8,128)(2,1)S(1)}, bf16[256,512]{1,0:T(8,128)(2,1)S(1)}, u32[]{:S(2)}, u32[]{:S(2)}) collective-permute-start(bf16[256,512]{1,0:T(8,128)(2,1)S(1)} %shard_map.94), channel_id=1, source_target_pairs={{0,3},{1,2},{2,1},{3,0},{4,7},{5,6},{6,5},{7,4},{8,11},{9,10},{10,... | collective-permute-start | bytes 786440 | tf_op jit(solution)/shard_map/ppermute | solution.py:399
  69.5 11.9 %collective-permute-start.11 = (bf16[256,512]{1,0:T(8,128)(2,1)S(1)}, bf16[256,512]{1,0:T(8,128)(2,1)S(1)}, u32[]{:S(2)}, u32[]{:S(2)}) collective-permute-start(bf16[256,512]{1,0:T(8,128)(2,1)S(1)} %shard_map.95), channel_id=1, source_target_pairs={{0,1},{1,0},{2,3},{3,2},{4,5},{5,4},{6,7},{7,6},{8,9},{9,8},{10,11... | collective-permute-start | bytes 786440 | tf_op jit(solution)/shard_map/ppermute | solution.py:399
  72.4 9.9 %collective-permute-start.12 = (bf16[256,512]{1,0:T(8,128)(2,1)S(1)}, bf16[256,512]{1,0:T(8,128)(2,1)S(1)}, u32[]{:S(2)}, u32[]{:S(2)}) collective-permute-start(bf16[256,512]{1,0:T(8,128)(2,1)S(1)} %shard_map.96), channel_id=1, source_target_pairs={{0,2},{1,3},{2,0},{3,1},{4,6},{5,7},{6,4},{7,5},{8,10},{9,11},{10,... | collective-permute-start | bytes 786440 | tf_op jit(solution)/shard_map/ppermute | solution.py:399

commit v10 on v8

--- a/solution.py
+++ b/solution.py
@@ -372,6 +372,7 @@
 
     kv, near = lax.optimization_barrier((kv, near))
     queries.insert(0, exchange(near, halves))
+    kv, *queries[1:6] = lax.optimization_barrier((kv, *queries[1:6]))
     reach = REACH_BLOCKS * block
     sizes = [run - reach, reach] * 2
     early_head, early_tail, late_head, late_tail = place(kv, slot, sizes)

time: 77.1 us -> 75.4 us (0.978)
  starting transfers between devices: 40.6 us -> 37.4 us
  waiting for transfers between devices: 8.71 us -> 10.3 us
    ppermute x1, waiting for transfers between devices: 0.01 us -> 2.88 us  [shards(): late_halo = lax.ppermute(late_tail, 'ctx', down)]
    ppermute x1, starting transfers between devices: 3.87 us -> 1.3 us  [shards(): early_halo = lax.ppermute(early_tail, 'ctx', up)]
    ppermute x8, waiting for transfers between devices: 4.9 us -> 2.66 us  [shards(): lax.ppermute(piece, 'ctx', [(j, j ^ distance) for j in range(devices)])]
    ppermute x3, waiting for transfers between devices: 3.8 us -> 4.71 us  [shards(): out = lax.ppermute(out, ('dp', 'ctx'), route)]
  transfers between devices with their start and end apart: 15 -> 15, of which waited for: 5 -> 4; matrix products, arithmetic and copies ran while one was open for 3% -> 3% of each run, Pallas kernels for 20% -> 20%
where the time goes in v10:
time: 75.4 us; the launch traced here: 75.1 us
  starting transfers between devices  37.4 us (50%)
  Pallas kernels  25 us (33%)
  waiting for transfers between devices  10.3 us (14%)
  other arithmetic  1.37 us (2%)
  local copies, waits for them, and re-layouts  0.93 us (1%)
    ppermute x8, starting transfers between devices, shards(): lax.ppermute(piece, 'ctx', [(j, j ^ distance) for j in range(devices)])  19.1 us
    pallas_call x2, Pallas kernels, project(): pl.pallas_call(functools.partial(project_kernel, kinds, devices, heads, a...  17.7 us
    all_to_all x2, starting transfers between devices, exchange(): lax.all_to_all(flat, 'ctx', split_axis=0, concat_axis=0, tiled=True, axis...  12 us
    pallas_call x4, Pallas kernels, attend(): pl.pallas_call(functools.partial(attend_kernel, block, turn, members, dev...  5.58 us
    ppermute x3, waiting for transfers between devices, shards(): out = lax.ppermute(out, ('dp', 'ctx'), route)  4.71 us
    ppermute x3, starting transfers between devices, shards(): out = lax.ppermute(out, ('dp', 'ctx'), route)  3.69 us
    ppermute x1, waiting for transfers between devices, shards(): late_halo = lax.ppermute(late_tail, 'ctx', down)  2.88 us
    ppermute x8, waiting for transfers between devices, shards(): lax.ppermute(piece, 'ctx', [(j, j ^ distance) for j in range(devices)])  2.66 us
  transfers between devices with their start and end apart: 15, of which 4 were waited for; matrix products, arithmetic and copies ran while one was open for 3% of the time, Pallas kernels for 20%

profile of v10, /device:TPU:0, one launch (start us, length us, event | category | flops | bytes accessed | tf_op | source)
XLA Modules:
  0.0 75.1 jit_solution(15930374579548383945)
XLA Ops:
  0.0 7.2 %shard_map.82 = bf16[4,4,64,256]{3,2,1,0:T(8,128)(2,1)} custom-call(s32[32,128]{1,0:T(8,128)} %bitcast.25, f32[1,128]{1,0:T(1,128)} %constant.83.clone.freq_hbm, bf16[4096]{0:T(1024)(128)(2,1)} %gain_hbm.3, bf16[256,4096]{1,0:T(8,128)(2,1)} %tokens_hbm.3, bf16[4096,512]{1,0:T(8,128)(2,1)} %rest_0_.2, bf16[4096,512]{1,0:T(8,128)(2,1)} %rest_1_.1), custom_call_target="tpu_custom_call" | custom-call | flops 2147483648 | bytes 11010048 | tf_op jit(solution)/shard_map/pallas_call | solution.py:156
  7.2 8.3 %all-to-all-start = ((bf16[16,64,256]{2,1,0:T(8,128)(2,1)}), bf16[16,64,256]{2,1,0:T(8,128)(2,1)S(1)}, u32[]{:S(2)}, u32[]{:S(2)}) async-start(bf16[16,64,256]{2,1,0:T(8,128)(2,1)} %bitcast.23), calls=%async_computation | async-start | bytes 1048576 | tf_op jit(solution)/shard_map/all_to_all | solution.py:347
  15.6 10.4 %shard_map.83 = (bf16[2,4,64,512]{3,2,1,0:T(8,128)(2,1)}, bf16[64,512]{1,0:T(8,128)(2,1)}, bf16[64,512]{1,0:T(8,128)(2,1)}, bf16[64,512]{1,0:T(8,128)(2,1)}, bf1...) custom-call(s32[32,128]{1,0:T(8,128)} %bitcast.26, ...), custom_call_target="tpu_custom_call" | custom-call | flops 4294967296 | bytes 19922944 | tf_op jit(solution)/shard_map/pallas_call | solution.py:156
  26.0 2.9 %collective-permute-start = (bf16[64,512]{1,0:T(8,128)(2,1)}, bf16[64,512]{1,0:T(8,128)(2,1)S(1)}, u32[]{:S(2)}, u32[]{:S(2)}) collective-permute-start(bf16[64,512]{1,0:T(8,128)(2,1)} %get-tuple-element.29), channel_id=1, source_target_pairs={{0,8},{1,9},{2,10},{3,11},{4,12},{5,13},{6,14},{7,15},{8,0},{9,1},... | collective-permute-start | bytes 196616 | tf_op jit(solution)/shard_map/ppermute | solution.py:356
  28.9 1.5 %collective-permute-start.1 = (bf16[64,512]{1,0:T(8,128)(2,1)}, bf16[64,512]{1,0:T(8,128)(2,1)S(1)}, u32[]{:S(2)}, u32[]{:S(2)}) collective-permute-start(bf16[64,512]{1,0:T(8,128)(2,1)} %get-tuple-element.30), channel_id=1, source_target_pairs={{0,9},{1,8},{2,11},{3,10},{4,13},{5,12},{6,15},{7,14},{8,1},{9,0},... | collective-permute-start | bytes 196616 | tf_op jit(solution)/shard_map/ppermute | solution.py:356
  30.4 3.3 %collective-permute-start.2 = (bf16[64,512]{1,0:T(8,128)(2,1)}, bf16[64,512]{1,0:T(8,128)(2,1)S(1)}, u32[]{:S(2)}, u32[]{:S(2)}) collective-permute-start(bf16[64,512]{1,0:T(8,128)(2,1)} %get-tuple-element.31), channel_id=1, source_target_pairs={{0,10},{1,11},{2,8},{3,9},{4,14},{5,15},{6,12},{7,13},{8,2},{9,3},... | collective-permute-start | bytes 196616 | tf_op jit(solution)/shard_map/ppermute | solution.py:356
  33.7 3.7 %collective-permute-start.4 = (bf16[64,512]{1,0:T(8,128)(2,1)}, bf16[64,512]{1,0:T(8,128)(2,1)S(1)}, u32[]{:S(2)}, u32[]{:S(2)}) collective-permute-start(bf16[64,512]{1,0:T(8,128)(2,1)} %get-tuple-element.33), channel_id=1, source_target_pairs={{0,12},{1,13},{2,14},{3,15},{4,8},{5,9},{6,10},{7,11},{8,4},{9,5},... | collective-permute-start | bytes 196616 | tf_op jit(solution)/shard_map/ppermute | solution.py:356
  37.5 3.7 %all-to-all-start.1 = ((bf16[8,64,512]{2,1,0:T(8,128)(2,1)}), bf16[8,64,512]{2,1,0:T(8,128)(2,1)S(1)}, u32[]{:S(2)}, u32[]{:S(2)}) async-start(bf16[8,64,512]{2,1,0:T(8,128)(2,1)} %bitcast.24), calls=%async_computation.1 | async-start | bytes 1048576 | tf_op jit(solution)/shard_map/all_to_all | solution.py:347
  42.8 2.9 %collective-permute-start.5 = (bf16[64,512]{1,0:T(8,128)(2,1)}, bf16[64,512]{1,0:T(8,128)(2,1)S(1)}, u32[]{:S(2)}, u32[]{:S(2)}) collective-permute-start(bf16[64,512]{1,0:T(8,128)(2,1)} %get-tuple-element.39), channel_id=1, source_target_pairs={{0,13},{1,12},{2,15},{3,14},{4,9},{5,8},{6,11},{7,10},{8,5},{9,4},... | collective-permute-start | bytes 196616 | tf_op jit(solution)/shard_map/ppermute | solution.py:356
  45.7 3.3 %collective-permute-start.6 = (bf16[64,512]{1,0:T(8,128)(2,1)}, bf16[64,512]{1,0:T(8,128)(2,1)S(1)}, u32[]{:S(2)}, u32[]{:S(2)}) collective-permute-start(bf16[64,512]{1,0:T(8,128)(2,1)} %get-tuple-element.40), channel_id=1, source_target_pairs={{0,14},{1,15},{2,12},{3,13},{4,10},{5,11},{6,8},{7,9},{8,6},{9,7},... | collective-permute-start | bytes 196616 | tf_op jit(solution)/shard_map/ppermute | solution.py:356
  49.0 1.5 %collective-permute-start.7 = (bf16[64,512]{1,0:T(8,128)(2,1)}, bf16[64,512]{1,0:T(8,128)(2,1)S(1)}, u32[]{:S(2)}, u32[]{:S(2)}) collective-permute-start(bf16[64,512]{1,0:T(8,128)(2,1)} %get-tuple-element.41), channel_id=1, source_target_pairs={{0,15},{1,14},{2,13},{3,12},{4,11},{5,10},{6,9},{7,8},{8,7},{9,6},... | collective-permute-start | bytes 196616 | tf_op jit(solution)/shard_map/ppermute | solution.py:356
  50.4 0.7 shard_map.84
  51.2 1.3 %collective-permute-start.8 = (bf16[384,256]{1,0:T(8,128)(2,1)S(1)}, bf16[384,256]{1,0:T(8,128)(2,1)S(1)}, u32[]{:S(2)}, u32[]{:S(2)}) collective-permute-start(bf16[384,256]{1,0:T(8,128)(2,1)S(1)} %get-tuple-element.43.rest_11_), channel_id=1, source_target_pairs={{0,4},{1,5},{2,6},{3,7},{4,8},{5,9},{6,10},{7,11},{8,12},{9,13},{1... | collective-permute-start | bytes 589832 | tf_op jit(solution)/shard_map/ppermute | solution.py:381
  52.5 1.3 %collective-permute-start.9 = (bf16[384,256]{1,0:T(8,128)(2,1)S(1)}, bf16[384,256]{1,0:T(8,128)(2,1)S(1)}, u32[]{:S(2)}, u32[]{:S(2)}) collective-permute-start(bf16[384,256]{1,0:T(8,128)(2,1)S(1)} %get-tuple-element.45.rest_14_), channel_id=1, source_target_pairs={{4,0},{5,1},{6,2},{7,3},{8,4},{9,5},{10,6},{11,7},{12,8},{13,9},{1... | collective-permute-start | bytes 589832 | tf_op jit(solution)/shard_map/ppermute | solution.py:382
  54.5 2.6 %collective-permute-done.7.rest_8_ = bf16[64,512]{1,0:T(8,128)(2,1)S(1)} collective-permute-done((bf16[64,512]{1,0:T(8,128)(2,1)}, bf16[64,512]{1,0:T(8,128)(2,1)S(1)}, u32[]{:S(2)}, u32[]{:S(2)}) %collective-permute-start.7) | collective-permute-done | bytes 65568 | tf_op jit(solution)/shard_map/ppermute | solution.py:356
  57.1 2.9 %collective-permute-done.9.rest_12_ = bf16[384,256]{1,0:T(8,128)(2,1)S(1)} collective-permute-done((bf16[384,256]{1,0:T(8,128)(2,1)S(1)}, bf16[384,256]{1,0:T(8,128)(2,1)S(1)}, u32[]{:S(2)}, u32[]{:S(2)}) %collective-permute-start.9) | collective-permute-done | bytes 196640 | tf_op jit(solution)/shard_map/ppermute | solution.py:382
  60.0 1.4 %shard_map.85 = bf16[256,512]{1,0:T(8,128)(2,1)S(1)} custom-call(s32[1,1024]{1,0:T(1,128)S(1)} %reshape.203.slot_ref, s32[1,32]{1,0:T(1,128)S(1)} %reduce-window_2_clone.1.ends_ref, bf16[512,512]{1,0:T(8,128)(2,1)S(1)} %bitcast.18, bf16[64,512]{1,0:T(8,128)(2,1)S(1)} %collective-permute-done.rest_1_, bf16[64,512]{1,0:T(8,128)(2,1)S(1)} %collective-permute-done.1.rest_2_, ...), custom_call_target="tpu_custom_call" | custom-call | flops 536870912 | bytes 1966080 | tf_op jit(solution)/shard_map/pallas_call | solution.py:286
  61.4 2.4 %collective-permute-start.10 = (bf16[256,512]{1,0:T(8,128)(2,1)S(1)}, bf16[256,512]{1,0:T(8,128)(2,1)S(1)}, u32[]{:S(2)}, u32[]{:S(2)}) collective-permute-start(bf16[256,512]{1,0:T(8,128)(2,1)S(1)} %shard_map.85), channel_id=1, source_target_pairs={{0,3},{1,2},{2,1},{3,0},{4,7},{5,6},{6,5},{7,4},{8,11},{9,10},{10,... | collective-permute-start | bytes 786440 | tf_op jit(solution)/shard_map/ppermute | solution.py:395
  63.9 1.4 %shard_map.86 = bf16[256,512]{1,0:T(8,128)(2,1)S(1)} custom-call(s32[1,1024]{1,0:T(1,128)S(1)} %reshape.203.slot_ref, s32[1,32]{1,0:T(1,128)S(1)} %reduce-window_2_clone.1.ends_ref, bf16[512,512]{1,0:T(8,128)(2,1)S(1)} %bitcast.19, bf16[64,512]{1,0:T(8,128)(2,1)S(1)} %collective-permute-done.rest_1_, bf16[64,512]{1,0:T(8,128)(2,1)S(1)} %collective-permute-done.1.rest_2_, ...), custom_call_target="tpu_custom_call" | custom-call | flops 536870912 | bytes 1966080 | tf_op jit(solution)/shard_map/pallas_call | solution.py:286
  65.9 1.4 %shard_map.87 = bf16[256,512]{1,0:T(8,128)(2,1)S(1)} custom-call(s32[1,1024]{1,0:T(1,128)S(1)} %reshape.203.slot_ref, s32[1,32]{1,0:T(1,128)S(1)} %reduce-window_2_clone.1.ends_ref, bf16[512,512]{1,0:T(8,128)(2,1)S(1)} %bitcast.20, bf16[64,512]{1,0:T(8,128)(2,1)S(1)} %collective-permute-done.rest_1_, bf16[64,512]{1,0:T(8,128)(2,1)S(1)} %collective-permute-done.1.rest_2_, ...), custom_call_target="tpu_custom_call" | custom-call | flops 536870912 | bytes 1966080 | tf_op jit(solution)/shard_map/pallas_call | solution.py:286
  67.9 1.4 %shard_map.88.refs_3_ = bf16[256,512]{1,0:T(8,128)(2,1)S(1)} custom-call(s32[1,1024]{1,0:T(1,128)S(1)} %reshape.203.slot_ref, s32[1,32]{1,0:T(1,128)S(1)} %reduce-window_2_clone.1.ends_ref, bf16[512,512]{1,0:T(8,128)(2,1)S(1)} %bitcast.21, bf16[64,512]{1,0:T(8,128)(2,1)S(1)} %collective-permute-done.rest_1_, ...), custom_call_target="tpu_custom_call" | custom-call | flops 536870912 | bytes 1966080 | tf_op jit(solution)/shard_map/pallas_call | solution.py:286
  69.3 2.0 %collective-permute-done.10.refs_0_ = bf16[256,512]{1,0:T(8,128)(2,1)S(1)} collective-permute-done((bf16[256,512]{1,0:T(8,128)(2,1)S(1)}, bf16[256,512]{1,0:T(8,128)(2,1)S(1)}, u32[]{:S(2)}, u32[]{:S(2)}) %collective-permute-start.10) | collective-permute-done | bytes 262176 | tf_op jit(solution)/shard_map/ppermute | solution.py:395
  71.3 2.7 %collective-permute-done.11.refs_1_ = bf16[256,512]{1,0:T(8,128)(2,1)S(1)} collective-permute-done((bf16[256,512]{1,0:T(8,128)(2,1)S(1)}, bf16[256,512]{1,0:T(8,128)(2,1)S(1)}, u32[]{:S(2)}, u32[]{:S(2)}) %collective-permute-start.11) | collective-permute-done | bytes 262176 | tf_op jit(solution)/shard_map/ppermute | solution.py:395
  74.0 1.1 %shard_map.89 = bf16[256,2048]{1,0:T(8,128)(2,1)} custom-call(bf16[256,512]{1,0:T(8,128)(2,1)S(1)} %collective-permute-done.10.refs_0_, bf16[256,512]{1,0:T(8,128)(2,1)S(1)} %collective-permute-done.11.refs_1_, bf16[256,512]{1,0:T(8,128)(2,1)S(1)} %collective-permute-done.12.refs_2_, bf16[256,512]{1,0:T(8,128)(2,1)S(1)} %shard_map.88.refs_3_), custom_call_target="tpu_custom_call" | custom-call | bytes 2097152 | tf_op jit(solution)/shard_map/pallas_call | solution.py:314
  (33 shorter events, 3.7 us)
Async XLA Ops:
  7.2 30.3 %all-to-all-start = ((bf16[16,64,256]{2,1,0:T(8,128)(2,1)}), bf16[16,64,256]{2,1,0:T(8,128)(2,1)S(1)}, u32[]{:S(2)}, u32[]{:S(2)}) async-start(bf16[16,64,256]{2,1,0:T(8,128)(2,1)} %bitcast.23), calls=%async_computation | async-start | bytes 1048576 | tf_op jit(solution)/shard_map/all_to_all | solution.py:347
  15.5 25.6 %copy-start = (s32[4096]{0:T(1024)S(1)}, s32[4096]{0:T(1024)}, u32[]{:S(2)}) copy-start(s32[4096]{0:T(1024)} %param.9) | copy-start | bytes 49156
  15.6 25.7 %copy-start.1 = (s32[32]{0:T(128)S(1)}, s32[32]{0:T(128)}, u32[]{:S(2)}) copy-start(s32[32]{0:T(128)} %param.10) | copy-start | bytes 388
  26.0 16.8 %collective-permute-start = (bf16[64,512]{1,0:T(8,128)(2,1)}, bf16[64,512]{1,0:T(8,128)(2,1)S(1)}, u32[]{:S(2)}, u32[]{:S(2)}) collective-permute-start(bf16[64,512]{1,0:T(8,128)(2,1)} %get-tuple-element.29), channel_id=1, source_target_pairs={{0,8},{1,9},{2,10},{3,11},{4,12},{5,13},{6,14},{7,15},{8,0},{9,1},... | collective-permute-start | bytes 196616 | tf_op jit(solution)/shard_map/ppermute | solution.py:356
  28.9 16.8 %collective-permute-start.1 = (bf16[64,512]{1,0:T(8,128)(2,1)}, bf16[64,512]{1,0:T(8,128)(2,1)S(1)}, u32[]{:S(2)}, u32[]{:S(2)}) collective-permute-start(bf16[64,512]{1,0:T(8,128)(2,1)} %get-tuple-element.30), channel_id=1, source_target_pairs={{0,9},{1,8},{2,11},{3,10},{4,13},{5,12},{6,15},{7,14},{8,1},{9,0},... | collective-permute-start | bytes 196616 | tf_op jit(solution)/shard_map/ppermute | solution.py:356
  30.4 18.6 %collective-permute-start.2 = (bf16[64,512]{1,0:T(8,128)(2,1)}, bf16[64,512]{1,0:T(8,128)(2,1)S(1)}, u32[]{:S(2)}, u32[]{:S(2)}) collective-permute-start(bf16[64,512]{1,0:T(8,128)(2,1)} %get-tuple-element.31), channel_id=1, source_target_pairs={{0,10},{1,11},{2,8},{3,9},{4,14},{5,15},{6,12},{7,13},{8,2},{9,3},... | collective-permute-start | bytes 196616 | tf_op jit(solution)/shard_map/ppermute | solution.py:356
  33.6 16.8 %collective-permute-start.3 = (bf16[64,512]{1,0:T(8,128)(2,1)}, bf16[64,512]{1,0:T(8,128)(2,1)S(1)}, u32[]{:S(2)}, u32[]{:S(2)}) collective-permute-start(bf16[64,512]{1,0:T(8,128)(2,1)} %get-tuple-element.32), channel_id=1, source_target_pairs={{0,11},{1,10},{2,9},{3,8},{4,15},{5,14},{6,13},{7,12},{8,3},{9,2},... | collective-permute-start | bytes 196616 | tf_op jit(solution)/shard_map/ppermute | solution.py:356
  33.7 16.7 %collective-permute-start.4 = (bf16[64,512]{1,0:T(8,128)(2,1)}, bf16[64,512]{1,0:T(8,128)(2,1)S(1)}, u32[]{:S(2)}, u32[]{:S(2)}) collective-permute-start(bf16[64,512]{1,0:T(8,128)(2,1)} %get-tuple-element.33), channel_id=1, source_target_pairs={{0,12},{1,13},{2,14},{3,15},{4,8},{5,9},{6,10},{7,11},{8,4},{9,5},... | collective-permute-start | bytes 196616 | tf_op jit(solution)/shard_map/ppermute | solution.py:356
  37.5 22.6 %all-to-all-start.1 = ((bf16[8,64,512]{2,1,0:T(8,128)(2,1)}), bf16[8,64,512]{2,1,0:T(8,128)(2,1)S(1)}, u32[]{:S(2)}, u32[]{:S(2)}) async-start(bf16[8,64,512]{2,1,0:T(8,128)(2,1)} %bitcast.24), calls=%async_computation.1 | async-start | bytes 1048576 | tf_op jit(solution)/shard_map/all_to_all | solution.py:347
  42.8 11.7 %collective-permute-start.5 = (bf16[64,512]{1,0:T(8,128)(2,1)}, bf16[64,512]{1,0:T(8,128)(2,1)S(1)}, u32[]{:S(2)}, u32[]{:S(2)}) collective-permute-start(bf16[64,512]{1,0:T(8,128)(2,1)} %get-tuple-element.39), channel_id=1, source_target_pairs={{0,13},{1,12},{2,15},{3,14},{4,9},{5,8},{6,11},{7,10},{8,5},{9,4},... | collective-permute-start | bytes 196616 | tf_op jit(solution)/shard_map/ppermute | solution.py:356
  45.7 8.8 %collective-permute-start.6 = (bf16[64,512]{1,0:T(8,128)(2,1)}, bf16[64,512]{1,0:T(8,128)(2,1)S(1)}, u32[]{:S(2)}, u32[]{:S(2)}) collective-permute-start(bf16[64,512]{1,0:T(8,128)(2,1)} %get-tuple-element.40), channel_id=1, source_target_pairs={{0,14},{1,15},{2,12},{3,13},{4,10},{5,11},{6,8},{7,9},{8,6},{9,7},... | collective-permute-start | bytes 196616 | tf_op jit(solution)/shard_map/ppermute | solution.py:356
  49.0 8.2 %collective-permute-start.7 = (bf16[64,512]{1,0:T(8,128)(2,1)}, bf16[64,512]{1,0:T(8,128)(2,1)S(1)}, u32[]{:S(2)}, u32[]{:S(2)}) collective-permute-start(bf16[64,512]{1,0:T(8,128)(2,1)} %get-tuple-element.41), channel_id=1, source_target_pairs={{0,15},{1,14},{2,13},{3,12},{4,11},{5,10},{6,9},{7,8},{8,7},{9,6},... | collective-permute-start | bytes 196616 | tf_op jit(solution)/shard_map/ppermute | solution.py:356
  51.2 6.0 %collective-permute-start.8 = (bf16[384,256]{1,0:T(8,128)(2,1)S(1)}, bf16[384,256]{1,0:T(8,128)(2,1)S(1)}, u32[]{:S(2)}, u32[]{:S(2)}) collective-permute-start(bf16[384,256]{1,0:T(8,128)(2,1)S(1)} %get-tuple-element.43.rest_11_), channel_id=1, source_target_pairs={{0,4},{1,5},{2,6},{3,7},{4,8},{5,9},{6,10},{7,11},{8,12},{9,13},{1... | collective-permute-start | bytes 589832 | tf_op jit(solution)/shard_map/ppermute | solution.py:381
  52.5 7.6 %collective-permute-start.9 = (bf16[384,256]{1,0:T(8,128)(2,1)S(1)}, bf16[384,256]{1,0:T(8,128)(2,1)S(1)}, u32[]{:S(2)}, u32[]{:S(2)}) collective-permute-start(bf16[384,256]{1,0:T(8,128)(2,1)S(1)} %get-tuple-element.45.rest_14_), channel_id=1, source_target_pairs={{4,0},{5,1},{6,2},{7,3},{8,4},{9,5},{10,6},{11,7},{12,8},{13,9},{1... | collective-permute-start | bytes 589832 | tf_op jit(solution)/shard_map/ppermute | solution.py:382
  61.4 9.9 %collective-permute-start.10 = (bf16[256,512]{1,0:T(8,128)(2,1)S(1)}, bf16[256,512]{1,0:T(8,128)(2,1)S(1)}, u32[]{:S(2)}, u32[]{:S(2)}) collective-permute-start(bf16[256,512]{1,0:T(8,128)(2,1)S(1)} %shard_map.85), channel_id=1, source_target_pairs={{0,3},{1,2},{2,1},{3,0},{4,7},{5,6},{6,5},{7,4},{8,11},{9,10},{10,... | collective-permute-start | bytes 786440 | tf_op jit(solution)/shard_map/ppermute | solution.py:395
  65.3 8.8 %collective-permute-start.11 = (bf16[256,512]{1,0:T(8,128)(2,1)S(1)}, bf16[256,512]{1,0:T(8,128)(2,1)S(1)}, u32[]{:S(2)}, u32[]{:S(2)}) collective-permute-start(bf16[256,512]{1,0:T(8,128)(2,1)S(1)} %shard_map.86), channel_id=1, source_target_pairs={{0,1},{1,0},{2,3},{3,2},{4,5},{5,4},{6,7},{7,6},{8,9},{9,8},{10,11... | collective-permute-start | bytes 786440 | tf_op jit(solution)/shard_map/ppermute | solution.py:395
  67.3 6.7 %collective-permute-start.12 = (bf16[256,512]{1,0:T(8,128)(2,1)S(1)}, bf16[256,512]{1,0:T(8,128)(2,1)S(1)}, u32[]{:S(2)}, u32[]{:S(2)}) collective-permute-start(bf16[256,512]{1,0:T(8,128)(2,1)S(1)} %shard_map.87), channel_id=1, source_target_pairs={{0,2},{1,3},{2,0},{3,1},{4,6},{5,7},{6,4},{7,5},{8,10},{9,11},{10,... | collective-permute-start | bytes 786440 | tf_op jit(solution)/shard_map/ppermute | solution.py:395

commit v11 on v10

--- a/solution.py
+++ b/solution.py
@@ -34,13 +34,14 @@
     return jnp.minimum(block_id, 2 * devices - 1 - block_id) // members
 
 
-def project_kernel(kinds, devices, members, apart, positions_hbm, freq_hbm, gain_hbm, tokens_hbm, *rest):
+def project_kernel(kinds, devices, members, apart, ready, positions_hbm, freq_hbm, gain_hbm, tokens_hbm, *rest):
     count = len(kinds)
     weights_hbm, rest = rest[:count], rest[count:]
-    outs_hbm, rest = rest[: 1 + apart], (None,) * (count + 1) + rest[1 + apart :]
-    positions_ref, freq_ref, gain_ref, tokens, normed, weights, out_ref = rest[count + 1 : count + 8]
-    small_sems, token_sems, sems, out_sems = rest[count + 8 :]
-    rows, width = tokens.shape
+    outputs = 1 + len(apart) + (not ready)
+    outs_hbm, rest = rest[:outputs], rest[outputs:]
+    positions_ref, freq_ref, gain_ref, tokens, normed, weights, out_ref = rest[:7]
+    small_sems, token_sems, sems, out_sems = rest[7:]
+    rows, width = normed.shape
     chunks, _, span = weights.shape
     parts = token_sems.shape[0]
     part = rows // parts
@@ -55,7 +56,8 @@
         copy.start()
     for i in range(parts):
         at = pl.ds(i * part, part)
-        token_copies.append(pltpu.make_async_copy(tokens_hbm.at[at], tokens.at[at], token_sems.at[i]))
+        target = normed.at[at] if ready else tokens.at[at]
+        token_copies.append(pltpu.make_async_copy(tokens_hbm.at[at], target, token_sems.at[i]))
         token_copies[i].start()
     for i in range(count):
         for first in range(0, weights_hbm[i].shape[1], span):
@@ -64,6 +66,8 @@
             copies.append(pltpu.make_async_copy(source, weights.at[j], sems.at[j]))
             origin.append((i, first))
     copies[0].start()
+    if ready and chunks > 1:
+        copies[1].start()
     for copy in small_copies:
         copy.wait()
     lanes = positions_ref.shape[1]
@@ -85,28 +89,34 @@
     order = jnp.where(order, 1.0, 0.0).astype(jnp.bfloat16)
     gain = gain_ref[...].astype(jnp.float32).reshape(1, width)
     step = 32
+    written = []
 
     for i in range(parts):
         token_copies[i].wait()
-
-        def norm(j, _):
-            at = pl.ds(pl.multiple_of(i * part + j * step, step), step)
+        for first in range(i * part, (i + 1) * part, step) if not ready else ():
+            at = slice(first, first + step)
             floats = tokens[at, :].astype(jnp.float32)
             mean = jnp.sum(floats * floats, axis=1, keepdims=True) * (1.0 / width)
             tokens[at, :] = (floats * lax.rsqrt(mean + EPSILON) * gain).astype(jnp.bfloat16)
-            return 0
-
-        lax.fori_loop(0, part // step, norm, 0, unroll=True)
-    if chunks > 1:
-        copies[1].start()
-    for first in range(0, width, 512):
-        columns = slice(first, first + 512)
-        normed[:, columns] = dot(order, tokens[:, columns]).astype(jnp.bfloat16)
+    if not ready:
+        if chunks > 1:
+            copies[1].start()
+        for first in range(0, width, 512):
+            columns = slice(first, first + 512)
+            normed[:, columns] = dot(order, tokens[:, columns]).astype(jnp.bfloat16)
+        written.append(pltpu.make_async_copy(normed, outs_hbm[-1], small_sems.at[0]))
+        written[0].start()
     groups, heads = out_ref.shape[:2]
     offsets = [0]
     for i in range(count):
         offsets.append(offsets[-1] + weights_hbm[i].shape[1] // heads)
-    written = []
+    me = lax.axis_index("ctx")
+    far = [
+        pltpu.make_async_copy(
+            out_ref.at[(me ^ distance) // members, (me ^ distance) % members], outs_hbm[1 + i], out_sems.at[chunks + i]
+        )
+        for i, distance in enumerate(apart)
+    ]
     for j in range(chunks):
         i, first = origin[j]
         copies[j].wait()
@@ -123,27 +133,23 @@
             out_ref[:, head, :, inside : inside + HEAD_SIZE] = values.astype(jnp.bfloat16).reshape(
                 groups, rows // groups, HEAD_SIZE
             )
-        if apart:
-            continue
-        done = (pl.ds(0, groups), pl.ds(first // per_head, max(span // per_head, 1)))
-        done += (pl.ds(0, rows // groups), pl.ds(offsets[i] + first % per_head, min(span, per_head)))
-        written.append(pltpu.make_async_copy(out_ref.at[done], outs_hbm[0].at[done], out_sems.at[j]))
-        written[j].start()
-    if apart:
-        me = lax.axis_index("ctx")
-        here = pl.ds(me // apart * (groups // 2), groups // 2)
-        written.append(pltpu.make_async_copy(out_ref.at[here], outs_hbm[0], out_sems.at[0]))
-        for i in range(apart):
-            to = me ^ (apart + i)
-            source = out_ref.at[to // members, to % members]
-            written.append(pltpu.make_async_copy(source, outs_hbm[1 + i], out_sems.at[1 + i]))
-        for copy in written:
-            copy.start()
-    for copy in written:
+        first_head, done_heads = first // per_head, max(span // per_head, 1)
+        done = (pl.ds(first_head, done_heads), pl.ds(0, rows // groups))
+        done += (pl.ds(offsets[i] + first % per_head, min(span, per_head)),)
+        taken = groups // 2 if apart else groups
+        start = me // members // taken * taken if apart else 0
+        source = out_ref.at[(pl.ds(start, taken),) + done]
+        written.append(pltpu.make_async_copy(source, outs_hbm[0].at[(pl.ds(0, taken),) + done], out_sems.at[j]))
+        written[-1].start()
+        if first % per_head + span >= per_head:
+            for distance, copy in zip(apart, far):
+                to = (me ^ distance) % members
+                pl.when((to >= first_head) & (to < first_head + done_heads))(copy.start)
+    for copy in written + far:
         copy.wait()
 
 
-def project(positions, freq, gain, tokens, weights, kinds, devices, heads, apart=0):
+def project(positions, freq, gain, tokens, weights, kinds, devices, heads, apart=(), ready=False):
     rows, width = tokens.shape
     groups = devices // heads
     columns = sum(w.shape[1] for w in weights)
@@ -152,24 +158,24 @@
     flops = 2 * rows * width * columns
     size = 2 * (width * columns + rows * width + rows * columns)
     out_shape = (groups // 2 if apart else groups, heads, rows // groups, columns // heads)
-    out_shapes = [out_shape] + [out_shape[2:]] * apart
+    out_shapes = [out_shape] + [out_shape[2:]] * len(apart) + [(rows, width)] * (not ready)
     return pl.pallas_call(
-        functools.partial(project_kernel, kinds, devices, heads, apart),
+        functools.partial(project_kernel, kinds, devices, heads, apart, ready),
         out_shape=[jax.ShapeDtypeStruct(shape, jnp.bfloat16) for shape in out_shapes],
         in_specs=[IN_PLACE] * (len(weights) + 4),
-        out_specs=[IN_PLACE] * (1 + apart),
+        out_specs=[IN_PLACE] * len(out_shapes),
         scratch_shapes=[
             pltpu.VMEM(positions.shape, jnp.int32),
             pltpu.VMEM(freq.shape, jnp.float32),
             pltpu.VMEM(gain.shape, jnp.bfloat16),
-            pltpu.VMEM((rows, width), jnp.bfloat16),
+            pltpu.VMEM((8 if ready else rows, width), jnp.bfloat16),
             pltpu.VMEM((rows, width), jnp.bfloat16),
             pltpu.VMEM((columns // span, width, span), jnp.bfloat16),
             pltpu.VMEM((groups, heads, rows // groups, columns // heads), jnp.bfloat16),
             pltpu.SemaphoreType.DMA((3,)),
             pltpu.SemaphoreType.DMA((parts,)),
             pltpu.SemaphoreType.DMA((columns // span,)),
-            pltpu.SemaphoreType.DMA((max(1 + apart, columns // span),)),
+            pltpu.SemaphoreType.DMA((columns // span + len(apart),)),
         ],
         compiler_params=pltpu.CompilerParams(vmem_limit_bytes=56 * MIB),
         cost_estimate=pl.CostEstimate(flops=flops, bytes_accessed=size, transcendentals=0),
@@ -336,7 +342,7 @@
 
     half = HEAD_SIZE // 2
     freq = np.float32(ROPE_THETA ** (-(np.arange(HEAD_SIZE) % half * 2.0 / HEAD_SIZE)))
-    operands = (positions.reshape(-1, 128), jnp.asarray(freq[None, :]), gain, tokens)
+    operands = (positions.reshape(-1, 128), jnp.asarray(freq[None, :]), gain)
 
     half_devices = devices // 2
     halves = [list(range(i, i + half_devices)) for i in (0, half_devices)]
@@ -347,9 +353,10 @@
         flat = lax.all_to_all(flat, "ctx", split_axis=0, concat_axis=0, tiled=True, axis_index_groups=among)
         return flat.reshape(-1, width)
 
-    (kv,) = project(*operands, (w_key, value_weight), (True, False), devices, members)
+    kv, normed = project(*operands, tokens, (w_key, value_weight), (True, False), devices, members)
     kv = exchange(kv, None)
-    near, *far = project(*operands, (w_query,), (True,), devices, members, half_devices)
+    apart = list(range(half_devices, devices))
+    near, *far = project(*operands, normed, (w_query,), (True,), devices, members, apart, True)
     queries = []
     for i, piece in enumerate(far):
         distance = half_devices + i
@@ -360,7 +367,9 @@
     first_run = group * run
     second_run = (2 * devices - members) * block - group * run
     slots = jnp.where(table // run == group, table - first_run, table - second_run + run)
-    place_in = jnp.cumsum(ours.astype(jnp.int32), axis=1) - 1
+    inner = jnp.arange(rows, dtype=jnp.int32)
+    before = (inner[:, None] < inner[None, :]).astype(jnp.bfloat16)
+    place_in = dot(ours.astype(jnp.bfloat16), before).astype(jnp.int32)
     place_in = jnp.where(ours, place_in, -1)
     wanted = jnp.arange(group_rows, dtype=jnp.int32)[None, :, None] == place_in[:, None, :]
     slot = jnp.sum(jnp.where(wanted, slots[:, None, :], 0), axis=2)

time: 75.4 us -> 74.6 us (0.989)
  transfers between devices with their start and end apart: 15 -> 15, of which waited for: 4 -> 4; matrix products, arithmetic and copies ran while one was open for 3% -> 2% of each run, Pallas kernels for 20% -> 20%
where the time goes in v11:
time: 74.6 us; the launch traced here: 74.3 us
  starting transfers between devices  37.6 us (50%)
  Pallas kernels  24.9 us (33%)
  waiting for transfers between devices  10.1 us (14%)
    ppermute x8, starting transfers between devices, shards(): lax.ppermute(piece, 'ctx', [(j, j ^ distance) for j in range(devices)])  19.1 us
    pallas_call x2, Pallas kernels, project(): pl.pallas_call(functools.partial(project_kernel, kinds, devices, heads, a...  17.5 us
    all_to_all x2, starting transfers between devices, exchange(): lax.all_to_all(flat, 'ctx', split_axis=0, concat_axis=0, tiled=True, axis...  12 us
    pallas_call x4, Pallas kernels, attend(): pl.pallas_call(functools.partial(attend_kernel, block, turn, members, dev...  5.59 us
    ppermute x3, waiting for transfers between devices, shards(): out = lax.ppermute(out, ('dp', 'ctx'), route)  4.72 us
    ppermute x3, starting transfers between devices, shards(): out = lax.ppermute(out, ('dp', 'ctx'), route)  3.7 us
    ppermute x1, waiting for transfers between devices, shards(): late_halo = lax.ppermute(late_tail, 'ctx', down)  2.88 us
    ppermute x8, waiting for transfers between devices, shards(): lax.ppermute(piece, 'ctx', [(j, j ^ distance) for j in range(devices)])  2.48 us
  transfers between devices with their start and end apart: 15, of which 4 were waited for; matrix products, arithmetic and copies ran while one was open for 2% of the time, Pallas kernels for 20%

profile of v11, /device:TPU:0, one launch (start us, length us, event | category | flops | bytes accessed | tf_op | source)
XLA Modules:
  0.0 74.3 jit_solution(10275053620931384060)
XLA Ops:
  0.0 7.7 %shard_map.82 = (bf16[4,4,64,256]{3,2,1,0:T(8,128)(2,1)}, bf16[256,4096]{1,0:T(8,128)(2,1)}) custom-call(s32[32,128]{1,0:T(8,128)} %bitcast.19, f32[1,128]{1,0:T(1,128)} %constant.78.clone.freq_hbm, bf16[4096]{0:T(1024)(128)(2,1)} %gain_hbm.3, bf16[256,4096]{1,0:T(8,128)(2,1)} %tokens_hbm.1, bf16[4096,512]{1,0:T(8,128)(2,1)} %rest_0_.2, ...), custom_call_target="tpu_custom_call" | custom-call | flops 2147483648 | bytes 11010048 | tf_op jit(solution)/shard_map/pallas_call | solution.py:162
  7.7 8.3 %all-to-all-start = ((bf16[16,64,256]{2,1,0:T(8,128)(2,1)}), bf16[16,64,256]{2,1,0:T(8,128)(2,1)S(1)}, u32[]{:S(2)}, u32[]{:S(2)}) async-start(bf16[16,64,256]{2,1,0:T(8,128)(2,1)} %bitcast.18), calls=%async_computation | async-start | bytes 1048576 | tf_op jit(solution)/shard_map/all_to_all | solution.py:353
  16.1 9.7 %shard_map.83 = (bf16[2,4,64,512]{3,2,1,0:T(8,128)(2,1)}, bf16[64,512]{1,0:T(8,128)(2,1)}, bf16[64,512]{1,0:T(8,128)(2,1)}, bf16[64,512]{1,0:T(8,128)(2,1)}, bf1...) custom-call(s32[32,128]{1,0:T(8,128)} %bitcast.20, ...), custom_call_target="tpu_custom_call" | custom-call | flops 4294967296 | bytes 19922944 | tf_op jit(solution)/shard_map/pallas_call | solution.py:162
  25.9 2.9 %collective-permute-start = (bf16[64,512]{1,0:T(8,128)(2,1)}, bf16[64,512]{1,0:T(8,128)(2,1)S(1)}, u32[]{:S(2)}, u32[]{:S(2)}) collective-permute-start(bf16[64,512]{1,0:T(8,128)(2,1)} %get-tuple-element.33), channel_id=1, source_target_pairs={{0,8},{1,9},{2,10},{3,11},{4,12},{5,13},{6,14},{7,15},{8,0},{9,1},... | collective-permute-start | bytes 196616 | tf_op jit(solution)/shard_map/ppermute | solution.py:363
  28.8 1.5 %collective-permute-start.1 = (bf16[64,512]{1,0:T(8,128)(2,1)}, bf16[64,512]{1,0:T(8,128)(2,1)S(1)}, u32[]{:S(2)}, u32[]{:S(2)}) collective-permute-start(bf16[64,512]{1,0:T(8,128)(2,1)} %get-tuple-element.34), channel_id=1, source_target_pairs={{0,9},{1,8},{2,11},{3,10},{4,13},{5,12},{6,15},{7,14},{8,1},{9,0},... | collective-permute-start | bytes 196616 | tf_op jit(solution)/shard_map/ppermute | solution.py:363
  30.2 3.3 %collective-permute-start.2 = (bf16[64,512]{1,0:T(8,128)(2,1)}, bf16[64,512]{1,0:T(8,128)(2,1)S(1)}, u32[]{:S(2)}, u32[]{:S(2)}) collective-permute-start(bf16[64,512]{1,0:T(8,128)(2,1)} %get-tuple-element.35), channel_id=1, source_target_pairs={{0,10},{1,11},{2,8},{3,9},{4,14},{5,15},{6,12},{7,13},{8,2},{9,3},... | collective-permute-start | bytes 196616 | tf_op jit(solution)/shard_map/ppermute | solution.py:363
  33.6 3.7 %collective-permute-start.4 = (bf16[64,512]{1,0:T(8,128)(2,1)}, bf16[64,512]{1,0:T(8,128)(2,1)S(1)}, u32[]{:S(2)}, u32[]{:S(2)}) collective-permute-start(bf16[64,512]{1,0:T(8,128)(2,1)} %get-tuple-element.37), channel_id=1, source_target_pairs={{0,12},{1,13},{2,14},{3,15},{4,8},{5,9},{6,10},{7,11},{8,4},{9,5},... | collective-permute-start | bytes 196616 | tf_op jit(solution)/shard_map/ppermute | solution.py:363
  37.6 3.6 %all-to-all-start.1 = ((bf16[8,64,512]{2,1,0:T(8,128)(2,1)}), bf16[8,64,512]{2,1,0:T(8,128)(2,1)S(1)}, u32[]{:S(2)}, u32[]{:S(2)}) async-start(bf16[8,64,512]{2,1,0:T(8,128)(2,1)} %bitcast.17), calls=%async_computation.1 | async-start | bytes 1048576 | tf_op jit(solution)/shard_map/all_to_all | solution.py:353
  41.8 3.0 %collective-permute-start.5 = (bf16[64,512]{1,0:T(8,128)(2,1)}, bf16[64,512]{1,0:T(8,128)(2,1)S(1)}, u32[]{:S(2)}, u32[]{:S(2)}) collective-permute-start(bf16[64,512]{1,0:T(8,128)(2,1)} %get-tuple-element.43), channel_id=1, source_target_pairs={{0,13},{1,12},{2,15},{3,14},{4,9},{5,8},{6,11},{7,10},{8,5},{9,4},... | collective-permute-start | bytes 196616 | tf_op jit(solution)/shard_map/ppermute | solution.py:363
  44.8 3.3 %collective-permute-start.6 = (bf16[64,512]{1,0:T(8,128)(2,1)}, bf16[64,512]{1,0:T(8,128)(2,1)S(1)}, u32[]{:S(2)}, u32[]{:S(2)}) collective-permute-start(bf16[64,512]{1,0:T(8,128)(2,1)} %get-tuple-element.44), channel_id=1, source_target_pairs={{0,14},{1,15},{2,12},{3,13},{4,10},{5,11},{6,8},{7,9},{8,6},{9,7},... | collective-permute-start | bytes 196616 | tf_op jit(solution)/shard_map/ppermute | solution.py:363
  48.1 1.5 %collective-permute-start.7 = (bf16[64,512]{1,0:T(8,128)(2,1)}, bf16[64,512]{1,0:T(8,128)(2,1)S(1)}, u32[]{:S(2)}, u32[]{:S(2)}) collective-permute-start(bf16[64,512]{1,0:T(8,128)(2,1)} %get-tuple-element.45), channel_id=1, source_target_pairs={{0,15},{1,14},{2,13},{3,12},{4,11},{5,10},{6,9},{7,8},{8,7},{9,6},... | collective-permute-start | bytes 196616 | tf_op jit(solution)/shard_map/ppermute | solution.py:363
  49.6 0.7 shard_map.84
  50.3 1.3 %collective-permute-start.8 = (bf16[384,256]{1,0:T(8,128)(2,1)S(1)}, bf16[384,256]{1,0:T(8,128)(2,1)S(1)}, u32[]{:S(2)}, u32[]{:S(2)}) collective-permute-start(bf16[384,256]{1,0:T(8,128)(2,1)S(1)} %get-tuple-element.47.rest_11_), channel_id=1, source_target_pairs={{0,4},{1,5},{2,6},{3,7},{4,8},{5,9},{6,10},{7,11},{8,12},{9,13},{1... | collective-permute-start | bytes 589832 | tf_op jit(solution)/shard_map/ppermute | solution.py:390
  51.6 1.5 %collective-permute-start.9 = (bf16[384,256]{1,0:T(8,128)(2,1)S(1)}, bf16[384,256]{1,0:T(8,128)(2,1)S(1)}, u32[]{:S(2)}, u32[]{:S(2)}) collective-permute-start(bf16[384,256]{1,0:T(8,128)(2,1)S(1)} %get-tuple-element.49.rest_14_), channel_id=1, source_target_pairs={{4,0},{5,1},{6,2},{7,3},{8,4},{9,5},{10,6},{11,7},{12,8},{13,9},{1... | collective-permute-start | bytes 589832 | tf_op jit(solution)/shard_map/ppermute | solution.py:391
  53.8 2.5 %collective-permute-done.7.rest_8_ = bf16[64,512]{1,0:T(8,128)(2,1)S(1)} collective-permute-done((bf16[64,512]{1,0:T(8,128)(2,1)}, bf16[64,512]{1,0:T(8,128)(2,1)S(1)}, u32[]{:S(2)}, u32[]{:S(2)}) %collective-permute-start.7) | collective-permute-done | bytes 65568 | tf_op jit(solution)/shard_map/ppermute | solution.py:363
  56.3 2.9 %collective-permute-done.9.rest_12_ = bf16[384,256]{1,0:T(8,128)(2,1)S(1)} collective-permute-done((bf16[384,256]{1,0:T(8,128)(2,1)S(1)}, bf16[384,256]{1,0:T(8,128)(2,1)S(1)}, u32[]{:S(2)}, u32[]{:S(2)}) %collective-permute-start.9) | collective-permute-done | bytes 196640 | tf_op jit(solution)/shard_map/ppermute | solution.py:391
  59.2 1.4 %shard_map.85 = bf16[256,512]{1,0:T(8,128)(2,1)S(1)} custom-call(s32[1,1024]{1,0:T(1,128)S(1)} %reshape.125.slot_ref, s32[1,32]{1,0:T(1,128)S(1)} %reduce-window_clone.1.ends_ref, bf16[512,512]{1,0:T(8,128)(2,1)S(1)} %bitcast.12, bf16[64,512]{1,0:T(8,128)(2,1)S(1)} %collective-permute-done.rest_1_, bf16[64,512]{1,0:T(8,128)(2,1)S(1)} %collective-permute-done.1.rest_2_, ...), custom_call_target="tpu_custom_call" | custom-call | flops 536870912 | bytes 1966080 | tf_op jit(solution)/shard_map/pallas_call | solution.py:292
  60.6 2.4 %collective-permute-start.10 = (bf16[256,512]{1,0:T(8,128)(2,1)S(1)}, bf16[256,512]{1,0:T(8,128)(2,1)S(1)}, u32[]{:S(2)}, u32[]{:S(2)}) collective-permute-start(bf16[256,512]{1,0:T(8,128)(2,1)S(1)} %shard_map.85), channel_id=1, source_target_pairs={{0,3},{1,2},{2,1},{3,0},{4,7},{5,6},{6,5},{7,4},{8,11},{9,10},{10,... | collective-permute-start | bytes 786440 | tf_op jit(solution)/shard_map/ppermute | solution.py:404
  63.0 1.4 %shard_map.86 = bf16[256,512]{1,0:T(8,128)(2,1)S(1)} custom-call(s32[1,1024]{1,0:T(1,128)S(1)} %reshape.125.slot_ref, s32[1,32]{1,0:T(1,128)S(1)} %reduce-window_clone.1.ends_ref, bf16[512,512]{1,0:T(8,128)(2,1)S(1)} %bitcast.13, bf16[64,512]{1,0:T(8,128)(2,1)S(1)} %collective-permute-done.rest_1_, bf16[64,512]{1,0:T(8,128)(2,1)S(1)} %collective-permute-done.1.rest_2_, ...), custom_call_target="tpu_custom_call" | custom-call | flops 536870912 | bytes 1966080 | tf_op jit(solution)/shard_map/pallas_call | solution.py:292
  65.0 1.4 %shard_map.87 = bf16[256,512]{1,0:T(8,128)(2,1)S(1)} custom-call(s32[1,1024]{1,0:T(1,128)S(1)} %reshape.125.slot_ref, s32[1,32]{1,0:T(1,128)S(1)} %reduce-window_clone.1.ends_ref, bf16[512,512]{1,0:T(8,128)(2,1)S(1)} %bitcast.14, bf16[64,512]{1,0:T(8,128)(2,1)S(1)} %collective-permute-done.rest_1_, bf16[64,512]{1,0:T(8,128)(2,1)S(1)} %collective-permute-done.1.rest_2_, ...), custom_call_target="tpu_custom_call" | custom-call | flops 536870912 | bytes 1966080 | tf_op jit(solution)/shard_map/pallas_call | solution.py:292
  67.1 1.4 %shard_map.88.refs_3_ = bf16[256,512]{1,0:T(8,128)(2,1)S(1)} custom-call(s32[1,1024]{1,0:T(1,128)S(1)} %reshape.125.slot_ref, s32[1,32]{1,0:T(1,128)S(1)} %reduce-window_clone.1.ends_ref, bf16[512,512]{1,0:T(8,128)(2,1)S(1)} %bitcast.15, bf16[64,512]{1,0:T(8,128)(2,1)S(1)} %collective-permute-done.rest_1_, ...), custom_call_target="tpu_custom_call" | custom-call | flops 536870912 | bytes 1966080 | tf_op jit(solution)/shard_map/pallas_call | solution.py:292
  68.5 1.9 %collective-permute-done.10.refs_0_ = bf16[256,512]{1,0:T(8,128)(2,1)S(1)} collective-permute-done((bf16[256,512]{1,0:T(8,128)(2,1)S(1)}, bf16[256,512]{1,0:T(8,128)(2,1)S(1)}, u32[]{:S(2)}, u32[]{:S(2)}) %collective-permute-start.10) | collective-permute-done | bytes 262176 | tf_op jit(solution)/shard_map/ppermute | solution.py:404
  70.4 2.8 %collective-permute-done.11.refs_1_ = bf16[256,512]{1,0:T(8,128)(2,1)S(1)} collective-permute-done((bf16[256,512]{1,0:T(8,128)(2,1)S(1)}, bf16[256,512]{1,0:T(8,128)(2,1)S(1)}, u32[]{:S(2)}, u32[]{:S(2)}) %collective-permute-start.11) | collective-permute-done | bytes 262176 | tf_op jit(solution)/shard_map/ppermute | solution.py:404
  73.2 1.1 %shard_map.89 = bf16[256,2048]{1,0:T(8,128)(2,1)} custom-call(bf16[256,512]{1,0:T(8,128)(2,1)S(1)} %collective-permute-done.10.refs_0_, bf16[256,512]{1,0:T(8,128)(2,1)S(1)} %collective-permute-done.11.refs_1_, bf16[256,512]{1,0:T(8,128)(2,1)S(1)} %collective-permute-done.12.refs_2_, bf16[256,512]{1,0:T(8,128)(2,1)S(1)} %shard_map.88.refs_3_), custom_call_target="tpu_custom_call" | custom-call | bytes 2097152 | tf_op jit(solution)/shard_map/pallas_call | solution.py:320
  (29 shorter events, 3.0 us)
Async XLA Ops:
  7.7 29.8 %all-to-all-start = ((bf16[16,64,256]{2,1,0:T(8,128)(2,1)}), bf16[16,64,256]{2,1,0:T(8,128)(2,1)S(1)}, u32[]{:S(2)}, u32[]{:S(2)}) async-start(bf16[16,64,256]{2,1,0:T(8,128)(2,1)} %bitcast.18), calls=%async_computation | async-start | bytes 1048576 | tf_op jit(solution)/shard_map/all_to_all | solution.py:353
  16.1 21.2 %copy-start = (s32[4096]{0:T(1024)S(1)}, s32[4096]{0:T(1024)}, u32[]{:S(2)}) copy-start(s32[4096]{0:T(1024)} %param.9) | copy-start | bytes 49156
  16.1 21.2 %copy-start.1 = (s32[32]{0:T(128)S(1)}, s32[32]{0:T(128)}, u32[]{:S(2)}) copy-start(s32[32]{0:T(128)} %param.10) | copy-start | bytes 388
  25.9 16.0 %collective-permute-start = (bf16[64,512]{1,0:T(8,128)(2,1)}, bf16[64,512]{1,0:T(8,128)(2,1)S(1)}, u32[]{:S(2)}, u32[]{:S(2)}) collective-permute-start(bf16[64,512]{1,0:T(8,128)(2,1)} %get-tuple-element.33), channel_id=1, source_target_pairs={{0,8},{1,9},{2,10},{3,11},{4,12},{5,13},{6,14},{7,15},{8,0},{9,1},... | collective-permute-start | bytes 196616 | tf_op jit(solution)/shard_map/ppermute | solution.py:363
  28.8 16.1 %collective-permute-start.1 = (bf16[64,512]{1,0:T(8,128)(2,1)}, bf16[64,512]{1,0:T(8,128)(2,1)S(1)}, u32[]{:S(2)}, u32[]{:S(2)}) collective-permute-start(bf16[64,512]{1,0:T(8,128)(2,1)} %get-tuple-element.34), channel_id=1, source_target_pairs={{0,9},{1,8},{2,11},{3,10},{4,13},{5,12},{6,15},{7,14},{8,1},{9,0},... | collective-permute-start | bytes 196616 | tf_op jit(solution)/shard_map/ppermute | solution.py:363
  30.2 17.9 %collective-permute-start.2 = (bf16[64,512]{1,0:T(8,128)(2,1)}, bf16[64,512]{1,0:T(8,128)(2,1)S(1)}, u32[]{:S(2)}, u32[]{:S(2)}) collective-permute-start(bf16[64,512]{1,0:T(8,128)(2,1)} %get-tuple-element.35), channel_id=1, source_target_pairs={{0,10},{1,11},{2,8},{3,9},{4,14},{5,15},{6,12},{7,13},{8,2},{9,3},... | collective-permute-start | bytes 196616 | tf_op jit(solution)/shard_map/ppermute | solution.py:363
  33.5 16.1 %collective-permute-start.3 = (bf16[64,512]{1,0:T(8,128)(2,1)}, bf16[64,512]{1,0:T(8,128)(2,1)S(1)}, u32[]{:S(2)}, u32[]{:S(2)}) collective-permute-start(bf16[64,512]{1,0:T(8,128)(2,1)} %get-tuple-element.36), channel_id=1, source_target_pairs={{0,11},{1,10},{2,9},{3,8},{4,15},{5,14},{6,13},{7,12},{8,3},{9,2},... | collective-permute-start | bytes 196616 | tf_op jit(solution)/shard_map/ppermute | solution.py:363
  33.6 16.0 %collective-permute-start.4 = (bf16[64,512]{1,0:T(8,128)(2,1)}, bf16[64,512]{1,0:T(8,128)(2,1)S(1)}, u32[]{:S(2)}, u32[]{:S(2)}) collective-permute-start(bf16[64,512]{1,0:T(8,128)(2,1)} %get-tuple-element.37), channel_id=1, source_target_pairs={{0,12},{1,13},{2,14},{3,15},{4,8},{5,9},{6,10},{7,11},{8,4},{9,5},... | collective-permute-start | bytes 196616 | tf_op jit(solution)/shard_map/ppermute | solution.py:363
  37.6 21.6 %all-to-all-start.1 = ((bf16[8,64,512]{2,1,0:T(8,128)(2,1)}), bf16[8,64,512]{2,1,0:T(8,128)(2,1)S(1)}, u32[]{:S(2)}, u32[]{:S(2)}) async-start(bf16[8,64,512]{2,1,0:T(8,128)(2,1)} %bitcast.17), calls=%async_computation.1 | async-start | bytes 1048576 | tf_op jit(solution)/shard_map/all_to_all | solution.py:353
  41.8 12.0 %collective-permute-start.5 = (bf16[64,512]{1,0:T(8,128)(2,1)}, bf16[64,512]{1,0:T(8,128)(2,1)S(1)}, u32[]{:S(2)}, u32[]{:S(2)}) collective-permute-start(bf16[64,512]{1,0:T(8,128)(2,1)} %get-tuple-element.43), channel_id=1, source_target_pairs={{0,13},{1,12},{2,15},{3,14},{4,9},{5,8},{6,11},{7,10},{8,5},{9,4},... | collective-permute-start | bytes 196616 | tf_op jit(solution)/shard_map/ppermute | solution.py:363
  44.8 9.0 %collective-permute-start.6 = (bf16[64,512]{1,0:T(8,128)(2,1)}, bf16[64,512]{1,0:T(8,128)(2,1)S(1)}, u32[]{:S(2)}, u32[]{:S(2)}) collective-permute-start(bf16[64,512]{1,0:T(8,128)(2,1)} %get-tuple-element.44), channel_id=1, source_target_pairs={{0,14},{1,15},{2,12},{3,13},{4,10},{5,11},{6,8},{7,9},{8,6},{9,7},... | collective-permute-start | bytes 196616 | tf_op jit(solution)/shard_map/ppermute | solution.py:363
  48.1 8.2 %collective-permute-start.7 = (bf16[64,512]{1,0:T(8,128)(2,1)}, bf16[64,512]{1,0:T(8,128)(2,1)S(1)}, u32[]{:S(2)}, u32[]{:S(2)}) collective-permute-start(bf16[64,512]{1,0:T(8,128)(2,1)} %get-tuple-element.45), channel_id=1, source_target_pairs={{0,15},{1,14},{2,13},{3,12},{4,11},{5,10},{6,9},{7,8},{8,7},{9,6},... | collective-permute-start | bytes 196616 | tf_op jit(solution)/shard_map/ppermute | solution.py:363
  50.3 6.0 %collective-permute-start.8 = (bf16[384,256]{1,0:T(8,128)(2,1)S(1)}, bf16[384,256]{1,0:T(8,128)(2,1)S(1)}, u32[]{:S(2)}, u32[]{:S(2)}) collective-permute-start(bf16[384,256]{1,0:T(8,128)(2,1)S(1)} %get-tuple-element.47.rest_11_), channel_id=1, source_target_pairs={{0,4},{1,5},{2,6},{3,7},{4,8},{5,9},{6,10},{7,11},{8,12},{9,13},{1... | collective-permute-start | bytes 589832 | tf_op jit(solution)/shard_map/ppermute | solution.py:390
  51.6 7.6 %collective-permute-start.9 = (bf16[384,256]{1,0:T(8,128)(2,1)S(1)}, bf16[384,256]{1,0:T(8,128)(2,1)S(1)}, u32[]{:S(2)}, u32[]{:S(2)}) collective-permute-start(bf16[384,256]{1,0:T(8,128)(2,1)S(1)} %get-tuple-element.49.rest_14_), channel_id=1, source_target_pairs={{4,0},{5,1},{6,2},{7,3},{8,4},{9,5},{10,6},{11,7},{12,8},{13,9},{1... | collective-permute-start | bytes 589832 | tf_op jit(solution)/shard_map/ppermute | solution.py:391
  60.6 9.8 %collective-permute-start.10 = (bf16[256,512]{1,0:T(8,128)(2,1)S(1)}, bf16[256,512]{1,0:T(8,128)(2,1)S(1)}, u32[]{:S(2)}, u32[]{:S(2)}) collective-permute-start(bf16[256,512]{1,0:T(8,128)(2,1)S(1)} %shard_map.85), channel_id=1, source_target_pairs={{0,3},{1,2},{2,1},{3,0},{4,7},{5,6},{6,5},{7,4},{8,11},{9,10},{10,... | collective-permute-start | bytes 786440 | tf_op jit(solution)/shard_map/ppermute | solution.py:404
  64.4 8.8 %collective-permute-start.11 = (bf16[256,512]{1,0:T(8,128)(2,1)S(1)}, bf16[256,512]{1,0:T(8,128)(2,1)S(1)}, u32[]{:S(2)}, u32[]{:S(2)}) collective-permute-start(bf16[256,512]{1,0:T(8,128)(2,1)S(1)} %shard_map.86), channel_id=1, source_target_pairs={{0,1},{1,0},{2,3},{3,2},{4,5},{5,4},{6,7},{7,6},{8,9},{9,8},{10,11... | collective-permute-start | bytes 786440 | tf_op jit(solution)/shard_map/ppermute | solution.py:404
  66.4 6.8 %collective-permute-start.12 = (bf16[256,512]{1,0:T(8,128)(2,1)S(1)}, bf16[256,512]{1,0:T(8,128)(2,1)S(1)}, u32[]{:S(2)}, u32[]{:S(2)}) collective-permute-start(bf16[256,512]{1,0:T(8,128)(2,1)S(1)} %shard_map.87), channel_id=1, source_target_pairs={{0,2},{1,3},{2,0},{3,1},{4,6},{5,7},{6,4},{7,5},{8,10},{9,11},{10,... | collective-permute-start | bytes 786440 | tf_op jit(solution)/shard_map/ppermute | solution.py:404

commit v12 on v11

--- a/solution.py
+++ b/solution.py
@@ -34,31 +34,24 @@
     return jnp.minimum(block_id, 2 * devices - 1 - block_id) // members
 
 
-def project_kernel(kinds, devices, members, apart, ready, positions_hbm, freq_hbm, gain_hbm, tokens_hbm, *rest):
+def project_kernel(kinds, devices, members, apart, positions_hbm, freq_hbm, gain_hbm, tokens_hbm, *rest):
     count = len(kinds)
     weights_hbm, rest = rest[:count], rest[count:]
-    outputs = 1 + len(apart) + (not ready)
+    outputs = 1 + len(apart)
     outs_hbm, rest = rest[:outputs], rest[outputs:]
     positions_ref, freq_ref, gain_ref, tokens, normed, weights, out_ref = rest[:7]
-    small_sems, token_sems, sems, out_sems = rest[7:]
+    small_sems, sems, out_sems = rest[7:]
     rows, width = normed.shape
     chunks, _, span = weights.shape
-    parts = token_sems.shape[0]
-    part = rows // parts
-    token_copies, copies, origin = [], [], []
+    copies, origin = [], []
     small_copies = [
         pltpu.make_async_copy(source, target, small_sems.at[i])
         for i, (source, target) in enumerate(
-            [(positions_hbm, positions_ref), (freq_hbm, freq_ref), (gain_hbm, gain_ref)]
+            [(positions_hbm, positions_ref), (freq_hbm, freq_ref), (gain_hbm, gain_ref), (tokens_hbm, tokens)]
         )
     ]
     for copy in small_copies:
         copy.start()
-    for i in range(parts):
-        at = pl.ds(i * part, part)
-        target = normed.at[at] if ready else tokens.at[at]
-        token_copies.append(pltpu.make_async_copy(tokens_hbm.at[at], target, token_sems.at[i]))
-        token_copies[i].start()
     for i in range(count):
         for first in range(0, weights_hbm[i].shape[1], span):
             j = len(copies)
@@ -66,9 +59,7 @@
             copies.append(pltpu.make_async_copy(source, weights.at[j], sems.at[j]))
             origin.append((i, first))
     copies[0].start()
-    if ready and chunks > 1:
-        copies[1].start()
-    for copy in small_copies:
+    for copy in small_copies[:-1]:
         copy.wait()
     lanes = positions_ref.shape[1]
     stripes = rows // lanes
@@ -91,21 +82,17 @@
     step = 32
     written = []
 
-    for i in range(parts):
-        token_copies[i].wait()
-        for first in range(i * part, (i + 1) * part, step) if not ready else ():
-            at = slice(first, first + step)
-            floats = tokens[at, :].astype(jnp.float32)
-            mean = jnp.sum(floats * floats, axis=1, keepdims=True) * (1.0 / width)
-            tokens[at, :] = (floats * lax.rsqrt(mean + EPSILON) * gain).astype(jnp.bfloat16)
-    if not ready:
-        if chunks > 1:
-            copies[1].start()
-        for first in range(0, width, 512):
-            columns = slice(first, first + 512)
-            normed[:, columns] = dot(order, tokens[:, columns]).astype(jnp.bfloat16)
-        written.append(pltpu.make_async_copy(normed, outs_hbm[-1], small_sems.at[0]))
-        written[0].start()
+    small_copies[-1].wait()
+    for first in range(0, rows, step):
+        at = slice(first, first + step)
+        floats = tokens[at, :].astype(jnp.float32)
+        mean = jnp.sum(floats * floats, axis=1, keepdims=True) * (1.0 / width)
+        tokens[at, :] = (floats * lax.rsqrt(mean + EPSILON) * gain).astype(jnp.bfloat16)
+    if chunks > 1:
+        copies[1].start()
+    for first in range(0, width, 512):
+        columns = slice(first, first + 512)
+        normed[:, columns] = dot(order, tokens[:, columns]).astype(jnp.bfloat16)
     groups, heads = out_ref.shape[:2]
     offsets = [0]
     for i in range(count):
@@ -149,18 +136,17 @@
         copy.wait()
 
 
-def project(positions, freq, gain, tokens, weights, kinds, devices, heads, apart=(), ready=False):
+def project(positions, freq, gain, tokens, weights, kinds, devices, heads, apart=()):
     rows, width = tokens.shape
     groups = devices // heads
     columns = sum(w.shape[1] for w in weights)
     span = 512
-    parts = 4
     flops = 2 * rows * width * columns
     size = 2 * (width * columns + rows * width + rows * columns)
     out_shape = (groups // 2 if apart else groups, heads, rows // groups, columns // heads)
-    out_shapes = [out_shape] + [out_shape[2:]] * len(apart) + [(rows, width)] * (not ready)
+    out_shapes = [out_shape] + [out_shape[2:]] * len(apart)
     return pl.pallas_call(
-        functools.partial(project_kernel, kinds, devices, heads, apart, ready),
+        functools.partial(project_kernel, kinds, devices, heads, apart),
         out_shape=[jax.ShapeDtypeStruct(shape, jnp.bfloat16) for shape in out_shapes],
         in_specs=[IN_PLACE] * (len(weights) + 4),
         out_specs=[IN_PLACE] * len(out_shapes),
@@ -168,12 +154,11 @@
             pltpu.VMEM(positions.shape, jnp.int32),
             pltpu.VMEM(freq.shape, jnp.float32),
             pltpu.VMEM(gain.shape, jnp.bfloat16),
-            pltpu.VMEM((8 if ready else rows, width), jnp.bfloat16),
+            pltpu.VMEM((rows, width), jnp.bfloat16),
             pltpu.VMEM((rows, width), jnp.bfloat16),
             pltpu.VMEM((columns // span, width, span), jnp.bfloat16),
             pltpu.VMEM((groups, heads, rows // groups, columns // heads), jnp.bfloat16),
-            pltpu.SemaphoreType.DMA((3,)),
-            pltpu.SemaphoreType.DMA((parts,)),
+            pltpu.SemaphoreType.DMA((4,)),
             pltpu.SemaphoreType.DMA((columns // span,)),
             pltpu.SemaphoreType.DMA((columns // span + len(apart),)),
         ],
@@ -342,7 +327,7 @@
 
     half = HEAD_SIZE // 2
     freq = np.float32(ROPE_THETA ** (-(np.arange(HEAD_SIZE) % half * 2.0 / HEAD_SIZE)))
-    operands = (positions.reshape(-1, 128), jnp.asarray(freq[None, :]), gain)
+    operands = (positions.reshape(-1, 128), jnp.asarray(freq[None, :]), gain, tokens)
 
     half_devices = devices // 2
     halves = [list(range(i, i + half_devices)) for i in (0, half_devices)]
@@ -353,10 +338,10 @@
         flat = lax.all_to_all(flat, "ctx", split_axis=0, concat_axis=0, tiled=True, axis_index_groups=among)
         return flat.reshape(-1, width)
 
-    kv, normed = project(*operands, tokens, (w_key, value_weight), (True, False), devices, members)
+    (kv,) = project(*operands, (w_key, value_weight), (True, False), devices, members)
     kv = exchange(kv, None)
     apart = list(range(half_devices, devices))
-    near, *far = project(*operands, normed, (w_query,), (True,), devices, members, apart, True)
+    near, *far = project(*operands, (w_query,), (True,), devices, members, apart)
     queries = []
     for i, piece in enumerate(far):
         distance = half_devices + i

time: 74.6 us -> 73.2 us (0.981)
  Pallas kernels: 24.9 us -> 23.4 us
    pallas_call x2, Pallas kernels: 17.5 us -> 16 us  [project(): pl.pallas_call(functools.partial(project_kernel, kinds, devices, heads, a...]
where the time goes in v12:
time: 73.2 us; the launch traced here: 72.8 us
  starting transfers between devices  37.4 us (51%)
  Pallas kernels  23.4 us (32%)
  waiting for transfers between devices  10.3 us (14%)
  local copies, waits for them, and re-layouts  0.74 us (1%)
    ppermute x8, starting transfers between devices, shards(): lax.ppermute(piece, 'ctx', [(j, j ^ distance) for j in range(devices)])  19.1 us
    pallas_call x2, Pallas kernels, project(): pl.pallas_call(functools.partial(project_kernel, kinds, devices, heads, a...  16 us
    all_to_all x2, starting transfers between devices, exchange(): lax.all_to_all(flat, 'ctx', split_axis=0, concat_axis=0, tiled=True, axis...  12 us
    pallas_call x4, Pallas kernels, attend(): pl.pallas_call(functools.partial(attend_kernel, block, turn, members, dev...  5.6 us
    ppermute x3, waiting for transfers between devices, shards(): out = lax.ppermute(out, ('dp', 'ctx'), route)  4.74 us
    ppermute x3, starting transfers between devices, shards(): out = lax.ppermute(out, ('dp', 'ctx'), route)  3.69 us
    ppermute x1, waiting for transfers between devices, shards(): late_halo = lax.ppermute(late_tail, 'ctx', down)  2.88 us
    ppermute x8, waiting for transfers between devices, shards(): lax.ppermute(piece, 'ctx', [(j, j ^ distance) for j in range(devices)])  2.66 us
  transfers between devices with their start and end apart: 15, of which 4 were waited for; matrix products, arithmetic and copies ran while one was open for 2% of the time, Pallas kernels for 20%

profile of v12, /device:TPU:0, one launch (start us, length us, event | category | flops | bytes accessed | tf_op | source)
XLA Modules:
  0.0 72.8 jit_solution(13160515864862919139)
XLA Ops:
  0.0 6.5 %shard_map.82 = bf16[4,4,64,256]{3,2,1,0:T(8,128)(2,1)} custom-call(s32[32,128]{1,0:T(8,128)} %bitcast.19, f32[1,128]{1,0:T(1,128)} %constant.78.clone.freq_hbm, bf16[4096]{0:T(1024)(128)(2,1)} %gain_hbm.3, bf16[256,4096]{1,0:T(8,128)(2,1)} %tokens_hbm.3, bf16[4096,512]{1,0:T(8,128)(2,1)} %rest_0_.2, bf16[4096,512]{1,0:T(8,128)(2,1)} %rest_1_.1), custom_call_target="tpu_custom_call" | custom-call | flops 2147483648 | bytes 11010048 | tf_op jit(solution)/shard_map/pallas_call | solution.py:148
  6.5 8.3 %all-to-all-start = ((bf16[16,64,256]{2,1,0:T(8,128)(2,1)}), bf16[16,64,256]{2,1,0:T(8,128)(2,1)S(1)}, u32[]{:S(2)}, u32[]{:S(2)}) async-start(bf16[16,64,256]{2,1,0:T(8,128)(2,1)} %bitcast.17), calls=%async_computation | async-start | bytes 1048576 | tf_op jit(solution)/shard_map/all_to_all | solution.py:338
  14.9 9.5 %shard_map.83 = (bf16[2,4,64,512]{3,2,1,0:T(8,128)(2,1)}, bf16[64,512]{1,0:T(8,128)(2,1)}, bf16[64,512]{1,0:T(8,128)(2,1)}, bf16[64,512]{1,0:T(8,128)(2,1)}, bf1...) custom-call(s32[32,128]{1,0:T(8,128)} %bitcast.20, ...), custom_call_target="tpu_custom_call" | custom-call | flops 4294967296 | bytes 19922944 | tf_op jit(solution)/shard_map/pallas_call | solution.py:148
  24.4 2.9 %collective-permute-start = (bf16[64,512]{1,0:T(8,128)(2,1)}, bf16[64,512]{1,0:T(8,128)(2,1)S(1)}, u32[]{:S(2)}, u32[]{:S(2)}) collective-permute-start(bf16[64,512]{1,0:T(8,128)(2,1)} %get-tuple-element.29), channel_id=1, source_target_pairs={{0,8},{1,9},{2,10},{3,11},{4,12},{5,13},{6,14},{7,15},{8,0},{9,1},... | collective-permute-start | bytes 196616 | tf_op jit(solution)/shard_map/ppermute | solution.py:348
  27.3 1.5 %collective-permute-start.1 = (bf16[64,512]{1,0:T(8,128)(2,1)}, bf16[64,512]{1,0:T(8,128)(2,1)S(1)}, u32[]{:S(2)}, u32[]{:S(2)}) collective-permute-start(bf16[64,512]{1,0:T(8,128)(2,1)} %get-tuple-element.30), channel_id=1, source_target_pairs={{0,9},{1,8},{2,11},{3,10},{4,13},{5,12},{6,15},{7,14},{8,1},{9,0},... | collective-permute-start | bytes 196616 | tf_op jit(solution)/shard_map/ppermute | solution.py:348
  28.8 3.3 %collective-permute-start.2 = (bf16[64,512]{1,0:T(8,128)(2,1)}, bf16[64,512]{1,0:T(8,128)(2,1)S(1)}, u32[]{:S(2)}, u32[]{:S(2)}) collective-permute-start(bf16[64,512]{1,0:T(8,128)(2,1)} %get-tuple-element.31), channel_id=1, source_target_pairs={{0,10},{1,11},{2,8},{3,9},{4,14},{5,15},{6,12},{7,13},{8,2},{9,3},... | collective-permute-start | bytes 196616 | tf_op jit(solution)/shard_map/ppermute | solution.py:348
  32.1 3.7 %collective-permute-start.4 = (bf16[64,512]{1,0:T(8,128)(2,1)}, bf16[64,512]{1,0:T(8,128)(2,1)S(1)}, u32[]{:S(2)}, u32[]{:S(2)}) collective-permute-start(bf16[64,512]{1,0:T(8,128)(2,1)} %get-tuple-element.33), channel_id=1, source_target_pairs={{0,12},{1,13},{2,14},{3,15},{4,8},{5,9},{6,10},{7,11},{8,4},{9,5},... | collective-permute-start | bytes 196616 | tf_op jit(solution)/shard_map/ppermute | solution.py:348
  36.1 3.7 %all-to-all-start.1 = ((bf16[8,64,512]{2,1,0:T(8,128)(2,1)}), bf16[8,64,512]{2,1,0:T(8,128)(2,1)S(1)}, u32[]{:S(2)}, u32[]{:S(2)}) async-start(bf16[8,64,512]{2,1,0:T(8,128)(2,1)} %bitcast.18), calls=%async_computation.1 | async-start | bytes 1048576 | tf_op jit(solution)/shard_map/all_to_all | solution.py:338
  40.4 2.9 %collective-permute-start.5 = (bf16[64,512]{1,0:T(8,128)(2,1)}, bf16[64,512]{1,0:T(8,128)(2,1)S(1)}, u32[]{:S(2)}, u32[]{:S(2)}) collective-permute-start(bf16[64,512]{1,0:T(8,128)(2,1)} %get-tuple-element.39), channel_id=1, source_target_pairs={{0,13},{1,12},{2,15},{3,14},{4,9},{5,8},{6,11},{7,10},{8,5},{9,4},... | collective-permute-start | bytes 196616 | tf_op jit(solution)/shard_map/ppermute | solution.py:348
  43.4 3.3 %collective-permute-start.6 = (bf16[64,512]{1,0:T(8,128)(2,1)}, bf16[64,512]{1,0:T(8,128)(2,1)S(1)}, u32[]{:S(2)}, u32[]{:S(2)}) collective-permute-start(bf16[64,512]{1,0:T(8,128)(2,1)} %get-tuple-element.40), channel_id=1, source_target_pairs={{0,14},{1,15},{2,12},{3,13},{4,10},{5,11},{6,8},{7,9},{8,6},{9,7},... | collective-permute-start | bytes 196616 | tf_op jit(solution)/shard_map/ppermute | solution.py:348
  46.6 1.5 %collective-permute-start.7 = (bf16[64,512]{1,0:T(8,128)(2,1)}, bf16[64,512]{1,0:T(8,128)(2,1)S(1)}, u32[]{:S(2)}, u32[]{:S(2)}) collective-permute-start(bf16[64,512]{1,0:T(8,128)(2,1)} %get-tuple-element.41), channel_id=1, source_target_pairs={{0,15},{1,14},{2,13},{3,12},{4,11},{5,10},{6,9},{7,8},{8,7},{9,6},... | collective-permute-start | bytes 196616 | tf_op jit(solution)/shard_map/ppermute | solution.py:348
  48.1 0.7 shard_map.84
  48.8 1.3 %collective-permute-start.8 = (bf16[384,256]{1,0:T(8,128)(2,1)S(1)}, bf16[384,256]{1,0:T(8,128)(2,1)S(1)}, u32[]{:S(2)}, u32[]{:S(2)}) collective-permute-start(bf16[384,256]{1,0:T(8,128)(2,1)S(1)} %get-tuple-element.43.rest_11_), channel_id=1, source_target_pairs={{0,4},{1,5},{2,6},{3,7},{4,8},{5,9},{6,10},{7,11},{8,12},{9,13},{1... | collective-permute-start | bytes 589832 | tf_op jit(solution)/shard_map/ppermute | solution.py:375
  50.1 1.3 %collective-permute-start.9 = (bf16[384,256]{1,0:T(8,128)(2,1)S(1)}, bf16[384,256]{1,0:T(8,128)(2,1)S(1)}, u32[]{:S(2)}, u32[]{:S(2)}) collective-permute-start(bf16[384,256]{1,0:T(8,128)(2,1)S(1)} %get-tuple-element.45.rest_14_), channel_id=1, source_target_pairs={{4,0},{5,1},{6,2},{7,3},{8,4},{9,5},{10,6},{11,7},{12,8},{13,9},{1... | collective-permute-start | bytes 589832 | tf_op jit(solution)/shard_map/ppermute | solution.py:376
  52.2 2.6 %collective-permute-done.7.rest_8_ = bf16[64,512]{1,0:T(8,128)(2,1)S(1)} collective-permute-done((bf16[64,512]{1,0:T(8,128)(2,1)}, bf16[64,512]{1,0:T(8,128)(2,1)S(1)}, u32[]{:S(2)}, u32[]{:S(2)}) %collective-permute-start.7) | collective-permute-done | bytes 65568 | tf_op jit(solution)/shard_map/ppermute | solution.py:348
  54.8 2.9 %collective-permute-done.9.rest_12_ = bf16[384,256]{1,0:T(8,128)(2,1)S(1)} collective-permute-done((bf16[384,256]{1,0:T(8,128)(2,1)S(1)}, bf16[384,256]{1,0:T(8,128)(2,1)S(1)}, u32[]{:S(2)}, u32[]{:S(2)}) %collective-permute-start.9) | collective-permute-done | bytes 196640 | tf_op jit(solution)/shard_map/ppermute | solution.py:376
  57.7 1.4 %shard_map.85 = bf16[256,512]{1,0:T(8,128)(2,1)S(1)} custom-call(s32[1,1024]{1,0:T(1,128)S(1)} %reshape.125.slot_ref, s32[1,32]{1,0:T(1,128)S(1)} %reduce-window_clone.1.ends_ref, bf16[512,512]{1,0:T(8,128)(2,1)S(1)} %bitcast.12, bf16[64,512]{1,0:T(8,128)(2,1)S(1)} %collective-permute-done.rest_1_, bf16[64,512]{1,0:T(8,128)(2,1)S(1)} %collective-permute-done.1.rest_2_, ...), custom_call_target="tpu_custom_call" | custom-call | flops 536870912 | bytes 1966080 | tf_op jit(solution)/shard_map/pallas_call | solution.py:277
  59.1 2.4 %collective-permute-start.10 = (bf16[256,512]{1,0:T(8,128)(2,1)S(1)}, bf16[256,512]{1,0:T(8,128)(2,1)S(1)}, u32[]{:S(2)}, u32[]{:S(2)}) collective-permute-start(bf16[256,512]{1,0:T(8,128)(2,1)S(1)} %shard_map.85), channel_id=1, source_target_pairs={{0,3},{1,2},{2,1},{3,0},{4,7},{5,6},{6,5},{7,4},{8,11},{9,10},{10,... | collective-permute-start | bytes 786440 | tf_op jit(solution)/shard_map/ppermute | solution.py:389
  61.5 1.4 %shard_map.86 = bf16[256,512]{1,0:T(8,128)(2,1)S(1)} custom-call(s32[1,1024]{1,0:T(1,128)S(1)} %reshape.125.slot_ref, s32[1,32]{1,0:T(1,128)S(1)} %reduce-window_clone.1.ends_ref, bf16[512,512]{1,0:T(8,128)(2,1)S(1)} %bitcast.13, bf16[64,512]{1,0:T(8,128)(2,1)S(1)} %collective-permute-done.rest_1_, bf16[64,512]{1,0:T(8,128)(2,1)S(1)} %collective-permute-done.1.rest_2_, ...), custom_call_target="tpu_custom_call" | custom-call | flops 536870912 | bytes 1966080 | tf_op jit(solution)/shard_map/pallas_call | solution.py:277
  63.6 1.4 %shard_map.87 = bf16[256,512]{1,0:T(8,128)(2,1)S(1)} custom-call(s32[1,1024]{1,0:T(1,128)S(1)} %reshape.125.slot_ref, s32[1,32]{1,0:T(1,128)S(1)} %reduce-window_clone.1.ends_ref, bf16[512,512]{1,0:T(8,128)(2,1)S(1)} %bitcast.14, bf16[64,512]{1,0:T(8,128)(2,1)S(1)} %collective-permute-done.rest_1_, bf16[64,512]{1,0:T(8,128)(2,1)S(1)} %collective-permute-done.1.rest_2_, ...), custom_call_target="tpu_custom_call" | custom-call | flops 536870912 | bytes 1966080 | tf_op jit(solution)/shard_map/pallas_call | solution.py:277
  65.6 1.4 %shard_map.88.refs_3_ = bf16[256,512]{1,0:T(8,128)(2,1)S(1)} custom-call(s32[1,1024]{1,0:T(1,128)S(1)} %reshape.125.slot_ref, s32[1,32]{1,0:T(1,128)S(1)} %reduce-window_clone.1.ends_ref, bf16[512,512]{1,0:T(8,128)(2,1)S(1)} %bitcast.15, bf16[64,512]{1,0:T(8,128)(2,1)S(1)} %collective-permute-done.rest_1_, ...), custom_call_target="tpu_custom_call" | custom-call | flops 536870912 | bytes 1966080 | tf_op jit(solution)/shard_map/pallas_call | solution.py:277
  67.0 2.0 %collective-permute-done.10.refs_0_ = bf16[256,512]{1,0:T(8,128)(2,1)S(1)} collective-permute-done((bf16[256,512]{1,0:T(8,128)(2,1)S(1)}, bf16[256,512]{1,0:T(8,128)(2,1)S(1)}, u32[]{:S(2)}, u32[]{:S(2)}) %collective-permute-start.10) | collective-permute-done | bytes 262176 | tf_op jit(solution)/shard_map/ppermute | solution.py:389
  69.0 2.8 %collective-permute-done.11.refs_1_ = bf16[256,512]{1,0:T(8,128)(2,1)S(1)} collective-permute-done((bf16[256,512]{1,0:T(8,128)(2,1)S(1)}, bf16[256,512]{1,0:T(8,128)(2,1)S(1)}, u32[]{:S(2)}, u32[]{:S(2)}) %collective-permute-start.11) | collective-permute-done | bytes 262176 | tf_op jit(solution)/shard_map/ppermute | solution.py:389
  71.8 1.1 %shard_map.89 = bf16[256,2048]{1,0:T(8,128)(2,1)} custom-call(bf16[256,512]{1,0:T(8,128)(2,1)S(1)} %collective-permute-done.10.refs_0_, bf16[256,512]{1,0:T(8,128)(2,1)S(1)} %collective-permute-done.11.refs_1_, bf16[256,512]{1,0:T(8,128)(2,1)S(1)} %collective-permute-done.12.refs_2_, bf16[256,512]{1,0:T(8,128)(2,1)S(1)} %shard_map.88.refs_3_), custom_call_target="tpu_custom_call" | custom-call | bytes 2097152 | tf_op jit(solution)/shard_map/pallas_call | solution.py:305
  (29 shorter events, 3.0 us)
Async XLA Ops:
  6.5 29.6 %all-to-all-start = ((bf16[16,64,256]{2,1,0:T(8,128)(2,1)}), bf16[16,64,256]{2,1,0:T(8,128)(2,1)S(1)}, u32[]{:S(2)}, u32[]{:S(2)}) async-start(bf16[16,64,256]{2,1,0:T(8,128)(2,1)} %bitcast.17), calls=%async_computation | async-start | bytes 1048576 | tf_op jit(solution)/shard_map/all_to_all | solution.py:338
  14.9 21.0 %copy-start = (s32[4096]{0:T(1024)S(1)}, s32[4096]{0:T(1024)}, u32[]{:S(2)}) copy-start(s32[4096]{0:T(1024)} %param.9) | copy-start | bytes 49156
  14.9 21.0 %copy-start.1 = (s32[32]{0:T(128)S(1)}, s32[32]{0:T(128)}, u32[]{:S(2)}) copy-start(s32[32]{0:T(128)} %param.10) | copy-start | bytes 388
  24.4 16.0 %collective-permute-start = (bf16[64,512]{1,0:T(8,128)(2,1)}, bf16[64,512]{1,0:T(8,128)(2,1)S(1)}, u32[]{:S(2)}, u32[]{:S(2)}) collective-permute-start(bf16[64,512]{1,0:T(8,128)(2,1)} %get-tuple-element.29), channel_id=1, source_target_pairs={{0,8},{1,9},{2,10},{3,11},{4,12},{5,13},{6,14},{7,15},{8,0},{9,1},... | collective-permute-start | bytes 196616 | tf_op jit(solution)/shard_map/ppermute | solution.py:348
  27.3 16.1 %collective-permute-start.1 = (bf16[64,512]{1,0:T(8,128)(2,1)}, bf16[64,512]{1,0:T(8,128)(2,1)S(1)}, u32[]{:S(2)}, u32[]{:S(2)}) collective-permute-start(bf16[64,512]{1,0:T(8,128)(2,1)} %get-tuple-element.30), channel_id=1, source_target_pairs={{0,9},{1,8},{2,11},{3,10},{4,13},{5,12},{6,15},{7,14},{8,1},{9,0},... | collective-permute-start | bytes 196616 | tf_op jit(solution)/shard_map/ppermute | solution.py:348
  28.8 17.9 %collective-permute-start.2 = (bf16[64,512]{1,0:T(8,128)(2,1)}, bf16[64,512]{1,0:T(8,128)(2,1)S(1)}, u32[]{:S(2)}, u32[]{:S(2)}) collective-permute-start(bf16[64,512]{1,0:T(8,128)(2,1)} %get-tuple-element.31), channel_id=1, source_target_pairs={{0,10},{1,11},{2,8},{3,9},{4,14},{5,15},{6,12},{7,13},{8,2},{9,3},... | collective-permute-start | bytes 196616 | tf_op jit(solution)/shard_map/ppermute | solution.py:348
  32.0 16.1 %collective-permute-start.3 = (bf16[64,512]{1,0:T(8,128)(2,1)}, bf16[64,512]{1,0:T(8,128)(2,1)S(1)}, u32[]{:S(2)}, u32[]{:S(2)}) collective-permute-start(bf16[64,512]{1,0:T(8,128)(2,1)} %get-tuple-element.32), channel_id=1, source_target_pairs={{0,11},{1,10},{2,9},{3,8},{4,15},{5,14},{6,13},{7,12},{8,3},{9,2},... | collective-permute-start | bytes 196616 | tf_op jit(solution)/shard_map/ppermute | solution.py:348
  32.1 16.0 %collective-permute-start.4 = (bf16[64,512]{1,0:T(8,128)(2,1)}, bf16[64,512]{1,0:T(8,128)(2,1)S(1)}, u32[]{:S(2)}, u32[]{:S(2)}) collective-permute-start(bf16[64,512]{1,0:T(8,128)(2,1)} %get-tuple-element.33), channel_id=1, source_target_pairs={{0,12},{1,13},{2,14},{3,15},{4,8},{5,9},{6,10},{7,11},{8,4},{9,5},... | collective-permute-start | bytes 196616 | tf_op jit(solution)/shard_map/ppermute | solution.py:348
  36.1 21.6 %all-to-all-start.1 = ((bf16[8,64,512]{2,1,0:T(8,128)(2,1)}), bf16[8,64,512]{2,1,0:T(8,128)(2,1)S(1)}, u32[]{:S(2)}, u32[]{:S(2)}) async-start(bf16[8,64,512]{2,1,0:T(8,128)(2,1)} %bitcast.18), calls=%async_computation.1 | async-start | bytes 1048576 | tf_op jit(solution)/shard_map/all_to_all | solution.py:338
  40.4 11.8 %collective-permute-start.5 = (bf16[64,512]{1,0:T(8,128)(2,1)}, bf16[64,512]{1,0:T(8,128)(2,1)S(1)}, u32[]{:S(2)}, u32[]{:S(2)}) collective-permute-start(bf16[64,512]{1,0:T(8,128)(2,1)} %get-tuple-element.39), channel_id=1, source_target_pairs={{0,13},{1,12},{2,15},{3,14},{4,9},{5,8},{6,11},{7,10},{8,5},{9,4},... | collective-permute-start | bytes 196616 | tf_op jit(solution)/shard_map/ppermute | solution.py:348
  43.4 8.8 %collective-permute-start.6 = (bf16[64,512]{1,0:T(8,128)(2,1)}, bf16[64,512]{1,0:T(8,128)(2,1)S(1)}, u32[]{:S(2)}, u32[]{:S(2)}) collective-permute-start(bf16[64,512]{1,0:T(8,128)(2,1)} %get-tuple-element.40), channel_id=1, source_target_pairs={{0,14},{1,15},{2,12},{3,13},{4,10},{5,11},{6,8},{7,9},{8,6},{9,7},... | collective-permute-start | bytes 196616 | tf_op jit(solution)/shard_map/ppermute | solution.py:348
  46.6 8.2 %collective-permute-start.7 = (bf16[64,512]{1,0:T(8,128)(2,1)}, bf16[64,512]{1,0:T(8,128)(2,1)S(1)}, u32[]{:S(2)}, u32[]{:S(2)}) collective-permute-start(bf16[64,512]{1,0:T(8,128)(2,1)} %get-tuple-element.41), channel_id=1, source_target_pairs={{0,15},{1,14},{2,13},{3,12},{4,11},{5,10},{6,9},{7,8},{8,7},{9,6},... | collective-permute-start | bytes 196616 | tf_op jit(solution)/shard_map/ppermute | solution.py:348
  48.8 6.0 %collective-permute-start.8 = (bf16[384,256]{1,0:T(8,128)(2,1)S(1)}, bf16[384,256]{1,0:T(8,128)(2,1)S(1)}, u32[]{:S(2)}, u32[]{:S(2)}) collective-permute-start(bf16[384,256]{1,0:T(8,128)(2,1)S(1)} %get-tuple-element.43.rest_11_), channel_id=1, source_target_pairs={{0,4},{1,5},{2,6},{3,7},{4,8},{5,9},{6,10},{7,11},{8,12},{9,13},{1... | collective-permute-start | bytes 589832 | tf_op jit(solution)/shard_map/ppermute | solution.py:375
  50.1 7.6 %collective-permute-start.9 = (bf16[384,256]{1,0:T(8,128)(2,1)S(1)}, bf16[384,256]{1,0:T(8,128)(2,1)S(1)}, u32[]{:S(2)}, u32[]{:S(2)}) collective-permute-start(bf16[384,256]{1,0:T(8,128)(2,1)S(1)} %get-tuple-element.45.rest_14_), channel_id=1, source_target_pairs={{4,0},{5,1},{6,2},{7,3},{8,4},{9,5},{10,6},{11,7},{12,8},{13,9},{1... | collective-permute-start | bytes 589832 | tf_op jit(solution)/shard_map/ppermute | solution.py:376
  59.1 9.9 %collective-permute-start.10 = (bf16[256,512]{1,0:T(8,128)(2,1)S(1)}, bf16[256,512]{1,0:T(8,128)(2,1)S(1)}, u32[]{:S(2)}, u32[]{:S(2)}) collective-permute-start(bf16[256,512]{1,0:T(8,128)(2,1)S(1)} %shard_map.85), channel_id=1, source_target_pairs={{0,3},{1,2},{2,1},{3,0},{4,7},{5,6},{6,5},{7,4},{8,11},{9,10},{10,... | collective-permute-start | bytes 786440 | tf_op jit(solution)/shard_map/ppermute | solution.py:389
  63.0 8.8 %collective-permute-start.11 = (bf16[256,512]{1,0:T(8,128)(2,1)S(1)}, bf16[256,512]{1,0:T(8,128)(2,1)S(1)}, u32[]{:S(2)}, u32[]{:S(2)}) collective-permute-start(bf16[256,512]{1,0:T(8,128)(2,1)S(1)} %shard_map.86), channel_id=1, source_target_pairs={{0,1},{1,0},{2,3},{3,2},{4,5},{5,4},{6,7},{7,6},{8,9},{9,8},{10,11... | collective-permute-start | bytes 786440 | tf_op jit(solution)/shard_map/ppermute | solution.py:389
  65.0 6.8 %collective-permute-start.12 = (bf16[256,512]{1,0:T(8,128)(2,1)S(1)}, bf16[256,512]{1,0:T(8,128)(2,1)S(1)}, u32[]{:S(2)}, u32[]{:S(2)}) collective-permute-start(bf16[256,512]{1,0:T(8,128)(2,1)S(1)} %shard_map.87), channel_id=1, source_target_pairs={{0,2},{1,3},{2,0},{3,1},{4,6},{5,7},{6,4},{7,5},{8,10},{9,11},{10,... | collective-permute-start | bytes 786440 | tf_op jit(solution)/shard_map/ppermute | solution.py:389

commit v13 on v12

--- a/solution.py
+++ b/solution.py
@@ -37,7 +37,8 @@
 def project_kernel(kinds, devices, members, apart, positions_hbm, freq_hbm, gain_hbm, tokens_hbm, *rest):
     count = len(kinds)
     weights_hbm, rest = rest[:count], rest[count:]
-    outputs = 1 + len(apart)
+    groups = devices // members
+    outputs = 1 + len(apart) if apart else groups
     outs_hbm, rest = rest[:outputs], rest[outputs:]
     positions_ref, freq_ref, gain_ref, tokens, normed, weights, out_ref = rest[:7]
     small_sems, sems, out_sems = rest[7:]
@@ -93,7 +94,7 @@
     for first in range(0, width, 512):
         columns = slice(first, first + 512)
         normed[:, columns] = dot(order, tokens[:, columns]).astype(jnp.bfloat16)
-    groups, heads = out_ref.shape[:2]
+    heads = out_ref.shape[1]
     offsets = [0]
     for i in range(count):
         offsets.append(offsets[-1] + weights_hbm[i].shape[1] // heads)
@@ -123,11 +124,16 @@
         first_head, done_heads = first // per_head, max(span // per_head, 1)
         done = (pl.ds(first_head, done_heads), pl.ds(0, rows // groups))
         done += (pl.ds(offsets[i] + first % per_head, min(span, per_head)),)
-        taken = groups // 2 if apart else groups
-        start = me // members // taken * taken if apart else 0
-        source = out_ref.at[(pl.ds(start, taken),) + done]
-        written.append(pltpu.make_async_copy(source, outs_hbm[0].at[(pl.ds(0, taken),) + done], out_sems.at[j]))
-        written[-1].start()
+        if apart:
+            near = groups // 2
+            source = out_ref.at[(pl.ds(me // members // near * near, near),) + done]
+            written.append(pltpu.make_async_copy(source, outs_hbm[0].at[(pl.ds(0, near),) + done], out_sems.at[j]))
+            written[-1].start()
+        for distance in () if apart else range(groups):
+            source = out_ref.at[(me // members ^ distance,) + done]
+            sem = out_sems.at[j * groups + distance]
+            written.append(pltpu.make_async_copy(source, outs_hbm[distance].at[done], sem))
+            written[-1].start()
         if first % per_head + span >= per_head:
             for distance, copy in zip(apart, far):
                 to = (me ^ distance) % members
@@ -143,8 +149,8 @@
     span = 512
     flops = 2 * rows * width * columns
     size = 2 * (width * columns + rows * width + rows * columns)
-    out_shape = (groups // 2 if apart else groups, heads, rows // groups, columns // heads)
-    out_shapes = [out_shape] + [out_shape[2:]] * len(apart)
+    piece = (rows // groups, columns // heads)
+    out_shapes = [(groups // 2, heads) + piece] + [piece] * len(apart) if apart else [(heads,) + piece] * groups
     return pl.pallas_call(
         functools.partial(project_kernel, kinds, devices, heads, apart),
         out_shape=[jax.ShapeDtypeStruct(shape, jnp.bfloat16) for shape in out_shapes],
@@ -160,38 +166,68 @@
             pltpu.VMEM((groups, heads, rows // groups, columns // heads), jnp.bfloat16),
             pltpu.SemaphoreType.DMA((4,)),
             pltpu.SemaphoreType.DMA((columns // span,)),
-            pltpu.SemaphoreType.DMA((columns // span + len(apart),)),
+            pltpu.SemaphoreType.DMA((columns // span * groups + len(apart),)),
         ],
         compiler_params=pltpu.CompilerParams(vmem_limit_bytes=56 * MIB),
         cost_estimate=pl.CostEstimate(flops=flops, bytes_accessed=size, transcendentals=0),
     )(positions, freq, gain, tokens, *weights)
 
 
-def place_kernel(arrived_ref, slot_ref, *outs):
-    rows = arrived_ref.shape[0]
+def pick_kernel(members, *refs):
+    pieces, outs = refs[:-members], refs[-members:]
+    rows = pieces[0].shape[1]
+    for distance, out_ref in enumerate(outs):
+        head = lax.axis_index("ctx") % members ^ distance
+        for i, piece in enumerate(pieces):
+            out_ref[i * rows : (i + 1) * rows, :] = piece[head]
+
+
+def pick(pieces):
+    members, rows, width = pieces[0].shape
+    shape = jax.ShapeDtypeStruct((len(pieces) * rows, width), jnp.bfloat16)
+    return pl.pallas_call(
+        functools.partial(pick_kernel, members),
+        out_shape=[shape] * members,
+        in_specs=[WHOLE] * len(pieces),
+        out_specs=[WHOLE] * members,
+        compiler_params=pltpu.CompilerParams(vmem_limit_bytes=8 * MIB),
+        cost_estimate=pl.CostEstimate(
+            flops=0, bytes_accessed=4 * len(pieces) * pieces[0].size, transcendentals=0
+        ),
+    )(*pieces)
+
+
+def place_kernel(count, slot_ref, *refs):
+    arrived, outs = refs[:count], refs[count:]
+    slot = slot_ref[...]
     first = 0
     for out_ref in outs:
         size = out_ref.shape[0]
-        slots = lax.broadcasted_iota(jnp.int32, (size, rows), 0) + first
-        chosen = (slots == slot_ref[...]).astype(jnp.bfloat16)
-        out_ref[...] = dot(chosen, arrived_ref[...]).astype(jnp.bfloat16)
+        slots = lax.broadcasted_iota(jnp.int32, (size, slot.shape[1]), 0) + first
+        chosen = (slots == slot).astype(jnp.bfloat16)
+        total = 0.0
+        at = 0
+        for ref in arrived:
+            total += dot(chosen[:, at : at + ref.shape[0]], ref[...])
+            at += ref.shape[0]
+        out_ref[...] = total.astype(jnp.bfloat16)
         first += size
 
 
 def place(arrived, slot, sizes):
-    width = arrived.shape[1]
+    width = arrived[0].shape[1]
     return pl.pallas_call(
-        place_kernel,
+        functools.partial(place_kernel, len(arrived)),
         out_shape=[jax.ShapeDtypeStruct((size, width), jnp.bfloat16) for size in sizes],
-        in_specs=[WHOLE, WHOLE],
+        in_specs=[WHOLE] * (1 + len(arrived)),
         out_specs=[WHOLE] * len(sizes),
         compiler_params=pltpu.CompilerParams(vmem_limit_bytes=16 * MIB),
         cost_estimate=pl.CostEstimate(
-            flops=2 * sum(sizes) * arrived.shape[0] * width,
-            bytes_accessed=4 * arrived.size,
+            flops=2 * sum(sizes) * slot.shape[1] * width,
+            bytes_accessed=4 * slot.shape[1] * width,
             transcendentals=0,
         ),
-    )(arrived, slot)
+    )(slot, *arrived)
 
 
 def taken_at(turn, members):
@@ -332,20 +368,14 @@
     half_devices = devices // 2
     halves = [list(range(i, i + half_devices)) for i in (0, half_devices)]
 
-    def exchange(ordered, among):
-        width = ordered.shape[3]
-        flat = ordered.reshape(-1, group_rows, width)
-        flat = lax.all_to_all(flat, "ctx", split_axis=0, concat_axis=0, tiled=True, axis_index_groups=among)
-        return flat.reshape(-1, width)
-
-    (kv,) = project(*operands, (w_key, value_weight), (True, False), devices, members)
-    kv = exchange(kv, None)
+    def permuted(piece, distance):
+        return lax.ppermute(piece, "ctx", [(j, j ^ distance) for j in range(devices)])
+
+    pieces = list(project(*operands, (w_key, value_weight), (True, False), devices, members))
+    pieces = pieces[:1] + [permuted(piece, i * members) for i, piece in enumerate(pieces) if i]
     apart = list(range(half_devices, devices))
     near, *far = project(*operands, (w_query,), (True,), devices, members, apart)
-    queries = []
-    for i, piece in enumerate(far):
-        distance = half_devices + i
-        queries.append(lax.ppermute(piece, "ctx", [(j, j ^ distance) for j in range(devices)]))
+    queries = [permuted(piece, distance) for distance, piece in zip(apart, far)]
 
     table = positions.reshape(devices, rows)
     ours = group_of(table, block, devices, members) == group
@@ -358,18 +388,24 @@
     place_in = jnp.where(ours, place_in, -1)
     wanted = jnp.arange(group_rows, dtype=jnp.int32)[None, :, None] == place_in[:, None, :]
     slot = jnp.sum(jnp.where(wanted, slots[:, None, :], 0), axis=2)
-    index = jnp.arange(half_devices, dtype=jnp.int32)
-    sources = [device // half_devices * half_devices + index, device ^ (half_devices + index)]
-    query_slot = slot[jnp.concatenate(sources)].reshape(1, devices * group_rows)
-    slot = slot.reshape(1, devices * group_rows)
+    index = jnp.arange(devices, dtype=jnp.int32)
+    kv_order = (device ^ (index // groups)) ^ (index % groups * members)
+    index = index[:half_devices]
+    query_order = [device // half_devices * half_devices + index, device ^ (half_devices + index)]
+    slots = slot[jnp.concatenate([kv_order] + query_order)].reshape(2, 1, devices * group_rows)
+    kv_slot, query_slot = slots[0], slots[1]
     ends = jnp.cumsum(lengths, dtype=jnp.int32)[None, :]
 
-    kv, near = lax.optimization_barrier((kv, near))
-    queries.insert(0, exchange(near, halves))
-    kv, *queries[1:6] = lax.optimization_barrier((kv, *queries[1:6]))
+    *pieces, queries[0], queries[1] = lax.optimization_barrier((*pieces, queries[0], queries[1]))
+    *picked, near = lax.optimization_barrier((*pick(pieces), near))
+    kv = picked[:1] + [permuted(piece, i) for i, piece in enumerate(picked) if i]
+    flat = near.reshape(half_devices, group_rows, -1)
+    flat = lax.all_to_all(flat, "ctx", split_axis=0, concat_axis=0, tiled=True, axis_index_groups=halves)
+    kv, queries[:5] = lax.optimization_barrier((kv, queries[:5]))
+    queries.insert(0, flat.reshape(half_devices * group_rows, -1))
     reach = REACH_BLOCKS * block
     sizes = [run - reach, reach] * 2
-    early_head, early_tail, late_head, late_tail = place(kv, slot, sizes)
+    early_head, early_tail, late_head, late_tail = place(kv, kv_slot, sizes)
     up = [(i, i + members) for i in range(devices - members)]
     down = [(i + members, i) for i in range(devices - members)]
     early_halo = lax.ppermute(early_tail, "ctx", up)

time: 73.2 us -> 86.7 us (1.18)
  starting transfers between devices: 37.4 us -> 44.5 us
  waiting for transfers between devices: 10.3 us -> 16.5 us
    ppermute x8 -> x14, starting transfers between devices: 19.1 us -> 32.2 us  [permuted(): lax.ppermute(piece, 'ctx', [(j, j ^ distance) for j in range(devices)])]
    ppermute x8 -> x14, waiting for transfers between devices: 2.66 us -> 11.8 us  [permuted(): lax.ppermute(piece, 'ctx', [(j, j ^ distance) for j in range(devices)])]
    all_to_all x2 -> x1, starting transfers between devices: 12 us -> 3.9 us  [shards(): lax.all_to_all(flat, 'ctx', split_axis=0, concat_axis=0, tiled=True, axis...]
    ppermute x1, waiting for transfers between devices: 2.88 us -> 0.01 us  [shards(): late_halo = lax.ppermute(late_tail, 'ctx', down)]
    ppermute x1, starting transfers between devices: 1.3 us -> 3.43 us  [shards(): early_halo = lax.ppermute(early_tail, 'ctx', up)]
  transfers between devices with their start and end apart: 15 -> 20, of which waited for: 4 -> 8; matrix products, arithmetic and copies ran while one was open for 2% -> 2% of each run, Pallas kernels for 20% -> 17%
where the time goes in v13:
time: 86.7 us; the launch traced here: 86.5 us
  starting transfers between devices  44.5 us (51%)
  Pallas kernels  23.6 us (27%)
  waiting for transfers between devices  16.5 us (19%)
    ppermute x14, starting transfers between devices, permuted(): lax.ppermute(piece, 'ctx', [(j, j ^ distance) for j in range(devices)])  32.2 us
    pallas_call x2, Pallas kernels, project(): pl.pallas_call(functools.partial(project_kernel, kinds, devices, heads, a...  16.2 us
    ppermute x14, waiting for transfers between devices, permuted(): lax.ppermute(piece, 'ctx', [(j, j ^ distance) for j in range(devices)])  11.8 us
    pallas_call x4, Pallas kernels, attend(): pl.pallas_call(functools.partial(attend_kernel, block, turn, members, dev...  5.59 us
    ppermute x3, waiting for transfers between devices, shards(): out = lax.ppermute(out, ('dp', 'ctx'), route)  4.69 us
    all_to_all x1, starting transfers between devices, shards(): lax.all_to_all(flat, 'ctx', split_axis=0, concat_axis=0, tiled=True, axis...  3.9 us
    ppermute x3, starting transfers between devices, shards(): out = lax.ppermute(out, ('dp', 'ctx'), route)  3.68 us
    ppermute x1, starting transfers between devices, shards(): early_halo = lax.ppermute(early_tail, 'ctx', up)  3.43 us
  transfers between devices with their start and end apart: 20, of which 8 were waited for; matrix products, arithmetic and copies ran while one was open for 2% of the time, Pallas kernels for 17%

profile of v13, /device:TPU:0, one launch (start us, length us, event | category | flops | bytes accessed | tf_op | source)
XLA Modules:
  0.0 86.5 jit_solution(10387125839274324938)
XLA Ops:
  0.0 6.6 %shard_map.82 = (bf16[4,64,256]{2,1,0:T(8,128)(2,1)}, bf16[4,64,256]{2,1,0:T(8,128)(2,1)}, bf16[4,64,256]{2,1,0:T(8,128)(2,1)}, bf16[4,64,256]{2,1,0:T(8,128)(2,1)}) custom-call(s32[32,128]{1,0:T(8,128)} %bitcast.17, f32[1,128]{1,0:T(1,128)} %constant.103.clone.freq_hbm, bf16[4096]{0:T(1024)(128)(2,1)} %gain_hbm.3, bf16[256,4096]{1,0:T(8,128)(2,1)} %tokens_hbm.3, ...), custom_call_target="tpu_custom_call" | custom-call | flops 2147483648 | bytes 11010048 | tf_op jit(solution)/shard_map/pallas_call | solution.py:154
  6.6 3.1 %collective-permute-start = (bf16[4,64,256]{2,1,0:T(8,128)(2,1)}, bf16[4,64,256]{2,1,0:T(8,128)(2,1)S(1)}, u32[]{:S(2)}, u32[]{:S(2)}) collective-permute-start(bf16[4,64,256]{2,1,0:T(8,128)(2,1)} %get-tuple-element.47), channel_id=1, source_target_pairs={{0,4},{1,5},{2,6},{3,7},{4,0},{5,1},{6,2},{7,3},{8,12},{9,13},{10,... | collective-permute-start | bytes 393224 | tf_op jit(solution)/shard_map/ppermute | solution.py:372
  9.7 2.6 %collective-permute-start.1 = (bf16[4,64,256]{2,1,0:T(8,128)(2,1)}, bf16[4,64,256]{2,1,0:T(8,128)(2,1)S(1)}, u32[]{:S(2)}, u32[]{:S(2)}) collective-permute-start(bf16[4,64,256]{2,1,0:T(8,128)(2,1)} %get-tuple-element.48), channel_id=1, source_target_pairs={{0,8},{1,9},{2,10},{3,11},{4,12},{5,13},{6,14},{7,15},{8,0},{9,1},... | collective-permute-start | bytes 393224 | tf_op jit(solution)/shard_map/ppermute | solution.py:372
  12.3 9.6 %shard_map.83 = (bf16[2,4,64,512]{3,2,1,0:T(8,128)(2,1)}, bf16[64,512]{1,0:T(8,128)(2,1)}, bf16[64,512]{1,0:T(8,128)(2,1)}, bf16[64,512]{1,0:T(8,128)(2,1)}, bf1...) custom-call(s32[32,128]{1,0:T(8,128)} %bitcast.18, ...), custom_call_target="tpu_custom_call" | custom-call | flops 4294967296 | bytes 19922944 | tf_op jit(solution)/shard_map/pallas_call | solution.py:154
  21.9 1.9 %collective-permute-start.3 = (bf16[64,512]{1,0:T(8,128)(2,1)}, bf16[64,512]{1,0:T(8,128)(2,1)S(1)}, u32[]{:S(2)}, u32[]{:S(2)}) collective-permute-start(bf16[64,512]{1,0:T(8,128)(2,1)} %get-tuple-element.50), channel_id=1, source_target_pairs={{0,8},{1,9},{2,10},{3,11},{4,12},{5,13},{6,14},{7,15},{8,0},{9,1},... | collective-permute-start | bytes 196616 | tf_op jit(solution)/shard_map/ppermute | solution.py:372
  23.9 2.2 %collective-permute-start.4 = (bf16[64,512]{1,0:T(8,128)(2,1)}, bf16[64,512]{1,0:T(8,128)(2,1)S(1)}, u32[]{:S(2)}, u32[]{:S(2)}) collective-permute-start(bf16[64,512]{1,0:T(8,128)(2,1)} %get-tuple-element.51), channel_id=1, source_target_pairs={{0,9},{1,8},{2,11},{3,10},{4,13},{5,12},{6,15},{7,14},{8,1},{9,0},... | collective-permute-start | bytes 196616 | tf_op jit(solution)/shard_map/ppermute | solution.py:372
  27.6 3.4 %collective-permute-start.8 = (bf16[64,512]{1,0:T(8,128)(2,1)}, bf16[64,512]{1,0:T(8,128)(2,1)S(1)}, u32[]{:S(2)}, u32[]{:S(2)}) collective-permute-start(bf16[64,512]{1,0:T(8,128)(2,1)} %get-tuple-element.68), channel_id=1, source_target_pairs={{0,10},{1,11},{2,8},{3,9},{4,14},{5,15},{6,12},{7,13},{8,2},{9,3},... | collective-permute-start | bytes 196616 | tf_op jit(solution)/shard_map/ppermute | solution.py:372
  31.0 3.1 %collective-permute-start.9 = (bf16[64,512]{1,0:T(8,128)(2,1)}, bf16[64,512]{1,0:T(8,128)(2,1)S(1)}, u32[]{:S(2)}, u32[]{:S(2)}) collective-permute-start(bf16[64,512]{1,0:T(8,128)(2,1)} %get-tuple-element.69), channel_id=1, source_target_pairs={{0,11},{1,10},{2,9},{3,8},{4,15},{5,14},{6,13},{7,12},{8,3},{9,2},... | collective-permute-start | bytes 196616 | tf_op jit(solution)/shard_map/ppermute | solution.py:372
  34.1 3.3 %collective-permute-start.10 = (bf16[64,512]{1,0:T(8,128)(2,1)}, bf16[64,512]{1,0:T(8,128)(2,1)S(1)}, u32[]{:S(2)}, u32[]{:S(2)}) collective-permute-start(bf16[64,512]{1,0:T(8,128)(2,1)} %get-tuple-element.70), channel_id=1, source_target_pairs={{0,12},{1,13},{2,14},{3,15},{4,8},{5,9},{6,10},{7,11},{8,4},{9,5},... | collective-permute-start | bytes 196616 | tf_op jit(solution)/shard_map/ppermute | solution.py:372
  37.5 3.9 %all-to-all-start = ((bf16[8,64,512]{2,1,0:T(8,128)(2,1)}), bf16[8,64,512]{2,1,0:T(8,128)(2,1)S(1)}, u32[]{:S(2)}, u32[]{:S(2)}) async-start(bf16[8,64,512]{2,1,0:T(8,128)(2,1)} %bitcast.16), calls=%async_computation | async-start | bytes 1048576 | tf_op jit(solution)/shard_map/all_to_all | solution.py:403
  42.3 2.1 %collective-permute-start.5 = (bf16[256,256]{1,0:T(8,128)(2,1)S(1)}, bf16[256,256]{1,0:T(8,128)(2,1)S(1)}, u32[]{:S(2)}, u32[]{:S(2)}) collective-permute-start(bf16[256,256]{1,0:T(8,128)(2,1)S(1)} %get-tuple-element.63), channel_id=1, source_target_pairs={{0,1},{1,0},{2,3},{3,2},{4,5},{5,4},{6,7},{7,6},{8,9},{9,8},{10,11... | collective-permute-start | bytes 393224 | tf_op jit(solution)/shard_map/ppermute | solution.py:372
  44.4 1.5 %collective-permute-start.6 = (bf16[256,256]{1,0:T(8,128)(2,1)S(1)}, bf16[256,256]{1,0:T(8,128)(2,1)S(1)}, u32[]{:S(2)}, u32[]{:S(2)}) collective-permute-start(bf16[256,256]{1,0:T(8,128)(2,1)S(1)} %get-tuple-element.64), channel_id=1, source_target_pairs={{0,2},{1,3},{2,0},{3,1},{4,6},{5,7},{6,4},{7,5},{8,10},{9,11},{10,... | collective-permute-start | bytes 393224 | tf_op jit(solution)/shard_map/ppermute | solution.py:372
  46.1 5.5 %collective-permute-done.5.refs_1_ = bf16[256,256]{1,0:T(8,128)(2,1)S(1)} collective-permute-done((bf16[256,256]{1,0:T(8,128)(2,1)S(1)}, bf16[256,256]{1,0:T(8,128)(2,1)S(1)}, u32[]{:S(2)}, u32[]{:S(2)}) %collective-permute-start.5) | collective-permute-done | bytes 131104 | tf_op jit(solution)/shard_map/ppermute | solution.py:372
  52.4 1.4 %collective-permute-done.7.refs_3_ = bf16[256,256]{1,0:T(8,128)(2,1)S(1)} collective-permute-done((bf16[256,256]{1,0:T(8,128)(2,1)S(1)}, bf16[256,256]{1,0:T(8,128)(2,1)S(1)}, u32[]{:S(2)}, u32[]{:S(2)}) %collective-permute-start.7) | collective-permute-done | bytes 131104 | tf_op jit(solution)/shard_map/ppermute | solution.py:372
  54.6 3.4 %collective-permute-start.14 = (bf16[384,256]{1,0:T(8,128)(2,1)S(1)}, bf16[384,256]{1,0:T(8,128)(2,1)S(1)}, u32[]{:S(2)}, u32[]{:S(2)}) collective-permute-start(bf16[384,256]{1,0:T(8,128)(2,1)S(1)} %get-tuple-element.83.rest_11_), channel_id=1, source_target_pairs={{0,4},{1,5},{2,6},{3,7},{4,8},{5,9},{6,10},{7,11},{8,12},{9,13},{1... | collective-permute-start | bytes 589832 | tf_op jit(solution)/shard_map/ppermute | solution.py:411
  59.3 3.4 %collective-permute-start.11 = (bf16[64,512]{1,0:T(8,128)(2,1)S(1)}, bf16[64,512]{1,0:T(8,128)(2,1)S(1)}, u32[]{:S(2)}, u32[]{:S(2)}) collective-permute-start(bf16[64,512]{1,0:T(8,128)(2,1)S(1)} %copy-done.4), channel_id=1, source_target_pairs={{0,13},{1,12},{2,15},{3,14},{4,9},{5,8},{6,11},{7,10},{8,5},{9,4},... | collective-permute-start | bytes 196616 | tf_op jit(solution)/shard_map/ppermute | solution.py:372
  63.1 5.3 %collective-permute-start.13 = (bf16[64,512]{1,0:T(8,128)(2,1)S(1)}, bf16[64,512]{1,0:T(8,128)(2,1)S(1)}, u32[]{:S(2)}, u32[]{:S(2)}) collective-permute-start(bf16[64,512]{1,0:T(8,128)(2,1)S(1)} %copy-done.2), channel_id=1, source_target_pairs={{0,15},{1,14},{2,13},{3,12},{4,11},{5,10},{6,9},{7,8},{8,7},{9,6},... | collective-permute-start | bytes 196616 | tf_op jit(solution)/shard_map/ppermute | solution.py:372
  69.7 1.6 %collective-permute-done.13.rest_8_ = bf16[64,512]{1,0:T(8,128)(2,1)S(1)} collective-permute-done((bf16[64,512]{1,0:T(8,128)(2,1)S(1)}, bf16[64,512]{1,0:T(8,128)(2,1)S(1)}, u32[]{:S(2)}, u32[]{:S(2)}) %collective-permute-start.13) | collective-permute-done | bytes 65568 | tf_op jit(solution)/shard_map/ppermute | solution.py:372
  71.4 1.4 %shard_map.86 = bf16[256,512]{1,0:T(8,128)(2,1)S(1)} custom-call(s32[1,1024]{1,0:T(1,128)S(1)} %squeeze.6.slot_ref, s32[1,32]{1,0:T(1,128)S(1)} %reduce-window_clone.1.ends_ref, bf16[512,512]{1,0:T(8,128)(2,1)S(1)} %bitcast.12, bf16[64,512]{1,0:T(8,128)(2,1)S(1)} %collective-permute-done.3.rest_1_, bf16[64,512]{1,0:T(8,128)(2,1)S(1)} %collective-permute-done.4.rest_2_, ...), custom_call_target="tpu_custom_call" | custom-call | flops 536870912 | bytes 1966080 | tf_op jit(solution)/shard_map/pallas_call | solution.py:313
  72.8 2.2 %collective-permute-start.16 = (bf16[256,512]{1,0:T(8,128)(2,1)S(1)}, bf16[256,512]{1,0:T(8,128)(2,1)S(1)}, u32[]{:S(2)}, u32[]{:S(2)}) collective-permute-start(bf16[256,512]{1,0:T(8,128)(2,1)S(1)} %shard_map.86), channel_id=1, source_target_pairs={{0,3},{1,2},{2,1},{3,0},{4,7},{5,6},{6,5},{7,4},{8,11},{9,10},{10,... | collective-permute-start | bytes 786440 | tf_op jit(solution)/shard_map/ppermute | solution.py:425
  75.1 1.4 %shard_map.87 = bf16[256,512]{1,0:T(8,128)(2,1)S(1)} custom-call(s32[1,1024]{1,0:T(1,128)S(1)} %squeeze.6.slot_ref, s32[1,32]{1,0:T(1,128)S(1)} %reduce-window_clone.1.ends_ref, bf16[512,512]{1,0:T(8,128)(2,1)S(1)} %bitcast.13, bf16[64,512]{1,0:T(8,128)(2,1)S(1)} %collective-permute-done.3.rest_1_, bf16[64,512]{1,0:T(8,128)(2,1)S(1)} %collective-permute-done.4.rest_2_, ...), custom_call_target="tpu_custom_call" | custom-call | flops 536870912 | bytes 1966080 | tf_op jit(solution)/shard_map/pallas_call | solution.py:313
  79.3 1.4 %shard_map.89.refs_3_ = bf16[256,512]{1,0:T(8,128)(2,1)S(1)} custom-call(s32[1,1024]{1,0:T(1,128)S(1)} %squeeze.6.slot_ref, s32[1,32]{1,0:T(1,128)S(1)} %reduce-window_clone.1.ends_ref, bf16[512,512]{1,0:T(8,128)(2,1)S(1)} %bitcast.15, bf16[64,512]{1,0:T(8,128)(2,1)S(1)} %collective-permute-done.3.rest_1_, ...), custom_call_target="tpu_custom_call" | custom-call | flops 536870912 | bytes 1966080 | tf_op jit(solution)/shard_map/pallas_call | solution.py:313
  80.7 1.7 %collective-permute-done.16.refs_0_ = bf16[256,512]{1,0:T(8,128)(2,1)S(1)} collective-permute-done((bf16[256,512]{1,0:T(8,128)(2,1)S(1)}, bf16[256,512]{1,0:T(8,128)(2,1)S(1)}, u32[]{:S(2)}, u32[]{:S(2)}) %collective-permute-start.16) | collective-permute-done | bytes 262176 | tf_op jit(solution)/shard_map/ppermute | solution.py:425
  82.4 3.0 %collective-permute-done.17.refs_1_ = bf16[256,512]{1,0:T(8,128)(2,1)S(1)} collective-permute-done((bf16[256,512]{1,0:T(8,128)(2,1)S(1)}, bf16[256,512]{1,0:T(8,128)(2,1)S(1)}, u32[]{:S(2)}, u32[]{:S(2)}) %collective-permute-start.17) | collective-permute-done | bytes 262176 | tf_op jit(solution)/shard_map/ppermute | solution.py:425
  (51 shorter events, 11.3 us)
Async XLA Ops:
  6.6 27.6 %collective-permute-start = (bf16[4,64,256]{2,1,0:T(8,128)(2,1)}, bf16[4,64,256]{2,1,0:T(8,128)(2,1)S(1)}, u32[]{:S(2)}, u32[]{:S(2)}) collective-permute-start(bf16[4,64,256]{2,1,0:T(8,128)(2,1)} %get-tuple-element.47), channel_id=1, source_target_pairs={{0,4},{1,5},{2,6},{3,7},{4,0},{5,1},{6,2},{7,3},{8,12},{9,13},{10,... | collective-permute-start | bytes 393224 | tf_op jit(solution)/shard_map/ppermute | solution.py:372
  9.7 27.7 %collective-permute-start.1 = (bf16[4,64,256]{2,1,0:T(8,128)(2,1)}, bf16[4,64,256]{2,1,0:T(8,128)(2,1)S(1)}, u32[]{:S(2)}, u32[]{:S(2)}) collective-permute-start(bf16[4,64,256]{2,1,0:T(8,128)(2,1)} %get-tuple-element.48), channel_id=1, source_target_pairs={{0,8},{1,9},{2,10},{3,11},{4,12},{5,13},{6,14},{7,15},{8,0},{9,1},... | collective-permute-start | bytes 393224 | tf_op jit(solution)/shard_map/ppermute | solution.py:372
  12.3 25.2 %collective-permute-start.2 = (bf16[4,64,256]{2,1,0:T(8,128)(2,1)}, bf16[4,64,256]{2,1,0:T(8,128)(2,1)S(1)}, u32[]{:S(2)}, u32[]{:S(2)}) collective-permute-start(bf16[4,64,256]{2,1,0:T(8,128)(2,1)} %get-tuple-element.49), channel_id=1, source_target_pairs={{0,12},{1,13},{2,14},{3,15},{4,8},{5,9},{6,10},{7,11},{8,4},{9,5},... | collective-permute-start | bytes 393224 | tf_op jit(solution)/shard_map/ppermute | solution.py:372
  21.9 37.4 %copy-start.4 = (bf16[64,512]{1,0:T(8,128)(2,1)S(1)}, bf16[64,512]{1,0:T(8,128)(2,1)}, u32[]{:S(2)}) copy-start(bf16[64,512]{1,0:T(8,128)(2,1)} %get-tuple-element.76) | copy-start | bytes 196612
  21.9 40.8 %copy-start.3 = (bf16[64,512]{1,0:T(8,128)(2,1)S(1)}, bf16[64,512]{1,0:T(8,128)(2,1)}, u32[]{:S(2)}) copy-start(bf16[64,512]{1,0:T(8,128)(2,1)} %get-tuple-element.77) | copy-start | bytes 196612
  21.9 41.2 %copy-start.2 = (bf16[64,512]{1,0:T(8,128)(2,1)S(1)}, bf16[64,512]{1,0:T(8,128)(2,1)}, u32[]{:S(2)}) copy-start(bf16[64,512]{1,0:T(8,128)(2,1)} %get-tuple-element.78) | copy-start | bytes 196612
  21.9 46.4 %copy-start.5 = (s32[32]{0:T(128)S(1)}, s32[32]{0:T(128)}, u32[]{:S(2)}) copy-start(s32[32]{0:T(128)} %param.10) | copy-start | bytes 388
  21.9 5.7 %collective-permute-start.3 = (bf16[64,512]{1,0:T(8,128)(2,1)}, bf16[64,512]{1,0:T(8,128)(2,1)S(1)}, u32[]{:S(2)}, u32[]{:S(2)}) collective-permute-start(bf16[64,512]{1,0:T(8,128)(2,1)} %get-tuple-element.50), channel_id=1, source_target_pairs={{0,8},{1,9},{2,10},{3,11},{4,12},{5,13},{6,14},{7,15},{8,0},{9,1},... | collective-permute-start | bytes 196616 | tf_op jit(solution)/shard_map/ppermute | solution.py:372
  23.9 7.1 %collective-permute-start.4 = (bf16[64,512]{1,0:T(8,128)(2,1)}, bf16[64,512]{1,0:T(8,128)(2,1)S(1)}, u32[]{:S(2)}, u32[]{:S(2)}) collective-permute-start(bf16[64,512]{1,0:T(8,128)(2,1)} %get-tuple-element.51), channel_id=1, source_target_pairs={{0,9},{1,8},{2,11},{3,10},{4,13},{5,12},{6,15},{7,14},{8,1},{9,0},... | collective-permute-start | bytes 196616 | tf_op jit(solution)/shard_map/ppermute | solution.py:372
  27.6 18.3 %collective-permute-start.8 = (bf16[64,512]{1,0:T(8,128)(2,1)}, bf16[64,512]{1,0:T(8,128)(2,1)S(1)}, u32[]{:S(2)}, u32[]{:S(2)}) collective-permute-start(bf16[64,512]{1,0:T(8,128)(2,1)} %get-tuple-element.68), channel_id=1, source_target_pairs={{0,10},{1,11},{2,8},{3,9},{4,14},{5,15},{6,12},{7,13},{8,2},{9,3},... | collective-permute-start | bytes 196616 | tf_op jit(solution)/shard_map/ppermute | solution.py:372
  31.0 15.0 %collective-permute-start.9 = (bf16[64,512]{1,0:T(8,128)(2,1)}, bf16[64,512]{1,0:T(8,128)(2,1)S(1)}, u32[]{:S(2)}, u32[]{:S(2)}) collective-permute-start(bf16[64,512]{1,0:T(8,128)(2,1)} %get-tuple-element.69), channel_id=1, source_target_pairs={{0,11},{1,10},{2,9},{3,8},{4,15},{5,14},{6,13},{7,12},{8,3},{9,2},... | collective-permute-start | bytes 196616 | tf_op jit(solution)/shard_map/ppermute | solution.py:372
  34.1 11.9 %collective-permute-start.10 = (bf16[64,512]{1,0:T(8,128)(2,1)}, bf16[64,512]{1,0:T(8,128)(2,1)S(1)}, u32[]{:S(2)}, u32[]{:S(2)}) collective-permute-start(bf16[64,512]{1,0:T(8,128)(2,1)} %get-tuple-element.70), channel_id=1, source_target_pairs={{0,12},{1,13},{2,14},{3,15},{4,8},{5,9},{6,10},{7,11},{8,4},{9,5},... | collective-permute-start | bytes 196616 | tf_op jit(solution)/shard_map/ppermute | solution.py:372
  37.5 33.9 %all-to-all-start = ((bf16[8,64,512]{2,1,0:T(8,128)(2,1)}), bf16[8,64,512]{2,1,0:T(8,128)(2,1)S(1)}, u32[]{:S(2)}, u32[]{:S(2)}) async-start(bf16[8,64,512]{2,1,0:T(8,128)(2,1)} %bitcast.16), calls=%async_computation | async-start | bytes 1048576 | tf_op jit(solution)/shard_map/all_to_all | solution.py:403
  42.3 9.2 %collective-permute-start.5 = (bf16[256,256]{1,0:T(8,128)(2,1)S(1)}, bf16[256,256]{1,0:T(8,128)(2,1)S(1)}, u32[]{:S(2)}, u32[]{:S(2)}) collective-permute-start(bf16[256,256]{1,0:T(8,128)(2,1)S(1)} %get-tuple-element.63), channel_id=1, source_target_pairs={{0,1},{1,0},{2,3},{3,2},{4,5},{5,4},{6,7},{7,6},{8,9},{9,8},{10,11... | collective-permute-start | bytes 393224 | tf_op jit(solution)/shard_map/ppermute | solution.py:372
  44.4 8.0 %collective-permute-start.6 = (bf16[256,256]{1,0:T(8,128)(2,1)S(1)}, bf16[256,256]{1,0:T(8,128)(2,1)S(1)}, u32[]{:S(2)}, u32[]{:S(2)}) collective-permute-start(bf16[256,256]{1,0:T(8,128)(2,1)S(1)} %get-tuple-element.64), channel_id=1, source_target_pairs={{0,2},{1,3},{2,0},{3,1},{4,6},{5,7},{6,4},{7,5},{8,10},{9,11},{10,... | collective-permute-start | bytes 393224 | tf_op jit(solution)/shard_map/ppermute | solution.py:372
  45.9 8.0 %collective-permute-start.7 = (bf16[256,256]{1,0:T(8,128)(2,1)S(1)}, bf16[256,256]{1,0:T(8,128)(2,1)S(1)}, u32[]{:S(2)}, u32[]{:S(2)}) collective-permute-start(bf16[256,256]{1,0:T(8,128)(2,1)S(1)} %get-tuple-element.65), channel_id=1, source_target_pairs={{0,3},{1,2},{2,1},{3,0},{4,7},{5,6},{6,5},{7,4},{8,11},{9,10},{10,... | collective-permute-start | bytes 393224 | tf_op jit(solution)/shard_map/ppermute | solution.py:372
  54.6 16.8 %collective-permute-start.14 = (bf16[384,256]{1,0:T(8,128)(2,1)S(1)}, bf16[384,256]{1,0:T(8,128)(2,1)S(1)}, u32[]{:S(2)}, u32[]{:S(2)}) collective-permute-start(bf16[384,256]{1,0:T(8,128)(2,1)S(1)} %get-tuple-element.83.rest_11_), channel_id=1, source_target_pairs={{0,4},{1,5},{2,6},{3,7},{4,8},{5,9},{6,10},{7,11},{8,12},{9,13},{1... | collective-permute-start | bytes 589832 | tf_op jit(solution)/shard_map/ppermute | solution.py:411
  58.0 13.4 %collective-permute-start.15 = (bf16[384,256]{1,0:T(8,128)(2,1)S(1)}, bf16[384,256]{1,0:T(8,128)(2,1)S(1)}, u32[]{:S(2)}, u32[]{:S(2)}) collective-permute-start(bf16[384,256]{1,0:T(8,128)(2,1)S(1)} %get-tuple-element.85.rest_14_), channel_id=1, source_target_pairs={{4,0},{5,1},{6,2},{7,3},{8,4},{9,5},{10,6},{11,7},{12,8},{13,9},{1... | collective-permute-start | bytes 589832 | tf_op jit(solution)/shard_map/ppermute | solution.py:412
  59.3 9.3 %collective-permute-start.11 = (bf16[64,512]{1,0:T(8,128)(2,1)S(1)}, bf16[64,512]{1,0:T(8,128)(2,1)S(1)}, u32[]{:S(2)}, u32[]{:S(2)}) collective-permute-start(bf16[64,512]{1,0:T(8,128)(2,1)S(1)} %copy-done.4), channel_id=1, source_target_pairs={{0,13},{1,12},{2,15},{3,14},{4,9},{5,8},{6,11},{7,10},{8,5},{9,4},... | collective-permute-start | bytes 196616 | tf_op jit(solution)/shard_map/ppermute | solution.py:372
  62.7 7.0 %collective-permute-start.12 = (bf16[64,512]{1,0:T(8,128)(2,1)S(1)}, bf16[64,512]{1,0:T(8,128)(2,1)S(1)}, u32[]{:S(2)}, u32[]{:S(2)}) collective-permute-start(bf16[64,512]{1,0:T(8,128)(2,1)S(1)} %copy-done.3), channel_id=1, source_target_pairs={{0,14},{1,15},{2,12},{3,13},{4,10},{5,11},{6,8},{7,9},{8,6},{9,7},... | collective-permute-start | bytes 196616 | tf_op jit(solution)/shard_map/ppermute | solution.py:372
  63.1 8.3 %collective-permute-start.13 = (bf16[64,512]{1,0:T(8,128)(2,1)S(1)}, bf16[64,512]{1,0:T(8,128)(2,1)S(1)}, u32[]{:S(2)}, u32[]{:S(2)}) collective-permute-start(bf16[64,512]{1,0:T(8,128)(2,1)S(1)} %copy-done.2), channel_id=1, source_target_pairs={{0,15},{1,14},{2,13},{3,12},{4,11},{5,10},{6,9},{7,8},{8,7},{9,6},... | collective-permute-start | bytes 196616 | tf_op jit(solution)/shard_map/ppermute | solution.py:372
  72.8 9.6 %collective-permute-start.16 = (bf16[256,512]{1,0:T(8,128)(2,1)S(1)}, bf16[256,512]{1,0:T(8,128)(2,1)S(1)}, u32[]{:S(2)}, u32[]{:S(2)}) collective-permute-start(bf16[256,512]{1,0:T(8,128)(2,1)S(1)} %shard_map.86), channel_id=1, source_target_pairs={{0,3},{1,2},{2,1},{3,0},{4,7},{5,6},{6,5},{7,4},{8,11},{9,10},{10,... | collective-permute-start | bytes 786440 | tf_op jit(solution)/shard_map/ppermute | solution.py:425
  76.5 8.9 %collective-permute-start.17 = (bf16[256,512]{1,0:T(8,128)(2,1)S(1)}, bf16[256,512]{1,0:T(8,128)(2,1)S(1)}, u32[]{:S(2)}, u32[]{:S(2)}) collective-permute-start(bf16[256,512]{1,0:T(8,128)(2,1)S(1)} %shard_map.87), channel_id=1, source_target_pairs={{0,1},{1,0},{2,3},{3,2},{4,5},{5,4},{6,7},{7,6},{8,9},{9,8},{10,11... | collective-permute-start | bytes 786440 | tf_op jit(solution)/shard_map/ppermute | solution.py:425
  78.3 7.1 %collective-permute-start.18 = (bf16[256,512]{1,0:T(8,128)(2,1)S(1)}, bf16[256,512]{1,0:T(8,128)(2,1)S(1)}, u32[]{:S(2)}, u32[]{:S(2)}) collective-permute-start(bf16[256,512]{1,0:T(8,128)(2,1)S(1)} %shard_map.88), channel_id=1, source_target_pairs={{0,2},{1,3},{2,0},{3,1},{4,6},{5,7},{6,4},{7,5},{8,10},{9,11},{10,... | collective-permute-start | bytes 786440 | tf_op jit(solution)/shard_map/ppermute | solution.py:425
  (2 other events, 39.0 us)

commit v14 on v12

--- a/solution.py
+++ b/solution.py
@@ -342,10 +342,11 @@
     kv = exchange(kv, None)
     apart = list(range(half_devices, devices))
     near, *far = project(*operands, (w_query,), (True,), devices, members, apart)
-    queries = []
-    for i, piece in enumerate(far):
-        distance = half_devices + i
-        queries.append(lax.ppermute(piece, "ctx", [(j, j ^ distance) for j in range(devices)]))
+    def to_other_half(piece, i):
+        return lax.ppermute(piece, "ctx", [(j, j ^ (half_devices + i)) for j in range(devices)])
+
+    held_back = 2
+    queries = [to_other_half(piece, i) for i, piece in enumerate(far[:-held_back])]
 
     table = positions.reshape(devices, rows)
     ours = group_of(table, block, devices, members) == group
@@ -370,10 +371,13 @@
     reach = REACH_BLOCKS * block
     sizes = [run - reach, reach] * 2
     early_head, early_tail, late_head, late_tail = place(kv, slot, sizes)
+    *late, early_tail, late_tail = lax.optimization_barrier((*far[-held_back:], early_tail, late_tail))
     up = [(i, i + members) for i in range(devices - members)]
     down = [(i + members, i) for i in range(devices - members)]
     early_halo = lax.ppermute(early_tail, "ctx", up)
     late_halo = lax.ppermute(late_tail, "ctx", down)
+    for i, piece in enumerate(late):
+        queries.append(to_other_half(piece, len(far) - held_back + i))
     pieces = (early_halo, early_head, early_tail, late_halo, late_head, late_tail)
 
     results = []

time: 73.2 us -> 76.8 us (1.049)
  waiting for transfers between devices: 10.3 us -> 12.2 us
  starting transfers between devices: 37.4 us -> 39.1 us
    ppermute x8, waiting for transfers between devices: 2.66 us -> 7.8 us  [to_other_half(): lax.ppermute(piece, 'ctx', [(j, j ^ half_devices + i) for j in range(devi...]
    ppermute x1, waiting for transfers between devices: 2.88 us -> 0.01 us  [shards(): late_halo = lax.ppermute(late_tail, 'ctx', down)]
    ppermute x8, starting transfers between devices: 19.1 us -> 20.7 us  [to_other_half(): lax.ppermute(piece, 'ctx', [(j, j ^ half_devices + i) for j in range(devi...]
  transfers between devices with their start and end apart: 15 -> 15, of which waited for: 4 -> 5; matrix products, arithmetic and copies ran while one was open for 2% -> 2% of each run, Pallas kernels for 20% -> 19%
where the time goes in v14:
time: 76.8 us; the launch traced here: 76.5 us
  starting transfers between devices  39.1 us (51%)
  Pallas kernels  23.4 us (30%)
  waiting for transfers between devices  12.2 us (16%)
    ppermute x8, starting transfers between devices, to_other_half(): lax.ppermute(piece, 'ctx', [(j, j ^ half_devices + i) for j in range(devi...  20.7 us
    pallas_call x2, Pallas kernels, project(): pl.pallas_call(functools.partial(project_kernel, kinds, devices, heads, a...  16 us
    all_to_all x2, starting transfers between devices, exchange(): lax.all_to_all(flat, 'ctx', split_axis=0, concat_axis=0, tiled=True, axis...  12 us
    ppermute x8, waiting for transfers between devices, to_other_half(): lax.ppermute(piece, 'ctx', [(j, j ^ half_devices + i) for j in range(devi...  7.8 us
    pallas_call x4, Pallas kernels, attend(): pl.pallas_call(functools.partial(attend_kernel, block, turn, members, dev...  5.6 us
    ppermute x3, waiting for transfers between devices, shards(): out = lax.ppermute(out, ('dp', 'ctx'), route)  4.38 us
    ppermute x3, starting transfers between devices, shards(): out = lax.ppermute(out, ('dp', 'ctx'), route)  3.69 us
  transfers between devices with their start and end apart: 15, of which 5 were waited for; matrix products, arithmetic and copies ran while one was open for 2% of the time, Pallas kernels for 19%

profile of v14, /device:TPU:0, one launch (start us, length us, event | category | flops | bytes accessed | tf_op | source)
XLA Modules:
  0.0 76.5 jit_solution(10084771764639201502)
XLA Ops:
  0.0 6.5 %shard_map.82 = bf16[4,4,64,256]{3,2,1,0:T(8,128)(2,1)} custom-call(s32[32,128]{1,0:T(8,128)} %bitcast.19, f32[1,128]{1,0:T(1,128)} %constant.78.clone.freq_hbm, bf16[4096]{0:T(1024)(128)(2,1)} %gain_hbm.3, bf16[256,4096]{1,0:T(8,128)(2,1)} %tokens_hbm.3, bf16[4096,512]{1,0:T(8,128)(2,1)} %rest_0_.2, bf16[4096,512]{1,0:T(8,128)(2,1)} %rest_1_.1), custom_call_target="tpu_custom_call" | custom-call | flops 2147483648 | bytes 11010048 | tf_op jit(solution)/shard_map/pallas_call | solution.py:148
  6.5 8.3 %all-to-all-start = ((bf16[16,64,256]{2,1,0:T(8,128)(2,1)}), bf16[16,64,256]{2,1,0:T(8,128)(2,1)S(1)}, u32[]{:S(2)}, u32[]{:S(2)}) async-start(bf16[16,64,256]{2,1,0:T(8,128)(2,1)} %bitcast.17), calls=%async_computation | async-start | bytes 1048576 | tf_op jit(solution)/shard_map/all_to_all | solution.py:338
  14.9 9.5 %shard_map.83 = (bf16[2,4,64,512]{3,2,1,0:T(8,128)(2,1)}, bf16[64,512]{1,0:T(8,128)(2,1)}, bf16[64,512]{1,0:T(8,128)(2,1)}, bf16[64,512]{1,0:T(8,128)(2,1)}, bf1...) custom-call(s32[32,128]{1,0:T(8,128)} %bitcast.20, ...), custom_call_target="tpu_custom_call" | custom-call | flops 4294967296 | bytes 19922944 | tf_op jit(solution)/shard_map/pallas_call | solution.py:148
  24.4 2.9 %collective-permute-start = (bf16[64,512]{1,0:T(8,128)(2,1)}, bf16[64,512]{1,0:T(8,128)(2,1)S(1)}, u32[]{:S(2)}, u32[]{:S(2)}) collective-permute-start(bf16[64,512]{1,0:T(8,128)(2,1)} %get-tuple-element.33), channel_id=1, source_target_pairs={{0,8},{1,9},{2,10},{3,11},{4,12},{5,13},{6,14},{7,15},{8,0},{9,1},... | collective-permute-start | bytes 196616 | tf_op jit(solution)/shard_map/ppermute | solution.py:346
  27.3 1.5 %collective-permute-start.1 = (bf16[64,512]{1,0:T(8,128)(2,1)}, bf16[64,512]{1,0:T(8,128)(2,1)S(1)}, u32[]{:S(2)}, u32[]{:S(2)}) collective-permute-start(bf16[64,512]{1,0:T(8,128)(2,1)} %get-tuple-element.34), channel_id=1, source_target_pairs={{0,9},{1,8},{2,11},{3,10},{4,13},{5,12},{6,15},{7,14},{8,1},{9,0},... | collective-permute-start | bytes 196616 | tf_op jit(solution)/shard_map/ppermute | solution.py:346
  28.8 3.3 %collective-permute-start.2 = (bf16[64,512]{1,0:T(8,128)(2,1)}, bf16[64,512]{1,0:T(8,128)(2,1)S(1)}, u32[]{:S(2)}, u32[]{:S(2)}) collective-permute-start(bf16[64,512]{1,0:T(8,128)(2,1)} %get-tuple-element.35), channel_id=1, source_target_pairs={{0,10},{1,11},{2,8},{3,9},{4,14},{5,15},{6,12},{7,13},{8,2},{9,3},... | collective-permute-start | bytes 196616 | tf_op jit(solution)/shard_map/ppermute | solution.py:346
  32.1 3.7 %collective-permute-start.4 = (bf16[64,512]{1,0:T(8,128)(2,1)}, bf16[64,512]{1,0:T(8,128)(2,1)S(1)}, u32[]{:S(2)}, u32[]{:S(2)}) collective-permute-start(bf16[64,512]{1,0:T(8,128)(2,1)} %get-tuple-element.37), channel_id=1, source_target_pairs={{0,12},{1,13},{2,14},{3,15},{4,8},{5,9},{6,10},{7,11},{8,4},{9,5},... | collective-permute-start | bytes 196616 | tf_op jit(solution)/shard_map/ppermute | solution.py:346
  36.1 3.7 %all-to-all-start.1 = ((bf16[8,64,512]{2,1,0:T(8,128)(2,1)}), bf16[8,64,512]{2,1,0:T(8,128)(2,1)S(1)}, u32[]{:S(2)}, u32[]{:S(2)}) async-start(bf16[8,64,512]{2,1,0:T(8,128)(2,1)} %bitcast.18), calls=%async_computation.1 | async-start | bytes 1048576 | tf_op jit(solution)/shard_map/all_to_all | solution.py:338
  40.4 3.0 %collective-permute-start.5 = (bf16[64,512]{1,0:T(8,128)(2,1)}, bf16[64,512]{1,0:T(8,128)(2,1)S(1)}, u32[]{:S(2)}, u32[]{:S(2)}) collective-permute-start(bf16[64,512]{1,0:T(8,128)(2,1)} %get-tuple-element.43), channel_id=1, source_target_pairs={{0,13},{1,12},{2,15},{3,14},{4,9},{5,8},{6,11},{7,10},{8,5},{9,4},... | collective-permute-start | bytes 196616 | tf_op jit(solution)/shard_map/ppermute | solution.py:346
  43.4 1.8 %collective-permute-done.3.rest_4_ = bf16[64,512]{1,0:T(8,128)(2,1)S(1)} collective-permute-done((bf16[64,512]{1,0:T(8,128)(2,1)}, bf16[64,512]{1,0:T(8,128)(2,1)S(1)}, u32[]{:S(2)}, u32[]{:S(2)}) %collective-permute-start.3) | collective-permute-done | bytes 65568 | tf_op jit(solution)/shard_map/ppermute | solution.py:346
  46.0 1.5 %collective-permute-start.8 = (bf16[384,256]{1,0:T(8,128)(2,1)S(1)}, bf16[384,256]{1,0:T(8,128)(2,1)S(1)}, u32[]{:S(2)}, u32[]{:S(2)}) collective-permute-start(bf16[384,256]{1,0:T(8,128)(2,1)S(1)} %get-tuple-element.51.rest_11_), channel_id=1, source_target_pairs={{0,4},{1,5},{2,6},{3,7},{4,8},{5,9},{6,10},{7,11},{8,12},{9,13},{1... | collective-permute-start | bytes 589832 | tf_op jit(solution)/shard_map/ppermute | solution.py:377
  47.4 1.3 %collective-permute-start.9 = (bf16[384,256]{1,0:T(8,128)(2,1)S(1)}, bf16[384,256]{1,0:T(8,128)(2,1)S(1)}, u32[]{:S(2)}, u32[]{:S(2)}) collective-permute-start(bf16[384,256]{1,0:T(8,128)(2,1)S(1)} %get-tuple-element.53.rest_14_), channel_id=1, source_target_pairs={{4,0},{5,1},{6,2},{7,3},{8,4},{9,5},{10,6},{11,7},{12,8},{13,9},{1... | collective-permute-start | bytes 589832 | tf_op jit(solution)/shard_map/ppermute | solution.py:378
  48.8 4.7 %collective-permute-start.6 = (bf16[64,512]{1,0:T(8,128)(2,1)}, bf16[64,512]{1,0:T(8,128)(2,1)S(1)}, u32[]{:S(2)}, u32[]{:S(2)}) collective-permute-start(bf16[64,512]{1,0:T(8,128)(2,1)} %get-tuple-element.49), channel_id=1, source_target_pairs={{0,14},{1,15},{2,12},{3,13},{4,10},{5,11},{6,8},{7,9},{8,6},{9,7},... | collective-permute-start | bytes 196616 | tf_op jit(solution)/shard_map/ppermute | solution.py:346
  53.5 1.6 %collective-permute-start.7 = (bf16[64,512]{1,0:T(8,128)(2,1)}, bf16[64,512]{1,0:T(8,128)(2,1)S(1)}, u32[]{:S(2)}, u32[]{:S(2)}) collective-permute-start(bf16[64,512]{1,0:T(8,128)(2,1)} %get-tuple-element.50), channel_id=1, source_target_pairs={{0,15},{1,14},{2,13},{3,12},{4,11},{5,10},{6,9},{7,8},{8,7},{9,6},... | collective-permute-start | bytes 196616 | tf_op jit(solution)/shard_map/ppermute | solution.py:346
  55.8 3.3 %collective-permute-done.6.rest_7_ = bf16[64,512]{1,0:T(8,128)(2,1)S(1)} collective-permute-done((bf16[64,512]{1,0:T(8,128)(2,1)}, bf16[64,512]{1,0:T(8,128)(2,1)S(1)}, u32[]{:S(2)}, u32[]{:S(2)}) %collective-permute-start.6) | collective-permute-done | bytes 65568 | tf_op jit(solution)/shard_map/ppermute | solution.py:346
  59.0 2.7 %collective-permute-done.7.rest_8_ = bf16[64,512]{1,0:T(8,128)(2,1)S(1)} collective-permute-done((bf16[64,512]{1,0:T(8,128)(2,1)}, bf16[64,512]{1,0:T(8,128)(2,1)S(1)}, u32[]{:S(2)}, u32[]{:S(2)}) %collective-permute-start.7) | collective-permute-done | bytes 65568 | tf_op jit(solution)/shard_map/ppermute | solution.py:346
  61.7 1.4 %shard_map.85 = bf16[256,512]{1,0:T(8,128)(2,1)S(1)} custom-call(s32[1,1024]{1,0:T(1,128)S(1)} %reshape.125.slot_ref, s32[1,32]{1,0:T(1,128)S(1)} %reduce-window_clone.1.ends_ref, bf16[512,512]{1,0:T(8,128)(2,1)S(1)} %bitcast.12, bf16[64,512]{1,0:T(8,128)(2,1)S(1)} %collective-permute-done.rest_1_, bf16[64,512]{1,0:T(8,128)(2,1)S(1)} %collective-permute-done.1.rest_2_, ...), custom_call_target="tpu_custom_call" | custom-call | flops 536870912 | bytes 1966080 | tf_op jit(solution)/shard_map/pallas_call | solution.py:277
  63.1 1.2 %collective-permute-start.10 = (bf16[256,512]{1,0:T(8,128)(2,1)S(1)}, bf16[256,512]{1,0:T(8,128)(2,1)S(1)}, u32[]{:S(2)}, u32[]{:S(2)}) collective-permute-start(bf16[256,512]{1,0:T(8,128)(2,1)S(1)} %shard_map.85), channel_id=1, source_target_pairs={{0,3},{1,2},{2,1},{3,0},{4,7},{5,6},{6,5},{7,4},{8,11},{9,10},{10,... | collective-permute-start | bytes 786440 | tf_op jit(solution)/shard_map/ppermute | solution.py:393
  64.4 1.4 %shard_map.86 = bf16[256,512]{1,0:T(8,128)(2,1)S(1)} custom-call(s32[1,1024]{1,0:T(1,128)S(1)} %reshape.125.slot_ref, s32[1,32]{1,0:T(1,128)S(1)} %reduce-window_clone.1.ends_ref, bf16[512,512]{1,0:T(8,128)(2,1)S(1)} %bitcast.13, bf16[64,512]{1,0:T(8,128)(2,1)S(1)} %collective-permute-done.rest_1_, bf16[64,512]{1,0:T(8,128)(2,1)S(1)} %collective-permute-done.1.rest_2_, ...), custom_call_target="tpu_custom_call" | custom-call | flops 536870912 | bytes 1966080 | tf_op jit(solution)/shard_map/pallas_call | solution.py:277
  66.9 1.4 %shard_map.87 = bf16[256,512]{1,0:T(8,128)(2,1)S(1)} custom-call(s32[1,1024]{1,0:T(1,128)S(1)} %reshape.125.slot_ref, s32[1,32]{1,0:T(1,128)S(1)} %reduce-window_clone.1.ends_ref, bf16[512,512]{1,0:T(8,128)(2,1)S(1)} %bitcast.14, bf16[64,512]{1,0:T(8,128)(2,1)S(1)} %collective-permute-done.rest_1_, bf16[64,512]{1,0:T(8,128)(2,1)S(1)} %collective-permute-done.1.rest_2_, ...), custom_call_target="tpu_custom_call" | custom-call | flops 536870912 | bytes 1966080 | tf_op jit(solution)/shard_map/pallas_call | solution.py:277
  68.3 1.3 %collective-permute-start.12 = (bf16[256,512]{1,0:T(8,128)(2,1)S(1)}, bf16[256,512]{1,0:T(8,128)(2,1)S(1)}, u32[]{:S(2)}, u32[]{:S(2)}) collective-permute-start(bf16[256,512]{1,0:T(8,128)(2,1)S(1)} %shard_map.87), channel_id=1, source_target_pairs={{0,2},{1,3},{2,0},{3,1},{4,6},{5,7},{6,4},{7,5},{8,10},{9,11},{10,... | collective-permute-start | bytes 786440 | tf_op jit(solution)/shard_map/ppermute | solution.py:393
  69.6 1.4 %shard_map.88.refs_3_ = bf16[256,512]{1,0:T(8,128)(2,1)S(1)} custom-call(s32[1,1024]{1,0:T(1,128)S(1)} %reshape.125.slot_ref, s32[1,32]{1,0:T(1,128)S(1)} %reduce-window_clone.1.ends_ref, bf16[512,512]{1,0:T(8,128)(2,1)S(1)} %bitcast.15, bf16[64,512]{1,0:T(8,128)(2,1)S(1)} %collective-permute-done.rest_1_, ...), custom_call_target="tpu_custom_call" | custom-call | flops 536870912 | bytes 1966080 | tf_op jit(solution)/shard_map/pallas_call | solution.py:277
  71.0 1.5 %collective-permute-done.10.refs_0_ = bf16[256,512]{1,0:T(8,128)(2,1)S(1)} collective-permute-done((bf16[256,512]{1,0:T(8,128)(2,1)S(1)}, bf16[256,512]{1,0:T(8,128)(2,1)S(1)}, u32[]{:S(2)}, u32[]{:S(2)}) %collective-permute-start.10) | collective-permute-done | bytes 262176 | tf_op jit(solution)/shard_map/ppermute | solution.py:393
  72.5 2.9 %collective-permute-done.11.refs_1_ = bf16[256,512]{1,0:T(8,128)(2,1)S(1)} collective-permute-done((bf16[256,512]{1,0:T(8,128)(2,1)S(1)}, bf16[256,512]{1,0:T(8,128)(2,1)S(1)}, u32[]{:S(2)}, u32[]{:S(2)}) %collective-permute-start.11) | collective-permute-done | bytes 262176 | tf_op jit(solution)/shard_map/ppermute | solution.py:393
  (29 shorter events, 4.6 us)
Async XLA Ops:
  6.5 29.6 %all-to-all-start = ((bf16[16,64,256]{2,1,0:T(8,128)(2,1)}), bf16[16,64,256]{2,1,0:T(8,128)(2,1)S(1)}, u32[]{:S(2)}, u32[]{:S(2)}) async-start(bf16[16,64,256]{2,1,0:T(8,128)(2,1)} %bitcast.17), calls=%async_computation | async-start | bytes 1048576 | tf_op jit(solution)/shard_map/all_to_all | solution.py:338
  14.9 21.0 %copy-start = (s32[4096]{0:T(1024)S(1)}, s32[4096]{0:T(1024)}, u32[]{:S(2)}) copy-start(s32[4096]{0:T(1024)} %param.9) | copy-start | bytes 49156
  14.9 21.0 %copy-start.1 = (s32[32]{0:T(128)S(1)}, s32[32]{0:T(128)}, u32[]{:S(2)}) copy-start(s32[32]{0:T(128)} %param.10) | copy-start | bytes 388
  24.4 16.0 %collective-permute-start = (bf16[64,512]{1,0:T(8,128)(2,1)}, bf16[64,512]{1,0:T(8,128)(2,1)S(1)}, u32[]{:S(2)}, u32[]{:S(2)}) collective-permute-start(bf16[64,512]{1,0:T(8,128)(2,1)} %get-tuple-element.33), channel_id=1, source_target_pairs={{0,8},{1,9},{2,10},{3,11},{4,12},{5,13},{6,14},{7,15},{8,0},{9,1},... | collective-permute-start | bytes 196616 | tf_op jit(solution)/shard_map/ppermute | solution.py:346
  27.3 16.1 %collective-permute-start.1 = (bf16[64,512]{1,0:T(8,128)(2,1)}, bf16[64,512]{1,0:T(8,128)(2,1)S(1)}, u32[]{:S(2)}, u32[]{:S(2)}) collective-permute-start(bf16[64,512]{1,0:T(8,128)(2,1)} %get-tuple-element.34), channel_id=1, source_target_pairs={{0,9},{1,8},{2,11},{3,10},{4,13},{5,12},{6,15},{7,14},{8,1},{9,0},... | collective-permute-start | bytes 196616 | tf_op jit(solution)/shard_map/ppermute | solution.py:346
  28.8 14.6 %collective-permute-start.2 = (bf16[64,512]{1,0:T(8,128)(2,1)}, bf16[64,512]{1,0:T(8,128)(2,1)S(1)}, u32[]{:S(2)}, u32[]{:S(2)}) collective-permute-start(bf16[64,512]{1,0:T(8,128)(2,1)} %get-tuple-element.35), channel_id=1, source_target_pairs={{0,10},{1,11},{2,8},{3,9},{4,14},{5,15},{6,12},{7,13},{8,2},{9,3},... | collective-permute-start | bytes 196616 | tf_op jit(solution)/shard_map/ppermute | solution.py:346
  32.0 13.2 %collective-permute-start.3 = (bf16[64,512]{1,0:T(8,128)(2,1)}, bf16[64,512]{1,0:T(8,128)(2,1)S(1)}, u32[]{:S(2)}, u32[]{:S(2)}) collective-permute-start(bf16[64,512]{1,0:T(8,128)(2,1)} %get-tuple-element.36), channel_id=1, source_target_pairs={{0,11},{1,10},{2,9},{3,8},{4,15},{5,14},{6,13},{7,12},{8,3},{9,2},... | collective-permute-start | bytes 196616 | tf_op jit(solution)/shard_map/ppermute | solution.py:346
  32.1 13.1 %collective-permute-start.4 = (bf16[64,512]{1,0:T(8,128)(2,1)}, bf16[64,512]{1,0:T(8,128)(2,1)S(1)}, u32[]{:S(2)}, u32[]{:S(2)}) collective-permute-start(bf16[64,512]{1,0:T(8,128)(2,1)} %get-tuple-element.37), channel_id=1, source_target_pairs={{0,12},{1,13},{2,14},{3,15},{4,8},{5,9},{6,10},{7,11},{8,4},{9,5},... | collective-permute-start | bytes 196616 | tf_op jit(solution)/shard_map/ppermute | solution.py:346
  36.1 25.6 %all-to-all-start.1 = ((bf16[8,64,512]{2,1,0:T(8,128)(2,1)}), bf16[8,64,512]{2,1,0:T(8,128)(2,1)S(1)}, u32[]{:S(2)}, u32[]{:S(2)}) async-start(bf16[8,64,512]{2,1,0:T(8,128)(2,1)} %bitcast.18), calls=%async_computation.1 | async-start | bytes 1048576 | tf_op jit(solution)/shard_map/all_to_all | solution.py:338
  40.4 15.4 %collective-permute-start.5 = (bf16[64,512]{1,0:T(8,128)(2,1)}, bf16[64,512]{1,0:T(8,128)(2,1)S(1)}, u32[]{:S(2)}, u32[]{:S(2)}) collective-permute-start(bf16[64,512]{1,0:T(8,128)(2,1)} %get-tuple-element.43), channel_id=1, source_target_pairs={{0,13},{1,12},{2,15},{3,14},{4,9},{5,8},{6,11},{7,10},{8,5},{9,4},... | collective-permute-start | bytes 196616 | tf_op jit(solution)/shard_map/ppermute | solution.py:346
  46.0 15.7 %collective-permute-start.8 = (bf16[384,256]{1,0:T(8,128)(2,1)S(1)}, bf16[384,256]{1,0:T(8,128)(2,1)S(1)}, u32[]{:S(2)}, u32[]{:S(2)}) collective-permute-start(bf16[384,256]{1,0:T(8,128)(2,1)S(1)} %get-tuple-element.51.rest_11_), channel_id=1, source_target_pairs={{0,4},{1,5},{2,6},{3,7},{4,8},{5,9},{6,10},{7,11},{8,12},{9,13},{1... | collective-permute-start | bytes 589832 | tf_op jit(solution)/shard_map/ppermute | solution.py:377
  47.4 14.3 %collective-permute-start.9 = (bf16[384,256]{1,0:T(8,128)(2,1)S(1)}, bf16[384,256]{1,0:T(8,128)(2,1)S(1)}, u32[]{:S(2)}, u32[]{:S(2)}) collective-permute-start(bf16[384,256]{1,0:T(8,128)(2,1)S(1)} %get-tuple-element.53.rest_14_), channel_id=1, source_target_pairs={{4,0},{5,1},{6,2},{7,3},{8,4},{9,5},{10,6},{11,7},{12,8},{13,9},{1... | collective-permute-start | bytes 589832 | tf_op jit(solution)/shard_map/ppermute | solution.py:378
  48.8 10.2 %collective-permute-start.6 = (bf16[64,512]{1,0:T(8,128)(2,1)}, bf16[64,512]{1,0:T(8,128)(2,1)S(1)}, u32[]{:S(2)}, u32[]{:S(2)}) collective-permute-start(bf16[64,512]{1,0:T(8,128)(2,1)} %get-tuple-element.49), channel_id=1, source_target_pairs={{0,14},{1,15},{2,12},{3,13},{4,10},{5,11},{6,8},{7,9},{8,6},{9,7},... | collective-permute-start | bytes 196616 | tf_op jit(solution)/shard_map/ppermute | solution.py:346
  53.5 8.2 %collective-permute-start.7 = (bf16[64,512]{1,0:T(8,128)(2,1)}, bf16[64,512]{1,0:T(8,128)(2,1)S(1)}, u32[]{:S(2)}, u32[]{:S(2)}) collective-permute-start(bf16[64,512]{1,0:T(8,128)(2,1)} %get-tuple-element.50), channel_id=1, source_target_pairs={{0,15},{1,14},{2,13},{3,12},{4,11},{5,10},{6,9},{7,8},{8,7},{9,6},... | collective-permute-start | bytes 196616 | tf_op jit(solution)/shard_map/ppermute | solution.py:346
  63.1 9.4 %collective-permute-start.10 = (bf16[256,512]{1,0:T(8,128)(2,1)S(1)}, bf16[256,512]{1,0:T(8,128)(2,1)S(1)}, u32[]{:S(2)}, u32[]{:S(2)}) collective-permute-start(bf16[256,512]{1,0:T(8,128)(2,1)S(1)} %shard_map.85), channel_id=1, source_target_pairs={{0,3},{1,2},{2,1},{3,0},{4,7},{5,6},{6,5},{7,4},{8,11},{9,10},{10,... | collective-permute-start | bytes 786440 | tf_op jit(solution)/shard_map/ppermute | solution.py:393
  65.8 9.6 %collective-permute-start.11 = (bf16[256,512]{1,0:T(8,128)(2,1)S(1)}, bf16[256,512]{1,0:T(8,128)(2,1)S(1)}, u32[]{:S(2)}, u32[]{:S(2)}) collective-permute-start(bf16[256,512]{1,0:T(8,128)(2,1)S(1)} %shard_map.86), channel_id=1, source_target_pairs={{0,1},{1,0},{2,3},{3,2},{4,5},{5,4},{6,7},{7,6},{8,9},{9,8},{10,11... | collective-permute-start | bytes 786440 | tf_op jit(solution)/shard_map/ppermute | solution.py:393
  68.3 7.1 %collective-permute-start.12 = (bf16[256,512]{1,0:T(8,128)(2,1)S(1)}, bf16[256,512]{1,0:T(8,128)(2,1)S(1)}, u32[]{:S(2)}, u32[]{:S(2)}) collective-permute-start(bf16[256,512]{1,0:T(8,128)(2,1)S(1)} %shard_map.87), channel_id=1, source_target_pairs={{0,2},{1,3},{2,0},{3,1},{4,6},{5,7},{6,4},{7,5},{8,10},{9,11},{10,... | collective-permute-start | bytes 786440 | tf_op jit(solution)/shard_map/ppermute | solution.py:393

commit v15 on v12

--- a/solution.py
+++ b/solution.py
@@ -167,31 +167,38 @@
     )(positions, freq, gain, tokens, *weights)
 
 
-def place_kernel(arrived_ref, slot_ref, *outs):
-    rows = arrived_ref.shape[0]
+def place_kernel(count, slot_ref, *refs):
+    pieces, outs, arrived = refs[:count], refs[count:-1], refs[-1]
+    rows = arrived.shape[0]
+    slot = slot_ref[...]
+    first = 0
+    for piece in pieces:
+        arrived[first : first + piece.shape[0], :] = piece[...]
+        first += piece.shape[0]
     first = 0
     for out_ref in outs:
         size = out_ref.shape[0]
         slots = lax.broadcasted_iota(jnp.int32, (size, rows), 0) + first
-        chosen = (slots == slot_ref[...]).astype(jnp.bfloat16)
-        out_ref[...] = dot(chosen, arrived_ref[...]).astype(jnp.bfloat16)
+        chosen = (slots == slot).astype(jnp.bfloat16)
+        out_ref[...] = dot(chosen, arrived[...]).astype(jnp.bfloat16)
         first += size
 
 
-def place(arrived, slot, sizes):
-    width = arrived.shape[1]
+def place(pieces, slot, sizes):
+    rows, width = slot.shape[1], pieces[0].shape[1]
     return pl.pallas_call(
-        place_kernel,
+        functools.partial(place_kernel, len(pieces)),
         out_shape=[jax.ShapeDtypeStruct((size, width), jnp.bfloat16) for size in sizes],
-        in_specs=[WHOLE, WHOLE],
+        in_specs=[WHOLE] * (1 + len(pieces)),
         out_specs=[WHOLE] * len(sizes),
+        scratch_shapes=[pltpu.VMEM((rows, width), jnp.bfloat16)],
         compiler_params=pltpu.CompilerParams(vmem_limit_bytes=16 * MIB),
         cost_estimate=pl.CostEstimate(
-            flops=2 * sum(sizes) * arrived.shape[0] * width,
-            bytes_accessed=4 * arrived.size,
+            flops=2 * sum(sizes) * rows * width,
+            bytes_accessed=4 * rows * width,
             transcendentals=0,
         ),
-    )(arrived, slot)
+    )(slot, *pieces)
 
 
 def taken_at(turn, members):
@@ -207,24 +214,17 @@
     return (turn, members - 1 - turn)
 
 
-def attend_kernel(block, turn, members, devices, slot_ref, ends_ref, *rest):
-    queries_refs, rest = rest[:-9], rest[-9:]
-    pieces, out_ref, held, query_ref = rest[:6], rest[6], rest[7], rest[8]
-    first = 0
-    for ref in queries_refs:
-        query_ref[first : first + ref.shape[0], :] = ref[...]
-        first += ref.shape[0]
+def attend_kernel(block, turn, members, devices, ends_ref, query_ref, *rest):
+    pieces, out_ref, held = rest[:6], rest[6], rest[7]
     target = taken_at(turn, members)
     group = lax.axis_index("ctx") // members
     starts = (group * members * block, (2 * devices - members - group * members) * block)
     last = group == devices // members - 1
     heads = query_ref.shape[1] // HEAD_SIZE
-    arrived = query_ref.shape[0]
-    run = arrived // 2
+    run = query_ref.shape[0] // 2
     per_run = run // block
     reach = REACH_BLOCKS * block
     keys = reach + block
-    slot = slot_ref[...]
     ends = ends_ref[...]
     factor = jnp.float32(np.log2(np.e) / HEAD_SIZE**0.5)
     for half in range(2):
@@ -237,15 +237,11 @@
             first += piece.shape[0]
     indices = (target, per_run - 1 - target)
     at = [pl.multiple_of(index * block, block) for index in indices]
-    iota = lax.broadcasted_iota(jnp.int32, (block, arrived), 0)
-    chosen = [(iota + (at[half] + half * run) == slot).astype(jnp.bfloat16) for half in range(2)]
-    queries = dot(jnp.concatenate(chosen, axis=0), query_ref[...]).astype(jnp.bfloat16)
     here = [slice(half * block, (half + 1) * block) for half in range(2)]
     scores, weights, totals = [], [], []
     for half in range(2):
-        stacked = jnp.concatenate(
-            [queries[here[half], h * HEAD_SIZE : (h + 1) * HEAD_SIZE] for h in range(heads)], axis=0
-        )
+        query = query_ref[pl.ds(pl.multiple_of(at[half] + half * run, block), block), :]
+        stacked = jnp.concatenate([query[:, h * HEAD_SIZE : (h + 1) * HEAD_SIZE] for h in range(heads)], axis=0)
         key = held[half, pl.ds(at[half], keys), :HEAD_SIZE]
         scores.append(
             lax.dot_general(stacked, key, (((1,), (1,)), ((), ())), preferred_element_type=jnp.float32)
@@ -269,27 +265,24 @@
             out_ref[here[half], h * HEAD_SIZE : (h + 1) * HEAD_SIZE] = mixed[h * block : (h + 1) * block]
 
 
-def attend(turn, members, devices, queries, slot, ends, pieces, block):
-    rows, width = slot.shape[1], queries[0].shape[1]
+def attend(turn, members, devices, query, ends, pieces, block):
+    rows, width = query.shape
     held = REACH_BLOCKS * block + rows // 2
     heads = width // HEAD_SIZE
     reach = (REACH_BLOCKS + 1) * block
     return pl.pallas_call(
         functools.partial(attend_kernel, block, turn, members, devices),
         out_shape=jax.ShapeDtypeStruct((2 * block, width), jnp.bfloat16),
-        in_specs=[WHOLE] * (8 + len(queries)),
+        in_specs=[WHOLE] * 8,
         out_specs=WHOLE,
-        scratch_shapes=[
-            pltpu.VMEM((2, held, 2 * HEAD_SIZE), jnp.bfloat16),
-            pltpu.VMEM((rows, width), jnp.bfloat16),
-        ],
+        scratch_shapes=[pltpu.VMEM((2, held, 2 * HEAD_SIZE), jnp.bfloat16)],
         compiler_params=pltpu.CompilerParams(vmem_limit_bytes=16 * MIB),
         cost_estimate=pl.CostEstimate(
-            flops=2 * 2 * heads * block * reach * HEAD_SIZE * 2 + 4 * block * rows * width,
+            flops=2 * 2 * heads * block * reach * HEAD_SIZE * 2,
             bytes_accessed=2 * rows * width + 8 * held * HEAD_SIZE,
             transcendentals=2 * heads * block * reach,
         ),
-    )(slot, ends, *queries, *pieces)
+    )(ends, query, *pieces)
 
 
 def assemble_kernel(*refs):
@@ -369,16 +362,17 @@
     kv, *queries[1:6] = lax.optimization_barrier((kv, *queries[1:6]))
     reach = REACH_BLOCKS * block
     sizes = [run - reach, reach] * 2
-    early_head, early_tail, late_head, late_tail = place(kv, slot, sizes)
+    early_head, early_tail, late_head, late_tail = place([kv], slot, sizes)
     up = [(i, i + members) for i in range(devices - members)]
     down = [(i + members, i) for i in range(devices - members)]
     early_halo = lax.ppermute(early_tail, "ctx", up)
     late_halo = lax.ppermute(late_tail, "ctx", down)
     pieces = (early_halo, early_head, early_tail, late_halo, late_head, late_tail)
 
+    (query,) = place(queries, query_slot, [2 * run])
     results = []
     for turn in range(members):
-        out = attend(turn, members, devices, queries, query_slot, ends, pieces, block)
+        out = attend(turn, members, devices, query, ends, pieces, block)
         if turn < members - 1:
             distances = distances_at(turn, members)
             route = [

time: 73.2 us -> 72.6 us (level)
    ppermute x1, waiting for transfers between devices: 2.88 us -> 1.62 us  [shards(): late_halo = lax.ppermute(late_tail, 'ctx', down)]
    pallas_call x1 -> x2, Pallas kernels: 0.72 us -> 1.96 us  [place(): pl.pallas_call(functools.partial(place_kernel, len(pieces)), out_shape=[j...]
    pallas_call x4, Pallas kernels: 5.6 us -> 4.56 us  [attend(): pl.pallas_call(functools.partial(attend_kernel, block, turn, members, dev...]
  transfers between devices with their start and end apart: 15 -> 15, of which waited for: 4 -> 5; matrix products, arithmetic and copies ran while one was open for 2% -> 2% of each run, Pallas kernels for 20% -> 21%
where the time goes in v15:
time: 72.6 us; the launch traced here: 72.3 us
  starting transfers between devices  37.3 us (51%)
  Pallas kernels  23.6 us (33%)
  waiting for transfers between devices  9.61 us (13%)
  local copies, waits for them, and re-layouts  0.74 us (1%)
    ppermute x8, starting transfers between devices, shards(): lax.ppermute(piece, 'ctx', [(j, j ^ distance) for j in range(devices)])  19 us
    pallas_call x2, Pallas kernels, project(): pl.pallas_call(functools.partial(project_kernel, kinds, devices, heads, a...  16 us
    all_to_all x2, starting transfers between devices, exchange(): lax.all_to_all(flat, 'ctx', split_axis=0, concat_axis=0, tiled=True, axis...  12 us
    ppermute x3, waiting for transfers between devices, shards(): out = lax.ppermute(out, ('dp', 'ctx'), route)  5.24 us
    pallas_call x4, Pallas kernels, attend(): pl.pallas_call(functools.partial(attend_kernel, block, turn, members, dev...  4.56 us
    ppermute x3, starting transfers between devices, shards(): out = lax.ppermute(out, ('dp', 'ctx'), route)  3.68 us
    ppermute x8, waiting for transfers between devices, shards(): lax.ppermute(piece, 'ctx', [(j, j ^ distance) for j in range(devices)])  2.74 us
    pallas_call x2, Pallas kernels, place(): pl.pallas_call(functools.partial(place_kernel, len(pieces)), out_shape=[j...  1.96 us
  transfers between devices with their start and end apart: 15, of which 5 were waited for; matrix products, arithmetic and copies ran while one was open for 2% of the time, Pallas kernels for 21%

profile of v15, /device:TPU:0, one launch (start us, length us, event | category | flops | bytes accessed | tf_op | source)
XLA Modules:
  0.0 72.3 jit_solution(10076505320495713428)
XLA Ops:
  0.0 6.5 %shard_map.82 = bf16[4,4,64,256]{3,2,1,0:T(8,128)(2,1)} custom-call(s32[32,128]{1,0:T(8,128)} %bitcast.16, f32[1,128]{1,0:T(1,128)} %constant.78.clone.freq_hbm, bf16[4096]{0:T(1024)(128)(2,1)} %gain_hbm.3, bf16[256,4096]{1,0:T(8,128)(2,1)} %tokens_hbm.3, bf16[4096,512]{1,0:T(8,128)(2,1)} %rest_0_.2, bf16[4096,512]{1,0:T(8,128)(2,1)} %rest_1_.1), custom_call_target="tpu_custom_call" | custom-call | flops 2147483648 | bytes 11010048 | tf_op jit(solution)/shard_map/pallas_call | solution.py:148
  6.5 8.3 %all-to-all-start = ((bf16[16,64,256]{2,1,0:T(8,128)(2,1)}), bf16[16,64,256]{2,1,0:T(8,128)(2,1)S(1)}, u32[]{:S(2)}, u32[]{:S(2)}) async-start(bf16[16,64,256]{2,1,0:T(8,128)(2,1)} %bitcast.14), calls=%async_computation | async-start | bytes 1048576 | tf_op jit(solution)/shard_map/all_to_all | solution.py:331
  14.9 9.5 %shard_map.83 = (bf16[2,4,64,512]{3,2,1,0:T(8,128)(2,1)}, bf16[64,512]{1,0:T(8,128)(2,1)}, bf16[64,512]{1,0:T(8,128)(2,1)}, bf16[64,512]{1,0:T(8,128)(2,1)}, bf1...) custom-call(s32[32,128]{1,0:T(8,128)} %bitcast.17, ...), custom_call_target="tpu_custom_call" | custom-call | flops 4294967296 | bytes 19922944 | tf_op jit(solution)/shard_map/pallas_call | solution.py:148
  24.4 2.9 %collective-permute-start = (bf16[64,512]{1,0:T(8,128)(2,1)}, bf16[64,512]{1,0:T(8,128)(2,1)S(1)}, u32[]{:S(2)}, u32[]{:S(2)}) collective-permute-start(bf16[64,512]{1,0:T(8,128)(2,1)} %get-tuple-element.29), channel_id=1, source_target_pairs={{0,8},{1,9},{2,10},{3,11},{4,12},{5,13},{6,14},{7,15},{8,0},{9,1},... | collective-permute-start | bytes 196616 | tf_op jit(solution)/shard_map/ppermute | solution.py:341
  27.3 1.5 %collective-permute-start.1 = (bf16[64,512]{1,0:T(8,128)(2,1)}, bf16[64,512]{1,0:T(8,128)(2,1)S(1)}, u32[]{:S(2)}, u32[]{:S(2)}) collective-permute-start(bf16[64,512]{1,0:T(8,128)(2,1)} %get-tuple-element.30), channel_id=1, source_target_pairs={{0,9},{1,8},{2,11},{3,10},{4,13},{5,12},{6,15},{7,14},{8,1},{9,0},... | collective-permute-start | bytes 196616 | tf_op jit(solution)/shard_map/ppermute | solution.py:341
  28.8 3.3 %collective-permute-start.2 = (bf16[64,512]{1,0:T(8,128)(2,1)}, bf16[64,512]{1,0:T(8,128)(2,1)S(1)}, u32[]{:S(2)}, u32[]{:S(2)}) collective-permute-start(bf16[64,512]{1,0:T(8,128)(2,1)} %get-tuple-element.31), channel_id=1, source_target_pairs={{0,10},{1,11},{2,8},{3,9},{4,14},{5,15},{6,12},{7,13},{8,2},{9,3},... | collective-permute-start | bytes 196616 | tf_op jit(solution)/shard_map/ppermute | solution.py:341
  32.1 3.7 %collective-permute-start.4 = (bf16[64,512]{1,0:T(8,128)(2,1)}, bf16[64,512]{1,0:T(8,128)(2,1)S(1)}, u32[]{:S(2)}, u32[]{:S(2)}) collective-permute-start(bf16[64,512]{1,0:T(8,128)(2,1)} %get-tuple-element.33), channel_id=1, source_target_pairs={{0,12},{1,13},{2,14},{3,15},{4,8},{5,9},{6,10},{7,11},{8,4},{9,5},... | collective-permute-start | bytes 196616 | tf_op jit(solution)/shard_map/ppermute | solution.py:341
  36.1 3.7 %all-to-all-start.1 = ((bf16[8,64,512]{2,1,0:T(8,128)(2,1)}), bf16[8,64,512]{2,1,0:T(8,128)(2,1)S(1)}, u32[]{:S(2)}, u32[]{:S(2)}) async-start(bf16[8,64,512]{2,1,0:T(8,128)(2,1)} %bitcast.15), calls=%async_computation.1 | async-start | bytes 1048576 | tf_op jit(solution)/shard_map/all_to_all | solution.py:331
  40.5 2.9 %collective-permute-start.5 = (bf16[64,512]{1,0:T(8,128)(2,1)}, bf16[64,512]{1,0:T(8,128)(2,1)S(1)}, u32[]{:S(2)}, u32[]{:S(2)}) collective-permute-start(bf16[64,512]{1,0:T(8,128)(2,1)} %get-tuple-element.39), channel_id=1, source_target_pairs={{0,13},{1,12},{2,15},{3,14},{4,9},{5,8},{6,11},{7,10},{8,5},{9,4},... | collective-permute-start | bytes 196616 | tf_op jit(solution)/shard_map/ppermute | solution.py:341
  43.4 3.3 %collective-permute-start.6 = (bf16[64,512]{1,0:T(8,128)(2,1)}, bf16[64,512]{1,0:T(8,128)(2,1)S(1)}, u32[]{:S(2)}, u32[]{:S(2)}) collective-permute-start(bf16[64,512]{1,0:T(8,128)(2,1)} %get-tuple-element.40), channel_id=1, source_target_pairs={{0,14},{1,15},{2,12},{3,13},{4,10},{5,11},{6,8},{7,9},{8,6},{9,7},... | collective-permute-start | bytes 196616 | tf_op jit(solution)/shard_map/ppermute | solution.py:341
  46.7 1.5 %collective-permute-start.7 = (bf16[64,512]{1,0:T(8,128)(2,1)}, bf16[64,512]{1,0:T(8,128)(2,1)S(1)}, u32[]{:S(2)}, u32[]{:S(2)}) collective-permute-start(bf16[64,512]{1,0:T(8,128)(2,1)} %get-tuple-element.41), channel_id=1, source_target_pairs={{0,15},{1,14},{2,13},{3,12},{4,11},{5,10},{6,9},{7,8},{8,7},{9,6},... | collective-permute-start | bytes 196616 | tf_op jit(solution)/shard_map/ppermute | solution.py:341
  48.8 1.3 %collective-permute-start.8 = (bf16[384,256]{1,0:T(8,128)(2,1)S(1)}, bf16[384,256]{1,0:T(8,128)(2,1)S(1)}, u32[]{:S(2)}, u32[]{:S(2)}) collective-permute-start(bf16[384,256]{1,0:T(8,128)(2,1)S(1)} %get-tuple-element.43.rest_2_), channel_id=1, source_target_pairs={{0,4},{1,5},{2,6},{3,7},{4,8},{5,9},{6,10},{7,11},{8,12},{9,13},{1... | collective-permute-start | bytes 589832 | tf_op jit(solution)/shard_map/ppermute | solution.py:368
  50.2 1.3 %collective-permute-start.9 = (bf16[384,256]{1,0:T(8,128)(2,1)S(1)}, bf16[384,256]{1,0:T(8,128)(2,1)S(1)}, u32[]{:S(2)}, u32[]{:S(2)}) collective-permute-start(bf16[384,256]{1,0:T(8,128)(2,1)S(1)} %get-tuple-element.45.rest_5_), channel_id=1, source_target_pairs={{4,0},{5,1},{6,2},{7,3},{8,4},{9,5},{10,6},{11,7},{12,8},{13,9},{1... | collective-permute-start | bytes 589832 | tf_op jit(solution)/shard_map/ppermute | solution.py:369
  52.1 2.7 %collective-permute-done.7.refs_8_ = bf16[64,512]{1,0:T(8,128)(2,1)S(1)} collective-permute-done((bf16[64,512]{1,0:T(8,128)(2,1)}, bf16[64,512]{1,0:T(8,128)(2,1)S(1)}, u32[]{:S(2)}, u32[]{:S(2)}) %collective-permute-start.7) | collective-permute-done | bytes 65568 | tf_op jit(solution)/shard_map/ppermute | solution.py:341
  54.8 1.2 %shard_map.84.query_ref = bf16[1024,512]{1,0:T(8,128)(2,1)S(1)} custom-call(s32[1,1024]{1,0:T(1,128)S(1)} %reshape.126.slot_ref, bf16[512,512]{1,0:T(8,128)(2,1)S(1)} %bitcast.13, bf16[64,512]{1,0:T(8,128)(2,1)S(1)} %collective-permute-done.refs_1_, bf16[64,512]{1,0:T(8,128)(2,1)S(1)} %collective-permute-done.1.refs_2_, ...), custom_call_target="tpu_custom_call" | custom-call | flops 1073741824 | bytes 2097152 | tf_op jit(solution)/shard_map/pallas_call | solution.py:189
  56.1 1.6 %collective-permute-done.9.rest_3_ = bf16[384,256]{1,0:T(8,128)(2,1)S(1)} collective-permute-done((bf16[384,256]{1,0:T(8,128)(2,1)S(1)}, bf16[384,256]{1,0:T(8,128)(2,1)S(1)}, u32[]{:S(2)}, u32[]{:S(2)}) %collective-permute-start.9) | collective-permute-done | bytes 196640 | tf_op jit(solution)/shard_map/ppermute | solution.py:369
  57.7 1.1 %shard_map.86 = bf16[256,512]{1,0:T(8,128)(2,1)S(1)} custom-call(s32[1,32]{1,0:T(1,128)S(1)} %reduce-window_clone.1.ends_ref, bf16[1024,512]{1,0:T(8,128)(2,1)S(1)} %shard_map.84.query_ref, bf16[384,256]{1,0:T(8,128)(2,1)S(1)} %collective-permute-done.8.rest_0_, bf16[128,256]{1,0:T(8,128)(2,1)S(1)} %get-tuple-element.44.rest_1_, ...), custom_call_target="tpu_custom_call" | custom-call | flops 268435456 | bytes 1966080 | tf_op jit(solution)/shard_map/pallas_call | solution.py:273
  58.9 2.4 %collective-permute-start.10 = (bf16[256,512]{1,0:T(8,128)(2,1)S(1)}, bf16[256,512]{1,0:T(8,128)(2,1)S(1)}, u32[]{:S(2)}, u32[]{:S(2)}) collective-permute-start(bf16[256,512]{1,0:T(8,128)(2,1)S(1)} %shard_map.86), channel_id=1, source_target_pairs={{0,3},{1,2},{2,1},{3,0},{4,7},{5,6},{6,5},{7,4},{8,11},{9,10},{10,... | collective-permute-start | bytes 786440 | tf_op jit(solution)/shard_map/ppermute | solution.py:383
  61.3 1.1 %shard_map.87 = bf16[256,512]{1,0:T(8,128)(2,1)S(1)} custom-call(s32[1,32]{1,0:T(1,128)S(1)} %reduce-window_clone.1.ends_ref, bf16[1024,512]{1,0:T(8,128)(2,1)S(1)} %shard_map.84.query_ref, bf16[384,256]{1,0:T(8,128)(2,1)S(1)} %collective-permute-done.8.rest_0_, bf16[128,256]{1,0:T(8,128)(2,1)S(1)} %get-tuple-element.44.rest_1_, ...), custom_call_target="tpu_custom_call" | custom-call | flops 268435456 | bytes 1966080 | tf_op jit(solution)/shard_map/pallas_call | solution.py:273
  63.1 1.1 %shard_map.88 = bf16[256,512]{1,0:T(8,128)(2,1)S(1)} custom-call(s32[1,32]{1,0:T(1,128)S(1)} %reduce-window_clone.1.ends_ref, bf16[1024,512]{1,0:T(8,128)(2,1)S(1)} %shard_map.84.query_ref, bf16[384,256]{1,0:T(8,128)(2,1)S(1)} %collective-permute-done.8.rest_0_, bf16[128,256]{1,0:T(8,128)(2,1)S(1)} %get-tuple-element.44.rest_1_, ...), custom_call_target="tpu_custom_call" | custom-call | flops 268435456 | bytes 1966080 | tf_op jit(solution)/shard_map/pallas_call | solution.py:273
  64.8 1.1 %shard_map.89.refs_3_ = bf16[256,512]{1,0:T(8,128)(2,1)S(1)} custom-call(s32[1,32]{1,0:T(1,128)S(1)} %reduce-window_clone.1.ends_ref, bf16[1024,512]{1,0:T(8,128)(2,1)S(1)} %shard_map.84.query_ref, bf16[384,256]{1,0:T(8,128)(2,1)S(1)} %collective-permute-done.8.rest_0_, bf16[128,256]{1,0:T(8,128)(2,1)S(1)} %get-tuple-element.44.rest_1_, ...), custom_call_target="tpu_custom_call" | custom-call | flops 268435456 | bytes 1966080 | tf_op jit(solution)/shard_map/pallas_call | solution.py:273
  66.0 3.0 %collective-permute-done.10.refs_0_ = bf16[256,512]{1,0:T(8,128)(2,1)S(1)} collective-permute-done((bf16[256,512]{1,0:T(8,128)(2,1)S(1)}, bf16[256,512]{1,0:T(8,128)(2,1)S(1)}, u32[]{:S(2)}, u32[]{:S(2)}) %collective-permute-start.10) | collective-permute-done | bytes 262176 | tf_op jit(solution)/shard_map/ppermute | solution.py:383
  69.0 2.0 %collective-permute-done.11.refs_1_ = bf16[256,512]{1,0:T(8,128)(2,1)S(1)} collective-permute-done((bf16[256,512]{1,0:T(8,128)(2,1)S(1)}, bf16[256,512]{1,0:T(8,128)(2,1)S(1)}, u32[]{:S(2)}, u32[]{:S(2)}) %collective-permute-start.11) | collective-permute-done | bytes 262176 | tf_op jit(solution)/shard_map/ppermute | solution.py:383
  71.2 1.1 %shard_map.90 = bf16[256,2048]{1,0:T(8,128)(2,1)} custom-call(bf16[256,512]{1,0:T(8,128)(2,1)S(1)} %collective-permute-done.10.refs_0_, bf16[256,512]{1,0:T(8,128)(2,1)S(1)} %collective-permute-done.11.refs_1_, bf16[256,512]{1,0:T(8,128)(2,1)S(1)} %collective-permute-done.12.refs_2_, bf16[256,512]{1,0:T(8,128)(2,1)S(1)} %shard_map.89.refs_3_), custom_call_target="tpu_custom_call" | custom-call | bytes 2097152 | tf_op jit(solution)/shard_map/pallas_call | solution.py:298
  (30 shorter events, 3.9 us)
Async XLA Ops:
  6.5 29.6 %all-to-all-start = ((bf16[16,64,256]{2,1,0:T(8,128)(2,1)}), bf16[16,64,256]{2,1,0:T(8,128)(2,1)S(1)}, u32[]{:S(2)}, u32[]{:S(2)}) async-start(bf16[16,64,256]{2,1,0:T(8,128)(2,1)} %bitcast.14), calls=%async_computation | async-start | bytes 1048576 | tf_op jit(solution)/shard_map/all_to_all | solution.py:331
  14.9 21.0 %copy-start = (s32[4096]{0:T(1024)S(1)}, s32[4096]{0:T(1024)}, u32[]{:S(2)}) copy-start(s32[4096]{0:T(1024)} %param.9) | copy-start | bytes 49156
  14.9 21.0 %copy-start.1 = (s32[32]{0:T(128)S(1)}, s32[32]{0:T(128)}, u32[]{:S(2)}) copy-start(s32[32]{0:T(128)} %param.10) | copy-start | bytes 388
  24.4 16.1 %collective-permute-start = (bf16[64,512]{1,0:T(8,128)(2,1)}, bf16[64,512]{1,0:T(8,128)(2,1)S(1)}, u32[]{:S(2)}, u32[]{:S(2)}) collective-permute-start(bf16[64,512]{1,0:T(8,128)(2,1)} %get-tuple-element.29), channel_id=1, source_target_pairs={{0,8},{1,9},{2,10},{3,11},{4,12},{5,13},{6,14},{7,15},{8,0},{9,1},... | collective-permute-start | bytes 196616 | tf_op jit(solution)/shard_map/ppermute | solution.py:341
  27.3 16.1 %collective-permute-start.1 = (bf16[64,512]{1,0:T(8,128)(2,1)}, bf16[64,512]{1,0:T(8,128)(2,1)S(1)}, u32[]{:S(2)}, u32[]{:S(2)}) collective-permute-start(bf16[64,512]{1,0:T(8,128)(2,1)} %get-tuple-element.30), channel_id=1, source_target_pairs={{0,9},{1,8},{2,11},{3,10},{4,13},{5,12},{6,15},{7,14},{8,1},{9,0},... | collective-permute-start | bytes 196616 | tf_op jit(solution)/shard_map/ppermute | solution.py:341
  28.8 17.9 %collective-permute-start.2 = (bf16[64,512]{1,0:T(8,128)(2,1)}, bf16[64,512]{1,0:T(8,128)(2,1)S(1)}, u32[]{:S(2)}, u32[]{:S(2)}) collective-permute-start(bf16[64,512]{1,0:T(8,128)(2,1)} %get-tuple-element.31), channel_id=1, source_target_pairs={{0,10},{1,11},{2,8},{3,9},{4,14},{5,15},{6,12},{7,13},{8,2},{9,3},... | collective-permute-start | bytes 196616 | tf_op jit(solution)/shard_map/ppermute | solution.py:341
  32.0 16.1 %collective-permute-start.3 = (bf16[64,512]{1,0:T(8,128)(2,1)}, bf16[64,512]{1,0:T(8,128)(2,1)S(1)}, u32[]{:S(2)}, u32[]{:S(2)}) collective-permute-start(bf16[64,512]{1,0:T(8,128)(2,1)} %get-tuple-element.32), channel_id=1, source_target_pairs={{0,11},{1,10},{2,9},{3,8},{4,15},{5,14},{6,13},{7,12},{8,3},{9,2},... | collective-permute-start | bytes 196616 | tf_op jit(solution)/shard_map/ppermute | solution.py:341
  32.1 16.0 %collective-permute-start.4 = (bf16[64,512]{1,0:T(8,128)(2,1)}, bf16[64,512]{1,0:T(8,128)(2,1)S(1)}, u32[]{:S(2)}, u32[]{:S(2)}) collective-permute-start(bf16[64,512]{1,0:T(8,128)(2,1)} %get-tuple-element.33), channel_id=1, source_target_pairs={{0,12},{1,13},{2,14},{3,15},{4,8},{5,9},{6,10},{7,11},{8,4},{9,5},... | collective-permute-start | bytes 196616 | tf_op jit(solution)/shard_map/ppermute | solution.py:341
  36.1 18.7 %all-to-all-start.1 = ((bf16[8,64,512]{2,1,0:T(8,128)(2,1)}), bf16[8,64,512]{2,1,0:T(8,128)(2,1)S(1)}, u32[]{:S(2)}, u32[]{:S(2)}) async-start(bf16[8,64,512]{2,1,0:T(8,128)(2,1)} %bitcast.15), calls=%async_computation.1 | async-start | bytes 1048576 | tf_op jit(solution)/shard_map/all_to_all | solution.py:331
  40.5 11.6 %collective-permute-start.5 = (bf16[64,512]{1,0:T(8,128)(2,1)}, bf16[64,512]{1,0:T(8,128)(2,1)S(1)}, u32[]{:S(2)}, u32[]{:S(2)}) collective-permute-start(bf16[64,512]{1,0:T(8,128)(2,1)} %get-tuple-element.39), channel_id=1, source_target_pairs={{0,13},{1,12},{2,15},{3,14},{4,9},{5,8},{6,11},{7,10},{8,5},{9,4},... | collective-permute-start | bytes 196616 | tf_op jit(solution)/shard_map/ppermute | solution.py:341
  43.4 8.7 %collective-permute-start.6 = (bf16[64,512]{1,0:T(8,128)(2,1)}, bf16[64,512]{1,0:T(8,128)(2,1)S(1)}, u32[]{:S(2)}, u32[]{:S(2)}) collective-permute-start(bf16[64,512]{1,0:T(8,128)(2,1)} %get-tuple-element.40), channel_id=1, source_target_pairs={{0,14},{1,15},{2,12},{3,13},{4,10},{5,11},{6,8},{7,9},{8,6},{9,7},... | collective-permute-start | bytes 196616 | tf_op jit(solution)/shard_map/ppermute | solution.py:341
  46.7 8.2 %collective-permute-start.7 = (bf16[64,512]{1,0:T(8,128)(2,1)}, bf16[64,512]{1,0:T(8,128)(2,1)S(1)}, u32[]{:S(2)}, u32[]{:S(2)}) collective-permute-start(bf16[64,512]{1,0:T(8,128)(2,1)} %get-tuple-element.41), channel_id=1, source_target_pairs={{0,15},{1,14},{2,13},{3,12},{4,11},{5,10},{6,9},{7,8},{8,7},{9,6},... | collective-permute-start | bytes 196616 | tf_op jit(solution)/shard_map/ppermute | solution.py:341
  48.8 7.2 %collective-permute-start.8 = (bf16[384,256]{1,0:T(8,128)(2,1)S(1)}, bf16[384,256]{1,0:T(8,128)(2,1)S(1)}, u32[]{:S(2)}, u32[]{:S(2)}) collective-permute-start(bf16[384,256]{1,0:T(8,128)(2,1)S(1)} %get-tuple-element.43.rest_2_), channel_id=1, source_target_pairs={{0,4},{1,5},{2,6},{3,7},{4,8},{5,9},{6,10},{7,11},{8,12},{9,13},{1... | collective-permute-start | bytes 589832 | tf_op jit(solution)/shard_map/ppermute | solution.py:368
  50.2 7.6 %collective-permute-start.9 = (bf16[384,256]{1,0:T(8,128)(2,1)S(1)}, bf16[384,256]{1,0:T(8,128)(2,1)S(1)}, u32[]{:S(2)}, u32[]{:S(2)}) collective-permute-start(bf16[384,256]{1,0:T(8,128)(2,1)S(1)} %get-tuple-element.45.rest_5_), channel_id=1, source_target_pairs={{4,0},{5,1},{6,2},{7,3},{8,4},{9,5},{10,6},{11,7},{12,8},{13,9},{1... | collective-permute-start | bytes 589832 | tf_op jit(solution)/shard_map/ppermute | solution.py:369
  58.9 10.1 %collective-permute-start.10 = (bf16[256,512]{1,0:T(8,128)(2,1)S(1)}, bf16[256,512]{1,0:T(8,128)(2,1)S(1)}, u32[]{:S(2)}, u32[]{:S(2)}) collective-permute-start(bf16[256,512]{1,0:T(8,128)(2,1)S(1)} %shard_map.86), channel_id=1, source_target_pairs={{0,3},{1,2},{2,1},{3,0},{4,7},{5,6},{6,5},{7,4},{8,11},{9,10},{10,... | collective-permute-start | bytes 786440 | tf_op jit(solution)/shard_map/ppermute | solution.py:383
  62.4 8.5 %collective-permute-start.11 = (bf16[256,512]{1,0:T(8,128)(2,1)S(1)}, bf16[256,512]{1,0:T(8,128)(2,1)S(1)}, u32[]{:S(2)}, u32[]{:S(2)}) collective-permute-start(bf16[256,512]{1,0:T(8,128)(2,1)S(1)} %shard_map.87), channel_id=1, source_target_pairs={{0,1},{1,0},{2,3},{3,2},{4,5},{5,4},{6,7},{7,6},{8,9},{9,8},{10,11... | collective-permute-start | bytes 786440 | tf_op jit(solution)/shard_map/ppermute | solution.py:383
  64.2 7.0 %collective-permute-start.12 = (bf16[256,512]{1,0:T(8,128)(2,1)S(1)}, bf16[256,512]{1,0:T(8,128)(2,1)S(1)}, u32[]{:S(2)}, u32[]{:S(2)}) collective-permute-start(bf16[256,512]{1,0:T(8,128)(2,1)S(1)} %shard_map.88), channel_id=1, source_target_pairs={{0,2},{1,3},{2,0},{3,1},{4,6},{5,7},{6,4},{7,5},{8,10},{9,11},{10,... | collective-permute-start | bytes 786440 | tf_op jit(solution)/shard_map/ppermute | solution.py:383

commit v16 on v15

--- a/solution.py
+++ b/solution.py
@@ -167,7 +167,7 @@
     )(positions, freq, gain, tokens, *weights)
 
 
-def place_kernel(count, slot_ref, *refs):
+def place_kernel(count, members, slot_ref, *refs):
     pieces, outs, arrived = refs[:count], refs[count:-1], refs[-1]
     rows = arrived.shape[0]
     slot = slot_ref[...]
@@ -175,6 +175,8 @@
     for piece in pieces:
         arrived[first : first + piece.shape[0], :] = piece[...]
         first += piece.shape[0]
+    if members:
+        outs, (even_ref, odd_ref) = outs[:-2], outs[-2:]
     first = 0
     for out_ref in outs:
         size = out_ref.shape[0]
@@ -182,15 +184,21 @@
         chosen = (slots == slot).astype(jnp.bfloat16)
         out_ref[...] = dot(chosen, arrived[...]).astype(jnp.bfloat16)
         first += size
-
-
-def place(pieces, slot, sizes):
+    if members:
+        even = lax.axis_index("ctx") // members % 2 == 0
+        early, late = outs[1][...], outs[3][...]
+        even_ref[...] = jnp.where(even, early, late)
+        odd_ref[...] = jnp.where(even, late, early)
+
+
+def place(pieces, slot, sizes, members=0):
     rows, width = slot.shape[1], pieces[0].shape[1]
+    out_sizes = sizes + [sizes[1], sizes[3]] if members else sizes
     return pl.pallas_call(
-        functools.partial(place_kernel, len(pieces)),
-        out_shape=[jax.ShapeDtypeStruct((size, width), jnp.bfloat16) for size in sizes],
+        functools.partial(place_kernel, len(pieces), members),
+        out_shape=[jax.ShapeDtypeStruct((size, width), jnp.bfloat16) for size in out_sizes],
         in_specs=[WHOLE] * (1 + len(pieces)),
-        out_specs=[WHOLE] * len(sizes),
+        out_specs=[WHOLE] * len(out_sizes),
         scratch_shapes=[pltpu.VMEM((rows, width), jnp.bfloat16)],
         compiler_params=pltpu.CompilerParams(vmem_limit_bytes=16 * MIB),
         cost_estimate=pl.CostEstimate(
@@ -227,14 +235,14 @@
     keys = reach + block
     ends = ends_ref[...]
     factor = jnp.float32(np.log2(np.e) / HEAD_SIZE**0.5)
-    for half in range(2):
-        first = 0
-        for piece in pieces[3 * half : 3 * half + 3]:
-            values = piece[...]
-            if half == 1 and first == 0:
-                values = jnp.where(last, pieces[2][...], values)
-            held[half, first : first + piece.shape[0], :] = values
-            first += piece.shape[0]
+    from_even, from_odd, early_head, early_tail, late_head, late_tail = pieces
+    second = 1 - group % 2
+    held[second, :reach, :] = from_even[...]
+    held[1 - second, :reach, :] = jnp.where(last, early_tail[...], from_odd[...])
+    for half, (head, tail) in enumerate([(early_head, early_tail), (late_head, late_tail)]):
+        cut = reach + head.shape[0]
+        held[half, reach:cut, :] = head[...]
+        held[half, cut:, :] = tail[...]
     indices = (target, per_run - 1 - target)
     at = [pl.multiple_of(index * block, block) for index in indices]
     here = [slice(half * block, (half + 1) * block) for half in range(2)]
@@ -362,12 +370,14 @@
     kv, *queries[1:6] = lax.optimization_barrier((kv, *queries[1:6]))
     reach = REACH_BLOCKS * block
     sizes = [run - reach, reach] * 2
-    early_head, early_tail, late_head, late_tail = place([kv], slot, sizes)
-    up = [(i, i + members) for i in range(devices - members)]
-    down = [(i + members, i) for i in range(devices - members)]
-    early_halo = lax.ppermute(early_tail, "ctx", up)
-    late_halo = lax.ppermute(late_tail, "ctx", down)
-    pieces = (early_halo, early_head, early_tail, late_halo, late_head, late_tail)
+    *runs, even_out, odd_out = place([kv], slot, sizes, members)
+    odd = [i for i in range(1, groups - 1, 2)]
+    even = [i for i in range(0, groups, 2)]
+    pieces = []
+    for lower, out in ((odd, odd_out), (even, even_out)):
+        up = [(i * members + j, (i + 1) * members + j) for i in lower for j in range(members)]
+        pieces.insert(0, lax.ppermute(out, "ctx", up + [(j, i) for i, j in up]))
+    pieces = (*pieces, *runs)
 
     (query,) = place(queries, query_slot, [2 * run])
     results = []

time: 72.6 us -> 72.2 us (level)
  starting transfers between devices: 37.3 us -> 35.5 us
  waiting for transfers between devices: 9.61 us -> 11 us
    ppermute x8, waiting for transfers between devices: 2.74 us -> 4.64 us  [shards(): lax.ppermute(piece, 'ctx', [(j, j ^ distance) for j in range(devices)])]
    ppermute x2, starting transfers between devices: 2.59 us -> 0.74 us  [shards(): pieces.insert(0, lax.ppermute(out, 'ctx', up + [(j, i) for i, j in up]))]
    ppermute x2, waiting for transfers between devices: 1.62 us -> 0.01 us  [shards(): pieces.insert(0, lax.ppermute(out, 'ctx', up + [(j, i) for i, j in up]))]
    ppermute x3, waiting for transfers between devices: 5.24 us -> 6.39 us  [shards(): out = lax.ppermute(out, ('dp', 'ctx'), route)]
where the time goes in v16:
time: 72.2 us; the launch traced here: 71.9 us
  starting transfers between devices  35.5 us (49%)
  Pallas kernels  23.7 us (33%)
  waiting for transfers between devices  11 us (15%)
  local copies, waits for them, and re-layouts  0.74 us (1%)
    ppermute x8, starting transfers between devices, shards(): lax.ppermute(piece, 'ctx', [(j, j ^ distance) for j in range(devices)])  19 us
    pallas_call x2, Pallas kernels, project(): pl.pallas_call(functools.partial(project_kernel, kinds, devices, heads, a...  16 us
    all_to_all x2, starting transfers between devices, exchange(): lax.all_to_all(flat, 'ctx', split_axis=0, concat_axis=0, tiled=True, axis...  12 us
    ppermute x3, waiting for transfers between devices, shards(): out = lax.ppermute(out, ('dp', 'ctx'), route)  6.39 us
    ppermute x8, waiting for transfers between devices, shards(): lax.ppermute(piece, 'ctx', [(j, j ^ distance) for j in range(devices)])  4.64 us
    pallas_call x4, Pallas kernels, attend(): pl.pallas_call(functools.partial(attend_kernel, block, turn, members, dev...  4.59 us
    ppermute x3, starting transfers between devices, shards(): out = lax.ppermute(out, ('dp', 'ctx'), route)  3.69 us
    pallas_call x2, Pallas kernels, place(): pl.pallas_call(functools.partial(place_kernel, len(pieces), members), out...  1.97 us
  transfers between devices with their start and end apart: 15, of which 5 were waited for; matrix products, arithmetic and copies ran while one was open for 2% of the time, Pallas kernels for 21%

profile of v16, /device:TPU:0, one launch (start us, length us, event | category | flops | bytes accessed | tf_op | source)
XLA Modules:
  0.0 71.9 jit_solution(7980305309911998687)
XLA Ops:
  0.0 6.5 %shard_map.82 = bf16[4,4,64,256]{3,2,1,0:T(8,128)(2,1)} custom-call(s32[32,128]{1,0:T(8,128)} %bitcast.16, f32[1,128]{1,0:T(1,128)} %constant.78.clone.freq_hbm, bf16[4096]{0:T(1024)(128)(2,1)} %gain_hbm.3, bf16[256,4096]{1,0:T(8,128)(2,1)} %tokens_hbm.3, bf16[4096,512]{1,0:T(8,128)(2,1)} %rest_0_.2, bf16[4096,512]{1,0:T(8,128)(2,1)} %rest_1_.1), custom_call_target="tpu_custom_call" | custom-call | flops 2147483648 | bytes 11010048 | tf_op jit(solution)/shard_map/pallas_call | solution.py:148
  6.5 8.3 %all-to-all-start = ((bf16[16,64,256]{2,1,0:T(8,128)(2,1)}), bf16[16,64,256]{2,1,0:T(8,128)(2,1)S(1)}, u32[]{:S(2)}, u32[]{:S(2)}) async-start(bf16[16,64,256]{2,1,0:T(8,128)(2,1)} %bitcast.14), calls=%async_computation | async-start | bytes 1048576 | tf_op jit(solution)/shard_map/all_to_all | solution.py:339
  14.9 9.5 %shard_map.83 = (bf16[2,4,64,512]{3,2,1,0:T(8,128)(2,1)}, bf16[64,512]{1,0:T(8,128)(2,1)}, bf16[64,512]{1,0:T(8,128)(2,1)}, bf16[64,512]{1,0:T(8,128)(2,1)}, bf1...) custom-call(s32[32,128]{1,0:T(8,128)} %bitcast.17, ...), custom_call_target="tpu_custom_call" | custom-call | flops 4294967296 | bytes 19922944 | tf_op jit(solution)/shard_map/pallas_call | solution.py:148
  24.4 2.9 %collective-permute-start = (bf16[64,512]{1,0:T(8,128)(2,1)}, bf16[64,512]{1,0:T(8,128)(2,1)S(1)}, u32[]{:S(2)}, u32[]{:S(2)}) collective-permute-start(bf16[64,512]{1,0:T(8,128)(2,1)} %get-tuple-element.31), channel_id=1, source_target_pairs={{0,8},{1,9},{2,10},{3,11},{4,12},{5,13},{6,14},{7,15},{8,0},{9,1},... | collective-permute-start | bytes 196616 | tf_op jit(solution)/shard_map/ppermute | solution.py:349
  27.3 1.5 %collective-permute-start.1 = (bf16[64,512]{1,0:T(8,128)(2,1)}, bf16[64,512]{1,0:T(8,128)(2,1)S(1)}, u32[]{:S(2)}, u32[]{:S(2)}) collective-permute-start(bf16[64,512]{1,0:T(8,128)(2,1)} %get-tuple-element.32), channel_id=1, source_target_pairs={{0,9},{1,8},{2,11},{3,10},{4,13},{5,12},{6,15},{7,14},{8,1},{9,0},... | collective-permute-start | bytes 196616 | tf_op jit(solution)/shard_map/ppermute | solution.py:349
  28.8 3.3 %collective-permute-start.2 = (bf16[64,512]{1,0:T(8,128)(2,1)}, bf16[64,512]{1,0:T(8,128)(2,1)S(1)}, u32[]{:S(2)}, u32[]{:S(2)}) collective-permute-start(bf16[64,512]{1,0:T(8,128)(2,1)} %get-tuple-element.33), channel_id=1, source_target_pairs={{0,10},{1,11},{2,8},{3,9},{4,14},{5,15},{6,12},{7,13},{8,2},{9,3},... | collective-permute-start | bytes 196616 | tf_op jit(solution)/shard_map/ppermute | solution.py:349
  32.1 3.7 %collective-permute-start.4 = (bf16[64,512]{1,0:T(8,128)(2,1)}, bf16[64,512]{1,0:T(8,128)(2,1)S(1)}, u32[]{:S(2)}, u32[]{:S(2)}) collective-permute-start(bf16[64,512]{1,0:T(8,128)(2,1)} %get-tuple-element.35), channel_id=1, source_target_pairs={{0,12},{1,13},{2,14},{3,15},{4,8},{5,9},{6,10},{7,11},{8,4},{9,5},... | collective-permute-start | bytes 196616 | tf_op jit(solution)/shard_map/ppermute | solution.py:349
  36.1 3.7 %all-to-all-start.1 = ((bf16[8,64,512]{2,1,0:T(8,128)(2,1)}), bf16[8,64,512]{2,1,0:T(8,128)(2,1)S(1)}, u32[]{:S(2)}, u32[]{:S(2)}) async-start(bf16[8,64,512]{2,1,0:T(8,128)(2,1)} %bitcast.15), calls=%async_computation.1 | async-start | bytes 1048576 | tf_op jit(solution)/shard_map/all_to_all | solution.py:339
  40.5 2.9 %collective-permute-start.5 = (bf16[64,512]{1,0:T(8,128)(2,1)}, bf16[64,512]{1,0:T(8,128)(2,1)S(1)}, u32[]{:S(2)}, u32[]{:S(2)}) collective-permute-start(bf16[64,512]{1,0:T(8,128)(2,1)} %get-tuple-element.41), channel_id=1, source_target_pairs={{0,13},{1,12},{2,15},{3,14},{4,9},{5,8},{6,11},{7,10},{8,5},{9,4},... | collective-permute-start | bytes 196616 | tf_op jit(solution)/shard_map/ppermute | solution.py:349
  43.4 3.3 %collective-permute-start.6 = (bf16[64,512]{1,0:T(8,128)(2,1)}, bf16[64,512]{1,0:T(8,128)(2,1)S(1)}, u32[]{:S(2)}, u32[]{:S(2)}) collective-permute-start(bf16[64,512]{1,0:T(8,128)(2,1)} %get-tuple-element.42), channel_id=1, source_target_pairs={{0,14},{1,15},{2,12},{3,13},{4,10},{5,11},{6,8},{7,9},{8,6},{9,7},... | collective-permute-start | bytes 196616 | tf_op jit(solution)/shard_map/ppermute | solution.py:349
  46.7 1.5 %collective-permute-start.7 = (bf16[64,512]{1,0:T(8,128)(2,1)}, bf16[64,512]{1,0:T(8,128)(2,1)S(1)}, u32[]{:S(2)}, u32[]{:S(2)}) collective-permute-start(bf16[64,512]{1,0:T(8,128)(2,1)} %get-tuple-element.43), channel_id=1, source_target_pairs={{0,15},{1,14},{2,13},{3,12},{4,11},{5,10},{6,9},{7,8},{8,7},{9,6},... | collective-permute-start | bytes 196616 | tf_op jit(solution)/shard_map/ppermute | solution.py:349
  48.1 0.7 %shard_map.85 = (bf16[128,256]{1,0:T(8,128)(2,1)S(1)}, bf16[384,256]{1,0:T(8,128)(2,1)S(1)}, bf16[128,256]{1,0:T(8,128)(2,1)S(1)}, bf16[384,256]{1,0:T(8,128)(2,...) custom-call(s32[1,1024]{1,0:T(1,128)S(1)} %reshape.132.slot_ref, bf16[1024,256]{1,0:T(8,128)(2,1)S(1)} %bitcast.12), custom_call_target="tpu_custom_call" | custom-call | flops 536870912 | bytes 1048576 | tf_op jit(solution)/shard_map/pallas_call | solution.py:197
  50.3 1.0 %collective-permute-done.6.refs_7_ = bf16[64,512]{1,0:T(8,128)(2,1)S(1)} collective-permute-done((bf16[64,512]{1,0:T(8,128)(2,1)}, bf16[64,512]{1,0:T(8,128)(2,1)S(1)}, u32[]{:S(2)}, u32[]{:S(2)}) %collective-permute-start.6) | collective-permute-done | bytes 65568 | tf_op jit(solution)/shard_map/ppermute | solution.py:349
  51.3 3.6 %collective-permute-done.7.refs_8_ = bf16[64,512]{1,0:T(8,128)(2,1)S(1)} collective-permute-done((bf16[64,512]{1,0:T(8,128)(2,1)}, bf16[64,512]{1,0:T(8,128)(2,1)S(1)}, u32[]{:S(2)}, u32[]{:S(2)}) %collective-permute-start.7) | collective-permute-done | bytes 65568 | tf_op jit(solution)/shard_map/ppermute | solution.py:349
  54.9 1.2 %shard_map.84.query_ref = bf16[1024,512]{1,0:T(8,128)(2,1)S(1)} custom-call(s32[1,1024]{1,0:T(1,128)S(1)} %reshape.126.slot_ref, bf16[512,512]{1,0:T(8,128)(2,1)S(1)} %bitcast.13, bf16[64,512]{1,0:T(8,128)(2,1)S(1)} %collective-permute-done.refs_1_, bf16[64,512]{1,0:T(8,128)(2,1)S(1)} %collective-permute-done.1.refs_2_, ...), custom_call_target="tpu_custom_call" | custom-call | flops 1073741824 | bytes 2097152 | tf_op jit(solution)/shard_map/pallas_call | solution.py:197
  56.2 1.2 %shard_map.86 = bf16[256,512]{1,0:T(8,128)(2,1)S(1)} custom-call(s32[1,32]{1,0:T(1,128)S(1)} %reduce-window_clone.1.ends_ref, bf16[1024,512]{1,0:T(8,128)(2,1)S(1)} %shard_map.84.query_ref, bf16[384,256]{1,0:T(8,128)(2,1)S(1)} %collective-permute-done.8.rest_0_, bf16[384,256]{1,0:T(8,128)(2,1)S(1)} %collective-permute-done.9.rest_1_, ...), custom_call_target="tpu_custom_call" | custom-call | flops 268435456 | bytes 1966080 | tf_op jit(solution)/shard_map/pallas_call | solution.py:281
  57.3 2.2 %collective-permute-start.10 = (bf16[256,512]{1,0:T(8,128)(2,1)S(1)}, bf16[256,512]{1,0:T(8,128)(2,1)S(1)}, u32[]{:S(2)}, u32[]{:S(2)}) collective-permute-start(bf16[256,512]{1,0:T(8,128)(2,1)S(1)} %shard_map.86), channel_id=1, source_target_pairs={{0,3},{1,2},{2,1},{3,0},{4,7},{5,6},{6,5},{7,4},{8,11},{9,10},{10,... | collective-permute-start | bytes 786440 | tf_op jit(solution)/shard_map/ppermute | solution.py:393
  59.5 1.1 %shard_map.87 = bf16[256,512]{1,0:T(8,128)(2,1)S(1)} custom-call(s32[1,32]{1,0:T(1,128)S(1)} %reduce-window_clone.1.ends_ref, bf16[1024,512]{1,0:T(8,128)(2,1)S(1)} %shard_map.84.query_ref, bf16[384,256]{1,0:T(8,128)(2,1)S(1)} %collective-permute-done.8.rest_0_, bf16[384,256]{1,0:T(8,128)(2,1)S(1)} %collective-permute-done.9.rest_1_, ...), custom_call_target="tpu_custom_call" | custom-call | flops 268435456 | bytes 1966080 | tf_op jit(solution)/shard_map/pallas_call | solution.py:281
  61.3 1.1 %shard_map.88 = bf16[256,512]{1,0:T(8,128)(2,1)S(1)} custom-call(s32[1,32]{1,0:T(1,128)S(1)} %reduce-window_clone.1.ends_ref, bf16[1024,512]{1,0:T(8,128)(2,1)S(1)} %shard_map.84.query_ref, bf16[384,256]{1,0:T(8,128)(2,1)S(1)} %collective-permute-done.8.rest_0_, bf16[384,256]{1,0:T(8,128)(2,1)S(1)} %collective-permute-done.9.rest_1_, ...), custom_call_target="tpu_custom_call" | custom-call | flops 268435456 | bytes 1966080 | tf_op jit(solution)/shard_map/pallas_call | solution.py:281
  62.5 0.9 %collective-permute-start.12 = (bf16[256,512]{1,0:T(8,128)(2,1)S(1)}, bf16[256,512]{1,0:T(8,128)(2,1)S(1)}, u32[]{:S(2)}, u32[]{:S(2)}) collective-permute-start(bf16[256,512]{1,0:T(8,128)(2,1)S(1)} %shard_map.88), channel_id=1, source_target_pairs={{0,2},{1,3},{2,0},{3,1},{4,6},{5,7},{6,4},{7,5},{8,10},{9,11},{10,... | collective-permute-start | bytes 786440 | tf_op jit(solution)/shard_map/ppermute | solution.py:393
  63.3 1.1 %shard_map.89.refs_3_ = bf16[256,512]{1,0:T(8,128)(2,1)S(1)} custom-call(s32[1,32]{1,0:T(1,128)S(1)} %reduce-window_clone.1.ends_ref, bf16[1024,512]{1,0:T(8,128)(2,1)S(1)} %shard_map.84.query_ref, bf16[384,256]{1,0:T(8,128)(2,1)S(1)} %collective-permute-done.8.rest_0_, bf16[384,256]{1,0:T(8,128)(2,1)S(1)} %collective-permute-done.9.rest_1_, ...), custom_call_target="tpu_custom_call" | custom-call | flops 268435456 | bytes 1966080 | tf_op jit(solution)/shard_map/pallas_call | solution.py:281
  64.5 1.9 %collective-permute-done.10.refs_0_ = bf16[256,512]{1,0:T(8,128)(2,1)S(1)} collective-permute-done((bf16[256,512]{1,0:T(8,128)(2,1)S(1)}, bf16[256,512]{1,0:T(8,128)(2,1)S(1)}, u32[]{:S(2)}, u32[]{:S(2)}) %collective-permute-start.10) | collective-permute-done | bytes 262176 | tf_op jit(solution)/shard_map/ppermute | solution.py:393
  66.3 4.3 %collective-permute-done.11.refs_1_ = bf16[256,512]{1,0:T(8,128)(2,1)S(1)} collective-permute-done((bf16[256,512]{1,0:T(8,128)(2,1)S(1)}, bf16[256,512]{1,0:T(8,128)(2,1)S(1)}, u32[]{:S(2)}, u32[]{:S(2)}) %collective-permute-start.11) | collective-permute-done | bytes 262176 | tf_op jit(solution)/shard_map/ppermute | solution.py:393
  70.9 1.1 %shard_map.90 = bf16[256,2048]{1,0:T(8,128)(2,1)} custom-call(bf16[256,512]{1,0:T(8,128)(2,1)S(1)} %collective-permute-done.10.refs_0_, bf16[256,512]{1,0:T(8,128)(2,1)S(1)} %collective-permute-done.11.refs_1_, bf16[256,512]{1,0:T(8,128)(2,1)S(1)} %collective-permute-done.12.refs_2_, bf16[256,512]{1,0:T(8,128)(2,1)S(1)} %shard_map.89.refs_3_), custom_call_target="tpu_custom_call" | custom-call | bytes 2097152 | tf_op jit(solution)/shard_map/pallas_call | solution.py:306
  (30 shorter events, 3.3 us)
Async XLA Ops:
  6.5 29.6 %all-to-all-start = ((bf16[16,64,256]{2,1,0:T(8,128)(2,1)}), bf16[16,64,256]{2,1,0:T(8,128)(2,1)S(1)}, u32[]{:S(2)}, u32[]{:S(2)}) async-start(bf16[16,64,256]{2,1,0:T(8,128)(2,1)} %bitcast.14), calls=%async_computation | async-start | bytes 1048576 | tf_op jit(solution)/shard_map/all_to_all | solution.py:339
  14.9 21.0 %copy-start = (s32[4096]{0:T(1024)S(1)}, s32[4096]{0:T(1024)}, u32[]{:S(2)}) copy-start(s32[4096]{0:T(1024)} %param.9) | copy-start | bytes 49156
  14.9 21.0 %copy-start.1 = (s32[32]{0:T(128)S(1)}, s32[32]{0:T(128)}, u32[]{:S(2)}) copy-start(s32[32]{0:T(128)} %param.10) | copy-start | bytes 388
  24.4 16.1 %collective-permute-start = (bf16[64,512]{1,0:T(8,128)(2,1)}, bf16[64,512]{1,0:T(8,128)(2,1)S(1)}, u32[]{:S(2)}, u32[]{:S(2)}) collective-permute-start(bf16[64,512]{1,0:T(8,128)(2,1)} %get-tuple-element.31), channel_id=1, source_target_pairs={{0,8},{1,9},{2,10},{3,11},{4,12},{5,13},{6,14},{7,15},{8,0},{9,1},... | collective-permute-start | bytes 196616 | tf_op jit(solution)/shard_map/ppermute | solution.py:349
  27.3 16.1 %collective-permute-start.1 = (bf16[64,512]{1,0:T(8,128)(2,1)}, bf16[64,512]{1,0:T(8,128)(2,1)S(1)}, u32[]{:S(2)}, u32[]{:S(2)}) collective-permute-start(bf16[64,512]{1,0:T(8,128)(2,1)} %get-tuple-element.32), channel_id=1, source_target_pairs={{0,9},{1,8},{2,11},{3,10},{4,13},{5,12},{6,15},{7,14},{8,1},{9,0},... | collective-permute-start | bytes 196616 | tf_op jit(solution)/shard_map/ppermute | solution.py:349
  28.8 17.9 %collective-permute-start.2 = (bf16[64,512]{1,0:T(8,128)(2,1)}, bf16[64,512]{1,0:T(8,128)(2,1)S(1)}, u32[]{:S(2)}, u32[]{:S(2)}) collective-permute-start(bf16[64,512]{1,0:T(8,128)(2,1)} %get-tuple-element.33), channel_id=1, source_target_pairs={{0,10},{1,11},{2,8},{3,9},{4,14},{5,15},{6,12},{7,13},{8,2},{9,3},... | collective-permute-start | bytes 196616 | tf_op jit(solution)/shard_map/ppermute | solution.py:349
  32.0 16.1 %collective-permute-start.3 = (bf16[64,512]{1,0:T(8,128)(2,1)}, bf16[64,512]{1,0:T(8,128)(2,1)S(1)}, u32[]{:S(2)}, u32[]{:S(2)}) collective-permute-start(bf16[64,512]{1,0:T(8,128)(2,1)} %get-tuple-element.34), channel_id=1, source_target_pairs={{0,11},{1,10},{2,9},{3,8},{4,15},{5,14},{6,13},{7,12},{8,3},{9,2},... | collective-permute-start | bytes 196616 | tf_op jit(solution)/shard_map/ppermute | solution.py:349
  32.1 16.0 %collective-permute-start.4 = (bf16[64,512]{1,0:T(8,128)(2,1)}, bf16[64,512]{1,0:T(8,128)(2,1)S(1)}, u32[]{:S(2)}, u32[]{:S(2)}) collective-permute-start(bf16[64,512]{1,0:T(8,128)(2,1)} %get-tuple-element.35), channel_id=1, source_target_pairs={{0,12},{1,13},{2,14},{3,15},{4,8},{5,9},{6,10},{7,11},{8,4},{9,5},... | collective-permute-start | bytes 196616 | tf_op jit(solution)/shard_map/ppermute | solution.py:349
  36.1 18.8 %all-to-all-start.1 = ((bf16[8,64,512]{2,1,0:T(8,128)(2,1)}), bf16[8,64,512]{2,1,0:T(8,128)(2,1)S(1)}, u32[]{:S(2)}, u32[]{:S(2)}) async-start(bf16[8,64,512]{2,1,0:T(8,128)(2,1)} %bitcast.15), calls=%async_computation.1 | async-start | bytes 1048576 | tf_op jit(solution)/shard_map/all_to_all | solution.py:339
  40.5 9.8 %collective-permute-start.5 = (bf16[64,512]{1,0:T(8,128)(2,1)}, bf16[64,512]{1,0:T(8,128)(2,1)S(1)}, u32[]{:S(2)}, u32[]{:S(2)}) collective-permute-start(bf16[64,512]{1,0:T(8,128)(2,1)} %get-tuple-element.41), channel_id=1, source_target_pairs={{0,13},{1,12},{2,15},{3,14},{4,9},{5,8},{6,11},{7,10},{8,5},{9,4},... | collective-permute-start | bytes 196616 | tf_op jit(solution)/shard_map/ppermute | solution.py:349
  43.4 7.9 %collective-permute-start.6 = (bf16[64,512]{1,0:T(8,128)(2,1)}, bf16[64,512]{1,0:T(8,128)(2,1)S(1)}, u32[]{:S(2)}, u32[]{:S(2)}) collective-permute-start(bf16[64,512]{1,0:T(8,128)(2,1)} %get-tuple-element.42), channel_id=1, source_target_pairs={{0,14},{1,15},{2,12},{3,13},{4,10},{5,11},{6,8},{7,9},{8,6},{9,7},... | collective-permute-start | bytes 196616 | tf_op jit(solution)/shard_map/ppermute | solution.py:349
  46.7 8.2 %collective-permute-start.7 = (bf16[64,512]{1,0:T(8,128)(2,1)}, bf16[64,512]{1,0:T(8,128)(2,1)S(1)}, u32[]{:S(2)}, u32[]{:S(2)}) collective-permute-start(bf16[64,512]{1,0:T(8,128)(2,1)} %get-tuple-element.43), channel_id=1, source_target_pairs={{0,15},{1,14},{2,13},{3,12},{4,11},{5,10},{6,9},{7,8},{8,7},{9,6},... | collective-permute-start | bytes 196616 | tf_op jit(solution)/shard_map/ppermute | solution.py:349
  48.9 7.3 %collective-permute-start.8 = (bf16[384,256]{1,0:T(8,128)(2,1)S(1)}, bf16[384,256]{1,0:T(8,128)(2,1)S(1)}, u32[]{:S(2)}, u32[]{:S(2)}) collective-permute-start(bf16[384,256]{1,0:T(8,128)(2,1)S(1)} %get-tuple-element.45), channel_id=1, source_target_pairs={{0,4},{1,5},{2,6},{3,7},{8,12},{9,13},{10,14},{11,15},{4,0},{5,1},... | collective-permute-start | bytes 589832 | tf_op jit(solution)/shard_map/ppermute | solution.py:379
  48.9 7.2 %collective-permute-start.9 = (bf16[384,256]{1,0:T(8,128)(2,1)S(1)}, bf16[384,256]{1,0:T(8,128)(2,1)S(1)}, u32[]{:S(2)}, u32[]{:S(2)}) collective-permute-start(bf16[384,256]{1,0:T(8,128)(2,1)S(1)} %get-tuple-element.46), channel_id=1, source_target_pairs={{4,8},{5,9},{6,10},{7,11},{8,4},{9,5},{10,6},{11,7},{20,24},{21,25... | collective-permute-start | bytes 589832 | tf_op jit(solution)/shard_map/ppermute | solution.py:379
  57.3 9.0 %collective-permute-start.10 = (bf16[256,512]{1,0:T(8,128)(2,1)S(1)}, bf16[256,512]{1,0:T(8,128)(2,1)S(1)}, u32[]{:S(2)}, u32[]{:S(2)}) collective-permute-start(bf16[256,512]{1,0:T(8,128)(2,1)S(1)} %shard_map.86), channel_id=1, source_target_pairs={{0,3},{1,2},{2,1},{3,0},{4,7},{5,6},{6,5},{7,4},{8,11},{9,10},{10,... | collective-permute-start | bytes 786440 | tf_op jit(solution)/shard_map/ppermute | solution.py:393
  60.7 10.0 %collective-permute-start.11 = (bf16[256,512]{1,0:T(8,128)(2,1)S(1)}, bf16[256,512]{1,0:T(8,128)(2,1)S(1)}, u32[]{:S(2)}, u32[]{:S(2)}) collective-permute-start(bf16[256,512]{1,0:T(8,128)(2,1)S(1)} %shard_map.87), channel_id=1, source_target_pairs={{0,1},{1,0},{2,3},{3,2},{4,5},{5,4},{6,7},{7,6},{8,9},{9,8},{10,11... | collective-permute-start | bytes 786440 | tf_op jit(solution)/shard_map/ppermute | solution.py:393
  62.5 8.4 %collective-permute-start.12 = (bf16[256,512]{1,0:T(8,128)(2,1)S(1)}, bf16[256,512]{1,0:T(8,128)(2,1)S(1)}, u32[]{:S(2)}, u32[]{:S(2)}) collective-permute-start(bf16[256,512]{1,0:T(8,128)(2,1)S(1)} %shard_map.88), channel_id=1, source_target_pairs={{0,2},{1,3},{2,0},{3,1},{4,6},{5,7},{6,4},{7,5},{8,10},{9,11},{10,... | collective-permute-start | bytes 786440 | tf_op jit(solution)/shard_map/ppermute | solution.py:393

commit v17 on v16

--- a/solution.py
+++ b/solution.py
@@ -341,11 +341,10 @@
 
     (kv,) = project(*operands, (w_key, value_weight), (True, False), devices, members)
     kv = exchange(kv, None)
-    apart = list(range(half_devices, devices))
+    apart = [half_devices + i * members + j for j in range(members)[::-1] for i in range(groups // 2)[::-1]]
     near, *far = project(*operands, (w_query,), (True,), devices, members, apart)
     queries = []
-    for i, piece in enumerate(far):
-        distance = half_devices + i
+    for distance, piece in zip(apart, far):
         queries.append(lax.ppermute(piece, "ctx", [(j, j ^ distance) for j in range(devices)]))
 
     table = positions.reshape(devices, rows)
@@ -360,7 +359,7 @@
     wanted = jnp.arange(group_rows, dtype=jnp.int32)[None, :, None] == place_in[:, None, :]
     slot = jnp.sum(jnp.where(wanted, slots[:, None, :], 0), axis=2)
     index = jnp.arange(half_devices, dtype=jnp.int32)
-    sources = [device // half_devices * half_devices + index, device ^ (half_devices + index)]
+    sources = [device // half_devices * half_devices + index, device ^ jnp.asarray(np.int32(apart))]
     query_slot = slot[jnp.concatenate(sources)].reshape(1, devices * group_rows)
     slot = slot.reshape(1, devices * group_rows)
     ends = jnp.cumsum(lengths, dtype=jnp.int32)[None, :]
@@ -374,9 +373,9 @@
     odd = [i for i in range(1, groups - 1, 2)]
     even = [i for i in range(0, groups, 2)]
     pieces = []
-    for lower, out in ((odd, odd_out), (even, even_out)):
+    for lower, out in ((even, even_out), (odd, odd_out)):
         up = [(i * members + j, (i + 1) * members + j) for i in lower for j in range(members)]
-        pieces.insert(0, lax.ppermute(out, "ctx", up + [(j, i) for i, j in up]))
+        pieces.append(lax.ppermute(out, "ctx", up + [(j, i) for i, j in up]))
     pieces = (*pieces, *runs)
 
     (query,) = place(queries, query_slot, [2 * run])

time: 72.2 us -> 72.6 us (level)
    ppermute x8, starting transfers between devices: 19 us -> 18.3 us  [shards(): lax.ppermute(piece, 'ctx', [(j, j ^ distance) for j in range(devices)])]
where the time goes in v17:
time: 72.6 us; the launch traced here: 72.3 us
  starting transfers between devices  35.3 us (49%)
  Pallas kernels  23.7 us (33%)
  waiting for transfers between devices  11.6 us (16%)
  local copies, waits for them, and re-layouts  0.74 us (1%)
    ppermute x8, starting transfers between devices, shards(): lax.ppermute(piece, 'ctx', [(j, j ^ distance) for j in range(devices)])  18.3 us
    pallas_call x2, Pallas kernels, project(): pl.pallas_call(functools.partial(project_kernel, kinds, devices, heads, a...  16 us
    all_to_all x2, starting transfers between devices, exchange(): lax.all_to_all(flat, 'ctx', split_axis=0, concat_axis=0, tiled=True, axis...  12 us
    ppermute x3, waiting for transfers between devices, shards(): out = lax.ppermute(out, ('dp', 'ctx'), route)  6.24 us
    ppermute x8, waiting for transfers between devices, shards(): lax.ppermute(piece, 'ctx', [(j, j ^ distance) for j in range(devices)])  5.35 us
    pallas_call x4, Pallas kernels, attend(): pl.pallas_call(functools.partial(attend_kernel, block, turn, members, dev...  4.58 us
    ppermute x3, starting transfers between devices, shards(): out = lax.ppermute(out, ('dp', 'ctx'), route)  3.68 us
    pallas_call x2, Pallas kernels, place(): pl.pallas_call(functools.partial(place_kernel, len(pieces), members), out...  1.97 us
  transfers between devices with their start and end apart: 15, of which 5 were waited for; matrix products, arithmetic and copies ran while one was open for 2% of the time, Pallas kernels for 21%

profile of v17, /device:TPU:0, one launch (start us, length us, event | category | flops | bytes accessed | tf_op | source)
XLA Modules:
  0.0 72.3 jit_solution(8703895147787518916)
XLA Ops:
  0.0 6.5 %shard_map.91 = bf16[4,4,64,256]{3,2,1,0:T(8,128)(2,1)} custom-call(s32[32,128]{1,0:T(8,128)} %bitcast.16, f32[1,128]{1,0:T(1,128)} %constant.79.clone.freq_hbm, bf16[4096]{0:T(1024)(128)(2,1)} %gain_hbm.3, bf16[256,4096]{1,0:T(8,128)(2,1)} %tokens_hbm.3, bf16[4096,512]{1,0:T(8,128)(2,1)} %rest_0_.2, bf16[4096,512]{1,0:T(8,128)(2,1)} %rest_1_.1), custom_call_target="tpu_custom_call" | custom-call | flops 2147483648 | bytes 11010048 | tf_op jit(solution)/shard_map/pallas_call | solution.py:148
  6.5 8.3 %all-to-all-start = ((bf16[16,64,256]{2,1,0:T(8,128)(2,1)}), bf16[16,64,256]{2,1,0:T(8,128)(2,1)S(1)}, u32[]{:S(2)}, u32[]{:S(2)}) async-start(bf16[16,64,256]{2,1,0:T(8,128)(2,1)} %bitcast.14), calls=%async_computation | async-start | bytes 1048576 | tf_op jit(solution)/shard_map/all_to_all | solution.py:339
  14.9 9.5 %shard_map.92 = (bf16[2,4,64,512]{3,2,1,0:T(8,128)(2,1)}, bf16[64,512]{1,0:T(8,128)(2,1)}, bf16[64,512]{1,0:T(8,128)(2,1)}, bf16[64,512]{1,0:T(8,128)(2,1)}, bf1...) custom-call(s32[32,128]{1,0:T(8,128)} %bitcast.17, ...), custom_call_target="tpu_custom_call" | custom-call | flops 4294967296 | bytes 19922944 | tf_op jit(solution)/shard_map/pallas_call | solution.py:148
  24.4 5.6 %collective-permute-start = (bf16[64,512]{1,0:T(8,128)(2,1)}, bf16[64,512]{1,0:T(8,128)(2,1)S(1)}, u32[]{:S(2)}, u32[]{:S(2)}) collective-permute-start(bf16[64,512]{1,0:T(8,128)(2,1)} %get-tuple-element.31), channel_id=1, source_target_pairs={{0,15},{1,14},{2,13},{3,12},{4,11},{5,10},{6,9},{7,8},{8,7},{9,6},... | collective-permute-start | bytes 196616 | tf_op jit(solution)/shard_map/ppermute | solution.py:348
  30.0 2.9 %collective-permute-start.2 = (bf16[64,512]{1,0:T(8,128)(2,1)}, bf16[64,512]{1,0:T(8,128)(2,1)S(1)}, u32[]{:S(2)}, u32[]{:S(2)}) collective-permute-start(bf16[64,512]{1,0:T(8,128)(2,1)} %get-tuple-element.33), channel_id=1, source_target_pairs={{0,14},{1,15},{2,12},{3,13},{4,10},{5,11},{6,8},{7,9},{8,6},{9,7},... | collective-permute-start | bytes 196616 | tf_op jit(solution)/shard_map/ppermute | solution.py:348
  32.9 0.9 %collective-permute-start.3 = (bf16[64,512]{1,0:T(8,128)(2,1)}, bf16[64,512]{1,0:T(8,128)(2,1)S(1)}, u32[]{:S(2)}, u32[]{:S(2)}) collective-permute-start(bf16[64,512]{1,0:T(8,128)(2,1)} %get-tuple-element.34), channel_id=1, source_target_pairs={{0,10},{1,11},{2,8},{3,9},{4,14},{5,15},{6,12},{7,13},{8,2},{9,3},... | collective-permute-start | bytes 196616 | tf_op jit(solution)/shard_map/ppermute | solution.py:348
  33.8 3.8 %collective-permute-start.4 = (bf16[64,512]{1,0:T(8,128)(2,1)}, bf16[64,512]{1,0:T(8,128)(2,1)S(1)}, u32[]{:S(2)}, u32[]{:S(2)}) collective-permute-start(bf16[64,512]{1,0:T(8,128)(2,1)} %get-tuple-element.35), channel_id=1, source_target_pairs={{0,13},{1,12},{2,15},{3,14},{4,9},{5,8},{6,11},{7,10},{8,5},{9,4},... | collective-permute-start | bytes 196616 | tf_op jit(solution)/shard_map/ppermute | solution.py:348
  37.7 3.7 %all-to-all-start.1 = ((bf16[8,64,512]{2,1,0:T(8,128)(2,1)}), bf16[8,64,512]{2,1,0:T(8,128)(2,1)S(1)}, u32[]{:S(2)}, u32[]{:S(2)}) async-start(bf16[8,64,512]{2,1,0:T(8,128)(2,1)} %bitcast.15), calls=%async_computation.1 | async-start | bytes 1048576 | tf_op jit(solution)/shard_map/all_to_all | solution.py:339
  42.3 1.1 %collective-permute-start.5 = (bf16[64,512]{1,0:T(8,128)(2,1)}, bf16[64,512]{1,0:T(8,128)(2,1)S(1)}, u32[]{:S(2)}, u32[]{:S(2)}) collective-permute-start(bf16[64,512]{1,0:T(8,128)(2,1)} %get-tuple-element.41), channel_id=1, source_target_pairs={{0,9},{1,8},{2,11},{3,10},{4,13},{5,12},{6,15},{7,14},{8,1},{9,0},... | collective-permute-start | bytes 196616 | tf_op jit(solution)/shard_map/ppermute | solution.py:348
  43.4 4.0 %collective-permute-start.6 = (bf16[64,512]{1,0:T(8,128)(2,1)}, bf16[64,512]{1,0:T(8,128)(2,1)S(1)}, u32[]{:S(2)}, u32[]{:S(2)}) collective-permute-start(bf16[64,512]{1,0:T(8,128)(2,1)} %get-tuple-element.42), channel_id=1, source_target_pairs={{0,12},{1,13},{2,14},{3,15},{4,8},{5,9},{6,10},{7,11},{8,4},{9,5},... | collective-permute-start | bytes 196616 | tf_op jit(solution)/shard_map/ppermute | solution.py:348
  47.4 0.7 %shard_map.94 = (bf16[128,256]{1,0:T(8,128)(2,1)S(1)}, bf16[384,256]{1,0:T(8,128)(2,1)S(1)}, bf16[128,256]{1,0:T(8,128)(2,1)S(1)}, bf16[384,256]{1,0:T(8,128)(2,...) custom-call(s32[1,1024]{1,0:T(1,128)S(1)} %reshape.147.slot_ref, bf16[1024,256]{1,0:T(8,128)(2,1)S(1)} %bitcast.12), custom_call_target="tpu_custom_call" | custom-call | flops 536870912 | bytes 1048576 | tf_op jit(solution)/shard_map/pallas_call | solution.py:197
  48.1 0.7 collective-permute-start.8
  50.2 1.1 %collective-permute-done.6.refs_7_ = bf16[64,512]{1,0:T(8,128)(2,1)S(1)} collective-permute-done((bf16[64,512]{1,0:T(8,128)(2,1)}, bf16[64,512]{1,0:T(8,128)(2,1)S(1)}, u32[]{:S(2)}, u32[]{:S(2)}) %collective-permute-start.6) | collective-permute-done | bytes 65568 | tf_op jit(solution)/shard_map/ppermute | solution.py:348
  51.4 4.1 %collective-permute-done.7.refs_8_ = bf16[64,512]{1,0:T(8,128)(2,1)S(1)} collective-permute-done((bf16[64,512]{1,0:T(8,128)(2,1)}, bf16[64,512]{1,0:T(8,128)(2,1)S(1)}, u32[]{:S(2)}, u32[]{:S(2)}) %collective-permute-start.7) | collective-permute-done | bytes 65568 | tf_op jit(solution)/shard_map/ppermute | solution.py:348
  55.5 1.2 %shard_map.93.query_ref = bf16[1024,512]{1,0:T(8,128)(2,1)S(1)} custom-call(s32[1,1024]{1,0:T(1,128)S(1)} %reshape.141.slot_ref, bf16[512,512]{1,0:T(8,128)(2,1)S(1)} %bitcast.13, bf16[64,512]{1,0:T(8,128)(2,1)S(1)} %collective-permute-done.refs_1_, bf16[64,512]{1,0:T(8,128)(2,1)S(1)} %collective-permute-done.1.refs_2_, ...), custom_call_target="tpu_custom_call" | custom-call | flops 1073741824 | bytes 2097152 | tf_op jit(solution)/shard_map/pallas_call | solution.py:197
  56.7 1.2 %shard_map.95 = bf16[256,512]{1,0:T(8,128)(2,1)S(1)} custom-call(s32[1,32]{1,0:T(1,128)S(1)} %reduce-window_clone.1.ends_ref, bf16[1024,512]{1,0:T(8,128)(2,1)S(1)} %shard_map.93.query_ref, bf16[384,256]{1,0:T(8,128)(2,1)S(1)} %collective-permute-done.8.rest_0_, bf16[384,256]{1,0:T(8,128)(2,1)S(1)} %collective-permute-done.9.rest_1_, ...), custom_call_target="tpu_custom_call" | custom-call | flops 268435456 | bytes 1966080 | tf_op jit(solution)/shard_map/pallas_call | solution.py:281
  57.9 1.9 %collective-permute-start.10 = (bf16[256,512]{1,0:T(8,128)(2,1)S(1)}, bf16[256,512]{1,0:T(8,128)(2,1)S(1)}, u32[]{:S(2)}, u32[]{:S(2)}) collective-permute-start(bf16[256,512]{1,0:T(8,128)(2,1)S(1)} %shard_map.95), channel_id=1, source_target_pairs={{0,3},{1,2},{2,1},{3,0},{4,7},{5,6},{6,5},{7,4},{8,11},{9,10},{10,... | collective-permute-start | bytes 786440 | tf_op jit(solution)/shard_map/ppermute | solution.py:392
  59.8 1.1 %shard_map.96 = bf16[256,512]{1,0:T(8,128)(2,1)S(1)} custom-call(s32[1,32]{1,0:T(1,128)S(1)} %reduce-window_clone.1.ends_ref, bf16[1024,512]{1,0:T(8,128)(2,1)S(1)} %shard_map.93.query_ref, bf16[384,256]{1,0:T(8,128)(2,1)S(1)} %collective-permute-done.8.rest_0_, bf16[384,256]{1,0:T(8,128)(2,1)S(1)} %collective-permute-done.9.rest_1_, ...), custom_call_target="tpu_custom_call" | custom-call | flops 268435456 | bytes 1966080 | tf_op jit(solution)/shard_map/pallas_call | solution.py:281
  60.9 1.2 %collective-permute-start.11 = (bf16[256,512]{1,0:T(8,128)(2,1)S(1)}, bf16[256,512]{1,0:T(8,128)(2,1)S(1)}, u32[]{:S(2)}, u32[]{:S(2)}) collective-permute-start(bf16[256,512]{1,0:T(8,128)(2,1)S(1)} %shard_map.96), channel_id=1, source_target_pairs={{0,1},{1,0},{2,3},{3,2},{4,5},{5,4},{6,7},{7,6},{8,9},{9,8},{10,11... | collective-permute-start | bytes 786440 | tf_op jit(solution)/shard_map/ppermute | solution.py:392
  62.1 1.1 %shard_map.97 = bf16[256,512]{1,0:T(8,128)(2,1)S(1)} custom-call(s32[1,32]{1,0:T(1,128)S(1)} %reduce-window_clone.1.ends_ref, bf16[1024,512]{1,0:T(8,128)(2,1)S(1)} %shard_map.93.query_ref, bf16[384,256]{1,0:T(8,128)(2,1)S(1)} %collective-permute-done.8.rest_0_, bf16[384,256]{1,0:T(8,128)(2,1)S(1)} %collective-permute-done.9.rest_1_, ...), custom_call_target="tpu_custom_call" | custom-call | flops 268435456 | bytes 1966080 | tf_op jit(solution)/shard_map/pallas_call | solution.py:281
  63.9 1.1 %shard_map.98.refs_3_ = bf16[256,512]{1,0:T(8,128)(2,1)S(1)} custom-call(s32[1,32]{1,0:T(1,128)S(1)} %reduce-window_clone.1.ends_ref, bf16[1024,512]{1,0:T(8,128)(2,1)S(1)} %shard_map.93.query_ref, bf16[384,256]{1,0:T(8,128)(2,1)S(1)} %collective-permute-done.8.rest_0_, bf16[384,256]{1,0:T(8,128)(2,1)S(1)} %collective-permute-done.9.rest_1_, ...), custom_call_target="tpu_custom_call" | custom-call | flops 268435456 | bytes 1966080 | tf_op jit(solution)/shard_map/pallas_call | solution.py:281
  65.0 2.2 %collective-permute-done.10.refs_0_ = bf16[256,512]{1,0:T(8,128)(2,1)S(1)} collective-permute-done((bf16[256,512]{1,0:T(8,128)(2,1)S(1)}, bf16[256,512]{1,0:T(8,128)(2,1)S(1)}, u32[]{:S(2)}, u32[]{:S(2)}) %collective-permute-start.10) | collective-permute-done | bytes 262176 | tf_op jit(solution)/shard_map/ppermute | solution.py:392
  67.2 4.1 %collective-permute-done.11.refs_1_ = bf16[256,512]{1,0:T(8,128)(2,1)S(1)} collective-permute-done((bf16[256,512]{1,0:T(8,128)(2,1)S(1)}, bf16[256,512]{1,0:T(8,128)(2,1)S(1)}, u32[]{:S(2)}, u32[]{:S(2)}) %collective-permute-start.11) | collective-permute-done | bytes 262176 | tf_op jit(solution)/shard_map/ppermute | solution.py:392
  71.3 1.1 %shard_map.99 = bf16[256,2048]{1,0:T(8,128)(2,1)} custom-call(bf16[256,512]{1,0:T(8,128)(2,1)S(1)} %collective-permute-done.10.refs_0_, bf16[256,512]{1,0:T(8,128)(2,1)S(1)} %collective-permute-done.11.refs_1_, bf16[256,512]{1,0:T(8,128)(2,1)S(1)} %collective-permute-done.12.refs_2_, bf16[256,512]{1,0:T(8,128)(2,1)S(1)} %shard_map.98.refs_3_), custom_call_target="tpu_custom_call" | custom-call | bytes 2097152 | tf_op jit(solution)/shard_map/pallas_call | solution.py:306
  (32 shorter events, 3.0 us)
Async XLA Ops:
  6.5 31.2 %all-to-all-start = ((bf16[16,64,256]{2,1,0:T(8,128)(2,1)}), bf16[16,64,256]{2,1,0:T(8,128)(2,1)S(1)}, u32[]{:S(2)}, u32[]{:S(2)}) async-start(bf16[16,64,256]{2,1,0:T(8,128)(2,1)} %bitcast.14), calls=%async_computation | async-start | bytes 1048576 | tf_op jit(solution)/shard_map/all_to_all | solution.py:339
  14.9 22.8 %copy-start = (s32[4096]{0:T(1024)S(1)}, s32[4096]{0:T(1024)}, u32[]{:S(2)}) copy-start(s32[4096]{0:T(1024)} %param.10) | copy-start | bytes 49156
  14.9 26.7 %copy-start.2 = (s32[32]{0:T(128)S(1)}, s32[32]{0:T(128)}, u32[]{:S(2)}) copy-start(s32[32]{0:T(128)} %param.11) | copy-start | bytes 388
  14.9 27.4 %copy-start.1 = (s32[8]{0:T(128)S(1)}, s32[8]{0:T(128)}, u32[]{:S(2)}) copy-start(s32[8]{0:T(128)} %constant.80.clone) | copy-start | bytes 100
  24.4 17.9 %collective-permute-start = (bf16[64,512]{1,0:T(8,128)(2,1)}, bf16[64,512]{1,0:T(8,128)(2,1)S(1)}, u32[]{:S(2)}, u32[]{:S(2)}) collective-permute-start(bf16[64,512]{1,0:T(8,128)(2,1)} %get-tuple-element.31), channel_id=1, source_target_pairs={{0,15},{1,14},{2,13},{3,12},{4,11},{5,10},{6,9},{7,8},{8,7},{9,6},... | collective-permute-start | bytes 196616 | tf_op jit(solution)/shard_map/ppermute | solution.py:348
  30.0 13.4 %collective-permute-start.1 = (bf16[64,512]{1,0:T(8,128)(2,1)}, bf16[64,512]{1,0:T(8,128)(2,1)S(1)}, u32[]{:S(2)}, u32[]{:S(2)}) collective-permute-start(bf16[64,512]{1,0:T(8,128)(2,1)} %get-tuple-element.32), channel_id=1, source_target_pairs={{0,11},{1,10},{2,9},{3,8},{4,15},{5,14},{6,13},{7,12},{8,3},{9,2},... | collective-permute-start | bytes 196616 | tf_op jit(solution)/shard_map/ppermute | solution.py:348
  30.0 17.4 %collective-permute-start.2 = (bf16[64,512]{1,0:T(8,128)(2,1)}, bf16[64,512]{1,0:T(8,128)(2,1)S(1)}, u32[]{:S(2)}, u32[]{:S(2)}) collective-permute-start(bf16[64,512]{1,0:T(8,128)(2,1)} %get-tuple-element.33), channel_id=1, source_target_pairs={{0,14},{1,15},{2,12},{3,13},{4,10},{5,11},{6,8},{7,9},{8,6},{9,7},... | collective-permute-start | bytes 196616 | tf_op jit(solution)/shard_map/ppermute | solution.py:348
  32.9 14.4 %collective-permute-start.3 = (bf16[64,512]{1,0:T(8,128)(2,1)}, bf16[64,512]{1,0:T(8,128)(2,1)S(1)}, u32[]{:S(2)}, u32[]{:S(2)}) collective-permute-start(bf16[64,512]{1,0:T(8,128)(2,1)} %get-tuple-element.34), channel_id=1, source_target_pairs={{0,10},{1,11},{2,8},{3,9},{4,14},{5,15},{6,12},{7,13},{8,2},{9,3},... | collective-permute-start | bytes 196616 | tf_op jit(solution)/shard_map/ppermute | solution.py:348
  33.8 13.5 %collective-permute-start.4 = (bf16[64,512]{1,0:T(8,128)(2,1)}, bf16[64,512]{1,0:T(8,128)(2,1)S(1)}, u32[]{:S(2)}, u32[]{:S(2)}) collective-permute-start(bf16[64,512]{1,0:T(8,128)(2,1)} %get-tuple-element.35), channel_id=1, source_target_pairs={{0,13},{1,12},{2,15},{3,14},{4,9},{5,8},{6,11},{7,10},{8,5},{9,4},... | collective-permute-start | bytes 196616 | tf_op jit(solution)/shard_map/ppermute | solution.py:348
  37.7 17.8 %all-to-all-start.1 = ((bf16[8,64,512]{2,1,0:T(8,128)(2,1)}), bf16[8,64,512]{2,1,0:T(8,128)(2,1)S(1)}, u32[]{:S(2)}, u32[]{:S(2)}) async-start(bf16[8,64,512]{2,1,0:T(8,128)(2,1)} %bitcast.15), calls=%async_computation.1 | async-start | bytes 1048576 | tf_op jit(solution)/shard_map/all_to_all | solution.py:339
  42.3 7.9 %collective-permute-start.5 = (bf16[64,512]{1,0:T(8,128)(2,1)}, bf16[64,512]{1,0:T(8,128)(2,1)S(1)}, u32[]{:S(2)}, u32[]{:S(2)}) collective-permute-start(bf16[64,512]{1,0:T(8,128)(2,1)} %get-tuple-element.41), channel_id=1, source_target_pairs={{0,9},{1,8},{2,11},{3,10},{4,13},{5,12},{6,15},{7,14},{8,1},{9,0},... | collective-permute-start | bytes 196616 | tf_op jit(solution)/shard_map/ppermute | solution.py:348
  43.4 8.0 %collective-permute-start.6 = (bf16[64,512]{1,0:T(8,128)(2,1)}, bf16[64,512]{1,0:T(8,128)(2,1)S(1)}, u32[]{:S(2)}, u32[]{:S(2)}) collective-permute-start(bf16[64,512]{1,0:T(8,128)(2,1)} %get-tuple-element.42), channel_id=1, source_target_pairs={{0,12},{1,13},{2,14},{3,15},{4,8},{5,9},{6,10},{7,11},{8,4},{9,5},... | collective-permute-start | bytes 196616 | tf_op jit(solution)/shard_map/ppermute | solution.py:348
  47.4 8.1 %collective-permute-start.7 = (bf16[64,512]{1,0:T(8,128)(2,1)}, bf16[64,512]{1,0:T(8,128)(2,1)S(1)}, u32[]{:S(2)}, u32[]{:S(2)}) collective-permute-start(bf16[64,512]{1,0:T(8,128)(2,1)} %get-tuple-element.43), channel_id=1, source_target_pairs={{0,8},{1,9},{2,10},{3,11},{4,12},{5,13},{6,14},{7,15},{8,0},{9,1},... | collective-permute-start | bytes 196616 | tf_op jit(solution)/shard_map/ppermute | solution.py:348
  48.1 8.6 %collective-permute-start.8 = (bf16[384,256]{1,0:T(8,128)(2,1)S(1)}, bf16[384,256]{1,0:T(8,128)(2,1)S(1)}, u32[]{:S(2)}, u32[]{:S(2)}) collective-permute-start(bf16[384,256]{1,0:T(8,128)(2,1)S(1)} %get-tuple-element.45), channel_id=1, source_target_pairs={{0,4},{1,5},{2,6},{3,7},{8,12},{9,13},{10,14},{11,15},{4,0},{5,1},... | collective-permute-start | bytes 589832 | tf_op jit(solution)/shard_map/ppermute | solution.py:378
  48.8 7.9 %collective-permute-start.9 = (bf16[384,256]{1,0:T(8,128)(2,1)S(1)}, bf16[384,256]{1,0:T(8,128)(2,1)S(1)}, u32[]{:S(2)}, u32[]{:S(2)}) collective-permute-start(bf16[384,256]{1,0:T(8,128)(2,1)S(1)} %get-tuple-element.46), channel_id=1, source_target_pairs={{4,8},{5,9},{6,10},{7,11},{8,4},{9,5},{10,6},{11,7},{20,24},{21,25... | collective-permute-start | bytes 589832 | tf_op jit(solution)/shard_map/ppermute | solution.py:378
  57.9 9.3 %collective-permute-start.10 = (bf16[256,512]{1,0:T(8,128)(2,1)S(1)}, bf16[256,512]{1,0:T(8,128)(2,1)S(1)}, u32[]{:S(2)}, u32[]{:S(2)}) collective-permute-start(bf16[256,512]{1,0:T(8,128)(2,1)S(1)} %shard_map.95), channel_id=1, source_target_pairs={{0,3},{1,2},{2,1},{3,0},{4,7},{5,6},{6,5},{7,4},{8,11},{9,10},{10,... | collective-permute-start | bytes 786440 | tf_op jit(solution)/shard_map/ppermute | solution.py:392
  60.9 10.3 %collective-permute-start.11 = (bf16[256,512]{1,0:T(8,128)(2,1)S(1)}, bf16[256,512]{1,0:T(8,128)(2,1)S(1)}, u32[]{:S(2)}, u32[]{:S(2)}) collective-permute-start(bf16[256,512]{1,0:T(8,128)(2,1)S(1)} %shard_map.96), channel_id=1, source_target_pairs={{0,1},{1,0},{2,3},{3,2},{4,5},{5,4},{6,7},{7,6},{8,9},{9,8},{10,11... | collective-permute-start | bytes 786440 | tf_op jit(solution)/shard_map/ppermute | solution.py:392
  63.3 8.0 %collective-permute-start.12 = (bf16[256,512]{1,0:T(8,128)(2,1)S(1)}, bf16[256,512]{1,0:T(8,128)(2,1)S(1)}, u32[]{:S(2)}, u32[]{:S(2)}) collective-permute-start(bf16[256,512]{1,0:T(8,128)(2,1)S(1)} %shard_map.97), channel_id=1, source_target_pairs={{0,2},{1,3},{2,0},{3,1},{4,6},{5,7},{6,4},{7,5},{8,10},{9,11},{10,... | collective-permute-start | bytes 786440 | tf_op jit(solution)/shard_map/ppermute | solution.py:392

commit v18 on v16

--- a/solution.py
+++ b/solution.py
@@ -343,11 +343,6 @@
     kv = exchange(kv, None)
     apart = list(range(half_devices, devices))
     near, *far = project(*operands, (w_query,), (True,), devices, members, apart)
-    queries = []
-    for i, piece in enumerate(far):
-        distance = half_devices + i
-        queries.append(lax.ppermute(piece, "ctx", [(j, j ^ distance) for j in range(devices)]))
-
     table = positions.reshape(devices, rows)
     ours = group_of(table, block, devices, members) == group
     first_run = group * run
@@ -365,6 +360,12 @@
     slot = slot.reshape(1, devices * group_rows)
     ends = jnp.cumsum(lengths, dtype=jnp.int32)[None, :]
 
+    *far, slot, query_slot = lax.optimization_barrier((*far, slot, query_slot))
+    queries = []
+    for i, piece in enumerate(far):
+        distance = half_devices + i
+        queries.append(lax.ppermute(piece, "ctx", [(j, j ^ distance) for j in range(devices)]))
+
     kv, near = lax.optimization_barrier((kv, near))
     queries.insert(0, exchange(near, halves))
     kv, *queries[1:6] = lax.optimization_barrier((kv, *queries[1:6]))

time: 72.2 us -> 85.6 us (1.19); the launches traced: 71.9 us -> 84 us
  waiting for transfers between devices: 11 us -> 24.7 us
  starting transfers between devices: 35.5 us -> 34 us
    ppermute x8, waiting for transfers between devices: 4.64 us -> 13.6 us  [shards(): lax.ppermute(piece, 'ctx', [(j, j ^ distance) for j in range(devices)])]
    all_to_all x2, waiting for transfers between devices: 0.01 us -> 5.55 us  [exchange(): lax.all_to_all(flat, 'ctx', split_axis=0, concat_axis=0, tiled=True, axis...]
    ppermute x8, starting transfers between devices: 19 us -> 17.2 us  [shards(): lax.ppermute(piece, 'ctx', [(j, j ^ distance) for j in range(devices)])]
    ppermute x3, waiting for transfers between devices: 6.39 us -> 5.48 us  [shards(): out = lax.ppermute(out, ('dp', 'ctx'), route)]
  transfers between devices with their start and end apart: 15 -> 15, of which waited for: 5 -> 8; matrix products, arithmetic and copies ran while one was open for 2% -> 2% of each run, Pallas kernels for 21% -> 18%
where the time goes in v18:
time: 85.6 us; the launch traced here: 84 us
  starting transfers between devices  34 us (40%)
  waiting for transfers between devices  24.7 us (29%)
  Pallas kernels  23.7 us (28%)
    ppermute x8, starting transfers between devices, shards(): lax.ppermute(piece, 'ctx', [(j, j ^ distance) for j in range(devices)])  17.2 us
    pallas_call x2, Pallas kernels, project(): pl.pallas_call(functools.partial(project_kernel, kinds, devices, heads, a...  16.1 us
    ppermute x8, waiting for transfers between devices, shards(): lax.ppermute(piece, 'ctx', [(j, j ^ distance) for j in range(devices)])  13.6 us
    all_to_all x2, starting transfers between devices, exchange(): lax.all_to_all(flat, 'ctx', split_axis=0, concat_axis=0, tiled=True, axis...  11.8 us
    all_to_all x2, waiting for transfers between devices, exchange(): lax.all_to_all(flat, 'ctx', split_axis=0, concat_axis=0, tiled=True, axis...  5.55 us
    ppermute x3, waiting for transfers between devices, shards(): out = lax.ppermute(out, ('dp', 'ctx'), route)  5.48 us
    pallas_call x4, Pallas kernels, attend(): pl.pallas_call(functools.partial(attend_kernel, block, turn, members, dev...  4.58 us
    ppermute x3, starting transfers between devices, shards(): out = lax.ppermute(out, ('dp', 'ctx'), route)  3.69 us
  transfers between devices with their start and end apart: 15, of which 8 were waited for; matrix products, arithmetic and copies ran while one was open for 2% of the time, Pallas kernels for 18%

profile of v18, /device:TPU:0, one launch (start us, length us, event | category | flops | bytes accessed | tf_op | source)
XLA Modules:
  0.0 84.0 jit_solution(818775219878921958)
XLA Ops:
  0.0 6.5 %shard_map.83 = bf16[4,4,64,256]{3,2,1,0:T(8,128)(2,1)} custom-call(s32[32,128]{1,0:T(8,128)} %bitcast.16, f32[1,128]{1,0:T(1,128)} %constant.78.clone.freq_hbm, bf16[4096]{0:T(1024)(128)(2,1)} %gain_hbm.3, bf16[256,4096]{1,0:T(8,128)(2,1)} %tokens_hbm.3, bf16[4096,512]{1,0:T(8,128)(2,1)} %rest_0_.3, bf16[4096,512]{1,0:T(8,128)(2,1)} %rest_1_.1), custom_call_target="tpu_custom_call" | custom-call | flops 2147483648 | bytes 11010048 | tf_op jit(solution)/shard_map/pallas_call | solution.py:148
  6.5 8.3 %all-to-all-start = ((bf16[16,64,256]{2,1,0:T(8,128)(2,1)}), bf16[16,64,256]{2,1,0:T(8,128)(2,1)S(1)}, u32[]{:S(2)}, u32[]{:S(2)}) async-start(bf16[16,64,256]{2,1,0:T(8,128)(2,1)} %bitcast.14), calls=%async_computation | async-start | bytes 1048576 | tf_op jit(solution)/shard_map/all_to_all | solution.py:339
  14.9 9.5 %shard_map.82 = (bf16[2,4,64,512]{3,2,1,0:T(8,128)(2,1)}, bf16[64,512]{1,0:T(8,128)(2,1)}, bf16[64,512]{1,0:T(8,128)(2,1)}, bf16[64,512]{1,0:T(8,128)(2,1)}, bf1...) custom-call(s32[32,128]{1,0:T(8,128)} %bitcast.17, ...), custom_call_target="tpu_custom_call" | custom-call | flops 4294967296 | bytes 19922944 | tf_op jit(solution)/shard_map/pallas_call | solution.py:148
  24.5 5.6 %all-to-all-done = bf16[16,64,256]{2,1,0:T(8,128)(2,1)S(1)} async-done(((bf16[16,64,256]{2,1,0:T(8,128)(2,1)}), bf16[16,64,256]{2,1,0:T(8,128)(2,1)S(1)}, u32[]{:S(2)}, u32[]{:S(2)}) %all-to-all-start) | async-done | bytes 524320 | tf_op jit(solution)/shard_map/all_to_all | solution.py:339
  30.0 3.5 %all-to-all-start.1 = ((bf16[8,64,512]{2,1,0:T(8,128)(2,1)}), bf16[8,64,512]{2,1,0:T(8,128)(2,1)S(1)}, u32[]{:S(2)}, u32[]{:S(2)}) async-start(bf16[8,64,512]{2,1,0:T(8,128)(2,1)} %bitcast.15), calls=%async_computation.1 | async-start | bytes 1048576 | tf_op jit(solution)/shard_map/all_to_all | solution.py:339
  35.7 3.4 %collective-permute-start.1 = (bf16[64,512]{1,0:T(8,128)(2,1)}, bf16[64,512]{1,0:T(8,128)(2,1)S(1)}, u32[]{:S(2)}, u32[]{:S(2)}) collective-permute-start(bf16[64,512]{1,0:T(8,128)(2,1)} %get-tuple-element.51), channel_id=1, source_target_pairs={{0,9},{1,8},{2,11},{3,10},{4,13},{5,12},{6,15},{7,14},{8,1},{9,0},... | collective-permute-start | bytes 196616 | tf_op jit(solution)/shard_map/ppermute | solution.py:367
  39.2 1.9 %collective-permute-start.2 = (bf16[64,512]{1,0:T(8,128)(2,1)}, bf16[64,512]{1,0:T(8,128)(2,1)S(1)}, u32[]{:S(2)}, u32[]{:S(2)}) collective-permute-start(bf16[64,512]{1,0:T(8,128)(2,1)} %get-tuple-element.52), channel_id=1, source_target_pairs={{0,10},{1,11},{2,8},{3,9},{4,14},{5,15},{6,12},{7,13},{8,2},{9,3},... | collective-permute-start | bytes 196616 | tf_op jit(solution)/shard_map/ppermute | solution.py:367
  41.0 1.5 %collective-permute-start.3 = (bf16[64,512]{1,0:T(8,128)(2,1)}, bf16[64,512]{1,0:T(8,128)(2,1)S(1)}, u32[]{:S(2)}, u32[]{:S(2)}) collective-permute-start(bf16[64,512]{1,0:T(8,128)(2,1)} %get-tuple-element.53), channel_id=1, source_target_pairs={{0,11},{1,10},{2,9},{3,8},{4,15},{5,14},{6,13},{7,12},{8,3},{9,2},... | collective-permute-start | bytes 196616 | tf_op jit(solution)/shard_map/ppermute | solution.py:367
  42.5 2.3 %collective-permute-start.4 = (bf16[64,512]{1,0:T(8,128)(2,1)}, bf16[64,512]{1,0:T(8,128)(2,1)S(1)}, u32[]{:S(2)}, u32[]{:S(2)}) collective-permute-start(bf16[64,512]{1,0:T(8,128)(2,1)} %get-tuple-element.54), channel_id=1, source_target_pairs={{0,12},{1,13},{2,14},{3,15},{4,8},{5,9},{6,10},{7,11},{8,4},{9,5},... | collective-permute-start | bytes 196616 | tf_op jit(solution)/shard_map/ppermute | solution.py:367
  44.8 5.6 %collective-permute-done.1.refs_2_ = bf16[64,512]{1,0:T(8,128)(2,1)S(1)} collective-permute-done((bf16[64,512]{1,0:T(8,128)(2,1)}, bf16[64,512]{1,0:T(8,128)(2,1)S(1)}, u32[]{:S(2)}, u32[]{:S(2)}) %collective-permute-start.1) | collective-permute-done | bytes 65568 | tf_op jit(solution)/shard_map/ppermute | solution.py:367
  50.4 1.4 %collective-permute-done.2.refs_3_ = bf16[64,512]{1,0:T(8,128)(2,1)S(1)} collective-permute-done((bf16[64,512]{1,0:T(8,128)(2,1)}, bf16[64,512]{1,0:T(8,128)(2,1)S(1)}, u32[]{:S(2)}, u32[]{:S(2)}) %collective-permute-start.2) | collective-permute-done | bytes 65568 | tf_op jit(solution)/shard_map/ppermute | solution.py:367
  54.9 2.0 %collective-permute-start.5 = (bf16[64,512]{1,0:T(8,128)(2,1)}, bf16[64,512]{1,0:T(8,128)(2,1)S(1)}, u32[]{:S(2)}, u32[]{:S(2)}) collective-permute-start(bf16[64,512]{1,0:T(8,128)(2,1)} %get-tuple-element.60), channel_id=1, source_target_pairs={{0,13},{1,12},{2,15},{3,14},{4,9},{5,8},{6,11},{7,10},{8,5},{9,4},... | collective-permute-start | bytes 196616 | tf_op jit(solution)/shard_map/ppermute | solution.py:367
  56.9 2.8 %collective-permute-start.6 = (bf16[64,512]{1,0:T(8,128)(2,1)}, bf16[64,512]{1,0:T(8,128)(2,1)S(1)}, u32[]{:S(2)}, u32[]{:S(2)}) collective-permute-start(bf16[64,512]{1,0:T(8,128)(2,1)} %get-tuple-element.61), channel_id=1, source_target_pairs={{0,14},{1,15},{2,12},{3,13},{4,10},{5,11},{6,8},{7,9},{8,6},{9,7},... | collective-permute-start | bytes 196616 | tf_op jit(solution)/shard_map/ppermute | solution.py:367
  59.7 2.5 %collective-permute-start.7 = (bf16[64,512]{1,0:T(8,128)(2,1)}, bf16[64,512]{1,0:T(8,128)(2,1)S(1)}, u32[]{:S(2)}, u32[]{:S(2)}) collective-permute-start(bf16[64,512]{1,0:T(8,128)(2,1)} %get-tuple-element.62), channel_id=1, source_target_pairs={{0,15},{1,14},{2,13},{3,12},{4,11},{5,10},{6,9},{7,8},{8,7},{9,6},... | collective-permute-start | bytes 196616 | tf_op jit(solution)/shard_map/ppermute | solution.py:367
  62.4 1.8 %collective-permute-done.6.refs_7_ = bf16[64,512]{1,0:T(8,128)(2,1)S(1)} collective-permute-done((bf16[64,512]{1,0:T(8,128)(2,1)}, bf16[64,512]{1,0:T(8,128)(2,1)S(1)}, u32[]{:S(2)}, u32[]{:S(2)}) %collective-permute-start.6) | collective-permute-done | bytes 65568 | tf_op jit(solution)/shard_map/ppermute | solution.py:367
  64.2 3.7 %collective-permute-done.7.refs_8_ = bf16[64,512]{1,0:T(8,128)(2,1)S(1)} collective-permute-done((bf16[64,512]{1,0:T(8,128)(2,1)}, bf16[64,512]{1,0:T(8,128)(2,1)S(1)}, u32[]{:S(2)}, u32[]{:S(2)}) %collective-permute-start.7) | collective-permute-done | bytes 65568 | tf_op jit(solution)/shard_map/ppermute | solution.py:367
  67.9 1.2 %shard_map.84.query_ref = bf16[1024,512]{1,0:T(8,128)(2,1)S(1)} custom-call(s32[1,1024]{1,0:T(1,128)S(1)} %reshape.128.slot_ref, bf16[512,512]{1,0:T(8,128)(2,1)S(1)} %bitcast.13, bf16[64,512]{1,0:T(8,128)(2,1)S(1)} %collective-permute-done.refs_1_, bf16[64,512]{1,0:T(8,128)(2,1)S(1)} %collective-permute-done.1.refs_2_, ...), custom_call_target="tpu_custom_call" | custom-call | flops 1073741824 | bytes 2097152 | tf_op jit(solution)/shard_map/pallas_call | solution.py:197
  69.2 1.2 %shard_map.86 = bf16[256,512]{1,0:T(8,128)(2,1)S(1)} custom-call(s32[1,32]{1,0:T(1,128)S(1)} %reduce-window_clone.1.ends_ref, bf16[1024,512]{1,0:T(8,128)(2,1)S(1)} %shard_map.84.query_ref, bf16[384,256]{1,0:T(8,128)(2,1)S(1)} %collective-permute-done.8.rest_0_, bf16[384,256]{1,0:T(8,128)(2,1)S(1)} %collective-permute-done.9.rest_1_, ...), custom_call_target="tpu_custom_call" | custom-call | flops 268435456 | bytes 1966080 | tf_op jit(solution)/shard_map/pallas_call | solution.py:281
  70.3 1.5 %collective-permute-start.10 = (bf16[256,512]{1,0:T(8,128)(2,1)S(1)}, bf16[256,512]{1,0:T(8,128)(2,1)S(1)}, u32[]{:S(2)}, u32[]{:S(2)}) collective-permute-start(bf16[256,512]{1,0:T(8,128)(2,1)S(1)} %shard_map.86), channel_id=1, source_target_pairs={{0,3},{1,2},{2,1},{3,0},{4,7},{5,6},{6,5},{7,4},{8,11},{9,10},{10,... | collective-permute-start | bytes 786440 | tf_op jit(solution)/shard_map/ppermute | solution.py:394
  73.0 1.2 %collective-permute-start.11 = (bf16[256,512]{1,0:T(8,128)(2,1)S(1)}, bf16[256,512]{1,0:T(8,128)(2,1)S(1)}, u32[]{:S(2)}, u32[]{:S(2)}) collective-permute-start(bf16[256,512]{1,0:T(8,128)(2,1)S(1)} %shard_map.87), channel_id=1, source_target_pairs={{0,1},{1,0},{2,3},{3,2},{4,5},{5,4},{6,7},{7,6},{8,9},{9,8},{10,11... | collective-permute-start | bytes 786440 | tf_op jit(solution)/shard_map/ppermute | solution.py:394
  74.2 1.1 %shard_map.88 = bf16[256,512]{1,0:T(8,128)(2,1)S(1)} custom-call(s32[1,32]{1,0:T(1,128)S(1)} %reduce-window_clone.1.ends_ref, bf16[1024,512]{1,0:T(8,128)(2,1)S(1)} %shard_map.84.query_ref, bf16[384,256]{1,0:T(8,128)(2,1)S(1)} %collective-permute-done.8.rest_0_, bf16[384,256]{1,0:T(8,128)(2,1)S(1)} %collective-permute-done.9.rest_1_, ...), custom_call_target="tpu_custom_call" | custom-call | flops 268435456 | bytes 1966080 | tf_op jit(solution)/shard_map/pallas_call | solution.py:281
  76.3 1.1 %shard_map.89.refs_3_ = bf16[256,512]{1,0:T(8,128)(2,1)S(1)} custom-call(s32[1,32]{1,0:T(1,128)S(1)} %reduce-window_clone.1.ends_ref, bf16[1024,512]{1,0:T(8,128)(2,1)S(1)} %shard_map.84.query_ref, bf16[384,256]{1,0:T(8,128)(2,1)S(1)} %collective-permute-done.8.rest_0_, bf16[384,256]{1,0:T(8,128)(2,1)S(1)} %collective-permute-done.9.rest_1_, ...), custom_call_target="tpu_custom_call" | custom-call | flops 268435456 | bytes 1966080 | tf_op jit(solution)/shard_map/pallas_call | solution.py:281
  77.5 2.4 %collective-permute-done.10.refs_0_ = bf16[256,512]{1,0:T(8,128)(2,1)S(1)} collective-permute-done((bf16[256,512]{1,0:T(8,128)(2,1)S(1)}, bf16[256,512]{1,0:T(8,128)(2,1)S(1)}, u32[]{:S(2)}, u32[]{:S(2)}) %collective-permute-start.10) | collective-permute-done | bytes 262176 | tf_op jit(solution)/shard_map/ppermute | solution.py:394
  79.9 3.1 %collective-permute-done.11.refs_1_ = bf16[256,512]{1,0:T(8,128)(2,1)S(1)} collective-permute-done((bf16[256,512]{1,0:T(8,128)(2,1)S(1)}, bf16[256,512]{1,0:T(8,128)(2,1)S(1)}, u32[]{:S(2)}, u32[]{:S(2)}) %collective-permute-start.11) | collective-permute-done | bytes 262176 | tf_op jit(solution)/shard_map/ppermute | solution.py:394
  (30 shorter events, 8.7 us)
Async XLA Ops:
  0.0 14.9 %copy-start = (s32[4096]{0:T(1024)S(1)}, s32[4096]{0:T(1024)}, u32[]{:S(2)}) copy-start(s32[4096]{0:T(1024)} %param.9) | copy-start | bytes 49156
  6.5 23.5 %all-to-all-start = ((bf16[16,64,256]{2,1,0:T(8,128)(2,1)}), bf16[16,64,256]{2,1,0:T(8,128)(2,1)S(1)}, u32[]{:S(2)}, u32[]{:S(2)}) async-start(bf16[16,64,256]{2,1,0:T(8,128)(2,1)} %bitcast.14), calls=%async_computation | async-start | bytes 1048576 | tf_op jit(solution)/shard_map/all_to_all | solution.py:339
  14.9 47.3 %copy-start.1 = (s32[32]{0:T(128)S(1)}, s32[32]{0:T(128)}, u32[]{:S(2)}) copy-start(s32[32]{0:T(128)} %param.10) | copy-start | bytes 388
  30.0 37.9 %all-to-all-start.1 = ((bf16[8,64,512]{2,1,0:T(8,128)(2,1)}), bf16[8,64,512]{2,1,0:T(8,128)(2,1)S(1)}, u32[]{:S(2)}, u32[]{:S(2)}) async-start(bf16[8,64,512]{2,1,0:T(8,128)(2,1)} %bitcast.15), calls=%async_computation.1 | async-start | bytes 1048576 | tf_op jit(solution)/shard_map/all_to_all | solution.py:339
  34.9 10.0 %collective-permute-start = (bf16[64,512]{1,0:T(8,128)(2,1)}, bf16[64,512]{1,0:T(8,128)(2,1)S(1)}, u32[]{:S(2)}, u32[]{:S(2)}) collective-permute-start(bf16[64,512]{1,0:T(8,128)(2,1)} %get-tuple-element.50), channel_id=1, source_target_pairs={{0,8},{1,9},{2,10},{3,11},{4,12},{5,13},{6,14},{7,15},{8,0},{9,1},... | collective-permute-start | bytes 196616 | tf_op jit(solution)/shard_map/ppermute | solution.py:367
  35.7 14.7 %collective-permute-start.1 = (bf16[64,512]{1,0:T(8,128)(2,1)}, bf16[64,512]{1,0:T(8,128)(2,1)S(1)}, u32[]{:S(2)}, u32[]{:S(2)}) collective-permute-start(bf16[64,512]{1,0:T(8,128)(2,1)} %get-tuple-element.51), channel_id=1, source_target_pairs={{0,9},{1,8},{2,11},{3,10},{4,13},{5,12},{6,15},{7,14},{8,1},{9,0},... | collective-permute-start | bytes 196616 | tf_op jit(solution)/shard_map/ppermute | solution.py:367
  39.2 12.7 %collective-permute-start.2 = (bf16[64,512]{1,0:T(8,128)(2,1)}, bf16[64,512]{1,0:T(8,128)(2,1)S(1)}, u32[]{:S(2)}, u32[]{:S(2)}) collective-permute-start(bf16[64,512]{1,0:T(8,128)(2,1)} %get-tuple-element.52), channel_id=1, source_target_pairs={{0,10},{1,11},{2,8},{3,9},{4,14},{5,15},{6,12},{7,13},{8,2},{9,3},... | collective-permute-start | bytes 196616 | tf_op jit(solution)/shard_map/ppermute | solution.py:367
  41.0 11.9 %collective-permute-start.3 = (bf16[64,512]{1,0:T(8,128)(2,1)}, bf16[64,512]{1,0:T(8,128)(2,1)S(1)}, u32[]{:S(2)}, u32[]{:S(2)}) collective-permute-start(bf16[64,512]{1,0:T(8,128)(2,1)} %get-tuple-element.53), channel_id=1, source_target_pairs={{0,11},{1,10},{2,9},{3,8},{4,15},{5,14},{6,13},{7,12},{8,3},{9,2},... | collective-permute-start | bytes 196616 | tf_op jit(solution)/shard_map/ppermute | solution.py:367
  42.5 10.4 %collective-permute-start.4 = (bf16[64,512]{1,0:T(8,128)(2,1)}, bf16[64,512]{1,0:T(8,128)(2,1)S(1)}, u32[]{:S(2)}, u32[]{:S(2)}) collective-permute-start(bf16[64,512]{1,0:T(8,128)(2,1)} %get-tuple-element.54), channel_id=1, source_target_pairs={{0,12},{1,13},{2,14},{3,15},{4,8},{5,9},{6,10},{7,11},{8,4},{9,5},... | collective-permute-start | bytes 196616 | tf_op jit(solution)/shard_map/ppermute | solution.py:367
  53.7 15.5 %collective-permute-start.8 = (bf16[384,256]{1,0:T(8,128)(2,1)S(1)}, bf16[384,256]{1,0:T(8,128)(2,1)S(1)}, u32[]{:S(2)}, u32[]{:S(2)}) collective-permute-start(bf16[384,256]{1,0:T(8,128)(2,1)S(1)} %get-tuple-element.65), channel_id=1, source_target_pairs={{0,4},{1,5},{2,6},{3,7},{8,12},{9,13},{10,14},{11,15},{4,0},{5,1},... | collective-permute-start | bytes 589832 | tf_op jit(solution)/shard_map/ppermute | solution.py:380
  54.1 15.1 %collective-permute-start.9 = (bf16[384,256]{1,0:T(8,128)(2,1)S(1)}, bf16[384,256]{1,0:T(8,128)(2,1)S(1)}, u32[]{:S(2)}, u32[]{:S(2)}) collective-permute-start(bf16[384,256]{1,0:T(8,128)(2,1)S(1)} %get-tuple-element.66), channel_id=1, source_target_pairs={{4,8},{5,9},{6,10},{7,11},{8,4},{9,5},{10,6},{11,7},{20,24},{21,25... | collective-permute-start | bytes 589832 | tf_op jit(solution)/shard_map/ppermute | solution.py:380
  54.9 7.5 %collective-permute-start.5 = (bf16[64,512]{1,0:T(8,128)(2,1)}, bf16[64,512]{1,0:T(8,128)(2,1)S(1)}, u32[]{:S(2)}, u32[]{:S(2)}) collective-permute-start(bf16[64,512]{1,0:T(8,128)(2,1)} %get-tuple-element.60), channel_id=1, source_target_pairs={{0,13},{1,12},{2,15},{3,14},{4,9},{5,8},{6,11},{7,10},{8,5},{9,4},... | collective-permute-start | bytes 196616 | tf_op jit(solution)/shard_map/ppermute | solution.py:367
  56.9 7.3 %collective-permute-start.6 = (bf16[64,512]{1,0:T(8,128)(2,1)}, bf16[64,512]{1,0:T(8,128)(2,1)S(1)}, u32[]{:S(2)}, u32[]{:S(2)}) collective-permute-start(bf16[64,512]{1,0:T(8,128)(2,1)} %get-tuple-element.61), channel_id=1, source_target_pairs={{0,14},{1,15},{2,12},{3,13},{4,10},{5,11},{6,8},{7,9},{8,6},{9,7},... | collective-permute-start | bytes 196616 | tf_op jit(solution)/shard_map/ppermute | solution.py:367
  59.7 8.2 %collective-permute-start.7 = (bf16[64,512]{1,0:T(8,128)(2,1)}, bf16[64,512]{1,0:T(8,128)(2,1)S(1)}, u32[]{:S(2)}, u32[]{:S(2)}) collective-permute-start(bf16[64,512]{1,0:T(8,128)(2,1)} %get-tuple-element.62), channel_id=1, source_target_pairs={{0,15},{1,14},{2,13},{3,12},{4,11},{5,10},{6,9},{7,8},{8,7},{9,6},... | collective-permute-start | bytes 196616 | tf_op jit(solution)/shard_map/ppermute | solution.py:367
  70.3 9.6 %collective-permute-start.10 = (bf16[256,512]{1,0:T(8,128)(2,1)S(1)}, bf16[256,512]{1,0:T(8,128)(2,1)S(1)}, u32[]{:S(2)}, u32[]{:S(2)}) collective-permute-start(bf16[256,512]{1,0:T(8,128)(2,1)S(1)} %shard_map.86), channel_id=1, source_target_pairs={{0,3},{1,2},{2,1},{3,0},{4,7},{5,6},{6,5},{7,4},{8,11},{9,10},{10,... | collective-permute-start | bytes 786440 | tf_op jit(solution)/shard_map/ppermute | solution.py:394
  73.0 10.0 %collective-permute-start.11 = (bf16[256,512]{1,0:T(8,128)(2,1)S(1)}, bf16[256,512]{1,0:T(8,128)(2,1)S(1)}, u32[]{:S(2)}, u32[]{:S(2)}) collective-permute-start(bf16[256,512]{1,0:T(8,128)(2,1)S(1)} %shard_map.87), channel_id=1, source_target_pairs={{0,1},{1,0},{2,3},{3,2},{4,5},{5,4},{6,7},{7,6},{8,9},{9,8},{10,11... | collective-permute-start | bytes 786440 | tf_op jit(solution)/shard_map/ppermute | solution.py:394
  75.4 7.6 %collective-permute-start.12 = (bf16[256,512]{1,0:T(8,128)(2,1)S(1)}, bf16[256,512]{1,0:T(8,128)(2,1)S(1)}, u32[]{:S(2)}, u32[]{:S(2)}) collective-permute-start(bf16[256,512]{1,0:T(8,128)(2,1)S(1)} %shard_map.88), channel_id=1, source_target_pairs={{0,2},{1,3},{2,0},{3,1},{4,6},{5,7},{6,4},{7,5},{8,10},{9,11},{10,... | collective-permute-start | bytes 786440 | tf_op jit(solution)/shard_map/ppermute | solution.py:394

commit v19 on v16

--- a/solution.py
+++ b/solution.py
@@ -367,7 +367,7 @@
 
     kv, near = lax.optimization_barrier((kv, near))
     queries.insert(0, exchange(near, halves))
-    kv, *queries[1:6] = lax.optimization_barrier((kv, *queries[1:6]))
+    kv, *queries[1:5] = lax.optimization_barrier((kv, *queries[1:5]))
     reach = REACH_BLOCKS * block
     sizes = [run - reach, reach] * 2
     *runs, even_out, odd_out = place([kv], slot, sizes, members)

time: 72.2 us -> 72.1 us (level)
  no operation moved by 1% of the time
where the time goes in v19:
time: 72.1 us; the launch traced here: 71.8 us
  starting transfers between devices  35.5 us (49%)
  Pallas kernels  23.6 us (33%)
  waiting for transfers between devices  10.9 us (15%)
  local copies, waits for them, and re-layouts  0.74 us (1%)
    ppermute x8, starting transfers between devices, shards(): lax.ppermute(piece, 'ctx', [(j, j ^ distance) for j in range(devices)])  19 us
    pallas_call x2, Pallas kernels, project(): pl.pallas_call(functools.partial(project_kernel, kinds, devices, heads, a...  16 us
    all_to_all x2, starting transfers between devices, exchange(): lax.all_to_all(flat, 'ctx', split_axis=0, concat_axis=0, tiled=True, axis...  12 us
    ppermute x3, waiting for transfers between devices, shards(): out = lax.ppermute(out, ('dp', 'ctx'), route)  6.3 us
    ppermute x8, waiting for transfers between devices, shards(): lax.ppermute(piece, 'ctx', [(j, j ^ distance) for j in range(devices)])  4.63 us
    pallas_call x4, Pallas kernels, attend(): pl.pallas_call(functools.partial(attend_kernel, block, turn, members, dev...  4.59 us
    ppermute x3, starting transfers between devices, shards(): out = lax.ppermute(out, ('dp', 'ctx'), route)  3.68 us
    pallas_call x2, Pallas kernels, place(): pl.pallas_call(functools.partial(place_kernel, len(pieces), members), out...  1.96 us
  transfers between devices with their start and end apart: 15, of which 5 were waited for; matrix products, arithmetic and copies ran while one was open for 2% of the time, Pallas kernels for 21%

profile of v19, /device:TPU:0, one launch (start us, length us, event | category | flops | bytes accessed | tf_op | source)
XLA Modules:
  0.0 71.8 jit_solution(10498132018745227552)
XLA Ops:
  0.0 6.5 %shard_map.82 = bf16[4,4,64,256]{3,2,1,0:T(8,128)(2,1)} custom-call(s32[32,128]{1,0:T(8,128)} %bitcast.16, f32[1,128]{1,0:T(1,128)} %constant.78.clone.freq_hbm, bf16[4096]{0:T(1024)(128)(2,1)} %gain_hbm.3, bf16[256,4096]{1,0:T(8,128)(2,1)} %tokens_hbm.3, bf16[4096,512]{1,0:T(8,128)(2,1)} %rest_0_.2, bf16[4096,512]{1,0:T(8,128)(2,1)} %rest_1_.1), custom_call_target="tpu_custom_call" | custom-call | flops 2147483648 | bytes 11010048 | tf_op jit(solution)/shard_map/pallas_call | solution.py:148
  6.5 8.3 %all-to-all-start = ((bf16[16,64,256]{2,1,0:T(8,128)(2,1)}), bf16[16,64,256]{2,1,0:T(8,128)(2,1)S(1)}, u32[]{:S(2)}, u32[]{:S(2)}) async-start(bf16[16,64,256]{2,1,0:T(8,128)(2,1)} %bitcast.14), calls=%async_computation | async-start | bytes 1048576 | tf_op jit(solution)/shard_map/all_to_all | solution.py:339
  14.9 9.5 %shard_map.83 = (bf16[2,4,64,512]{3,2,1,0:T(8,128)(2,1)}, bf16[64,512]{1,0:T(8,128)(2,1)}, bf16[64,512]{1,0:T(8,128)(2,1)}, bf16[64,512]{1,0:T(8,128)(2,1)}, bf1...) custom-call(s32[32,128]{1,0:T(8,128)} %bitcast.17, ...), custom_call_target="tpu_custom_call" | custom-call | flops 4294967296 | bytes 19922944 | tf_op jit(solution)/shard_map/pallas_call | solution.py:148
  24.4 2.9 %collective-permute-start = (bf16[64,512]{1,0:T(8,128)(2,1)}, bf16[64,512]{1,0:T(8,128)(2,1)S(1)}, u32[]{:S(2)}, u32[]{:S(2)}) collective-permute-start(bf16[64,512]{1,0:T(8,128)(2,1)} %get-tuple-element.30), channel_id=1, source_target_pairs={{0,8},{1,9},{2,10},{3,11},{4,12},{5,13},{6,14},{7,15},{8,0},{9,1},... | collective-permute-start | bytes 196616 | tf_op jit(solution)/shard_map/ppermute | solution.py:349
  27.3 1.5 %collective-permute-start.1 = (bf16[64,512]{1,0:T(8,128)(2,1)}, bf16[64,512]{1,0:T(8,128)(2,1)S(1)}, u32[]{:S(2)}, u32[]{:S(2)}) collective-permute-start(bf16[64,512]{1,0:T(8,128)(2,1)} %get-tuple-element.31), channel_id=1, source_target_pairs={{0,9},{1,8},{2,11},{3,10},{4,13},{5,12},{6,15},{7,14},{8,1},{9,0},... | collective-permute-start | bytes 196616 | tf_op jit(solution)/shard_map/ppermute | solution.py:349
  28.8 3.3 %collective-permute-start.2 = (bf16[64,512]{1,0:T(8,128)(2,1)}, bf16[64,512]{1,0:T(8,128)(2,1)S(1)}, u32[]{:S(2)}, u32[]{:S(2)}) collective-permute-start(bf16[64,512]{1,0:T(8,128)(2,1)} %get-tuple-element.32), channel_id=1, source_target_pairs={{0,10},{1,11},{2,8},{3,9},{4,14},{5,15},{6,12},{7,13},{8,2},{9,3},... | collective-permute-start | bytes 196616 | tf_op jit(solution)/shard_map/ppermute | solution.py:349
  32.1 3.7 %collective-permute-start.4 = (bf16[64,512]{1,0:T(8,128)(2,1)}, bf16[64,512]{1,0:T(8,128)(2,1)S(1)}, u32[]{:S(2)}, u32[]{:S(2)}) collective-permute-start(bf16[64,512]{1,0:T(8,128)(2,1)} %get-tuple-element.38), channel_id=1, source_target_pairs={{0,12},{1,13},{2,14},{3,15},{4,8},{5,9},{6,10},{7,11},{8,4},{9,5},... | collective-permute-start | bytes 196616 | tf_op jit(solution)/shard_map/ppermute | solution.py:349
  35.8 3.7 %all-to-all-start.1 = ((bf16[8,64,512]{2,1,0:T(8,128)(2,1)}), bf16[8,64,512]{2,1,0:T(8,128)(2,1)S(1)}, u32[]{:S(2)}, u32[]{:S(2)}) async-start(bf16[8,64,512]{2,1,0:T(8,128)(2,1)} %bitcast.15), calls=%async_computation.1 | async-start | bytes 1048576 | tf_op jit(solution)/shard_map/all_to_all | solution.py:339
  40.5 2.9 %collective-permute-start.5 = (bf16[64,512]{1,0:T(8,128)(2,1)}, bf16[64,512]{1,0:T(8,128)(2,1)S(1)}, u32[]{:S(2)}, u32[]{:S(2)}) collective-permute-start(bf16[64,512]{1,0:T(8,128)(2,1)} %get-tuple-element.39), channel_id=1, source_target_pairs={{0,13},{1,12},{2,15},{3,14},{4,9},{5,8},{6,11},{7,10},{8,5},{9,4},... | collective-permute-start | bytes 196616 | tf_op jit(solution)/shard_map/ppermute | solution.py:349
  43.4 3.3 %collective-permute-start.6 = (bf16[64,512]{1,0:T(8,128)(2,1)}, bf16[64,512]{1,0:T(8,128)(2,1)S(1)}, u32[]{:S(2)}, u32[]{:S(2)}) collective-permute-start(bf16[64,512]{1,0:T(8,128)(2,1)} %get-tuple-element.40), channel_id=1, source_target_pairs={{0,14},{1,15},{2,12},{3,13},{4,10},{5,11},{6,8},{7,9},{8,6},{9,7},... | collective-permute-start | bytes 196616 | tf_op jit(solution)/shard_map/ppermute | solution.py:349
  46.7 1.5 %collective-permute-start.7 = (bf16[64,512]{1,0:T(8,128)(2,1)}, bf16[64,512]{1,0:T(8,128)(2,1)S(1)}, u32[]{:S(2)}, u32[]{:S(2)}) collective-permute-start(bf16[64,512]{1,0:T(8,128)(2,1)} %get-tuple-element.41), channel_id=1, source_target_pairs={{0,15},{1,14},{2,13},{3,12},{4,11},{5,10},{6,9},{7,8},{8,7},{9,6},... | collective-permute-start | bytes 196616 | tf_op jit(solution)/shard_map/ppermute | solution.py:349
  48.1 0.7 %shard_map.85 = (bf16[128,256]{1,0:T(8,128)(2,1)S(1)}, bf16[384,256]{1,0:T(8,128)(2,1)S(1)}, bf16[128,256]{1,0:T(8,128)(2,1)S(1)}, bf16[384,256]{1,0:T(8,128)(2,...) custom-call(s32[1,1024]{1,0:T(1,128)S(1)} %reshape.132.slot_ref, bf16[1024,256]{1,0:T(8,128)(2,1)S(1)} %bitcast.12), custom_call_target="tpu_custom_call" | custom-call | flops 536870912 | bytes 1048576 | tf_op jit(solution)/shard_map/pallas_call | solution.py:197
  50.3 1.0 %collective-permute-done.6.refs_7_ = bf16[64,512]{1,0:T(8,128)(2,1)S(1)} collective-permute-done((bf16[64,512]{1,0:T(8,128)(2,1)}, bf16[64,512]{1,0:T(8,128)(2,1)S(1)}, u32[]{:S(2)}, u32[]{:S(2)}) %collective-permute-start.6) | collective-permute-done | bytes 65568 | tf_op jit(solution)/shard_map/ppermute | solution.py:349
  51.3 3.6 %collective-permute-done.7.refs_8_ = bf16[64,512]{1,0:T(8,128)(2,1)S(1)} collective-permute-done((bf16[64,512]{1,0:T(8,128)(2,1)}, bf16[64,512]{1,0:T(8,128)(2,1)S(1)}, u32[]{:S(2)}, u32[]{:S(2)}) %collective-permute-start.7) | collective-permute-done | bytes 65568 | tf_op jit(solution)/shard_map/ppermute | solution.py:349
  54.9 1.2 %shard_map.84.query_ref = bf16[1024,512]{1,0:T(8,128)(2,1)S(1)} custom-call(s32[1,1024]{1,0:T(1,128)S(1)} %reshape.126.slot_ref, bf16[512,512]{1,0:T(8,128)(2,1)S(1)} %bitcast.13, bf16[64,512]{1,0:T(8,128)(2,1)S(1)} %collective-permute-done.refs_1_, bf16[64,512]{1,0:T(8,128)(2,1)S(1)} %collective-permute-done.1.refs_2_, ...), custom_call_target="tpu_custom_call" | custom-call | flops 1073741824 | bytes 2097152 | tf_op jit(solution)/shard_map/pallas_call | solution.py:197
  56.2 1.2 %shard_map.86 = bf16[256,512]{1,0:T(8,128)(2,1)S(1)} custom-call(s32[1,32]{1,0:T(1,128)S(1)} %reduce-window_clone.1.ends_ref, bf16[1024,512]{1,0:T(8,128)(2,1)S(1)} %shard_map.84.query_ref, bf16[384,256]{1,0:T(8,128)(2,1)S(1)} %collective-permute-done.8.rest_0_, bf16[384,256]{1,0:T(8,128)(2,1)S(1)} %collective-permute-done.9.rest_1_, ...), custom_call_target="tpu_custom_call" | custom-call | flops 268435456 | bytes 1966080 | tf_op jit(solution)/shard_map/pallas_call | solution.py:281
  57.3 2.2 %collective-permute-start.10 = (bf16[256,512]{1,0:T(8,128)(2,1)S(1)}, bf16[256,512]{1,0:T(8,128)(2,1)S(1)}, u32[]{:S(2)}, u32[]{:S(2)}) collective-permute-start(bf16[256,512]{1,0:T(8,128)(2,1)S(1)} %shard_map.86), channel_id=1, source_target_pairs={{0,3},{1,2},{2,1},{3,0},{4,7},{5,6},{6,5},{7,4},{8,11},{9,10},{10,... | collective-permute-start | bytes 786440 | tf_op jit(solution)/shard_map/ppermute | solution.py:393
  59.5 1.1 %shard_map.87 = bf16[256,512]{1,0:T(8,128)(2,1)S(1)} custom-call(s32[1,32]{1,0:T(1,128)S(1)} %reduce-window_clone.1.ends_ref, bf16[1024,512]{1,0:T(8,128)(2,1)S(1)} %shard_map.84.query_ref, bf16[384,256]{1,0:T(8,128)(2,1)S(1)} %collective-permute-done.8.rest_0_, bf16[384,256]{1,0:T(8,128)(2,1)S(1)} %collective-permute-done.9.rest_1_, ...), custom_call_target="tpu_custom_call" | custom-call | flops 268435456 | bytes 1966080 | tf_op jit(solution)/shard_map/pallas_call | solution.py:281
  61.3 1.1 %shard_map.88 = bf16[256,512]{1,0:T(8,128)(2,1)S(1)} custom-call(s32[1,32]{1,0:T(1,128)S(1)} %reduce-window_clone.1.ends_ref, bf16[1024,512]{1,0:T(8,128)(2,1)S(1)} %shard_map.84.query_ref, bf16[384,256]{1,0:T(8,128)(2,1)S(1)} %collective-permute-done.8.rest_0_, bf16[384,256]{1,0:T(8,128)(2,1)S(1)} %collective-permute-done.9.rest_1_, ...), custom_call_target="tpu_custom_call" | custom-call | flops 268435456 | bytes 1966080 | tf_op jit(solution)/shard_map/pallas_call | solution.py:281
  62.5 0.8 %collective-permute-start.12 = (bf16[256,512]{1,0:T(8,128)(2,1)S(1)}, bf16[256,512]{1,0:T(8,128)(2,1)S(1)}, u32[]{:S(2)}, u32[]{:S(2)}) collective-permute-start(bf16[256,512]{1,0:T(8,128)(2,1)S(1)} %shard_map.88), channel_id=1, source_target_pairs={{0,2},{1,3},{2,0},{3,1},{4,6},{5,7},{6,4},{7,5},{8,10},{9,11},{10,... | collective-permute-start | bytes 786440 | tf_op jit(solution)/shard_map/ppermute | solution.py:393
  63.3 1.1 %shard_map.89.refs_3_ = bf16[256,512]{1,0:T(8,128)(2,1)S(1)} custom-call(s32[1,32]{1,0:T(1,128)S(1)} %reduce-window_clone.1.ends_ref, bf16[1024,512]{1,0:T(8,128)(2,1)S(1)} %shard_map.84.query_ref, bf16[384,256]{1,0:T(8,128)(2,1)S(1)} %collective-permute-done.8.rest_0_, bf16[384,256]{1,0:T(8,128)(2,1)S(1)} %collective-permute-done.9.rest_1_, ...), custom_call_target="tpu_custom_call" | custom-call | flops 268435456 | bytes 1966080 | tf_op jit(solution)/shard_map/pallas_call | solution.py:281
  64.4 1.9 %collective-permute-done.10.refs_0_ = bf16[256,512]{1,0:T(8,128)(2,1)S(1)} collective-permute-done((bf16[256,512]{1,0:T(8,128)(2,1)S(1)}, bf16[256,512]{1,0:T(8,128)(2,1)S(1)}, u32[]{:S(2)}, u32[]{:S(2)}) %collective-permute-start.10) | collective-permute-done | bytes 262176 | tf_op jit(solution)/shard_map/ppermute | solution.py:393
  66.3 4.3 %collective-permute-done.11.refs_1_ = bf16[256,512]{1,0:T(8,128)(2,1)S(1)} collective-permute-done((bf16[256,512]{1,0:T(8,128)(2,1)S(1)}, bf16[256,512]{1,0:T(8,128)(2,1)S(1)}, u32[]{:S(2)}, u32[]{:S(2)}) %collective-permute-start.11) | collective-permute-done | bytes 262176 | tf_op jit(solution)/shard_map/ppermute | solution.py:393
  70.8 1.1 %shard_map.90 = bf16[256,2048]{1,0:T(8,128)(2,1)} custom-call(bf16[256,512]{1,0:T(8,128)(2,1)S(1)} %collective-permute-done.10.refs_0_, bf16[256,512]{1,0:T(8,128)(2,1)S(1)} %collective-permute-done.11.refs_1_, bf16[256,512]{1,0:T(8,128)(2,1)S(1)} %collective-permute-done.12.refs_2_, bf16[256,512]{1,0:T(8,128)(2,1)S(1)} %shard_map.89.refs_3_), custom_call_target="tpu_custom_call" | custom-call | bytes 2097152 | tf_op jit(solution)/shard_map/pallas_call | solution.py:306
  (30 shorter events, 3.1 us)
Async XLA Ops:
  6.5 29.3 %all-to-all-start = ((bf16[16,64,256]{2,1,0:T(8,128)(2,1)}), bf16[16,64,256]{2,1,0:T(8,128)(2,1)S(1)}, u32[]{:S(2)}, u32[]{:S(2)}) async-start(bf16[16,64,256]{2,1,0:T(8,128)(2,1)} %bitcast.14), calls=%async_computation | async-start | bytes 1048576 | tf_op jit(solution)/shard_map/all_to_all | solution.py:339
  14.9 24.7 %copy-start = (s32[4096]{0:T(1024)S(1)}, s32[4096]{0:T(1024)}, u32[]{:S(2)}) copy-start(s32[4096]{0:T(1024)} %param.9) | copy-start | bytes 49156
  14.9 25.3 %copy-start.1 = (s32[32]{0:T(128)S(1)}, s32[32]{0:T(128)}, u32[]{:S(2)}) copy-start(s32[32]{0:T(128)} %param.10) | copy-start | bytes 388
  24.4 16.1 %collective-permute-start = (bf16[64,512]{1,0:T(8,128)(2,1)}, bf16[64,512]{1,0:T(8,128)(2,1)S(1)}, u32[]{:S(2)}, u32[]{:S(2)}) collective-permute-start(bf16[64,512]{1,0:T(8,128)(2,1)} %get-tuple-element.30), channel_id=1, source_target_pairs={{0,8},{1,9},{2,10},{3,11},{4,12},{5,13},{6,14},{7,15},{8,0},{9,1},... | collective-permute-start | bytes 196616 | tf_op jit(solution)/shard_map/ppermute | solution.py:349
  27.3 16.1 %collective-permute-start.1 = (bf16[64,512]{1,0:T(8,128)(2,1)}, bf16[64,512]{1,0:T(8,128)(2,1)S(1)}, u32[]{:S(2)}, u32[]{:S(2)}) collective-permute-start(bf16[64,512]{1,0:T(8,128)(2,1)} %get-tuple-element.31), channel_id=1, source_target_pairs={{0,9},{1,8},{2,11},{3,10},{4,13},{5,12},{6,15},{7,14},{8,1},{9,0},... | collective-permute-start | bytes 196616 | tf_op jit(solution)/shard_map/ppermute | solution.py:349
  28.8 17.9 %collective-permute-start.2 = (bf16[64,512]{1,0:T(8,128)(2,1)}, bf16[64,512]{1,0:T(8,128)(2,1)S(1)}, u32[]{:S(2)}, u32[]{:S(2)}) collective-permute-start(bf16[64,512]{1,0:T(8,128)(2,1)} %get-tuple-element.32), channel_id=1, source_target_pairs={{0,10},{1,11},{2,8},{3,9},{4,14},{5,15},{6,12},{7,13},{8,2},{9,3},... | collective-permute-start | bytes 196616 | tf_op jit(solution)/shard_map/ppermute | solution.py:349
  32.0 16.1 %collective-permute-start.3 = (bf16[64,512]{1,0:T(8,128)(2,1)}, bf16[64,512]{1,0:T(8,128)(2,1)S(1)}, u32[]{:S(2)}, u32[]{:S(2)}) collective-permute-start(bf16[64,512]{1,0:T(8,128)(2,1)} %get-tuple-element.33), channel_id=1, source_target_pairs={{0,11},{1,10},{2,9},{3,8},{4,15},{5,14},{6,13},{7,12},{8,3},{9,2},... | collective-permute-start | bytes 196616 | tf_op jit(solution)/shard_map/ppermute | solution.py:349
  32.1 16.8 %collective-permute-start.4 = (bf16[64,512]{1,0:T(8,128)(2,1)}, bf16[64,512]{1,0:T(8,128)(2,1)S(1)}, u32[]{:S(2)}, u32[]{:S(2)}) collective-permute-start(bf16[64,512]{1,0:T(8,128)(2,1)} %get-tuple-element.38), channel_id=1, source_target_pairs={{0,12},{1,13},{2,14},{3,15},{4,8},{5,9},{6,10},{7,11},{8,4},{9,5},... | collective-permute-start | bytes 196616 | tf_op jit(solution)/shard_map/ppermute | solution.py:349
  35.8 19.0 %all-to-all-start.1 = ((bf16[8,64,512]{2,1,0:T(8,128)(2,1)}), bf16[8,64,512]{2,1,0:T(8,128)(2,1)S(1)}, u32[]{:S(2)}, u32[]{:S(2)}) async-start(bf16[8,64,512]{2,1,0:T(8,128)(2,1)} %bitcast.15), calls=%async_computation.1 | async-start | bytes 1048576 | tf_op jit(solution)/shard_map/all_to_all | solution.py:339
  40.5 9.8 %collective-permute-start.5 = (bf16[64,512]{1,0:T(8,128)(2,1)}, bf16[64,512]{1,0:T(8,128)(2,1)S(1)}, u32[]{:S(2)}, u32[]{:S(2)}) collective-permute-start(bf16[64,512]{1,0:T(8,128)(2,1)} %get-tuple-element.39), channel_id=1, source_target_pairs={{0,13},{1,12},{2,15},{3,14},{4,9},{5,8},{6,11},{7,10},{8,5},{9,4},... | collective-permute-start | bytes 196616 | tf_op jit(solution)/shard_map/ppermute | solution.py:349
  43.4 7.9 %collective-permute-start.6 = (bf16[64,512]{1,0:T(8,128)(2,1)}, bf16[64,512]{1,0:T(8,128)(2,1)S(1)}, u32[]{:S(2)}, u32[]{:S(2)}) collective-permute-start(bf16[64,512]{1,0:T(8,128)(2,1)} %get-tuple-element.40), channel_id=1, source_target_pairs={{0,14},{1,15},{2,12},{3,13},{4,10},{5,11},{6,8},{7,9},{8,6},{9,7},... | collective-permute-start | bytes 196616 | tf_op jit(solution)/shard_map/ppermute | solution.py:349
  46.7 8.2 %collective-permute-start.7 = (bf16[64,512]{1,0:T(8,128)(2,1)}, bf16[64,512]{1,0:T(8,128)(2,1)S(1)}, u32[]{:S(2)}, u32[]{:S(2)}) collective-permute-start(bf16[64,512]{1,0:T(8,128)(2,1)} %get-tuple-element.41), channel_id=1, source_target_pairs={{0,15},{1,14},{2,13},{3,12},{4,11},{5,10},{6,9},{7,8},{8,7},{9,6},... | collective-permute-start | bytes 196616 | tf_op jit(solution)/shard_map/ppermute | solution.py:349
  48.8 7.3 %collective-permute-start.8 = (bf16[384,256]{1,0:T(8,128)(2,1)S(1)}, bf16[384,256]{1,0:T(8,128)(2,1)S(1)}, u32[]{:S(2)}, u32[]{:S(2)}) collective-permute-start(bf16[384,256]{1,0:T(8,128)(2,1)S(1)} %get-tuple-element.43), channel_id=1, source_target_pairs={{0,4},{1,5},{2,6},{3,7},{8,12},{9,13},{10,14},{11,15},{4,0},{5,1},... | collective-permute-start | bytes 589832 | tf_op jit(solution)/shard_map/ppermute | solution.py:379
  48.9 7.2 %collective-permute-start.9 = (bf16[384,256]{1,0:T(8,128)(2,1)S(1)}, bf16[384,256]{1,0:T(8,128)(2,1)S(1)}, u32[]{:S(2)}, u32[]{:S(2)}) collective-permute-start(bf16[384,256]{1,0:T(8,128)(2,1)S(1)} %get-tuple-element.44), channel_id=1, source_target_pairs={{4,8},{5,9},{6,10},{7,11},{8,4},{9,5},{10,6},{11,7},{20,24},{21,25... | collective-permute-start | bytes 589832 | tf_op jit(solution)/shard_map/ppermute | solution.py:379
  57.3 9.0 %collective-permute-start.10 = (bf16[256,512]{1,0:T(8,128)(2,1)S(1)}, bf16[256,512]{1,0:T(8,128)(2,1)S(1)}, u32[]{:S(2)}, u32[]{:S(2)}) collective-permute-start(bf16[256,512]{1,0:T(8,128)(2,1)S(1)} %shard_map.86), channel_id=1, source_target_pairs={{0,3},{1,2},{2,1},{3,0},{4,7},{5,6},{6,5},{7,4},{8,11},{9,10},{10,... | collective-permute-start | bytes 786440 | tf_op jit(solution)/shard_map/ppermute | solution.py:393
  60.7 10.0 %collective-permute-start.11 = (bf16[256,512]{1,0:T(8,128)(2,1)S(1)}, bf16[256,512]{1,0:T(8,128)(2,1)S(1)}, u32[]{:S(2)}, u32[]{:S(2)}) collective-permute-start(bf16[256,512]{1,0:T(8,128)(2,1)S(1)} %shard_map.87), channel_id=1, source_target_pairs={{0,1},{1,0},{2,3},{3,2},{4,5},{5,4},{6,7},{7,6},{8,9},{9,8},{10,11... | collective-permute-start | bytes 786440 | tf_op jit(solution)/shard_map/ppermute | solution.py:393
  62.5 8.3 %collective-permute-start.12 = (bf16[256,512]{1,0:T(8,128)(2,1)S(1)}, bf16[256,512]{1,0:T(8,128)(2,1)S(1)}, u32[]{:S(2)}, u32[]{:S(2)}) collective-permute-start(bf16[256,512]{1,0:T(8,128)(2,1)S(1)} %shard_map.88), channel_id=1, source_target_pairs={{0,2},{1,3},{2,0},{3,1},{4,6},{5,7},{6,4},{7,5},{8,10},{9,11},{10,... | collective-permute-start | bytes 786440 | tf_op jit(solution)/shard_map/ppermute | solution.py:393

commit v20 on v19

--- a/solution.py
+++ b/solution.py
@@ -367,7 +367,7 @@
 
     kv, near = lax.optimization_barrier((kv, near))
     queries.insert(0, exchange(near, halves))
-    kv, *queries[1:5] = lax.optimization_barrier((kv, *queries[1:5]))
+    kv, *queries[1:4] = lax.optimization_barrier((kv, *queries[1:4]))
     reach = REACH_BLOCKS * block
     sizes = [run - reach, reach] * 2
     *runs, even_out, odd_out = place([kv], slot, sizes, members)

time: 72.1 us -> 72.1 us (level)
  no operation moved by 1% of the time
where the time goes in v20:
time: 72.1 us; the launch traced here: 71.8 us
  starting transfers between devices  35.5 us (49%)
  Pallas kernels  23.6 us (33%)
  waiting for transfers between devices  10.9 us (15%)
  local copies, waits for them, and re-layouts  0.74 us (1%)
    ppermute x8, starting transfers between devices, shards(): lax.ppermute(piece, 'ctx', [(j, j ^ distance) for j in range(devices)])  19 us
    pallas_call x2, Pallas kernels, project(): pl.pallas_call(functools.partial(project_kernel, kinds, devices, heads, a...  16 us
    all_to_all x2, starting transfers between devices, exchange(): lax.all_to_all(flat, 'ctx', split_axis=0, concat_axis=0, tiled=True, axis...  12 us
    ppermute x3, waiting for transfers between devices, shards(): out = lax.ppermute(out, ('dp', 'ctx'), route)  6.3 us
    ppermute x8, waiting for transfers between devices, shards(): lax.ppermute(piece, 'ctx', [(j, j ^ distance) for j in range(devices)])  4.62 us
    pallas_call x4, Pallas kernels, attend(): pl.pallas_call(functools.partial(attend_kernel, block, turn, members, dev...  4.59 us
    ppermute x3, starting transfers between devices, shards(): out = lax.ppermute(out, ('dp', 'ctx'), route)  3.68 us
    pallas_call x2, Pallas kernels, place(): pl.pallas_call(functools.partial(place_kernel, len(pieces), members), out...  1.96 us
  transfers between devices with their start and end apart: 15, of which 5 were waited for; matrix products, arithmetic and copies ran while one was open for 2% of the time, Pallas kernels for 21%

profile of v20, /device:TPU:0, one launch (start us, length us, event | category | flops | bytes accessed | tf_op | source)
XLA Modules:
  0.0 71.8 jit_solution(9848659961647283984)
XLA Ops:
  0.0 6.5 %shard_map.82 = bf16[4,4,64,256]{3,2,1,0:T(8,128)(2,1)} custom-call(s32[32,128]{1,0:T(8,128)} %bitcast.16, f32[1,128]{1,0:T(1,128)} %constant.78.clone.freq_hbm, bf16[4096]{0:T(1024)(128)(2,1)} %gain_hbm.3, bf16[256,4096]{1,0:T(8,128)(2,1)} %tokens_hbm.3, bf16[4096,512]{1,0:T(8,128)(2,1)} %rest_0_.2, bf16[4096,512]{1,0:T(8,128)(2,1)} %rest_1_.1), custom_call_target="tpu_custom_call" | custom-call | flops 2147483648 | bytes 11010048 | tf_op jit(solution)/shard_map/pallas_call | solution.py:148
  6.5 8.3 %all-to-all-start = ((bf16[16,64,256]{2,1,0:T(8,128)(2,1)}), bf16[16,64,256]{2,1,0:T(8,128)(2,1)S(1)}, u32[]{:S(2)}, u32[]{:S(2)}) async-start(bf16[16,64,256]{2,1,0:T(8,128)(2,1)} %bitcast.14), calls=%async_computation | async-start | bytes 1048576 | tf_op jit(solution)/shard_map/all_to_all | solution.py:339
  14.9 9.5 %shard_map.83 = (bf16[2,4,64,512]{3,2,1,0:T(8,128)(2,1)}, bf16[64,512]{1,0:T(8,128)(2,1)}, bf16[64,512]{1,0:T(8,128)(2,1)}, bf16[64,512]{1,0:T(8,128)(2,1)}, bf1...) custom-call(s32[32,128]{1,0:T(8,128)} %bitcast.17, ...), custom_call_target="tpu_custom_call" | custom-call | flops 4294967296 | bytes 19922944 | tf_op jit(solution)/shard_map/pallas_call | solution.py:148
  24.4 2.9 %collective-permute-start = (bf16[64,512]{1,0:T(8,128)(2,1)}, bf16[64,512]{1,0:T(8,128)(2,1)S(1)}, u32[]{:S(2)}, u32[]{:S(2)}) collective-permute-start(bf16[64,512]{1,0:T(8,128)(2,1)} %get-tuple-element.29), channel_id=1, source_target_pairs={{0,8},{1,9},{2,10},{3,11},{4,12},{5,13},{6,14},{7,15},{8,0},{9,1},... | collective-permute-start | bytes 196616 | tf_op jit(solution)/shard_map/ppermute | solution.py:349
  27.3 1.5 %collective-permute-start.1 = (bf16[64,512]{1,0:T(8,128)(2,1)}, bf16[64,512]{1,0:T(8,128)(2,1)S(1)}, u32[]{:S(2)}, u32[]{:S(2)}) collective-permute-start(bf16[64,512]{1,0:T(8,128)(2,1)} %get-tuple-element.30), channel_id=1, source_target_pairs={{0,9},{1,8},{2,11},{3,10},{4,13},{5,12},{6,15},{7,14},{8,1},{9,0},... | collective-permute-start | bytes 196616 | tf_op jit(solution)/shard_map/ppermute | solution.py:349
  28.8 3.3 %collective-permute-start.2 = (bf16[64,512]{1,0:T(8,128)(2,1)}, bf16[64,512]{1,0:T(8,128)(2,1)S(1)}, u32[]{:S(2)}, u32[]{:S(2)}) collective-permute-start(bf16[64,512]{1,0:T(8,128)(2,1)} %get-tuple-element.31), channel_id=1, source_target_pairs={{0,10},{1,11},{2,8},{3,9},{4,14},{5,15},{6,12},{7,13},{8,2},{9,3},... | collective-permute-start | bytes 196616 | tf_op jit(solution)/shard_map/ppermute | solution.py:349
  32.1 3.7 %collective-permute-start.4 = (bf16[64,512]{1,0:T(8,128)(2,1)}, bf16[64,512]{1,0:T(8,128)(2,1)S(1)}, u32[]{:S(2)}, u32[]{:S(2)}) collective-permute-start(bf16[64,512]{1,0:T(8,128)(2,1)} %get-tuple-element.36), channel_id=1, source_target_pairs={{0,12},{1,13},{2,14},{3,15},{4,8},{5,9},{6,10},{7,11},{8,4},{9,5},... | collective-permute-start | bytes 196616 | tf_op jit(solution)/shard_map/ppermute | solution.py:349
  35.8 3.7 %all-to-all-start.1 = ((bf16[8,64,512]{2,1,0:T(8,128)(2,1)}), bf16[8,64,512]{2,1,0:T(8,128)(2,1)S(1)}, u32[]{:S(2)}, u32[]{:S(2)}) async-start(bf16[8,64,512]{2,1,0:T(8,128)(2,1)} %bitcast.15), calls=%async_computation.1 | async-start | bytes 1048576 | tf_op jit(solution)/shard_map/all_to_all | solution.py:339
  40.5 2.9 %collective-permute-start.5 = (bf16[64,512]{1,0:T(8,128)(2,1)}, bf16[64,512]{1,0:T(8,128)(2,1)S(1)}, u32[]{:S(2)}, u32[]{:S(2)}) collective-permute-start(bf16[64,512]{1,0:T(8,128)(2,1)} %get-tuple-element.37), channel_id=1, source_target_pairs={{0,13},{1,12},{2,15},{3,14},{4,9},{5,8},{6,11},{7,10},{8,5},{9,4},... | collective-permute-start | bytes 196616 | tf_op jit(solution)/shard_map/ppermute | solution.py:349
  43.4 3.3 %collective-permute-start.6 = (bf16[64,512]{1,0:T(8,128)(2,1)}, bf16[64,512]{1,0:T(8,128)(2,1)S(1)}, u32[]{:S(2)}, u32[]{:S(2)}) collective-permute-start(bf16[64,512]{1,0:T(8,128)(2,1)} %get-tuple-element.38), channel_id=1, source_target_pairs={{0,14},{1,15},{2,12},{3,13},{4,10},{5,11},{6,8},{7,9},{8,6},{9,7},... | collective-permute-start | bytes 196616 | tf_op jit(solution)/shard_map/ppermute | solution.py:349
  46.7 1.5 %collective-permute-start.7 = (bf16[64,512]{1,0:T(8,128)(2,1)}, bf16[64,512]{1,0:T(8,128)(2,1)S(1)}, u32[]{:S(2)}, u32[]{:S(2)}) collective-permute-start(bf16[64,512]{1,0:T(8,128)(2,1)} %get-tuple-element.39), channel_id=1, source_target_pairs={{0,15},{1,14},{2,13},{3,12},{4,11},{5,10},{6,9},{7,8},{8,7},{9,6},... | collective-permute-start | bytes 196616 | tf_op jit(solution)/shard_map/ppermute | solution.py:349
  48.1 0.7 %shard_map.85 = (bf16[128,256]{1,0:T(8,128)(2,1)S(1)}, bf16[384,256]{1,0:T(8,128)(2,1)S(1)}, bf16[128,256]{1,0:T(8,128)(2,1)S(1)}, bf16[384,256]{1,0:T(8,128)(2,...) custom-call(s32[1,1024]{1,0:T(1,128)S(1)} %reshape.132.slot_ref, bf16[1024,256]{1,0:T(8,128)(2,1)S(1)} %bitcast.12), custom_call_target="tpu_custom_call" | custom-call | flops 536870912 | bytes 1048576 | tf_op jit(solution)/shard_map/pallas_call | solution.py:197
  50.3 1.0 %collective-permute-done.6.refs_7_ = bf16[64,512]{1,0:T(8,128)(2,1)S(1)} collective-permute-done((bf16[64,512]{1,0:T(8,128)(2,1)}, bf16[64,512]{1,0:T(8,128)(2,1)S(1)}, u32[]{:S(2)}, u32[]{:S(2)}) %collective-permute-start.6) | collective-permute-done | bytes 65568 | tf_op jit(solution)/shard_map/ppermute | solution.py:349
  51.3 3.6 %collective-permute-done.7.refs_8_ = bf16[64,512]{1,0:T(8,128)(2,1)S(1)} collective-permute-done((bf16[64,512]{1,0:T(8,128)(2,1)}, bf16[64,512]{1,0:T(8,128)(2,1)S(1)}, u32[]{:S(2)}, u32[]{:S(2)}) %collective-permute-start.7) | collective-permute-done | bytes 65568 | tf_op jit(solution)/shard_map/ppermute | solution.py:349
  54.9 1.2 %shard_map.84.query_ref = bf16[1024,512]{1,0:T(8,128)(2,1)S(1)} custom-call(s32[1,1024]{1,0:T(1,128)S(1)} %reshape.126.slot_ref, bf16[512,512]{1,0:T(8,128)(2,1)S(1)} %bitcast.13, bf16[64,512]{1,0:T(8,128)(2,1)S(1)} %collective-permute-done.refs_1_, bf16[64,512]{1,0:T(8,128)(2,1)S(1)} %collective-permute-done.1.refs_2_, ...), custom_call_target="tpu_custom_call" | custom-call | flops 1073741824 | bytes 2097152 | tf_op jit(solution)/shard_map/pallas_call | solution.py:197
  56.2 1.2 %shard_map.86 = bf16[256,512]{1,0:T(8,128)(2,1)S(1)} custom-call(s32[1,32]{1,0:T(1,128)S(1)} %reduce-window_clone.1.ends_ref, bf16[1024,512]{1,0:T(8,128)(2,1)S(1)} %shard_map.84.query_ref, bf16[384,256]{1,0:T(8,128)(2,1)S(1)} %collective-permute-done.8.rest_0_, bf16[384,256]{1,0:T(8,128)(2,1)S(1)} %collective-permute-done.9.rest_1_, ...), custom_call_target="tpu_custom_call" | custom-call | flops 268435456 | bytes 1966080 | tf_op jit(solution)/shard_map/pallas_call | solution.py:281
  57.3 2.2 %collective-permute-start.10 = (bf16[256,512]{1,0:T(8,128)(2,1)S(1)}, bf16[256,512]{1,0:T(8,128)(2,1)S(1)}, u32[]{:S(2)}, u32[]{:S(2)}) collective-permute-start(bf16[256,512]{1,0:T(8,128)(2,1)S(1)} %shard_map.86), channel_id=1, source_target_pairs={{0,3},{1,2},{2,1},{3,0},{4,7},{5,6},{6,5},{7,4},{8,11},{9,10},{10,... | collective-permute-start | bytes 786440 | tf_op jit(solution)/shard_map/ppermute | solution.py:393
  59.5 1.1 %shard_map.87 = bf16[256,512]{1,0:T(8,128)(2,1)S(1)} custom-call(s32[1,32]{1,0:T(1,128)S(1)} %reduce-window_clone.1.ends_ref, bf16[1024,512]{1,0:T(8,128)(2,1)S(1)} %shard_map.84.query_ref, bf16[384,256]{1,0:T(8,128)(2,1)S(1)} %collective-permute-done.8.rest_0_, bf16[384,256]{1,0:T(8,128)(2,1)S(1)} %collective-permute-done.9.rest_1_, ...), custom_call_target="tpu_custom_call" | custom-call | flops 268435456 | bytes 1966080 | tf_op jit(solution)/shard_map/pallas_call | solution.py:281
  61.3 1.1 %shard_map.88 = bf16[256,512]{1,0:T(8,128)(2,1)S(1)} custom-call(s32[1,32]{1,0:T(1,128)S(1)} %reduce-window_clone.1.ends_ref, bf16[1024,512]{1,0:T(8,128)(2,1)S(1)} %shard_map.84.query_ref, bf16[384,256]{1,0:T(8,128)(2,1)S(1)} %collective-permute-done.8.rest_0_, bf16[384,256]{1,0:T(8,128)(2,1)S(1)} %collective-permute-done.9.rest_1_, ...), custom_call_target="tpu_custom_call" | custom-call | flops 268435456 | bytes 1966080 | tf_op jit(solution)/shard_map/pallas_call | solution.py:281
  62.5 0.8 %collective-permute-start.12 = (bf16[256,512]{1,0:T(8,128)(2,1)S(1)}, bf16[256,512]{1,0:T(8,128)(2,1)S(1)}, u32[]{:S(2)}, u32[]{:S(2)}) collective-permute-start(bf16[256,512]{1,0:T(8,128)(2,1)S(1)} %shard_map.88), channel_id=1, source_target_pairs={{0,2},{1,3},{2,0},{3,1},{4,6},{5,7},{6,4},{7,5},{8,10},{9,11},{10,... | collective-permute-start | bytes 786440 | tf_op jit(solution)/shard_map/ppermute | solution.py:393
  63.3 1.1 %shard_map.89.refs_3_ = bf16[256,512]{1,0:T(8,128)(2,1)S(1)} custom-call(s32[1,32]{1,0:T(1,128)S(1)} %reduce-window_clone.1.ends_ref, bf16[1024,512]{1,0:T(8,128)(2,1)S(1)} %shard_map.84.query_ref, bf16[384,256]{1,0:T(8,128)(2,1)S(1)} %collective-permute-done.8.rest_0_, bf16[384,256]{1,0:T(8,128)(2,1)S(1)} %collective-permute-done.9.rest_1_, ...), custom_call_target="tpu_custom_call" | custom-call | flops 268435456 | bytes 1966080 | tf_op jit(solution)/shard_map/pallas_call | solution.py:281
  64.4 1.9 %collective-permute-done.10.refs_0_ = bf16[256,512]{1,0:T(8,128)(2,1)S(1)} collective-permute-done((bf16[256,512]{1,0:T(8,128)(2,1)S(1)}, bf16[256,512]{1,0:T(8,128)(2,1)S(1)}, u32[]{:S(2)}, u32[]{:S(2)}) %collective-permute-start.10) | collective-permute-done | bytes 262176 | tf_op jit(solution)/shard_map/ppermute | solution.py:393
  66.3 4.3 %collective-permute-done.11.refs_1_ = bf16[256,512]{1,0:T(8,128)(2,1)S(1)} collective-permute-done((bf16[256,512]{1,0:T(8,128)(2,1)S(1)}, bf16[256,512]{1,0:T(8,128)(2,1)S(1)}, u32[]{:S(2)}, u32[]{:S(2)}) %collective-permute-start.11) | collective-permute-done | bytes 262176 | tf_op jit(solution)/shard_map/ppermute | solution.py:393
  70.8 1.1 %shard_map.90 = bf16[256,2048]{1,0:T(8,128)(2,1)} custom-call(bf16[256,512]{1,0:T(8,128)(2,1)S(1)} %collective-permute-done.10.refs_0_, bf16[256,512]{1,0:T(8,128)(2,1)S(1)} %collective-permute-done.11.refs_1_, bf16[256,512]{1,0:T(8,128)(2,1)S(1)} %collective-permute-done.12.refs_2_, bf16[256,512]{1,0:T(8,128)(2,1)S(1)} %shard_map.89.refs_3_), custom_call_target="tpu_custom_call" | custom-call | bytes 2097152 | tf_op jit(solution)/shard_map/pallas_call | solution.py:306
  (30 shorter events, 3.1 us)
Async XLA Ops:
  6.5 29.3 %all-to-all-start = ((bf16[16,64,256]{2,1,0:T(8,128)(2,1)}), bf16[16,64,256]{2,1,0:T(8,128)(2,1)S(1)}, u32[]{:S(2)}, u32[]{:S(2)}) async-start(bf16[16,64,256]{2,1,0:T(8,128)(2,1)} %bitcast.14), calls=%async_computation | async-start | bytes 1048576 | tf_op jit(solution)/shard_map/all_to_all | solution.py:339
  14.9 24.7 %copy-start = (s32[4096]{0:T(1024)S(1)}, s32[4096]{0:T(1024)}, u32[]{:S(2)}) copy-start(s32[4096]{0:T(1024)} %param.9) | copy-start | bytes 49156
  14.9 25.3 %copy-start.1 = (s32[32]{0:T(128)S(1)}, s32[32]{0:T(128)}, u32[]{:S(2)}) copy-start(s32[32]{0:T(128)} %param.10) | copy-start | bytes 388
  24.4 16.1 %collective-permute-start = (bf16[64,512]{1,0:T(8,128)(2,1)}, bf16[64,512]{1,0:T(8,128)(2,1)S(1)}, u32[]{:S(2)}, u32[]{:S(2)}) collective-permute-start(bf16[64,512]{1,0:T(8,128)(2,1)} %get-tuple-element.29), channel_id=1, source_target_pairs={{0,8},{1,9},{2,10},{3,11},{4,12},{5,13},{6,14},{7,15},{8,0},{9,1},... | collective-permute-start | bytes 196616 | tf_op jit(solution)/shard_map/ppermute | solution.py:349
  27.3 16.1 %collective-permute-start.1 = (bf16[64,512]{1,0:T(8,128)(2,1)}, bf16[64,512]{1,0:T(8,128)(2,1)S(1)}, u32[]{:S(2)}, u32[]{:S(2)}) collective-permute-start(bf16[64,512]{1,0:T(8,128)(2,1)} %get-tuple-element.30), channel_id=1, source_target_pairs={{0,9},{1,8},{2,11},{3,10},{4,13},{5,12},{6,15},{7,14},{8,1},{9,0},... | collective-permute-start | bytes 196616 | tf_op jit(solution)/shard_map/ppermute | solution.py:349
  28.8 17.9 %collective-permute-start.2 = (bf16[64,512]{1,0:T(8,128)(2,1)}, bf16[64,512]{1,0:T(8,128)(2,1)S(1)}, u32[]{:S(2)}, u32[]{:S(2)}) collective-permute-start(bf16[64,512]{1,0:T(8,128)(2,1)} %get-tuple-element.31), channel_id=1, source_target_pairs={{0,10},{1,11},{2,8},{3,9},{4,14},{5,15},{6,12},{7,13},{8,2},{9,3},... | collective-permute-start | bytes 196616 | tf_op jit(solution)/shard_map/ppermute | solution.py:349
  32.0 16.8 %collective-permute-start.3 = (bf16[64,512]{1,0:T(8,128)(2,1)}, bf16[64,512]{1,0:T(8,128)(2,1)S(1)}, u32[]{:S(2)}, u32[]{:S(2)}) collective-permute-start(bf16[64,512]{1,0:T(8,128)(2,1)} %get-tuple-element.35), channel_id=1, source_target_pairs={{0,11},{1,10},{2,9},{3,8},{4,15},{5,14},{6,13},{7,12},{8,3},{9,2},... | collective-permute-start | bytes 196616 | tf_op jit(solution)/shard_map/ppermute | solution.py:349
  32.1 16.8 %collective-permute-start.4 = (bf16[64,512]{1,0:T(8,128)(2,1)}, bf16[64,512]{1,0:T(8,128)(2,1)S(1)}, u32[]{:S(2)}, u32[]{:S(2)}) collective-permute-start(bf16[64,512]{1,0:T(8,128)(2,1)} %get-tuple-element.36), channel_id=1, source_target_pairs={{0,12},{1,13},{2,14},{3,15},{4,8},{5,9},{6,10},{7,11},{8,4},{9,5},... | collective-permute-start | bytes 196616 | tf_op jit(solution)/shard_map/ppermute | solution.py:349
  35.8 19.0 %all-to-all-start.1 = ((bf16[8,64,512]{2,1,0:T(8,128)(2,1)}), bf16[8,64,512]{2,1,0:T(8,128)(2,1)S(1)}, u32[]{:S(2)}, u32[]{:S(2)}) async-start(bf16[8,64,512]{2,1,0:T(8,128)(2,1)} %bitcast.15), calls=%async_computation.1 | async-start | bytes 1048576 | tf_op jit(solution)/shard_map/all_to_all | solution.py:339
  40.5 9.8 %collective-permute-start.5 = (bf16[64,512]{1,0:T(8,128)(2,1)}, bf16[64,512]{1,0:T(8,128)(2,1)S(1)}, u32[]{:S(2)}, u32[]{:S(2)}) collective-permute-start(bf16[64,512]{1,0:T(8,128)(2,1)} %get-tuple-element.37), channel_id=1, source_target_pairs={{0,13},{1,12},{2,15},{3,14},{4,9},{5,8},{6,11},{7,10},{8,5},{9,4},... | collective-permute-start | bytes 196616 | tf_op jit(solution)/shard_map/ppermute | solution.py:349
  43.4 7.9 %collective-permute-start.6 = (bf16[64,512]{1,0:T(8,128)(2,1)}, bf16[64,512]{1,0:T(8,128)(2,1)S(1)}, u32[]{:S(2)}, u32[]{:S(2)}) collective-permute-start(bf16[64,512]{1,0:T(8,128)(2,1)} %get-tuple-element.38), channel_id=1, source_target_pairs={{0,14},{1,15},{2,12},{3,13},{4,10},{5,11},{6,8},{7,9},{8,6},{9,7},... | collective-permute-start | bytes 196616 | tf_op jit(solution)/shard_map/ppermute | solution.py:349
  46.7 8.2 %collective-permute-start.7 = (bf16[64,512]{1,0:T(8,128)(2,1)}, bf16[64,512]{1,0:T(8,128)(2,1)S(1)}, u32[]{:S(2)}, u32[]{:S(2)}) collective-permute-start(bf16[64,512]{1,0:T(8,128)(2,1)} %get-tuple-element.39), channel_id=1, source_target_pairs={{0,15},{1,14},{2,13},{3,12},{4,11},{5,10},{6,9},{7,8},{8,7},{9,6},... | collective-permute-start | bytes 196616 | tf_op jit(solution)/shard_map/ppermute | solution.py:349
  48.8 7.3 %collective-permute-start.8 = (bf16[384,256]{1,0:T(8,128)(2,1)S(1)}, bf16[384,256]{1,0:T(8,128)(2,1)S(1)}, u32[]{:S(2)}, u32[]{:S(2)}) collective-permute-start(bf16[384,256]{1,0:T(8,128)(2,1)S(1)} %get-tuple-element.41), channel_id=1, source_target_pairs={{0,4},{1,5},{2,6},{3,7},{8,12},{9,13},{10,14},{11,15},{4,0},{5,1},... | collective-permute-start | bytes 589832 | tf_op jit(solution)/shard_map/ppermute | solution.py:379
  48.9 7.2 %collective-permute-start.9 = (bf16[384,256]{1,0:T(8,128)(2,1)S(1)}, bf16[384,256]{1,0:T(8,128)(2,1)S(1)}, u32[]{:S(2)}, u32[]{:S(2)}) collective-permute-start(bf16[384,256]{1,0:T(8,128)(2,1)S(1)} %get-tuple-element.42), channel_id=1, source_target_pairs={{4,8},{5,9},{6,10},{7,11},{8,4},{9,5},{10,6},{11,7},{20,24},{21,25... | collective-permute-start | bytes 589832 | tf_op jit(solution)/shard_map/ppermute | solution.py:379
  57.3 9.0 %collective-permute-start.10 = (bf16[256,512]{1,0:T(8,128)(2,1)S(1)}, bf16[256,512]{1,0:T(8,128)(2,1)S(1)}, u32[]{:S(2)}, u32[]{:S(2)}) collective-permute-start(bf16[256,512]{1,0:T(8,128)(2,1)S(1)} %shard_map.86), channel_id=1, source_target_pairs={{0,3},{1,2},{2,1},{3,0},{4,7},{5,6},{6,5},{7,4},{8,11},{9,10},{10,... | collective-permute-start | bytes 786440 | tf_op jit(solution)/shard_map/ppermute | solution.py:393
  60.7 10.0 %collective-permute-start.11 = (bf16[256,512]{1,0:T(8,128)(2,1)S(1)}, bf16[256,512]{1,0:T(8,128)(2,1)S(1)}, u32[]{:S(2)}, u32[]{:S(2)}) collective-permute-start(bf16[256,512]{1,0:T(8,128)(2,1)S(1)} %shard_map.87), channel_id=1, source_target_pairs={{0,1},{1,0},{2,3},{3,2},{4,5},{5,4},{6,7},{7,6},{8,9},{9,8},{10,11... | collective-permute-start | bytes 786440 | tf_op jit(solution)/shard_map/ppermute | solution.py:393
  62.5 8.3 %collective-permute-start.12 = (bf16[256,512]{1,0:T(8,128)(2,1)S(1)}, bf16[256,512]{1,0:T(8,128)(2,1)S(1)}, u32[]{:S(2)}, u32[]{:S(2)}) collective-permute-start(bf16[256,512]{1,0:T(8,128)(2,1)S(1)} %shard_map.88), channel_id=1, source_target_pairs={{0,2},{1,3},{2,0},{3,1},{4,6},{5,7},{6,4},{7,5},{8,10},{9,11},{10,... | collective-permute-start | bytes 786440 | tf_op jit(solution)/shard_map/ppermute | solution.py:393

commit v21 on v19

--- a/solution.py
+++ b/solution.py
@@ -217,9 +217,9 @@
 
 
 def distances_at(turn, members):
-    if turn in (0, members - 1):
-        return (members - 1 - turn,) * 2
-    return (turn, members - 1 - turn)
+    if turn >= members - 2:
+        return (members - 1 if turn == members - 2 else 0,) * 2
+    return (turn + 1, members - 2 - turn)
 
 
 def attend_kernel(block, turn, members, devices, ends_ref, query_ref, *rest):

time: 72.1 us -> 73.6 us (1.021)
  waiting for transfers between devices: 10.9 us -> 12.4 us
    ppermute x3, waiting for transfers between devices: 6.3 us -> 7.78 us  [shards(): out = lax.ppermute(out, ('dp', 'ctx'), route)]
  transfers between devices with their start and end apart: 15 -> 15, of which waited for: 5 -> 4; matrix products, arithmetic and copies ran while one was open for 2% -> 2% of each run, Pallas kernels for 21% -> 20%
where the time goes in v21:
time: 73.6 us; the launch traced here: 73.3 us
  starting transfers between devices  35.5 us (48%)
  Pallas kernels  23.6 us (32%)
  waiting for transfers between devices  12.4 us (17%)
  local copies, waits for them, and re-layouts  0.74 us (1%)
    ppermute x8, starting transfers between devices, shards(): lax.ppermute(piece, 'ctx', [(j, j ^ distance) for j in range(devices)])  19 us
    pallas_call x2, Pallas kernels, project(): pl.pallas_call(functools.partial(project_kernel, kinds, devices, heads, a...  16 us
    all_to_all x2, starting transfers between devices, exchange(): lax.all_to_all(flat, 'ctx', split_axis=0, concat_axis=0, tiled=True, axis...  12 us
    ppermute x3, waiting for transfers between devices, shards(): out = lax.ppermute(out, ('dp', 'ctx'), route)  7.78 us
    ppermute x8, waiting for transfers between devices, shards(): lax.ppermute(piece, 'ctx', [(j, j ^ distance) for j in range(devices)])  4.63 us
    pallas_call x4, Pallas kernels, attend(): pl.pallas_call(functools.partial(attend_kernel, block, turn, members, dev...  4.59 us
    ppermute x3, starting transfers between devices, shards(): out = lax.ppermute(out, ('dp', 'ctx'), route)  3.68 us
    pallas_call x2, Pallas kernels, place(): pl.pallas_call(functools.partial(place_kernel, len(pieces), members), out...  1.96 us
  transfers between devices with their start and end apart: 15, of which 4 were waited for; matrix products, arithmetic and copies ran while one was open for 2% of the time, Pallas kernels for 20%

profile of v21, /device:TPU:0, one launch (start us, length us, event | category | flops | bytes accessed | tf_op | source)
XLA Modules:
  0.0 73.3 jit_solution(5580127521735330479)
XLA Ops:
  0.0 6.5 %shard_map.82 = bf16[4,4,64,256]{3,2,1,0:T(8,128)(2,1)} custom-call(s32[32,128]{1,0:T(8,128)} %bitcast.16, f32[1,128]{1,0:T(1,128)} %constant.78.clone.freq_hbm, bf16[4096]{0:T(1024)(128)(2,1)} %gain_hbm.3, bf16[256,4096]{1,0:T(8,128)(2,1)} %tokens_hbm.3, bf16[4096,512]{1,0:T(8,128)(2,1)} %rest_0_.2, bf16[4096,512]{1,0:T(8,128)(2,1)} %rest_1_.1), custom_call_target="tpu_custom_call" | custom-call | flops 2147483648 | bytes 11010048 | tf_op jit(solution)/shard_map/pallas_call | solution.py:148
  6.5 8.3 %all-to-all-start = ((bf16[16,64,256]{2,1,0:T(8,128)(2,1)}), bf16[16,64,256]{2,1,0:T(8,128)(2,1)S(1)}, u32[]{:S(2)}, u32[]{:S(2)}) async-start(bf16[16,64,256]{2,1,0:T(8,128)(2,1)} %bitcast.14), calls=%async_computation | async-start | bytes 1048576 | tf_op jit(solution)/shard_map/all_to_all | solution.py:339
  14.9 9.5 %shard_map.83 = (bf16[2,4,64,512]{3,2,1,0:T(8,128)(2,1)}, bf16[64,512]{1,0:T(8,128)(2,1)}, bf16[64,512]{1,0:T(8,128)(2,1)}, bf16[64,512]{1,0:T(8,128)(2,1)}, bf1...) custom-call(s32[32,128]{1,0:T(8,128)} %bitcast.17, ...), custom_call_target="tpu_custom_call" | custom-call | flops 4294967296 | bytes 19922944 | tf_op jit(solution)/shard_map/pallas_call | solution.py:148
  24.4 2.9 %collective-permute-start = (bf16[64,512]{1,0:T(8,128)(2,1)}, bf16[64,512]{1,0:T(8,128)(2,1)S(1)}, u32[]{:S(2)}, u32[]{:S(2)}) collective-permute-start(bf16[64,512]{1,0:T(8,128)(2,1)} %get-tuple-element.30), channel_id=1, source_target_pairs={{0,8},{1,9},{2,10},{3,11},{4,12},{5,13},{6,14},{7,15},{8,0},{9,1},... | collective-permute-start | bytes 196616 | tf_op jit(solution)/shard_map/ppermute | solution.py:349
  27.3 1.5 %collective-permute-start.1 = (bf16[64,512]{1,0:T(8,128)(2,1)}, bf16[64,512]{1,0:T(8,128)(2,1)S(1)}, u32[]{:S(2)}, u32[]{:S(2)}) collective-permute-start(bf16[64,512]{1,0:T(8,128)(2,1)} %get-tuple-element.31), channel_id=1, source_target_pairs={{0,9},{1,8},{2,11},{3,10},{4,13},{5,12},{6,15},{7,14},{8,1},{9,0},... | collective-permute-start | bytes 196616 | tf_op jit(solution)/shard_map/ppermute | solution.py:349
  28.8 3.3 %collective-permute-start.2 = (bf16[64,512]{1,0:T(8,128)(2,1)}, bf16[64,512]{1,0:T(8,128)(2,1)S(1)}, u32[]{:S(2)}, u32[]{:S(2)}) collective-permute-start(bf16[64,512]{1,0:T(8,128)(2,1)} %get-tuple-element.32), channel_id=1, source_target_pairs={{0,10},{1,11},{2,8},{3,9},{4,14},{5,15},{6,12},{7,13},{8,2},{9,3},... | collective-permute-start | bytes 196616 | tf_op jit(solution)/shard_map/ppermute | solution.py:349
  32.1 3.7 %collective-permute-start.4 = (bf16[64,512]{1,0:T(8,128)(2,1)}, bf16[64,512]{1,0:T(8,128)(2,1)S(1)}, u32[]{:S(2)}, u32[]{:S(2)}) collective-permute-start(bf16[64,512]{1,0:T(8,128)(2,1)} %get-tuple-element.38), channel_id=1, source_target_pairs={{0,12},{1,13},{2,14},{3,15},{4,8},{5,9},{6,10},{7,11},{8,4},{9,5},... | collective-permute-start | bytes 196616 | tf_op jit(solution)/shard_map/ppermute | solution.py:349
  35.8 3.7 %all-to-all-start.1 = ((bf16[8,64,512]{2,1,0:T(8,128)(2,1)}), bf16[8,64,512]{2,1,0:T(8,128)(2,1)S(1)}, u32[]{:S(2)}, u32[]{:S(2)}) async-start(bf16[8,64,512]{2,1,0:T(8,128)(2,1)} %bitcast.15), calls=%async_computation.1 | async-start | bytes 1048576 | tf_op jit(solution)/shard_map/all_to_all | solution.py:339
  40.5 2.9 %collective-permute-start.5 = (bf16[64,512]{1,0:T(8,128)(2,1)}, bf16[64,512]{1,0:T(8,128)(2,1)S(1)}, u32[]{:S(2)}, u32[]{:S(2)}) collective-permute-start(bf16[64,512]{1,0:T(8,128)(2,1)} %get-tuple-element.39), channel_id=1, source_target_pairs={{0,13},{1,12},{2,15},{3,14},{4,9},{5,8},{6,11},{7,10},{8,5},{9,4},... | collective-permute-start | bytes 196616 | tf_op jit(solution)/shard_map/ppermute | solution.py:349
  43.4 3.3 %collective-permute-start.6 = (bf16[64,512]{1,0:T(8,128)(2,1)}, bf16[64,512]{1,0:T(8,128)(2,1)S(1)}, u32[]{:S(2)}, u32[]{:S(2)}) collective-permute-start(bf16[64,512]{1,0:T(8,128)(2,1)} %get-tuple-element.40), channel_id=1, source_target_pairs={{0,14},{1,15},{2,12},{3,13},{4,10},{5,11},{6,8},{7,9},{8,6},{9,7},... | collective-permute-start | bytes 196616 | tf_op jit(solution)/shard_map/ppermute | solution.py:349
  46.7 1.5 %collective-permute-start.7 = (bf16[64,512]{1,0:T(8,128)(2,1)}, bf16[64,512]{1,0:T(8,128)(2,1)S(1)}, u32[]{:S(2)}, u32[]{:S(2)}) collective-permute-start(bf16[64,512]{1,0:T(8,128)(2,1)} %get-tuple-element.41), channel_id=1, source_target_pairs={{0,15},{1,14},{2,13},{3,12},{4,11},{5,10},{6,9},{7,8},{8,7},{9,6},... | collective-permute-start | bytes 196616 | tf_op jit(solution)/shard_map/ppermute | solution.py:349
  50.3 1.0 %collective-permute-done.6.refs_7_ = bf16[64,512]{1,0:T(8,128)(2,1)S(1)} collective-permute-done((bf16[64,512]{1,0:T(8,128)(2,1)}, bf16[64,512]{1,0:T(8,128)(2,1)S(1)}, u32[]{:S(2)}, u32[]{:S(2)}) %collective-permute-start.6) | collective-permute-done | bytes 65568 | tf_op jit(solution)/shard_map/ppermute | solution.py:349
  51.3 3.6 %collective-permute-done.7.refs_8_ = bf16[64,512]{1,0:T(8,128)(2,1)S(1)} collective-permute-done((bf16[64,512]{1,0:T(8,128)(2,1)}, bf16[64,512]{1,0:T(8,128)(2,1)S(1)}, u32[]{:S(2)}, u32[]{:S(2)}) %collective-permute-start.7) | collective-permute-done | bytes 65568 | tf_op jit(solution)/shard_map/ppermute | solution.py:349
  54.9 1.2 %shard_map.84.query_ref = bf16[1024,512]{1,0:T(8,128)(2,1)S(1)} custom-call(s32[1,1024]{1,0:T(1,128)S(1)} %reshape.126.slot_ref, bf16[512,512]{1,0:T(8,128)(2,1)S(1)} %bitcast.13, bf16[64,512]{1,0:T(8,128)(2,1)S(1)} %collective-permute-done.refs_1_, bf16[64,512]{1,0:T(8,128)(2,1)S(1)} %collective-permute-done.1.refs_2_, ...), custom_call_target="tpu_custom_call" | custom-call | flops 1073741824 | bytes 2097152 | tf_op jit(solution)/shard_map/pallas_call | solution.py:197
  56.2 1.1 %shard_map.86 = bf16[256,512]{1,0:T(8,128)(2,1)S(1)} custom-call(s32[1,32]{1,0:T(1,128)S(1)} %reduce-window_clone.1.ends_ref, bf16[1024,512]{1,0:T(8,128)(2,1)S(1)} %shard_map.84.query_ref, bf16[384,256]{1,0:T(8,128)(2,1)S(1)} %collective-permute-done.8.rest_0_, bf16[384,256]{1,0:T(8,128)(2,1)S(1)} %collective-permute-done.9.rest_1_, ...), custom_call_target="tpu_custom_call" | custom-call | flops 268435456 | bytes 1966080 | tf_op jit(solution)/shard_map/pallas_call | solution.py:281
  57.3 1.3 %collective-permute-start.10 = (bf16[256,512]{1,0:T(8,128)(2,1)S(1)}, bf16[256,512]{1,0:T(8,128)(2,1)S(1)}, u32[]{:S(2)}, u32[]{:S(2)}) collective-permute-start(bf16[256,512]{1,0:T(8,128)(2,1)S(1)} %shard_map.86), channel_id=1, source_target_pairs={{0,1},{1,0},{2,3},{3,2},{4,5},{5,4},{6,7},{7,6},{8,9},{9,8},{10,11... | collective-permute-start | bytes 786440 | tf_op jit(solution)/shard_map/ppermute | solution.py:393
  58.6 1.1 %shard_map.87 = bf16[256,512]{1,0:T(8,128)(2,1)S(1)} custom-call(s32[1,32]{1,0:T(1,128)S(1)} %reduce-window_clone.1.ends_ref, bf16[1024,512]{1,0:T(8,128)(2,1)S(1)} %shard_map.84.query_ref, bf16[384,256]{1,0:T(8,128)(2,1)S(1)} %collective-permute-done.8.rest_0_, bf16[384,256]{1,0:T(8,128)(2,1)S(1)} %collective-permute-done.9.rest_1_, ...), custom_call_target="tpu_custom_call" | custom-call | flops 268435456 | bytes 1966080 | tf_op jit(solution)/shard_map/pallas_call | solution.py:281
  59.8 1.5 %collective-permute-start.11 = (bf16[256,512]{1,0:T(8,128)(2,1)S(1)}, bf16[256,512]{1,0:T(8,128)(2,1)S(1)}, u32[]{:S(2)}, u32[]{:S(2)}) collective-permute-start(bf16[256,512]{1,0:T(8,128)(2,1)S(1)} %shard_map.87), channel_id=1, source_target_pairs={{0,2},{1,3},{2,0},{3,1},{4,6},{5,7},{6,4},{7,5},{8,10},{9,11},{10,... | collective-permute-start | bytes 786440 | tf_op jit(solution)/shard_map/ppermute | solution.py:393
  61.3 1.1 %shard_map.88 = bf16[256,512]{1,0:T(8,128)(2,1)S(1)} custom-call(s32[1,32]{1,0:T(1,128)S(1)} %reduce-window_clone.1.ends_ref, bf16[1024,512]{1,0:T(8,128)(2,1)S(1)} %shard_map.84.query_ref, bf16[384,256]{1,0:T(8,128)(2,1)S(1)} %collective-permute-done.8.rest_0_, bf16[384,256]{1,0:T(8,128)(2,1)S(1)} %collective-permute-done.9.rest_1_, ...), custom_call_target="tpu_custom_call" | custom-call | flops 268435456 | bytes 1966080 | tf_op jit(solution)/shard_map/pallas_call | solution.py:281
  62.5 0.8 %collective-permute-start.12 = (bf16[256,512]{1,0:T(8,128)(2,1)S(1)}, bf16[256,512]{1,0:T(8,128)(2,1)S(1)}, u32[]{:S(2)}, u32[]{:S(2)}) collective-permute-start(bf16[256,512]{1,0:T(8,128)(2,1)S(1)} %shard_map.88), channel_id=1, source_target_pairs={{0,3},{1,2},{2,1},{3,0},{4,7},{5,6},{6,5},{7,4},{8,11},{9,10},{10,... | collective-permute-start | bytes 786440 | tf_op jit(solution)/shard_map/ppermute | solution.py:393
  63.3 1.2 %shard_map.89.refs_3_ = bf16[256,512]{1,0:T(8,128)(2,1)S(1)} custom-call(s32[1,32]{1,0:T(1,128)S(1)} %reduce-window_clone.1.ends_ref, bf16[1024,512]{1,0:T(8,128)(2,1)S(1)} %shard_map.84.query_ref, bf16[384,256]{1,0:T(8,128)(2,1)S(1)} %collective-permute-done.8.rest_0_, bf16[384,256]{1,0:T(8,128)(2,1)S(1)} %collective-permute-done.9.rest_1_, ...), custom_call_target="tpu_custom_call" | custom-call | flops 268435456 | bytes 1966080 | tf_op jit(solution)/shard_map/pallas_call | solution.py:281
  64.5 2.1 %collective-permute-done.10.refs_0_ = bf16[256,512]{1,0:T(8,128)(2,1)S(1)} collective-permute-done((bf16[256,512]{1,0:T(8,128)(2,1)S(1)}, bf16[256,512]{1,0:T(8,128)(2,1)S(1)}, u32[]{:S(2)}, u32[]{:S(2)}) %collective-permute-start.10) | collective-permute-done | bytes 262176 | tf_op jit(solution)/shard_map/ppermute | solution.py:393
  66.6 5.7 %collective-permute-done.12.refs_2_ = bf16[256,512]{1,0:T(8,128)(2,1)S(1)} collective-permute-done((bf16[256,512]{1,0:T(8,128)(2,1)S(1)}, bf16[256,512]{1,0:T(8,128)(2,1)S(1)}, u32[]{:S(2)}, u32[]{:S(2)}) %collective-permute-start.12) | collective-permute-done | bytes 262176 | tf_op jit(solution)/shard_map/ppermute | solution.py:393
  72.2 1.1 %shard_map.90 = bf16[256,2048]{1,0:T(8,128)(2,1)} custom-call(bf16[256,512]{1,0:T(8,128)(2,1)S(1)} %collective-permute-done.10.refs_0_, bf16[256,512]{1,0:T(8,128)(2,1)S(1)} %collective-permute-done.11.refs_1_, bf16[256,512]{1,0:T(8,128)(2,1)S(1)} %collective-permute-done.12.refs_2_, bf16[256,512]{1,0:T(8,128)(2,1)S(1)} %shard_map.89.refs_3_), custom_call_target="tpu_custom_call" | custom-call | bytes 2097152 | tf_op jit(solution)/shard_map/pallas_call | solution.py:306
  (30 shorter events, 3.2 us)
Async XLA Ops:
  6.5 29.3 %all-to-all-start = ((bf16[16,64,256]{2,1,0:T(8,128)(2,1)}), bf16[16,64,256]{2,1,0:T(8,128)(2,1)S(1)}, u32[]{:S(2)}, u32[]{:S(2)}) async-start(bf16[16,64,256]{2,1,0:T(8,128)(2,1)} %bitcast.14), calls=%async_computation | async-start | bytes 1048576 | tf_op jit(solution)/shard_map/all_to_all | solution.py:339
  14.9 24.7 %copy-start = (s32[4096]{0:T(1024)S(1)}, s32[4096]{0:T(1024)}, u32[]{:S(2)}) copy-start(s32[4096]{0:T(1024)} %param.9) | copy-start | bytes 49156
  14.9 25.3 %copy-start.1 = (s32[32]{0:T(128)S(1)}, s32[32]{0:T(128)}, u32[]{:S(2)}) copy-start(s32[32]{0:T(128)} %param.10) | copy-start | bytes 388
  24.4 16.1 %collective-permute-start = (bf16[64,512]{1,0:T(8,128)(2,1)}, bf16[64,512]{1,0:T(8,128)(2,1)S(1)}, u32[]{:S(2)}, u32[]{:S(2)}) collective-permute-start(bf16[64,512]{1,0:T(8,128)(2,1)} %get-tuple-element.30), channel_id=1, source_target_pairs={{0,8},{1,9},{2,10},{3,11},{4,12},{5,13},{6,14},{7,15},{8,0},{9,1},... | collective-permute-start | bytes 196616 | tf_op jit(solution)/shard_map/ppermute | solution.py:349
  27.3 16.1 %collective-permute-start.1 = (bf16[64,512]{1,0:T(8,128)(2,1)}, bf16[64,512]{1,0:T(8,128)(2,1)S(1)}, u32[]{:S(2)}, u32[]{:S(2)}) collective-permute-start(bf16[64,512]{1,0:T(8,128)(2,1)} %get-tuple-element.31), channel_id=1, source_target_pairs={{0,9},{1,8},{2,11},{3,10},{4,13},{5,12},{6,15},{7,14},{8,1},{9,0},... | collective-permute-start | bytes 196616 | tf_op jit(solution)/shard_map/ppermute | solution.py:349
  28.8 17.9 %collective-permute-start.2 = (bf16[64,512]{1,0:T(8,128)(2,1)}, bf16[64,512]{1,0:T(8,128)(2,1)S(1)}, u32[]{:S(2)}, u32[]{:S(2)}) collective-permute-start(bf16[64,512]{1,0:T(8,128)(2,1)} %get-tuple-element.32), channel_id=1, source_target_pairs={{0,10},{1,11},{2,8},{3,9},{4,14},{5,15},{6,12},{7,13},{8,2},{9,3},... | collective-permute-start | bytes 196616 | tf_op jit(solution)/shard_map/ppermute | solution.py:349
  32.0 16.1 %collective-permute-start.3 = (bf16[64,512]{1,0:T(8,128)(2,1)}, bf16[64,512]{1,0:T(8,128)(2,1)S(1)}, u32[]{:S(2)}, u32[]{:S(2)}) collective-permute-start(bf16[64,512]{1,0:T(8,128)(2,1)} %get-tuple-element.33), channel_id=1, source_target_pairs={{0,11},{1,10},{2,9},{3,8},{4,15},{5,14},{6,13},{7,12},{8,3},{9,2},... | collective-permute-start | bytes 196616 | tf_op jit(solution)/shard_map/ppermute | solution.py:349
  32.1 16.8 %collective-permute-start.4 = (bf16[64,512]{1,0:T(8,128)(2,1)}, bf16[64,512]{1,0:T(8,128)(2,1)S(1)}, u32[]{:S(2)}, u32[]{:S(2)}) collective-permute-start(bf16[64,512]{1,0:T(8,128)(2,1)} %get-tuple-element.38), channel_id=1, source_target_pairs={{0,12},{1,13},{2,14},{3,15},{4,8},{5,9},{6,10},{7,11},{8,4},{9,5},... | collective-permute-start | bytes 196616 | tf_op jit(solution)/shard_map/ppermute | solution.py:349
  35.8 19.0 %all-to-all-start.1 = ((bf16[8,64,512]{2,1,0:T(8,128)(2,1)}), bf16[8,64,512]{2,1,0:T(8,128)(2,1)S(1)}, u32[]{:S(2)}, u32[]{:S(2)}) async-start(bf16[8,64,512]{2,1,0:T(8,128)(2,1)} %bitcast.15), calls=%async_computation.1 | async-start | bytes 1048576 | tf_op jit(solution)/shard_map/all_to_all | solution.py:339
  40.5 9.8 %collective-permute-start.5 = (bf16[64,512]{1,0:T(8,128)(2,1)}, bf16[64,512]{1,0:T(8,128)(2,1)S(1)}, u32[]{:S(2)}, u32[]{:S(2)}) collective-permute-start(bf16[64,512]{1,0:T(8,128)(2,1)} %get-tuple-element.39), channel_id=1, source_target_pairs={{0,13},{1,12},{2,15},{3,14},{4,9},{5,8},{6,11},{7,10},{8,5},{9,4},... | collective-permute-start | bytes 196616 | tf_op jit(solution)/shard_map/ppermute | solution.py:349
  43.4 7.9 %collective-permute-start.6 = (bf16[64,512]{1,0:T(8,128)(2,1)}, bf16[64,512]{1,0:T(8,128)(2,1)S(1)}, u32[]{:S(2)}, u32[]{:S(2)}) collective-permute-start(bf16[64,512]{1,0:T(8,128)(2,1)} %get-tuple-element.40), channel_id=1, source_target_pairs={{0,14},{1,15},{2,12},{3,13},{4,10},{5,11},{6,8},{7,9},{8,6},{9,7},... | collective-permute-start | bytes 196616 | tf_op jit(solution)/shard_map/ppermute | solution.py:349
  46.7 8.2 %collective-permute-start.7 = (bf16[64,512]{1,0:T(8,128)(2,1)}, bf16[64,512]{1,0:T(8,128)(2,1)S(1)}, u32[]{:S(2)}, u32[]{:S(2)}) collective-permute-start(bf16[64,512]{1,0:T(8,128)(2,1)} %get-tuple-element.41), channel_id=1, source_target_pairs={{0,15},{1,14},{2,13},{3,12},{4,11},{5,10},{6,9},{7,8},{8,7},{9,6},... | collective-permute-start | bytes 196616 | tf_op jit(solution)/shard_map/ppermute | solution.py:349
  48.8 7.3 %collective-permute-start.8 = (bf16[384,256]{1,0:T(8,128)(2,1)S(1)}, bf16[384,256]{1,0:T(8,128)(2,1)S(1)}, u32[]{:S(2)}, u32[]{:S(2)}) collective-permute-start(bf16[384,256]{1,0:T(8,128)(2,1)S(1)} %get-tuple-element.43), channel_id=1, source_target_pairs={{0,4},{1,5},{2,6},{3,7},{8,12},{9,13},{10,14},{11,15},{4,0},{5,1},... | collective-permute-start | bytes 589832 | tf_op jit(solution)/shard_map/ppermute | solution.py:379
  48.9 7.2 %collective-permute-start.9 = (bf16[384,256]{1,0:T(8,128)(2,1)S(1)}, bf16[384,256]{1,0:T(8,128)(2,1)S(1)}, u32[]{:S(2)}, u32[]{:S(2)}) collective-permute-start(bf16[384,256]{1,0:T(8,128)(2,1)S(1)} %get-tuple-element.44), channel_id=1, source_target_pairs={{4,8},{5,9},{6,10},{7,11},{8,4},{9,5},{10,6},{11,7},{20,24},{21,25... | collective-permute-start | bytes 589832 | tf_op jit(solution)/shard_map/ppermute | solution.py:379
  57.3 9.2 %collective-permute-start.10 = (bf16[256,512]{1,0:T(8,128)(2,1)S(1)}, bf16[256,512]{1,0:T(8,128)(2,1)S(1)}, u32[]{:S(2)}, u32[]{:S(2)}) collective-permute-start(bf16[256,512]{1,0:T(8,128)(2,1)S(1)} %shard_map.86), channel_id=1, source_target_pairs={{0,1},{1,0},{2,3},{3,2},{4,5},{5,4},{6,7},{7,6},{8,9},{9,8},{10,11... | collective-permute-start | bytes 786440 | tf_op jit(solution)/shard_map/ppermute | solution.py:393
  59.8 6.8 %collective-permute-start.11 = (bf16[256,512]{1,0:T(8,128)(2,1)S(1)}, bf16[256,512]{1,0:T(8,128)(2,1)S(1)}, u32[]{:S(2)}, u32[]{:S(2)}) collective-permute-start(bf16[256,512]{1,0:T(8,128)(2,1)S(1)} %shard_map.87), channel_id=1, source_target_pairs={{0,2},{1,3},{2,0},{3,1},{4,6},{5,7},{6,4},{7,5},{8,10},{9,11},{10,... | collective-permute-start | bytes 786440 | tf_op jit(solution)/shard_map/ppermute | solution.py:393
  62.5 9.8 %collective-permute-start.12 = (bf16[256,512]{1,0:T(8,128)(2,1)S(1)}, bf16[256,512]{1,0:T(8,128)(2,1)S(1)}, u32[]{:S(2)}, u32[]{:S(2)}) collective-permute-start(bf16[256,512]{1,0:T(8,128)(2,1)S(1)} %shard_map.88), channel_id=1, source_target_pairs={{0,3},{1,2},{2,1},{3,0},{4,7},{5,6},{6,5},{7,4},{8,11},{9,10},{10,... | collective-permute-start | bytes 786440 | tf_op jit(solution)/shard_map/ppermute | solution.py:393

commit v22 on v19

--- a/solution.py
+++ b/solution.py
@@ -79,7 +79,7 @@
     sine = jnp.where(lane < HEAD_SIZE // 2, -1.0, 1.0) * jnp.sin(angle)
     order = jnp.where(order, 1.0, 0.0).astype(jnp.bfloat16)
     gain = gain_ref[...].astype(jnp.float32).reshape(1, width)
-    step = 32
+    step = 16
     written = []
 
     small_copies[-1].wait()
@@ -90,8 +90,8 @@
         tokens[at, :] = (floats * lax.rsqrt(mean + EPSILON) * gain).astype(jnp.bfloat16)
     if chunks > 1:
         copies[1].start()
-    for first in range(0, width, 512):
-        columns = slice(first, first + 512)
+    for first in range(0, width, 2048):
+        columns = slice(first, first + 2048)
         normed[:, columns] = dot(order, tokens[:, columns]).astype(jnp.bfloat16)
     groups, heads = out_ref.shape[:2]
     offsets = [0]

time: 72.1 us -> 72.1 us (level)
  no operation moved by 1% of the time
where the time goes in v22:
time: 72.1 us; the launch traced here: 71.8 us
  starting transfers between devices  35.7 us (50%)
  Pallas kernels  23.7 us (33%)
  waiting for transfers between devices  10.8 us (15%)
  local copies, waits for them, and re-layouts  0.74 us (1%)
    ppermute x8, starting transfers between devices, shards(): lax.ppermute(piece, 'ctx', [(j, j ^ distance) for j in range(devices)])  19.1 us
    pallas_call x2, Pallas kernels, project(): pl.pallas_call(functools.partial(project_kernel, kinds, devices, heads, a...  16 us
    all_to_all x2, starting transfers between devices, exchange(): lax.all_to_all(flat, 'ctx', split_axis=0, concat_axis=0, tiled=True, axis...  12 us
    ppermute x3, waiting for transfers between devices, shards(): out = lax.ppermute(out, ('dp', 'ctx'), route)  6.3 us
    pallas_call x4, Pallas kernels, attend(): pl.pallas_call(functools.partial(attend_kernel, block, turn, members, dev...  4.59 us
    ppermute x8, waiting for transfers between devices, shards(): lax.ppermute(piece, 'ctx', [(j, j ^ distance) for j in range(devices)])  4.45 us
    ppermute x3, starting transfers between devices, shards(): out = lax.ppermute(out, ('dp', 'ctx'), route)  3.68 us
    pallas_call x2, Pallas kernels, place(): pl.pallas_call(functools.partial(place_kernel, len(pieces), members), out...  1.96 us
  transfers between devices with their start and end apart: 15, of which 5 were waited for; matrix products, arithmetic and copies ran while one was open for 2% of the time, Pallas kernels for 21%

profile of v22, /device:TPU:0, one launch (start us, length us, event | category | flops | bytes accessed | tf_op | source)
XLA Modules:
  0.0 71.8 jit_solution(2020775089205544995)
XLA Ops:
  0.0 6.5 %shard_map.82 = bf16[4,4,64,256]{3,2,1,0:T(8,128)(2,1)} custom-call(s32[32,128]{1,0:T(8,128)} %bitcast.16, f32[1,128]{1,0:T(1,128)} %constant.78.clone.freq_hbm, bf16[4096]{0:T(1024)(128)(2,1)} %gain_hbm.3, bf16[256,4096]{1,0:T(8,128)(2,1)} %tokens_hbm.3, bf16[4096,512]{1,0:T(8,128)(2,1)} %rest_0_.2, bf16[4096,512]{1,0:T(8,128)(2,1)} %rest_1_.1), custom_call_target="tpu_custom_call" | custom-call | flops 2147483648 | bytes 11010048 | tf_op jit(solution)/shard_map/pallas_call | solution.py:148
  6.5 8.3 %all-to-all-start = ((bf16[16,64,256]{2,1,0:T(8,128)(2,1)}), bf16[16,64,256]{2,1,0:T(8,128)(2,1)S(1)}, u32[]{:S(2)}, u32[]{:S(2)}) async-start(bf16[16,64,256]{2,1,0:T(8,128)(2,1)} %bitcast.14), calls=%async_computation | async-start | bytes 1048576 | tf_op jit(solution)/shard_map/all_to_all | solution.py:339
  14.9 9.5 %shard_map.83 = (bf16[2,4,64,512]{3,2,1,0:T(8,128)(2,1)}, bf16[64,512]{1,0:T(8,128)(2,1)}, bf16[64,512]{1,0:T(8,128)(2,1)}, bf16[64,512]{1,0:T(8,128)(2,1)}, bf1...) custom-call(s32[32,128]{1,0:T(8,128)} %bitcast.17, ...), custom_call_target="tpu_custom_call" | custom-call | flops 4294967296 | bytes 19922944 | tf_op jit(solution)/shard_map/pallas_call | solution.py:148
  24.4 2.9 %collective-permute-start = (bf16[64,512]{1,0:T(8,128)(2,1)}, bf16[64,512]{1,0:T(8,128)(2,1)S(1)}, u32[]{:S(2)}, u32[]{:S(2)}) collective-permute-start(bf16[64,512]{1,0:T(8,128)(2,1)} %get-tuple-element.30), channel_id=1, source_target_pairs={{0,8},{1,9},{2,10},{3,11},{4,12},{5,13},{6,14},{7,15},{8,0},{9,1},... | collective-permute-start | bytes 196616 | tf_op jit(solution)/shard_map/ppermute | solution.py:349
  27.3 1.4 %collective-permute-start.1 = (bf16[64,512]{1,0:T(8,128)(2,1)}, bf16[64,512]{1,0:T(8,128)(2,1)S(1)}, u32[]{:S(2)}, u32[]{:S(2)}) collective-permute-start(bf16[64,512]{1,0:T(8,128)(2,1)} %get-tuple-element.31), channel_id=1, source_target_pairs={{0,9},{1,8},{2,11},{3,10},{4,13},{5,12},{6,15},{7,14},{8,1},{9,0},... | collective-permute-start | bytes 196616 | tf_op jit(solution)/shard_map/ppermute | solution.py:349
  28.7 3.3 %collective-permute-start.2 = (bf16[64,512]{1,0:T(8,128)(2,1)}, bf16[64,512]{1,0:T(8,128)(2,1)S(1)}, u32[]{:S(2)}, u32[]{:S(2)}) collective-permute-start(bf16[64,512]{1,0:T(8,128)(2,1)} %get-tuple-element.32), channel_id=1, source_target_pairs={{0,10},{1,11},{2,8},{3,9},{4,14},{5,15},{6,12},{7,13},{8,2},{9,3},... | collective-permute-start | bytes 196616 | tf_op jit(solution)/shard_map/ppermute | solution.py:349
  32.1 3.7 %collective-permute-start.4 = (bf16[64,512]{1,0:T(8,128)(2,1)}, bf16[64,512]{1,0:T(8,128)(2,1)S(1)}, u32[]{:S(2)}, u32[]{:S(2)}) collective-permute-start(bf16[64,512]{1,0:T(8,128)(2,1)} %get-tuple-element.38), channel_id=1, source_target_pairs={{0,12},{1,13},{2,14},{3,15},{4,8},{5,9},{6,10},{7,11},{8,4},{9,5},... | collective-permute-start | bytes 196616 | tf_op jit(solution)/shard_map/ppermute | solution.py:349
  35.8 3.7 %all-to-all-start.1 = ((bf16[8,64,512]{2,1,0:T(8,128)(2,1)}), bf16[8,64,512]{2,1,0:T(8,128)(2,1)S(1)}, u32[]{:S(2)}, u32[]{:S(2)}) async-start(bf16[8,64,512]{2,1,0:T(8,128)(2,1)} %bitcast.15), calls=%async_computation.1 | async-start | bytes 1048576 | tf_op jit(solution)/shard_map/all_to_all | solution.py:339
  40.5 2.9 %collective-permute-start.5 = (bf16[64,512]{1,0:T(8,128)(2,1)}, bf16[64,512]{1,0:T(8,128)(2,1)S(1)}, u32[]{:S(2)}, u32[]{:S(2)}) collective-permute-start(bf16[64,512]{1,0:T(8,128)(2,1)} %get-tuple-element.39), channel_id=1, source_target_pairs={{0,13},{1,12},{2,15},{3,14},{4,9},{5,8},{6,11},{7,10},{8,5},{9,4},... | collective-permute-start | bytes 196616 | tf_op jit(solution)/shard_map/ppermute | solution.py:349
  43.4 3.3 %collective-permute-start.6 = (bf16[64,512]{1,0:T(8,128)(2,1)}, bf16[64,512]{1,0:T(8,128)(2,1)S(1)}, u32[]{:S(2)}, u32[]{:S(2)}) collective-permute-start(bf16[64,512]{1,0:T(8,128)(2,1)} %get-tuple-element.40), channel_id=1, source_target_pairs={{0,14},{1,15},{2,12},{3,13},{4,10},{5,11},{6,8},{7,9},{8,6},{9,7},... | collective-permute-start | bytes 196616 | tf_op jit(solution)/shard_map/ppermute | solution.py:349
  46.6 1.5 %collective-permute-start.7 = (bf16[64,512]{1,0:T(8,128)(2,1)}, bf16[64,512]{1,0:T(8,128)(2,1)S(1)}, u32[]{:S(2)}, u32[]{:S(2)}) collective-permute-start(bf16[64,512]{1,0:T(8,128)(2,1)} %get-tuple-element.41), channel_id=1, source_target_pairs={{0,15},{1,14},{2,13},{3,12},{4,11},{5,10},{6,9},{7,8},{8,7},{9,6},... | collective-permute-start | bytes 196616 | tf_op jit(solution)/shard_map/ppermute | solution.py:349
  48.9 0.9 %collective-permute-start.9 = (bf16[384,256]{1,0:T(8,128)(2,1)S(1)}, bf16[384,256]{1,0:T(8,128)(2,1)S(1)}, u32[]{:S(2)}, u32[]{:S(2)}) collective-permute-start(bf16[384,256]{1,0:T(8,128)(2,1)S(1)} %get-tuple-element.44), channel_id=1, source_target_pairs={{4,8},{5,9},{6,10},{7,11},{8,4},{9,5},{10,6},{11,7},{20,24},{21,25... | collective-permute-start | bytes 589832 | tf_op jit(solution)/shard_map/ppermute | solution.py:379
  50.4 0.8 %collective-permute-done.6.refs_7_ = bf16[64,512]{1,0:T(8,128)(2,1)S(1)} collective-permute-done((bf16[64,512]{1,0:T(8,128)(2,1)}, bf16[64,512]{1,0:T(8,128)(2,1)S(1)}, u32[]{:S(2)}, u32[]{:S(2)}) %collective-permute-start.6) | collective-permute-done | bytes 65568 | tf_op jit(solution)/shard_map/ppermute | solution.py:349
  51.3 3.6 %collective-permute-done.7.refs_8_ = bf16[64,512]{1,0:T(8,128)(2,1)S(1)} collective-permute-done((bf16[64,512]{1,0:T(8,128)(2,1)}, bf16[64,512]{1,0:T(8,128)(2,1)S(1)}, u32[]{:S(2)}, u32[]{:S(2)}) %collective-permute-start.7) | collective-permute-done | bytes 65568 | tf_op jit(solution)/shard_map/ppermute | solution.py:349
  54.9 1.2 %shard_map.84.query_ref = bf16[1024,512]{1,0:T(8,128)(2,1)S(1)} custom-call(s32[1,1024]{1,0:T(1,128)S(1)} %reshape.126.slot_ref, bf16[512,512]{1,0:T(8,128)(2,1)S(1)} %bitcast.13, bf16[64,512]{1,0:T(8,128)(2,1)S(1)} %collective-permute-done.refs_1_, bf16[64,512]{1,0:T(8,128)(2,1)S(1)} %collective-permute-done.1.refs_2_, ...), custom_call_target="tpu_custom_call" | custom-call | flops 1073741824 | bytes 2097152 | tf_op jit(solution)/shard_map/pallas_call | solution.py:197
  56.2 1.2 %shard_map.86 = bf16[256,512]{1,0:T(8,128)(2,1)S(1)} custom-call(s32[1,32]{1,0:T(1,128)S(1)} %reduce-window_clone.1.ends_ref, bf16[1024,512]{1,0:T(8,128)(2,1)S(1)} %shard_map.84.query_ref, bf16[384,256]{1,0:T(8,128)(2,1)S(1)} %collective-permute-done.8.rest_0_, bf16[384,256]{1,0:T(8,128)(2,1)S(1)} %collective-permute-done.9.rest_1_, ...), custom_call_target="tpu_custom_call" | custom-call | flops 268435456 | bytes 1966080 | tf_op jit(solution)/shard_map/pallas_call | solution.py:281
  57.3 2.2 %collective-permute-start.10 = (bf16[256,512]{1,0:T(8,128)(2,1)S(1)}, bf16[256,512]{1,0:T(8,128)(2,1)S(1)}, u32[]{:S(2)}, u32[]{:S(2)}) collective-permute-start(bf16[256,512]{1,0:T(8,128)(2,1)S(1)} %shard_map.86), channel_id=1, source_target_pairs={{0,3},{1,2},{2,1},{3,0},{4,7},{5,6},{6,5},{7,4},{8,11},{9,10},{10,... | collective-permute-start | bytes 786440 | tf_op jit(solution)/shard_map/ppermute | solution.py:393
  59.5 1.1 %shard_map.87 = bf16[256,512]{1,0:T(8,128)(2,1)S(1)} custom-call(s32[1,32]{1,0:T(1,128)S(1)} %reduce-window_clone.1.ends_ref, bf16[1024,512]{1,0:T(8,128)(2,1)S(1)} %shard_map.84.query_ref, bf16[384,256]{1,0:T(8,128)(2,1)S(1)} %collective-permute-done.8.rest_0_, bf16[384,256]{1,0:T(8,128)(2,1)S(1)} %collective-permute-done.9.rest_1_, ...), custom_call_target="tpu_custom_call" | custom-call | flops 268435456 | bytes 1966080 | tf_op jit(solution)/shard_map/pallas_call | solution.py:281
  61.3 1.1 %shard_map.88 = bf16[256,512]{1,0:T(8,128)(2,1)S(1)} custom-call(s32[1,32]{1,0:T(1,128)S(1)} %reduce-window_clone.1.ends_ref, bf16[1024,512]{1,0:T(8,128)(2,1)S(1)} %shard_map.84.query_ref, bf16[384,256]{1,0:T(8,128)(2,1)S(1)} %collective-permute-done.8.rest_0_, bf16[384,256]{1,0:T(8,128)(2,1)S(1)} %collective-permute-done.9.rest_1_, ...), custom_call_target="tpu_custom_call" | custom-call | flops 268435456 | bytes 1966080 | tf_op jit(solution)/shard_map/pallas_call | solution.py:281
  62.4 0.9 %collective-permute-start.12 = (bf16[256,512]{1,0:T(8,128)(2,1)S(1)}, bf16[256,512]{1,0:T(8,128)(2,1)S(1)}, u32[]{:S(2)}, u32[]{:S(2)}) collective-permute-start(bf16[256,512]{1,0:T(8,128)(2,1)S(1)} %shard_map.88), channel_id=1, source_target_pairs={{0,2},{1,3},{2,0},{3,1},{4,6},{5,7},{6,4},{7,5},{8,10},{9,11},{10,... | collective-permute-start | bytes 786440 | tf_op jit(solution)/shard_map/ppermute | solution.py:393
  63.3 1.1 %shard_map.89.refs_3_ = bf16[256,512]{1,0:T(8,128)(2,1)S(1)} custom-call(s32[1,32]{1,0:T(1,128)S(1)} %reduce-window_clone.1.ends_ref, bf16[1024,512]{1,0:T(8,128)(2,1)S(1)} %shard_map.84.query_ref, bf16[384,256]{1,0:T(8,128)(2,1)S(1)} %collective-permute-done.8.rest_0_, bf16[384,256]{1,0:T(8,128)(2,1)S(1)} %collective-permute-done.9.rest_1_, ...), custom_call_target="tpu_custom_call" | custom-call | flops 268435456 | bytes 1966080 | tf_op jit(solution)/shard_map/pallas_call | solution.py:281
  64.5 1.9 %collective-permute-done.10.refs_0_ = bf16[256,512]{1,0:T(8,128)(2,1)S(1)} collective-permute-done((bf16[256,512]{1,0:T(8,128)(2,1)S(1)}, bf16[256,512]{1,0:T(8,128)(2,1)S(1)}, u32[]{:S(2)}, u32[]{:S(2)}) %collective-permute-start.10) | collective-permute-done | bytes 262176 | tf_op jit(solution)/shard_map/ppermute | solution.py:393
  66.3 4.3 %collective-permute-done.11.refs_1_ = bf16[256,512]{1,0:T(8,128)(2,1)S(1)} collective-permute-done((bf16[256,512]{1,0:T(8,128)(2,1)S(1)}, bf16[256,512]{1,0:T(8,128)(2,1)S(1)}, u32[]{:S(2)}, u32[]{:S(2)}) %collective-permute-start.11) | collective-permute-done | bytes 262176 | tf_op jit(solution)/shard_map/ppermute | solution.py:393
  70.8 1.1 %shard_map.90 = bf16[256,2048]{1,0:T(8,128)(2,1)} custom-call(bf16[256,512]{1,0:T(8,128)(2,1)S(1)} %collective-permute-done.10.refs_0_, bf16[256,512]{1,0:T(8,128)(2,1)S(1)} %collective-permute-done.11.refs_1_, bf16[256,512]{1,0:T(8,128)(2,1)S(1)} %collective-permute-done.12.refs_2_, bf16[256,512]{1,0:T(8,128)(2,1)S(1)} %shard_map.89.refs_3_), custom_call_target="tpu_custom_call" | custom-call | bytes 2097152 | tf_op jit(solution)/shard_map/pallas_call | solution.py:306
  (30 shorter events, 3.2 us)
Async XLA Ops:
  6.5 29.3 %all-to-all-start = ((bf16[16,64,256]{2,1,0:T(8,128)(2,1)}), bf16[16,64,256]{2,1,0:T(8,128)(2,1)S(1)}, u32[]{:S(2)}, u32[]{:S(2)}) async-start(bf16[16,64,256]{2,1,0:T(8,128)(2,1)} %bitcast.14), calls=%async_computation | async-start | bytes 1048576 | tf_op jit(solution)/shard_map/all_to_all | solution.py:339
  14.9 24.6 %copy-start = (s32[4096]{0:T(1024)S(1)}, s32[4096]{0:T(1024)}, u32[]{:S(2)}) copy-start(s32[4096]{0:T(1024)} %param.9) | copy-start | bytes 49156
  14.9 25.3 %copy-start.1 = (s32[32]{0:T(128)S(1)}, s32[32]{0:T(128)}, u32[]{:S(2)}) copy-start(s32[32]{0:T(128)} %param.10) | copy-start | bytes 388
  24.4 16.1 %collective-permute-start = (bf16[64,512]{1,0:T(8,128)(2,1)}, bf16[64,512]{1,0:T(8,128)(2,1)S(1)}, u32[]{:S(2)}, u32[]{:S(2)}) collective-permute-start(bf16[64,512]{1,0:T(8,128)(2,1)} %get-tuple-element.30), channel_id=1, source_target_pairs={{0,8},{1,9},{2,10},{3,11},{4,12},{5,13},{6,14},{7,15},{8,0},{9,1},... | collective-permute-start | bytes 196616 | tf_op jit(solution)/shard_map/ppermute | solution.py:349
  27.3 16.1 %collective-permute-start.1 = (bf16[64,512]{1,0:T(8,128)(2,1)}, bf16[64,512]{1,0:T(8,128)(2,1)S(1)}, u32[]{:S(2)}, u32[]{:S(2)}) collective-permute-start(bf16[64,512]{1,0:T(8,128)(2,1)} %get-tuple-element.31), channel_id=1, source_target_pairs={{0,9},{1,8},{2,11},{3,10},{4,13},{5,12},{6,15},{7,14},{8,1},{9,0},... | collective-permute-start | bytes 196616 | tf_op jit(solution)/shard_map/ppermute | solution.py:349
  28.7 17.9 %collective-permute-start.2 = (bf16[64,512]{1,0:T(8,128)(2,1)}, bf16[64,512]{1,0:T(8,128)(2,1)S(1)}, u32[]{:S(2)}, u32[]{:S(2)}) collective-permute-start(bf16[64,512]{1,0:T(8,128)(2,1)} %get-tuple-element.32), channel_id=1, source_target_pairs={{0,10},{1,11},{2,8},{3,9},{4,14},{5,15},{6,12},{7,13},{8,2},{9,3},... | collective-permute-start | bytes 196616 | tf_op jit(solution)/shard_map/ppermute | solution.py:349
  32.0 16.1 %collective-permute-start.3 = (bf16[64,512]{1,0:T(8,128)(2,1)}, bf16[64,512]{1,0:T(8,128)(2,1)S(1)}, u32[]{:S(2)}, u32[]{:S(2)}) collective-permute-start(bf16[64,512]{1,0:T(8,128)(2,1)} %get-tuple-element.33), channel_id=1, source_target_pairs={{0,11},{1,10},{2,9},{3,8},{4,15},{5,14},{6,13},{7,12},{8,3},{9,2},... | collective-permute-start | bytes 196616 | tf_op jit(solution)/shard_map/ppermute | solution.py:349
  32.1 16.8 %collective-permute-start.4 = (bf16[64,512]{1,0:T(8,128)(2,1)}, bf16[64,512]{1,0:T(8,128)(2,1)S(1)}, u32[]{:S(2)}, u32[]{:S(2)}) collective-permute-start(bf16[64,512]{1,0:T(8,128)(2,1)} %get-tuple-element.38), channel_id=1, source_target_pairs={{0,12},{1,13},{2,14},{3,15},{4,8},{5,9},{6,10},{7,11},{8,4},{9,5},... | collective-permute-start | bytes 196616 | tf_op jit(solution)/shard_map/ppermute | solution.py:349
  35.8 19.0 %all-to-all-start.1 = ((bf16[8,64,512]{2,1,0:T(8,128)(2,1)}), bf16[8,64,512]{2,1,0:T(8,128)(2,1)S(1)}, u32[]{:S(2)}, u32[]{:S(2)}) async-start(bf16[8,64,512]{2,1,0:T(8,128)(2,1)} %bitcast.15), calls=%async_computation.1 | async-start | bytes 1048576 | tf_op jit(solution)/shard_map/all_to_all | solution.py:339
  40.5 10.0 %collective-permute-start.5 = (bf16[64,512]{1,0:T(8,128)(2,1)}, bf16[64,512]{1,0:T(8,128)(2,1)S(1)}, u32[]{:S(2)}, u32[]{:S(2)}) collective-permute-start(bf16[64,512]{1,0:T(8,128)(2,1)} %get-tuple-element.39), channel_id=1, source_target_pairs={{0,13},{1,12},{2,15},{3,14},{4,9},{5,8},{6,11},{7,10},{8,5},{9,4},... | collective-permute-start | bytes 196616 | tf_op jit(solution)/shard_map/ppermute | solution.py:349
  43.4 7.9 %collective-permute-start.6 = (bf16[64,512]{1,0:T(8,128)(2,1)}, bf16[64,512]{1,0:T(8,128)(2,1)S(1)}, u32[]{:S(2)}, u32[]{:S(2)}) collective-permute-start(bf16[64,512]{1,0:T(8,128)(2,1)} %get-tuple-element.40), channel_id=1, source_target_pairs={{0,14},{1,15},{2,12},{3,13},{4,10},{5,11},{6,8},{7,9},{8,6},{9,7},... | collective-permute-start | bytes 196616 | tf_op jit(solution)/shard_map/ppermute | solution.py:349
  46.6 8.2 %collective-permute-start.7 = (bf16[64,512]{1,0:T(8,128)(2,1)}, bf16[64,512]{1,0:T(8,128)(2,1)S(1)}, u32[]{:S(2)}, u32[]{:S(2)}) collective-permute-start(bf16[64,512]{1,0:T(8,128)(2,1)} %get-tuple-element.41), channel_id=1, source_target_pairs={{0,15},{1,14},{2,13},{3,12},{4,11},{5,10},{6,9},{7,8},{8,7},{9,6},... | collective-permute-start | bytes 196616 | tf_op jit(solution)/shard_map/ppermute | solution.py:349
  48.8 7.3 %collective-permute-start.8 = (bf16[384,256]{1,0:T(8,128)(2,1)S(1)}, bf16[384,256]{1,0:T(8,128)(2,1)S(1)}, u32[]{:S(2)}, u32[]{:S(2)}) collective-permute-start(bf16[384,256]{1,0:T(8,128)(2,1)S(1)} %get-tuple-element.43), channel_id=1, source_target_pairs={{0,4},{1,5},{2,6},{3,7},{8,12},{9,13},{10,14},{11,15},{4,0},{5,1},... | collective-permute-start | bytes 589832 | tf_op jit(solution)/shard_map/ppermute | solution.py:379
  48.9 7.2 %collective-permute-start.9 = (bf16[384,256]{1,0:T(8,128)(2,1)S(1)}, bf16[384,256]{1,0:T(8,128)(2,1)S(1)}, u32[]{:S(2)}, u32[]{:S(2)}) collective-permute-start(bf16[384,256]{1,0:T(8,128)(2,1)S(1)} %get-tuple-element.44), channel_id=1, source_target_pairs={{4,8},{5,9},{6,10},{7,11},{8,4},{9,5},{10,6},{11,7},{20,24},{21,25... | collective-permute-start | bytes 589832 | tf_op jit(solution)/shard_map/ppermute | solution.py:379
  57.3 9.0 %collective-permute-start.10 = (bf16[256,512]{1,0:T(8,128)(2,1)S(1)}, bf16[256,512]{1,0:T(8,128)(2,1)S(1)}, u32[]{:S(2)}, u32[]{:S(2)}) collective-permute-start(bf16[256,512]{1,0:T(8,128)(2,1)S(1)} %shard_map.86), channel_id=1, source_target_pairs={{0,3},{1,2},{2,1},{3,0},{4,7},{5,6},{6,5},{7,4},{8,11},{9,10},{10,... | collective-permute-start | bytes 786440 | tf_op jit(solution)/shard_map/ppermute | solution.py:393
  60.7 10.0 %collective-permute-start.11 = (bf16[256,512]{1,0:T(8,128)(2,1)S(1)}, bf16[256,512]{1,0:T(8,128)(2,1)S(1)}, u32[]{:S(2)}, u32[]{:S(2)}) collective-permute-start(bf16[256,512]{1,0:T(8,128)(2,1)S(1)} %shard_map.87), channel_id=1, source_target_pairs={{0,1},{1,0},{2,3},{3,2},{4,5},{5,4},{6,7},{7,6},{8,9},{9,8},{10,11... | collective-permute-start | bytes 786440 | tf_op jit(solution)/shard_map/ppermute | solution.py:393
  62.4 8.3 %collective-permute-start.12 = (bf16[256,512]{1,0:T(8,128)(2,1)S(1)}, bf16[256,512]{1,0:T(8,128)(2,1)S(1)}, u32[]{:S(2)}, u32[]{:S(2)}) collective-permute-start(bf16[256,512]{1,0:T(8,128)(2,1)S(1)} %shard_map.88), channel_id=1, source_target_pairs={{0,2},{1,3},{2,0},{3,1},{4,6},{5,7},{6,4},{7,5},{8,10},{9,11},{10,... | collective-permute-start | bytes 786440 | tf_op jit(solution)/shard_map/ppermute | solution.py:393
